TPU v7x, 32 devices: a whole 2x2x4 slice. The times are simulated.
32 devices in a mesh: expert: 16 (over z, y, x), tensor: 2 (over core).
Axes of the slice: x: 2, y: 2, z: 4, core: 2. Of those that a mesh axis runs over, the one named last changes fastest.
Arguments:
- tokens: bfloat16 [2048, 2048], P(('expert', 'tensor')), may hold values from -40 to 40
- cotangent: bfloat16 [2048, 2048], P(('expert', 'tensor')), may hold values from -32 to 32
- gain: float32 [2048], replicated, may hold values from 0.1 to 1.9
- expert_ids: int32 [2048, 8], P('expert'), may hold values from 0 to 31, all different within a row; in each aligned block of 128 rows (0 to 127, 128 to 255, ...) at most 48 rows name the same one
- gate_probs: float32 [2048, 8], P('expert'), may hold values from 0.05 to 0.3
- gate_up_weight: bfloat16 [32, 2048, 1536], P(('expert', 'tensor')), may hold values from -0.125 to 0.125
- down_weight: bfloat16 [32, 768, 2048], P(('expert', 'tensor')), may hold values from -0.21875 to 0.21875
Outputs:
- mixed: bfloat16 [2048, 2048], P(('expert', 'tensor'))
- token_grad: bfloat16 [2048, 2048], P(('expert', 'tensor'))
- prob_grad: float32 [2048, 8], P(('expert', 'tensor'))
- gain_grad: float32 [2048], replicated
- gate_up_grad: bfloat16 [32, 2048, 1536], P(('expert', 'tensor'))
- down_grad: bfloat16 [32, 768, 2048], P(('expert', 'tensor'))
Inputs may be any that keep to these rules, and one draw needn't show every extreme that they name: `expert_ids`: in each aligned block of 128 rows, the tokens of one index of the expert axis, no expert is named by more than 48 rows.
All inputs are finite; a program needn't handle non-finite values.
Results may differ from a plain program's by a relative error of at most 0.009.
Values may be sent and summed in bfloat16 or wider, within the bound.
No kernel may reach another device: no remote copies, remote signals or barrier semaphores. Data moves between devices by JAX's collectives and lax.ppermute only.
A program may use at most 128 MiB of HBM per device.

v0:
```python
import jax
import jax.numpy as jnp
from jax import lax
from jax.sharding import PartitionSpec as P

TOP = 8
EXP_DEV = 2


def normalize(rows):
    values = rows.astype(jnp.float32)
    inv_rms = lax.rsqrt(jnp.mean(values * values, axis=1, keepdims=True) + 1e-06)
    return (values * inv_rms, inv_rms)


def expert_forward(rows, gate_up, down_proj):
    projected = jnp.dot(rows, gate_up, preferred_element_type=jnp.float32)
    half_width = down_proj.shape[0]
    gate_pre = projected[:, :half_width]
    up_pre = projected[:, half_width:]
    sigmoid_gate = jax.nn.sigmoid(gate_pre)
    hidden = (gate_pre * sigmoid_gate * up_pre).astype(jnp.bfloat16)
    block_out = jnp.dot(hidden, down_proj, preferred_element_type=jnp.float32).astype(jnp.bfloat16)
    return (gate_pre, up_pre, sigmoid_gate, hidden, block_out)


def expert_backward(rows, slot_grads, gate_up, down_proj, gate_pre, up_pre, sigmoid_gate, hidden):
    hidden_grad = lax.dot_general(
        slot_grads, down_proj, (((1,), (1,)), ((), ())), preferred_element_type=jnp.float32
    )
    gate_grad = (
        hidden_grad * up_pre * sigmoid_gate * (1.0 + gate_pre * (1.0 - sigmoid_gate))
    ).astype(jnp.bfloat16)
    up_grad = (hidden_grad * gate_pre * sigmoid_gate).astype(jnp.bfloat16)
    joined_grad = jnp.concatenate([gate_grad, up_grad], axis=1)
    down_part = lax.dot_general(
        hidden, slot_grads, (((0,), (0,)), ((), ())), preferred_element_type=jnp.float32
    ).astype(jnp.bfloat16)
    gate_up_part = lax.dot_general(
        rows, joined_grad, (((0,), (0,)), ((), ())), preferred_element_type=jnp.float32
    ).astype(jnp.bfloat16)
    input_grad = lax.dot_general(
        joined_grad, gate_up, (((1,), (1,)), ((), ())), preferred_element_type=jnp.float32
    ).astype(jnp.bfloat16)
    return (input_grad, gate_up_part, down_part)


def shards(tokens, cotangent, gain, expert_ids, gate_probs, gate_up_weight, down_weight):
    tensor_size = lax.axis_size("tensor")
    expert_size = lax.axis_size("expert")
    my_rank = lax.axis_index("tensor")
    blocks_each = tensor_size // EXP_DEV
    my_type = my_rank // blocks_each
    group_rows = expert_ids.shape[0]
    features = tokens.shape[1]
    capacity = 3 * group_rows * TOP // (2 * EXP_DEV * expert_size)
    highest = lax.Precision.HIGHEST
    scaled_own, inv_own = normalize(tokens)
    carried = (scaled_own * gain[None, :]).astype(jnp.bfloat16)
    group_first, group_grads = (
        lax.all_gather(carried, "tensor", axis=0, tiled=True),
        lax.all_gather(cotangent, "tensor", axis=0, tiled=True),
    )
    targets = jnp.arange(expert_size, dtype=jnp.int32) * EXP_DEV + my_type
    matches = expert_ids[:, :, None] == targets[None, None, :]
    chosen = jnp.any(matches, axis=1)
    weight_of = jnp.sum(jnp.where(matches, gate_probs[:, :, None], 0.0), axis=1)
    slot_of = jnp.sum(
        jnp.where(matches, jnp.arange(TOP, dtype=jnp.int32)[None, :, None], 0), axis=1
    )
    row_ids = jnp.arange(group_rows, dtype=jnp.int32)
    earlier = (row_ids[None, :] < row_ids[:, None]).astype(jnp.bfloat16)
    rank_in = jnp.dot(
        earlier, chosen.astype(jnp.bfloat16), preferred_element_type=jnp.float32
    ).astype(jnp.int32)
    placed = chosen.T[:, None, :] & (
        rank_in.T[:, None, :] == jnp.arange(capacity, dtype=jnp.int32)[None, :, None]
    )
    source = jnp.sum(jnp.where(placed, row_ids[None, None, :], 0), axis=2)
    filled = jnp.any(placed, axis=2)
    slot_prob = jnp.sum(jnp.where(placed, weight_of.T[:, None, :], 0.0), axis=2)
    slot_index = jnp.sum(jnp.where(placed, slot_of.T[:, None, :], 0), axis=2)
    sent_rows = jnp.where(
        filled[:, :, None], jnp.take(group_first, source, axis=0), jnp.zeros((), jnp.bfloat16)
    )
    sent_grads = (
        slot_prob[:, :, None] * jnp.take(group_grads, source, axis=0).astype(jnp.float32)
    ).astype(jnp.bfloat16)
    gate_up = gate_up_weight[0]
    down_proj = down_weight[0]
    arrived_rows, arrived_grads = (
        lax.all_to_all(sent_rows, "expert", split_axis=0, concat_axis=0, tiled=True),
        lax.all_to_all(sent_grads, "expert", split_axis=0, concat_axis=0, tiled=True),
    )
    rows = arrived_rows.reshape(-1, features)
    slot_grads = arrived_grads.reshape(-1, features)
    gate_pre, up_pre, sigmoid_gate, hidden, block_out = expert_forward(rows, gate_up, down_proj)
    out_slots = block_out.reshape(expert_size, capacity, features)
    input_grad, gate_up_part, down_part = expert_backward(
        rows, slot_grads, gate_up, down_proj, gate_pre, up_pre, sigmoid_gate, hidden
    )
    input_slots = input_grad.reshape(expert_size, capacity, features)
    out_back, input_back = (
        lax.all_to_all(out_slots, "expert", split_axis=0, concat_axis=0, tiled=True),
        lax.all_to_all(input_slots, "expert", split_axis=0, concat_axis=0, tiled=True),
    )
    out_flat = out_back.reshape(-1, features)
    input_flat = input_back.reshape(-1, features)
    used_source = source.reshape(-1)
    used_filled = filled.reshape(-1)
    used_prob = slot_prob.reshape(-1)
    used_index = slot_index.reshape(-1)
    cot_slots = jnp.take(group_grads, used_source, axis=0)
    prob_values = jnp.einsum("sd,sd->s", cot_slots, out_flat, preferred_element_type=jnp.float32)
    hit = (row_ids[:, None] == used_source[None, :]) & used_filled[None, :]
    input_part = jnp.dot(hit.astype(jnp.bfloat16), input_flat, preferred_element_type=jnp.float32)
    weighting = jnp.where(hit, used_prob[None, :], 0.0)
    out_part = jnp.dot(
        weighting,
        out_flat.astype(jnp.float32),
        precision=highest,
        preferred_element_type=jnp.float32,
    )
    prob_columns = jnp.where(
        used_index[:, None] == jnp.arange(TOP, dtype=jnp.int32)[None, :], prob_values[:, None], 0.0
    )
    prob_part = jnp.dot(
        hit.astype(jnp.float32), prob_columns, precision=highest, preferred_element_type=jnp.float32
    )
    out_sum, normed_grad, prob_grad = (
        lax.psum_scatter(out_part, "tensor", scatter_dimension=0, tiled=True),
        lax.psum_scatter(input_part, "tensor", scatter_dimension=0, tiled=True),
        lax.psum_scatter(prob_part, "tensor", scatter_dimension=0, tiled=True),
    )
    mixed = (tokens.astype(jnp.float32) + out_sum).astype(jnp.bfloat16)
    gain_side = normed_grad * gain[None, :]
    token_grad = (
        cotangent.astype(jnp.float32)
        + inv_own
        * (gain_side - scaled_own * jnp.mean(gain_side * scaled_own, axis=1, keepdims=True))
    ).astype(jnp.bfloat16)
    gain_grad = lax.psum(jnp.sum(normed_grad * scaled_own, axis=0), ("expert", "tensor"))
    return (mixed, token_grad, prob_grad, gain_grad, gate_up_part[None], down_part[None])


def solution(mesh):
    in_specs = (
        P(("expert", "tensor"), None),
        P(("expert", "tensor"), None),
        P(),
        P("expert", None),
        P("expert", None),
        P(("expert", "tensor"), None, None),
        P(("expert", "tensor"), None, None),
    )
    out_specs = (
        P(("expert", "tensor"), None),
        P(("expert", "tensor"), None),
        P(("expert", "tensor"), None),
        P(),
        P(("expert", "tensor"), None, None),
        P(("expert", "tensor"), None, None),
    )
    return jax.shard_map(shards, mesh=mesh, in_specs=in_specs, out_specs=out_specs, check_vma=False)
```

profile of v0, /device:TPU:0, one launch (start us, length us, event | category | flops | bytes accessed | tf_op | source)
XLA Modules:
  0.0 419.2 jit_solution(12232638008321275434)
XLA Ops:
  12.3 2.4 all_gather.6
  14.8 8.2 %gather_fusion.1 = bf16[768,2048]{1,0:T(8,128)(2,1)} fusion(bf16[128,2048]{1,0:T(8,128)(2,1)} %all_gather.6, s32[1024]{0:T(1024)S(1)} %pad_clamp_fusion.1), kind=kCustom, calls=%fused_computation.clone | custom fusion | bytes 6294528 | tf_op jit(solution)/shard_map/jit(_take)/gather | solution.py:84
  23.0 3.3 select_select_fusion
  26.3 8.4 %all-to-all-start = ((bf16[16,48,2048]{2,1,0:T(8,128)(2,1)}), bf16[16,48,2048]{2,1,0:T(8,128)(2,1)}, u32[]{:S(2)}, u32[]{:S(2)}) async-start(bf16[16,48,2048]{2,1,0:T(8,128)(2,1)} %select_select_fusion), calls=%async_computation | async-start | bytes 6291456 | tf_op jit(solution)/shard_map/all_to_all | solution.py:92
  37.0 8.2 %gather_fusion.2 = bf16[768,2048]{1,0:T(8,128)(2,1)} fusion(bf16[128,2048]{1,0:T(8,128)(2,1)} %all_gather.7, s32[1024]{0:T(1024)S(1)} %pad_clamp_fusion.1), kind=kCustom, calls=%fused_computation.1.clone | custom fusion | bytes 6294528 | tf_op jit(solution)/shard_map/jit(_take)/gather | solution.py:87
  45.5 4.4 %multiply_convert_fusion = bf16[16,48,2048]{2,1,0:T(8,128)(2,1)} fusion(bf16[16,48,2048]{2,1,0:T(8,128)(2,1)} %bitcast.41, f32[16,48]{1,0:T(8,128)S(1)} %select_reduce_fusion.1, pred[16,48]{1,0:T(8,128)(4,1)S(1)} %compare_and_fusion), kind=kLoop, calls=%fused_computation.11 | loop fusion | flops 6291456 | bytes 6295296 | tf_op jit(solution)/shard_map/convert_element_type | solution.py:88
  49.9 46.0 %all-to-all-done = bf16[16,48,2048]{2,1,0:T(8,128)(2,1)} async-done(((bf16[16,48,2048]{2,1,0:T(8,128)(2,1)}), bf16[16,48,2048]{2,1,0:T(8,128)(2,1)}, u32[]{:S(2)}, u32[]{:S(2)}) %all-to-all-start) | async-done | bytes 3145760 | tf_op jit(solution)/shard_map/all_to_all | solution.py:92
  96.0 15.7 %all-to-all-start.2 = ((bf16[16,48,2048]{2,1,0:T(8,128)(2,1)}), bf16[16,48,2048]{2,1,0:T(8,128)(2,1)}, u32[]{:S(2)}, u32[]{:S(2)}) async-start(bf16[16,48,2048]{2,1,0:T(8,128)(2,1)} %multiply_convert_fusion), calls=%async_computation.3 | async-start | bytes 6291456 | tf_op jit(solution)/shard_map/all_to_all | solution.py:93
  111.6 9.5 %fusion.4 = f32[768,1536]{1,0:T(8,128)} fusion(bf16[768,2048]{1,0:T(8,128)(2,1)} %bitcast.3, bf16[1,2048,1536]{2,1,0:T(8,128)(2,1)} %param.14), kind=kOutput, calls=%fused_computation.9 | convolution fusion | flops 4831838208 | bytes 14155776 | tf_op jit(solution)/shard_map/dot_general | solution.py:17
  121.1 51.3 %all-to-all-done.2 = bf16[16,48,2048]{2,1,0:T(8,128)(2,1)} async-done(((bf16[16,48,2048]{2,1,0:T(8,128)(2,1)}), bf16[16,48,2048]{2,1,0:T(8,128)(2,1)}, u32[]{:S(2)}, u32[]{:S(2)}) %all-to-all-start.2) | async-done | bytes 3145760 | tf_op jit(solution)/shard_map/all_to_all | solution.py:93
  172.4 8.1 %multiply_convert_fusion.2 = (bf16[768,768]{1,0:T(8,128)(2,1)}, bf16[768,768]{1,0:T(8,128)(2,1)}, bf16[768,768]{1,0:T(8,128)(2,1)S(1)}) fusion(f32[768,1536]{1,0:T(8,128)} %fusion.4, bf16[768,2048]{1,0:T(8,128)(2,1)} %bitcast.9, bf16[1,768,2048]{2,1,0:T(8,128)(2,1)S(1)} %copy-done), kind=kOutput, calls=%fused_computation.22 | convolution fusion | flops 2425356288 | bytes 14548992 | tf_op jit(solution)/shard_map/dot_general | solution.py:28
  180.5 4.0 convolution_convert_fusion.2
  184.5 14.1 %all-to-all-start.1 = ((bf16[16,48,2048]{2,1,0:T(8,128)(2,1)}), bf16[16,48,2048]{2,1,0:T(8,128)(2,1)S(1)}, u32[]{:S(2)}, u32[]{:S(2)}) async-start(bf16[16,48,2048]{2,1,0:T(8,128)(2,1)} %bitcast.44), calls=%async_computation.1 | async-start | bytes 6291456 | tf_op jit(solution)/shard_map/all_to_all | solution.py:104
  198.6 9.0 %fusion.6 = bf16[768,2048]{1,0:T(8,128)(2,1)} fusion(bf16[1,2048,1536]{2,1,0:T(8,128)(2,1)} %param.14, bf16[768,768]{1,0:T(8,128)(2,1)} %get-tuple-element.12, bf16[768,768]{1,0:T(8,128)(2,1)} %get-tuple-element.11), kind=kOutput, calls=%fused_computation.14 | convolution fusion | flops 4838129664 | bytes 11796480 | tf_op jit(solution)/shard_map/dot_general | solution.py:42
  207.6 51.6 %all-to-all-done.1 = bf16[16,48,2048]{2,1,0:T(8,128)(2,1)S(1)} async-done(((bf16[16,48,2048]{2,1,0:T(8,128)(2,1)}), bf16[16,48,2048]{2,1,0:T(8,128)(2,1)S(1)}, u32[]{:S(2)}, u32[]{:S(2)}) %all-to-all-start.1) | async-done | bytes 3145760 | tf_op jit(solution)/shard_map/all_to_all | solution.py:104
  260.9 14.2 %all-to-all-start.3 = ((bf16[16,48,2048]{2,1,0:T(8,128)(2,1)}), bf16[16,48,2048]{2,1,0:T(8,128)(2,1)}, u32[]{:S(2)}, u32[]{:S(2)}) async-start(bf16[16,48,2048]{2,1,0:T(8,128)(2,1)} %bitcast.43), calls=%async_computation.4 | async-start | bytes 6291456 | tf_op jit(solution)/shard_map/all_to_all | solution.py:105
  275.4 4.2 %gather_fusion = bf16[768,2048]{1,0:T(8,128)(2,1)} fusion(bf16[128,2048]{1,0:T(8,128)(2,1)S(1)} %copy-done.2, s32[1024]{0:T(1024)S(1)} %pad_clamp_fusion), kind=kCustom, calls=%fused_computation.2 | custom fusion | bytes 6294528 | tf_op jit(solution)/shard_map/jit(_take)/gather | solution.py:113
  279.8 4.0 fusion.1
  285.0 50.7 %all-to-all-done.3 = bf16[16,48,2048]{2,1,0:T(8,128)(2,1)} async-done(((bf16[16,48,2048]{2,1,0:T(8,128)(2,1)}), bf16[16,48,2048]{2,1,0:T(8,128)(2,1)}, u32[]{:S(2)}, u32[]{:S(2)}) %all-to-all-start.3) | async-done | bytes 3145760 | tf_op jit(solution)/shard_map/all_to_all | solution.py:105
  335.8 3.4 fusion.32
  339.6 2.4 fusion.28
  342.1 6.7 %fusion.12 = bf16[1,768,2048]{2,1,0:T(8,128)(2,1)} fusion(bf16[768,768]{1,0:T(8,128)(2,1)} %copy-done.10, bf16[768,2048]{1,0:T(8,128)(2,1)} %bitcast.9), kind=kOutput, calls=%fused_computation.19 | convolution fusion | flops 2417491968 | bytes 7471104 | tf_op jit(solution)/shard_map/dot_general | solution.py:36
  348.8 9.3 %fusion = bf16[1,2048,1536]{2,1,0:T(8,128)(2,1)} fusion(bf16[768,2048]{1,0:T(8,128)(2,1)} %bitcast.3, bf16[768,768]{1,0:T(8,128)(2,1)S(1)} %copy-done.12, bf16[768,768]{1,0:T(8,128)(2,1)S(1)} %copy-done.11), kind=kOutput, calls=%fused_computation.4 | convolution fusion | flops 4839702528 | bytes 11796480 | tf_op jit(solution)/shard_map/dot_general | solution.py:39
  360.9 49.5 %psum.7 = f32[2048]{0:T(1024)} all-reduce(f32[2048]{0:T(1024)S(1)} %get-tuple-element.7), channel_id=1, replica_groups=mesh['expert'=16,'tensor'=2] {'expert','tensor'}, use_global_device_ids=true, to_apply=%region_13.15 | all-reduce | flops 2048 | bytes 16384 | tf_op jit(solution)/shard_map/psum | solution.py:142
  (64 shorter events, 16.5 us)
Async XLA Ops:
  7.2 165.2 %copy-start = (bf16[1,768,2048]{2,1,0:T(8,128)(2,1)S(1)}, bf16[1,768,2048]{2,1,0:T(8,128)(2,1)}, u32[]{:S(2)}) copy-start(bf16[1,768,2048]{2,1,0:T(8,128)(2,1)} %param.15) | copy-start | bytes 9437188
  26.3 8.4 %copy-start.6 = (bf16[64,2048]{1,0:T(8,128)(2,1)S(1)}, bf16[64,2048]{1,0:T(8,128)(2,1)}, u32[]{:S(2)}) copy-start(bf16[64,2048]{1,0:T(8,128)(2,1)} %param.10) | copy-start | bytes 786436
  26.3 69.7 %all-to-all-start = ((bf16[16,48,2048]{2,1,0:T(8,128)(2,1)}), bf16[16,48,2048]{2,1,0:T(8,128)(2,1)}, u32[]{:S(2)}, u32[]{:S(2)}) async-start(bf16[16,48,2048]{2,1,0:T(8,128)(2,1)} %select_select_fusion), calls=%async_computation | async-start | bytes 6291456 | tf_op jit(solution)/shard_map/all_to_all | solution.py:92
  37.0 8.2 %copy-start.8 = (s32[128,8]{0,1:T(8,128)S(1)}, s32[128,8]{0,1:T(8,128)}, u32[]{:S(2)}) copy-start(s32[128,8]{0,1:T(8,128)} %param.12) | copy-start | bytes 12292
  37.0 8.2 %copy-start.9 = (f32[128,8]{0,1:T(8,128)S(1)}, f32[128,8]{0,1:T(8,128)}, u32[]{:S(2)}) copy-start(f32[128,8]{0,1:T(8,128)} %param.13) | copy-start | bytes 12292
  96.0 76.4 %all-to-all-start.2 = ((bf16[16,48,2048]{2,1,0:T(8,128)(2,1)}), bf16[16,48,2048]{2,1,0:T(8,128)(2,1)}, u32[]{:S(2)}, u32[]{:S(2)}) async-start(bf16[16,48,2048]{2,1,0:T(8,128)(2,1)} %multiply_convert_fusion), calls=%async_computation.3 | async-start | bytes 6291456 | tf_op jit(solution)/shard_map/all_to_all | solution.py:93
  180.5 4.0 copy-start.10
  184.5 74.7 %all-to-all-start.1 = ((bf16[16,48,2048]{2,1,0:T(8,128)(2,1)}), bf16[16,48,2048]{2,1,0:T(8,128)(2,1)S(1)}, u32[]{:S(2)}, u32[]{:S(2)}) async-start(bf16[16,48,2048]{2,1,0:T(8,128)(2,1)} %bitcast.44), calls=%async_computation.1 | async-start | bytes 6291456 | tf_op jit(solution)/shard_map/all_to_all | solution.py:104
  259.2 1.7 copy-start.3
  260.9 14.6 %copy-start.2 = (bf16[128,2048]{1,0:T(8,128)(2,1)S(1)}, bf16[128,2048]{1,0:T(8,128)(2,1)}, u32[]{:S(2)}) copy-start(bf16[128,2048]{1,0:T(8,128)(2,1)} %all_gather.7) | copy-start | bytes 1572868
  260.9 74.9 %all-to-all-start.3 = ((bf16[16,48,2048]{2,1,0:T(8,128)(2,1)}), bf16[16,48,2048]{2,1,0:T(8,128)(2,1)}, u32[]{:S(2)}, u32[]{:S(2)}) async-start(bf16[16,48,2048]{2,1,0:T(8,128)(2,1)} %bitcast.43), calls=%async_computation.4 | async-start | bytes 6291456 | tf_op jit(solution)/shard_map/all_to_all | solution.py:105
  275.1 83.0 %reduce-scatter.10.cloned.1.call-start = ((), (), s32[]{:S(2)}) async-start(), calls=%async_computation.9 | async-start | bytes 98304
  283.8 55.8 %copy-start.4 = (bf16[16,48,2048]{2,1,0:T(8,128)(2,1)S(1)}, bf16[16,48,2048]{2,1,0:T(8,128)(2,1)}, u32[]{:S(2)}) copy-start(bf16[16,48,2048]{2,1,0:T(8,128)(2,1)} %copy-done.3) | copy-start | bytes 9437188
  285.0 74.5 %reduce-scatter.8.cloned.1.call-start = ((), (), s32[]{:S(2)}) async-start(), calls=%async_computation.8 | async-start | bytes 1572864 | tf_op jit(solution)/shard_map/reduce_scatter | solution.py:132
  339.2 71.1 %reduce-scatter.6.cloned.1.call-start = ((), (), s32[]{:S(2)}) async-start(), calls=%async_computation.7 | async-start | bytes 1572864 | tf_op jit(solution)/shard_map/reduce_scatter | solution.py:131
  342.0 6.7 %copy-start.11 = (bf16[768,768]{1,0:T(8,128)(2,1)S(1)}, bf16[768,768]{1,0:T(8,128)(2,1)}, u32[]{:S(2)}) copy-start(bf16[768,768]{1,0:T(8,128)(2,1)} %get-tuple-element.11) | copy-start | bytes 3538948
  342.1 6.7 %copy-start.12 = (bf16[768,768]{1,0:T(8,128)(2,1)S(1)}, bf16[768,768]{1,0:T(8,128)(2,1)}, u32[]{:S(2)}) copy-start(bf16[768,768]{1,0:T(8,128)(2,1)} %get-tuple-element.12) | copy-start | bytes 3538948
  348.8 10.7 %copy-start.5 = (bf16[64,2048]{1,0:T(8,128)(2,1)S(1)}, bf16[64,2048]{1,0:T(8,128)(2,1)}, u32[]{:S(2)}) copy-start(bf16[64,2048]{1,0:T(8,128)(2,1)} %param.9) | copy-start | bytes 786436
  348.8 10.7 %copy-start.7 = (f32[2048]{0:T(1024)S(1)}, f32[2048]{0:T(1024)}, u32[]{:S(2)}) copy-start(f32[2048]{0:T(1024)} %param.11) | copy-start | bytes 24580
  348.8 63.9 %copy-start.1 = (bf16[1,768,2048]{2,1,0:T(8,128)(2,1)S(1)}, bf16[1,768,2048]{2,1,0:T(8,128)(2,1)}, u32[]{:S(2)}) copy-start(bf16[1,768,2048]{2,1,0:T(8,128)(2,1)} %param.15) | copy-start | bytes 9437188
Sparse Core Ops, SparseCore 0:
  285.1 8.6 reduce-scatter.9
  339.4 16.9 reduce-scatter.7
  358.7 9.6 reduce-scatter.5
where the time goes:
time: 420 us; the launch traced here: 419 us
  waiting for transfers between devices  200 us (48%)
  blocking collectives  54.2 us (13%)
  matrix products  53.8 us (13%)
  starting transfers between devices  52.7 us (13%)
  local copies, waits for them, and re-layouts  24.3 us (6%)
  other arithmetic  20.6 us (5%)
  between operations  13.9 us (3%)
    all_to_all x1, waiting for transfers between devices, shards(): lax.all_to_all(out_slots, 'expert', split_axis=0, concat_axis=0, tiled=True)  51.6 us
    all_to_all x1, waiting for transfers between devices, shards(): lax.all_to_all(sent_grads, 'expert', split_axis=0, concat_axis=0, tiled=T...  51.3 us
    all_to_all x1, waiting for transfers between devices, shards(): lax.all_to_all(input_slots, 'expert', split_axis=0, concat_axis=0, tiled=...  50.7 us
    psum x1, blocking collectives, shards(): lax.psum(jnp.sum(normed_grad * scaled_own, axis=0), ('expert', 'tensor'))  49.5 us
    all_to_all x1, waiting for transfers between devices, shards(): lax.all_to_all(sent_rows, 'expert', split_axis=0, concat_axis=0, tiled=True)  46 us
    all_to_all x1, starting transfers between devices, shards(): lax.all_to_all(sent_grads, 'expert', split_axis=0, concat_axis=0, tiled=T...  15.7 us
    all_to_all x1, starting transfers between devices, shards(): lax.all_to_all(input_slots, 'expert', split_axis=0, concat_axis=0, tiled=...  14.2 us
    all_to_all x1, starting transfers between devices, shards(): lax.all_to_all(out_slots, 'expert', split_axis=0, concat_axis=0, tiled=True)  14.1 us
  transfers between devices with their start and end apart: 7, of which 4 were waited for; matrix products, arithmetic and copies ran while one was open for 16% of the time, Pallas kernels for 0%

commit v1 on v0

--- a/solution.py
+++ b/solution.py
@@ -1,10 +1,15 @@
+import functools
+
 import jax
 import jax.numpy as jnp
 from jax import lax
+from jax.experimental import pallas as pl
+from jax.experimental.pallas import tpu as pltpu
 from jax.sharding import PartitionSpec as P
 
 TOP = 8
 EXP_DEV = 2
+VMEM_LIMIT = 48 * 1024 * 1024
 
 
 def normalize(rows):
@@ -45,7 +50,7 @@
     return (input_grad, gate_up_part, down_part)
 
 
-def shards(tokens, cotangent, gain, expert_ids, gate_probs, gate_up_weight, down_weight):
+def routed_shards(tokens, cotangent, gain, expert_ids, gate_probs, gate_up_weight, down_weight):
     tensor_size = lax.axis_size("tensor")
     expert_size = lax.axis_size("expert")
     my_rank = lax.axis_index("tensor")
@@ -143,6 +148,259 @@
     return (mixed, token_grad, prob_grad, gain_grad, gate_up_part[None], down_part[None])
 
 
+BOTH = ("expert", "tensor")
+
+
+def flip_first(expert, core):
+    return expert ^ (2 if core == 0 else 1)
+
+
+def flip_second(expert, core):
+    return expert ^ (1 if core == 0 else 2)
+
+
+def send(array, expert_size, place):
+    pairs = []
+    for expert in range(expert_size):
+        for core in range(2):
+            to_expert, to_core = place(expert, core)
+            pairs.append((expert * 2 + core, to_expert * 2 + to_core))
+    return lax.ppermute(array, BOTH, pairs)
+
+
+def send_first(array, expert_size):
+    return send(array, expert_size, lambda e, c: (flip_first(e, c), c))
+
+
+def send_second(array, expert_size):
+    return send(array, expert_size, lambda e, c: (flip_second(e, c), c))
+
+
+def send_core(array, expert_size):
+    return send(array, expert_size, lambda e, c: (e, 1 - c))
+
+
+def send_along(array, expert_size, step):
+    return send(array, expert_size, lambda e, c: ((e + 4 * step) % expert_size, c))
+
+
+def gather_rows(own, expert_size):
+    gathered = []
+    for step in range(expert_size // 4):
+        block = own if step == 0 else send_along(own, expert_size, -step)
+        pair = jnp.stack([block, send_second(block, expert_size)])
+        quad = jnp.concatenate([pair, send_first(pair, expert_size)])
+        gathered.append((quad, send_core(quad, expert_size)))
+    return gathered
+
+
+def add_half(left, right):
+    return (left.astype(jnp.float32) + right.astype(jnp.float32)).astype(jnp.bfloat16)
+
+
+def scatter_sum(parts, expert_size):
+    total = None
+    for step in list(range(1, expert_size // 4)) + [0]:
+        mine, other = parts[step]
+        quad = add_half(mine, send_core(other, expert_size))
+        pair = add_half(quad[:2], send_first(quad[2:], expert_size))
+        block = add_half(pair[0], send_second(pair[1], expert_size))
+        if step:
+            block = send_along(block, expert_size, step)
+        total = block.astype(jnp.float32) if total is None else total + block.astype(jnp.float32)
+    return total
+
+
+def swapped(index):
+    return (index % 2) * 2 + index // 2
+
+
+def select_norm_kernel(pick_ref, mine_ref, other_ref, gain_ref, normed_ref, scaled_ref):
+    half = mine_ref.shape[1]
+    rows = jnp.dot(pick_ref[0][:, :half], mine_ref[0], preferred_element_type=jnp.float32)
+    rows += jnp.dot(pick_ref[0][:, half:], other_ref[0], preferred_element_type=jnp.float32)
+    inv_rms = lax.rsqrt(jnp.mean(rows * rows, axis=1, keepdims=True) + 1e-06)
+    scaled = rows * inv_rms
+    scaled_ref[0] = scaled.astype(jnp.bfloat16)
+    normed_ref[0] = (scaled * gain_ref[...]).astype(jnp.bfloat16)
+
+
+def select_grad_kernel(pick_ref, mine_ref, other_ref, prob_ref, cot_ref, grad_ref):
+    half = mine_ref.shape[1]
+    rows = jnp.dot(pick_ref[0][:, :half], mine_ref[0], preferred_element_type=jnp.float32)
+    rows += jnp.dot(pick_ref[0][:, half:], other_ref[0], preferred_element_type=jnp.float32)
+    cot_ref[0] = rows.astype(jnp.bfloat16)
+    grad_ref[0] = (rows * prob_ref[0]).astype(jnp.bfloat16)
+
+
+def select(kernel, pick, mine, other, extra, extra_spec):
+    _, capacity, group_rows = pick.shape
+    half, features = mine.shape[1:]
+    out = jax.ShapeDtypeStruct((4, capacity, features), jnp.bfloat16)
+    return pl.pallas_call(
+        kernel,
+        grid=(4,),
+        in_specs=[
+            pl.BlockSpec((1, capacity, group_rows), lambda i: (i, 0, 0)),
+            pl.BlockSpec((1, half, features), lambda i: (i, 0, 0)),
+            pl.BlockSpec((1, half, features), lambda i: (swapped(i), 0, 0)),
+            extra_spec,
+        ],
+        out_specs=[pl.BlockSpec((1, capacity, features), lambda i: (i, 0, 0))] * 2,
+        out_shape=[out, out],
+        compiler_params=pltpu.CompilerParams(vmem_limit_bytes=VMEM_LIMIT),
+        cost_estimate=pl.CostEstimate(
+            flops=8 * capacity * group_rows * features,
+            bytes_accessed=16 * half * features + 16 * capacity * features,
+            transcendentals=0,
+        ),
+    )(pick, mine, other, extra)
+
+
+def expand_kernel(pick_ref, rows_ref, prob_ref, mine_ref, other_ref):
+    half = mine_ref.shape[1]
+    rows = (rows_ref[0].astype(jnp.float32) * prob_ref[0]).astype(jnp.bfloat16)
+    pick = pick_ref[0]
+    for columns, out_ref in ((pick[:, :half], mine_ref), (pick[:, half:], other_ref)):
+        out_ref[0] = lax.dot_general(
+            columns, rows, (((0,), (0,)), ((), ())), preferred_element_type=jnp.float32
+        ).astype(jnp.bfloat16)
+
+
+def expand(pick, rows, prob):
+    _, capacity, group_rows = pick.shape
+    half, features = group_rows // 2, rows.shape[2]
+    out = jax.ShapeDtypeStruct((4, half, features), jnp.bfloat16)
+    return pl.pallas_call(
+        expand_kernel,
+        grid=(4,),
+        in_specs=[
+            pl.BlockSpec((1, capacity, group_rows), lambda i: (i, 0, 0)),
+            pl.BlockSpec((1, capacity, features), lambda i: (i, 0, 0)),
+            pl.BlockSpec((1, capacity, 1), lambda i: (i, 0, 0)),
+        ],
+        out_specs=[
+            pl.BlockSpec((1, half, features), lambda i: (i, 0, 0)),
+            pl.BlockSpec((1, half, features), lambda i: (swapped(i), 0, 0)),
+        ],
+        out_shape=[out, out],
+        compiler_params=pltpu.CompilerParams(vmem_limit_bytes=VMEM_LIMIT),
+        cost_estimate=pl.CostEstimate(
+            flops=8 * capacity * group_rows * features,
+            bytes_accessed=16 * half * features + 8 * capacity * features,
+            transcendentals=0,
+        ),
+    )(pick, rows, prob)
+
+
+def broadcast_shards(tokens, cotangent, gain, expert_ids, gate_probs, gate_up_weight, down_weight):
+    expert_size = lax.axis_size("expert")
+    steps = expert_size // 4
+    expert, core = lax.axis_index("expert"), lax.axis_index("tensor")
+    my_expert = expert * EXP_DEV + core
+    group_rows = expert_ids.shape[0]
+    half = group_rows // 2
+    features = tokens.shape[1]
+    capacity = 3 * group_rows * TOP // (2 * EXP_DEV * expert_size)
+    gate_up, down_proj = gate_up_weight[0], down_weight[0]
+
+    tables = jnp.concatenate([expert_ids.T.astype(jnp.float32), gate_probs.T])
+    tables = lax.all_gather(tables, "expert", axis=0)
+    token_blocks = gather_rows(tokens, expert_size)
+    cot_blocks = gather_rows(cotangent, expert_size)
+
+    plane = expert % 4
+    step_ids, firsts, seconds = (
+        jnp.arange(steps)[:, None, None], jnp.arange(2)[None, :, None], jnp.arange(2)[None, None, :]
+    )
+    bits = jnp.where(core == 0, firsts * 2 + seconds, seconds * 2 + firsts)
+    group = (((expert // 4 + step_ids) % steps) * 4 + (plane ^ bits)).reshape(-1)
+    all_groups = jnp.arange(expert_size)
+    far = (all_groups % 4) ^ plane
+    place = ((all_groups // 4 - expert // 4) % steps) * 4 + jnp.where(core == 0, far, swapped(far))
+
+    near = jnp.take(tables, group, axis=0)
+    near = jnp.where(core == 0, near, jnp.roll(near, half, axis=2))
+    matches = near[:, :TOP] == my_expert.astype(jnp.float32)
+    chosen = jnp.any(matches, axis=1)
+    weight_of = jnp.sum(jnp.where(matches, near[:, TOP:], 0.0), axis=1)
+    row_ids = jnp.arange(group_rows, dtype=jnp.int32)
+    earlier = (row_ids[:, None] < row_ids[None, :]).astype(jnp.bfloat16)
+    rank_in = jnp.dot(chosen.astype(jnp.bfloat16), earlier, preferred_element_type=jnp.float32)
+    placed = chosen[:, None, :] & (
+        rank_in.astype(jnp.int32)[:, None, :] == jnp.arange(capacity, dtype=jnp.int32)[None, :, None]
+    )
+    pick = placed.astype(jnp.bfloat16)
+    slot_prob = jnp.sum(jnp.where(placed, weight_of[:, None, :], 0.0), axis=2, keepdims=True)
+
+    def part(array, step):
+        return array[step * 4:(step + 1) * 4]
+
+    normed_rows, scaled_rows, cot_rows, slot_grads = [], [], [], []
+    for step in range(steps):
+        mine, other = token_blocks[step]
+        one, two = select(
+            select_norm_kernel, part(pick, step), mine, other, gain[None, :],
+            pl.BlockSpec((1, features), lambda i: (0, 0)),
+        )
+        normed_rows.append(one)
+        scaled_rows.append(two)
+    for step in range(steps):
+        mine, other = cot_blocks[step]
+        one, two = select(
+            select_grad_kernel, part(pick, step), mine, other, part(slot_prob, step),
+            pl.BlockSpec((1, capacity, 1), lambda i: (i, 0, 0)),
+        )
+        cot_rows.append(one)
+        slot_grads.append(two)
+    rows = jnp.concatenate(normed_rows).reshape(-1, features)
+    gate_pre, up_pre, sigmoid_gate, hidden, block_out = expert_forward(rows, gate_up, down_proj)
+    out_slots = block_out.reshape(expert_size, capacity, features)
+    out_parts = [
+        expand(part(pick, step), part(out_slots, step), part(slot_prob, step)) for step in range(steps)
+    ]
+    out_sum = scatter_sum(out_parts, expert_size)
+
+    grads = jnp.concatenate(slot_grads).reshape(-1, features)
+    input_grad, gate_up_part, down_part = expert_backward(
+        rows, grads, gate_up, down_proj, gate_pre, up_pre, sigmoid_gate, hidden
+    )
+    input_slots = input_grad.reshape(expert_size, capacity, features)
+    ones = jnp.ones_like(slot_prob)
+    input_parts = [
+        expand(part(pick, step), part(input_slots, step), part(ones, step)) for step in range(steps)
+    ]
+
+    scaled = jnp.concatenate(scaled_rows)
+    gain_term = jnp.sum(input_slots.astype(jnp.float32) * scaled.astype(jnp.float32), axis=(0, 1))
+    cots = jnp.concatenate(cot_rows)
+    prob_value = jnp.sum(cots.astype(jnp.float32) * out_slots.astype(jnp.float32), axis=2)
+    prob_rows = jnp.sum(jnp.where(placed, prob_value[:, :, None], 0.0), axis=1)
+    prob_rows = jnp.where(core == 0, prob_rows, jnp.roll(prob_rows, half, axis=1))
+    prob_rows = jnp.take(prob_rows, place, axis=0).reshape(-1)
+    terms = jnp.concatenate([prob_rows, gain_term]).reshape(-1, 128)
+    terms = lax.all_gather(terms, BOTH, axis=0)
+    terms = terms.reshape(terms.shape[0], -1)
+
+    normed_grad = scatter_sum(input_parts, expert_size)
+
+    gain_grad = jnp.sum(terms[:, expert_size * group_rows:], axis=0)
+    own_values = lax.dynamic_slice_in_dim(terms, expert * group_rows + core * half, half, axis=1)
+    own_ids = lax.dynamic_slice_in_dim(expert_ids, core * half, half, axis=0)
+    named = own_ids.T[None, :, :] == jnp.arange(terms.shape[0], dtype=jnp.int32)[:, None, None]
+    prob_grad = jnp.sum(jnp.where(named, own_values[:, None, :], 0.0), axis=0).T
+
+    scaled_own, inv_own = normalize(tokens)
+    mixed = (tokens.astype(jnp.float32) + out_sum).astype(jnp.bfloat16)
+    gain_side = normed_grad * gain[None, :]
+    token_grad = (
+        cotangent.astype(jnp.float32)
+        + inv_own
+        * (gain_side - scaled_own * jnp.mean(gain_side * scaled_own, axis=1, keepdims=True))
+    ).astype(jnp.bfloat16)
+    return (mixed, token_grad, prob_grad, gain_grad, gate_up_part[None], down_part[None])
+
+
 def solution(mesh):
     in_specs = (
         P(("expert", "tensor"), None),
@@ -161,4 +419,7 @@
         P(("expert", "tensor"), None, None),
         P(("expert", "tensor"), None, None),
     )
+    expert_size, tensor_size = mesh.shape["expert"], mesh.shape["tensor"]
+    few = tensor_size == EXP_DEV and expert_size % 4 == 0 and expert_size <= 4 * TOP
+    shards = broadcast_shards if few else routed_shards
     return jax.shard_map(shards, mesh=mesh, in_specs=in_specs, out_specs=out_specs, check_vma=False)

time: 420 us -> 407 us (0.969)
  waiting for transfers between devices: 200 us -> 120 us
  blocking collectives: 54.2 us -> 91.6 us
  Pallas kernels: 0 us -> 35.2 us
  other arithmetic: 20.6 us -> 44.9 us
  between operations: 13.9 us -> 1.76 us
  matrix products: 53.8 us -> 44.3 us
  starting transfers between devices: 52.7 us -> 46.7 us
    all_to_all x4 -> x0, waiting for transfers between devices: 200 us -> none  [the longest x1 51.6 us: shards(): lax.all_to_all(out_slots, 'expert', split_axis=0, concat_axis=0, tiled=True)]
    ppermute x0 -> x60, waiting for transfers between devices: none -> 120 us  [send(): return lax.ppermute(array, BOTH, pairs)]
    all_gather x2, blocking collectives: 4.71 us -> 91.6 us  [the longest x1 49.2 us: broadcast_shards(): tables = lax.all_gather(tables, 'expert', axis=0)]
    all_to_all x4 -> x0, starting transfers between devices: 52.4 us -> none  [the longest x1 15.7 us: shards(): lax.all_to_all(sent_grads, 'expert', split_axis=0, concat_axis=0, tiled=T...]
    psum x1 -> x0, blocking collectives: 49.5 us -> none  [shards(): lax.psum(jnp.sum(normed_grad * scaled_own, axis=0), ('expert', 'tensor'))]
    ppermute x0 -> x60, starting transfers between devices: none -> 46.7 us  [send(): return lax.ppermute(array, BOTH, pairs)]
    pallas_call x0 -> x16, Pallas kernels: none -> 35.2 us  [the longest x8 21.3 us: select(): pl.pallas_call(kernel, grid=(4,), in_specs=[pl.BlockSpec((1, capacity, gr...]
    gather x3 -> x2, local copies, waits for them, and re-layouts: 20.7 us -> 2.15 us  [the longest x1 1.46 us: broadcast_shards(): near = jnp.take(tables, group, axis=0)]
  transfers between devices with their start and end apart: 7 -> 60, of which waited for: 4 -> 22; matrix products, arithmetic and copies ran while one was open for 16% -> 16% of each run, Pallas kernels for 0% -> 8%
where the time goes in v1:
time: 407 us; the launch traced here: 405 us
  waiting for transfers between devices  120 us (29%)
  blocking collectives  91.6 us (23%)
  starting transfers between devices  46.7 us (11%)
  other arithmetic  44.9 us (11%)
  matrix products  44.3 us (11%)
  Pallas kernels  35.2 us (9%)
  local copies, waits for them, and re-layouts  20.5 us (5%)
    ppermute x60, waiting for transfers between devices, send(): return lax.ppermute(array, BOTH, pairs)  120 us
    all_gather x1, blocking collectives, broadcast_shards(): tables = lax.all_gather(tables, 'expert', axis=0)  49.2 us
    ppermute x60, starting transfers between devices, send(): return lax.ppermute(array, BOTH, pairs)  46.7 us
    all_gather x1, blocking collectives, broadcast_shards(): terms = lax.all_gather(terms, BOTH, axis=0)  42.5 us
    pallas_call x8, Pallas kernels, select(): pl.pallas_call(kernel, grid=(4,), in_specs=[pl.BlockSpec((1, capacity, gr...  21.3 us
    pallas_call x8, Pallas kernels, expand(): pl.pallas_call(expand_kernel, grid=(4,), in_specs=[pl.BlockSpec((1, capac...  13.9 us
    concatenate x8, other arithmetic, gather_rows(): quad = jnp.concatenate([pair, send_first(pair, expert_size)])  12.1 us
    convert_element_type x22, other arithmetic, add_half(): (left.astype(jnp.float32) + right.astype(jnp.float32)).astype(jnp.bfloat16)  10.6 us
  transfers between devices with their start and end apart: 60, of which 22 were waited for; matrix products, arithmetic and copies ran while one was open for 16% of the time, Pallas kernels for 8%

profile of v1, /device:TPU:0, one launch (start us, length us, event | category | flops | bytes accessed | tf_op | source)
XLA Modules:
  0.0 405.4 jit_solution(3315831425936059600)
XLA Ops:
  0.7 5.1 %collective-permute-start.33 = (bf16[64,2048]{1,0:T(8,128)(2,1)}, bf16[64,2048]{1,0:T(8,128)(2,1)}, u32[]{:S(2)}, u32[]{:S(2)}) collective-permute-start(bf16[64,2048]{1,0:T(8,128)(2,1)} %param.8), channel_id=1, source_target_pairs={{0,24},{1,25},{2,26},{3,27},{4,28},{5,29},{6,30},{7,31},{8,0},{9,1... | collective-permute-start | bytes 786440 | tf_op jit(solution)/shard_map/ppermute | solution.py:168
  10.6 49.2 %all-gather = f32[256,128]{1,0:T(8,128)} all-gather(f32[16,128]{1,0:T(8,128)S(1)} %pad_maximum_fusion.23), channel_id=2, replica_groups=mesh['expert'=16,'tensor'=2] {'expert'}, dimensions={0}, use_global_device_ids=true | all-gather | bytes 139264 | tf_op jit(solution)/shard_map/all_gather | solution.py:308
  70.7 3.8 collective-permute-start.3
  75.7 7.6 %collective-permute-done.37 = bf16[64,2048]{1,0:T(8,128)(2,1)S(1)} collective-permute-done((bf16[64,2048]{1,0:T(8,128)(2,1)}, bf16[64,2048]{1,0:T(8,128)(2,1)S(1)}, u32[]{:S(2)}, u32[]{:S(2)}) %collective-permute-start.37) | collective-permute-done | bytes 262176 | tf_op jit(solution)/shard_map/ppermute | solution.py:168
  94.7 9.1 %collective-permute-done.4 = bf16[64,2048]{1,0:T(8,128)(2,1)S(1)} collective-permute-done((bf16[64,2048]{1,0:T(8,128)(2,1)S(1)}, bf16[64,2048]{1,0:T(8,128)(2,1)S(1)}, u32[]{:S(2)}, u32[]{:S(2)}) %collective-permute-start.4) | collective-permute-done | bytes 262176 | tf_op jit(solution)/shard_map/ppermute | solution.py:168
  126.3 3.6 collective-permute-done.13
  167.2 4.5 %pad_maximum_fusion = (bf16[16,48,2048]{2,1,0:T(8,128)(2,1)}, bf16[16,48,2048]{2,1,0:T(8,128)(2,1)}) fusion(bf16[4,48,2048]{2,1,0:T(8,128)(2,1)} %copy-done.10, bf16[4,48,2048]{2,1,0:T(8,128)(2,1)S(1)} %get-tuple-element.40, bf16[4,48,2048]{2,1,0:T(8,128)(2,1)} %copy-done.12, bf16[4,48,2048]{2,1,0:T(8,128)(2,1)S(1)} %get-tuple-element.38, ...), kind=kLoop, calls=%fused_computation.15 | loop fusion | flops 9437184 | bytes 12582912 | tf_op jit(solution)/shard_map/concatenate | solution.py:356
  173.0 9.5 %fusion.5 = f32[768,1536]{1,0:T(8,128)} fusion(bf16[768,2048]{1,0:T(8,128)(2,1)} %bitcast.165, bf16[1,2048,1536]{2,1,0:T(8,128)(2,1)} %param.12), kind=kOutput, calls=%fused_computation.10 | convolution fusion | flops 4831838208 | bytes 14155776 | tf_op jit(solution)/shard_map/dot_general | solution.py:22
  187.2 4.7 %multiply_convert_fusion.1 = (bf16[768,768]{1,0:T(8,128)(2,1)}, bf16[768,768]{1,0:T(8,128)(2,1)}, bf16[768,768]{1,0:T(8,128)(2,1)S(1)}) fusion(f32[768,1536]{1,0:T(8,128)S(1)} %copy-done.30, bf16[768,2048]{1,0:T(8,128)(2,1)S(1)} %bitcast.163, bf16[1,768,2048]{2,1,0:T(8,128)(2,1)S(1)} %copy-done), kind=kOutput, calls=%fused_computation.25 | convolution fusion | flops 2425356288 | bytes 14548992 | tf_op jit(solution)/shard_map/dot_general | solution.py:33
  191.9 4.9 %fusion.2 = (f32[768]{0:T(1024)}, bf16[768,2048]{1,0:T(8,128)(2,1)}) fusion(bf16[16,48,2048]{2,1,0:T(8,128)(2,1)S(1)} %get-tuple-element.104, bf16[768,768]{1,0:T(8,128)(2,1)S(1)} %get-tuple-element.74, bf16[1,768,2048]{2,1,0:T(8,128)(2,1)S(1)} %copy-done), kind=kOutput, calls=%fused_computation.7 | convolution fusion | flops 2423782656 | bytes 10619904 | tf_op jit(solution)/shard_map/dot_general | solution.py:28
  198.5 9.3 %fusion = bf16[1,2048,1536]{2,1,0:T(8,128)(2,1)} fusion(bf16[768,2048]{1,0:T(8,128)(2,1)} %bitcast.166, bf16[768,768]{1,0:T(8,128)(2,1)} %get-tuple-element.73, bf16[768,768]{1,0:T(8,128)(2,1)} %get-tuple-element.72), kind=kOutput, calls=%fused_computation.3 | convolution fusion | flops 4839702528 | bytes 11796480 | tf_op jit(solution)/shard_map/dot_general | solution.py:44
  207.7 9.3 %fusion.1 = (f32[2048]{0:T(1024)S(1)}, bf16[768,2048]{1,0:T(8,128)(2,1)}) fusion(bf16[16,48,2048]{2,1,0:T(8,128)(2,1)S(1)} %copy-done.18, bf16[1,2048,1536]{2,1,0:T(8,128)(2,1)} %param.12, bf16[768,768]{1,0:T(8,128)(2,1)S(1)} %copy-done.32, bf16[768,768]{1,0:T(8,128)(2,1)S(1)} %copy-done.31), kind=kOutput, calls=%fused_computation.5 | convolution fusion | flops 4844419072 | bytes 14950400 | tf_op jit(solution)/shard_map/dot_general | solution.py:47
  218.6 42.5 %all_gather.11 = f32[32,32,128]{2,1,0:T(8,128)S(1)} all-gather(f32[1,32,128]{2,1,0:T(8,128)S(1)} %maximum_bitcast_fusion), channel_id=1, replica_groups=mesh['expert'=16,'tensor'=2] {'expert','tensor'}, dimensions={0}, use_global_device_ids=true | all-gather | bytes 540672 | tf_op jit(solution)/shard_map/all_gather | solution.py:382
  282.9 6.6 %fusion.13 = bf16[1,768,2048]{2,1,0:T(8,128)(2,1)} fusion(bf16[768,768]{1,0:T(8,128)(2,1)} %copy-done.29, bf16[768,2048]{1,0:T(8,128)(2,1)} %bitcast.164), kind=kOutput, calls=%fused_computation.22 | convolution fusion | flops 2417491968 | bytes 7471104 | tf_op jit(solution)/shard_map/dot_general | solution.py:41
  310.2 5.5 %collective-permute-done.50 = bf16[2,64,2048]{2,1,0:T(8,128)(2,1)S(1)} collective-permute-done((bf16[2,64,2048]{2,1,0:T(8,128)(2,1)S(1)}, bf16[2,64,2048]{2,1,0:T(8,128)(2,1)S(1)}, u32[]{:S(2)}, u32[]{:S(2)}) %collective-permute-start.50) | collective-permute-done | bytes 524320 | tf_op jit(solution)/shard_map/ppermute | solution.py:168
  315.9 5.4 %collective-permute-done.46 = bf16[2,64,2048]{2,1,0:T(8,128)(2,1)S(1)} collective-permute-done((bf16[2,64,2048]{2,1,0:T(8,128)(2,1)S(1)}, bf16[2,64,2048]{2,1,0:T(8,128)(2,1)S(1)}, u32[]{:S(2)}, u32[]{:S(2)}) %collective-permute-start.46) | collective-permute-done | bytes 524320 | tf_op jit(solution)/shard_map/ppermute | solution.py:168
  321.4 8.3 %collective-permute-done.24 = bf16[2,64,2048]{2,1,0:T(8,128)(2,1)S(1)} collective-permute-done((bf16[2,64,2048]{2,1,0:T(8,128)(2,1)S(1)}, bf16[2,64,2048]{2,1,0:T(8,128)(2,1)S(1)}, u32[]{:S(2)}, u32[]{:S(2)}) %collective-permute-start.24) | collective-permute-done | bytes 524320 | tf_op jit(solution)/shard_map/ppermute | solution.py:168
  329.9 8.2 %collective-permute-done.28 = bf16[2,64,2048]{2,1,0:T(8,128)(2,1)S(1)} collective-permute-done((bf16[2,64,2048]{2,1,0:T(8,128)(2,1)S(1)}, bf16[2,64,2048]{2,1,0:T(8,128)(2,1)S(1)}, u32[]{:S(2)}, u32[]{:S(2)}) %collective-permute-start.28) | collective-permute-done | bytes 524320 | tf_op jit(solution)/shard_map/ppermute | solution.py:168
  338.3 8.3 %collective-permute-done.20 = bf16[2,64,2048]{2,1,0:T(8,128)(2,1)S(1)} collective-permute-done((bf16[2,64,2048]{2,1,0:T(8,128)(2,1)S(1)}, bf16[2,64,2048]{2,1,0:T(8,128)(2,1)S(1)}, u32[]{:S(2)}, u32[]{:S(2)}) %collective-permute-start.20) | collective-permute-done | bytes 524320 | tf_op jit(solution)/shard_map/ppermute | solution.py:168
  346.8 8.2 %collective-permute-done.16 = bf16[2,64,2048]{2,1,0:T(8,128)(2,1)S(1)} collective-permute-done((bf16[2,64,2048]{2,1,0:T(8,128)(2,1)S(1)}, bf16[2,64,2048]{2,1,0:T(8,128)(2,1)S(1)}, u32[]{:S(2)}, u32[]{:S(2)}) %collective-permute-start.16) | collective-permute-done | bytes 524320 | tf_op jit(solution)/shard_map/ppermute | solution.py:168
  361.5 5.5 %collective-permute-done.21 = bf16[64,2048]{1,0:T(8,128)(2,1)S(1)} collective-permute-done((bf16[64,2048]{1,0:T(8,128)(2,1)S(1)}, bf16[64,2048]{1,0:T(8,128)(2,1)S(1)}, u32[]{:S(2)}, u32[]{:S(2)}) %collective-permute-start.21) | collective-permute-done | bytes 262176 | tf_op jit(solution)/shard_map/ppermute | solution.py:168
  369.9 3.9 collective-permute-start.26
  373.8 11.8 %collective-permute-done.52 = bf16[64,2048]{1,0:T(8,128)(2,1)S(1)} collective-permute-done((bf16[64,2048]{1,0:T(8,128)(2,1)S(1)}, bf16[64,2048]{1,0:T(8,128)(2,1)S(1)}, u32[]{:S(2)}, u32[]{:S(2)}) %collective-permute-start.52) | collective-permute-done | bytes 262176 | tf_op jit(solution)/shard_map/ppermute | solution.py:168
  386.9 17.1 %collective-permute-done.22 = bf16[64,2048]{1,0:T(8,128)(2,1)S(1)} collective-permute-done((bf16[64,2048]{1,0:T(8,128)(2,1)S(1)}, bf16[64,2048]{1,0:T(8,128)(2,1)S(1)}, u32[]{:S(2)}, u32[]{:S(2)}) %collective-permute-start.22) | collective-permute-done | bytes 262176 | tf_op jit(solution)/shard_map/ppermute | solution.py:168
  (291 shorter events, 151.8 us)
Async XLA Ops:
  0.7 70.1 %collective-permute-start.33 = (bf16[64,2048]{1,0:T(8,128)(2,1)}, bf16[64,2048]{1,0:T(8,128)(2,1)}, u32[]{:S(2)}, u32[]{:S(2)}) collective-permute-start(bf16[64,2048]{1,0:T(8,128)(2,1)} %param.8), channel_id=1, source_target_pairs={{0,24},{1,25},{2,26},{3,27},{4,28},{5,29},{6,30},{7,31},{8,0},{9,1... | collective-permute-start | bytes 786440 | tf_op jit(solution)/shard_map/ppermute | solution.py:168
  5.8 61.7 %collective-permute-start.30 = (bf16[64,2048]{1,0:T(8,128)(2,1)}, bf16[64,2048]{1,0:T(8,128)(2,1)}, u32[]{:S(2)}, u32[]{:S(2)}) collective-permute-start(bf16[64,2048]{1,0:T(8,128)(2,1)} %param.8), channel_id=1, source_target_pairs={{0,2},{1,5},{2,0},{3,7},{4,6},{5,1},{6,4},{7,3},{8,10},{9,13},{10,... | collective-permute-start | bytes 786440 | tf_op jit(solution)/shard_map/ppermute | solution.py:168
  7.3 59.0 %collective-permute-start = (bf16[64,2048]{1,0:T(8,128)(2,1)}, bf16[64,2048]{1,0:T(8,128)(2,1)}, u32[]{:S(2)}, u32[]{:S(2)}) collective-permute-start(bf16[64,2048]{1,0:T(8,128)(2,1)} %param.7), channel_id=1, source_target_pairs={{0,2},{1,5},{2,0},{3,7},{4,6},{5,1},{6,4},{7,3},{8,10},{9,13},{10,... | collective-permute-start | bytes 786440 | tf_op jit(solution)/shard_map/ppermute | solution.py:168
  7.8 60.9 %collective-permute-start.11 = (bf16[64,2048]{1,0:T(8,128)(2,1)}, bf16[64,2048]{1,0:T(8,128)(2,1)}, u32[]{:S(2)}, u32[]{:S(2)}) collective-permute-start(bf16[64,2048]{1,0:T(8,128)(2,1)} %param.7), channel_id=1, source_target_pairs={{0,8},{1,9},{2,10},{3,11},{4,12},{5,13},{6,14},{7,15},{8,16},{9,17... | collective-permute-start | bytes 786440 | tf_op jit(solution)/shard_map/ppermute | solution.py:168
  7.8 58.5 %collective-permute-start.7 = (bf16[64,2048]{1,0:T(8,128)(2,1)}, bf16[64,2048]{1,0:T(8,128)(2,1)}, u32[]{:S(2)}, u32[]{:S(2)}) collective-permute-start(bf16[64,2048]{1,0:T(8,128)(2,1)} %param.7), channel_id=1, source_target_pairs={{0,16},{1,17},{2,18},{3,19},{4,20},{5,21},{6,22},{7,23},{8,24},{9,... | collective-permute-start | bytes 786440 | tf_op jit(solution)/shard_map/ppermute | solution.py:168
  83.3 25.9 %collective-permute-start.31 = (bf16[2,64,2048]{2,1,0:T(8,128)(2,1)S(1)}, bf16[2,64,2048]{2,1,0:T(8,128)(2,1)S(1)}, u32[]{:S(2)}, u32[]{:S(2)}) collective-permute-start(bf16[2,64,2048]{2,1,0:T(8,128)(2,1)S(1)} %pad_maximum_fusion.19), channel_id=1, source_target_pairs={{0,4},{1,3},{2,6},{3,1},{4,0},{5,7},{6,2},{7,5},{8,12},{9,11},{10,... | collective-permute-start | bytes 1572872 | tf_op jit(solution)/shard_map/ppermute | solution.py:168
  92.6 39.3 %collective-permute-start.35 = (bf16[2,64,2048]{2,1,0:T(8,128)(2,1)S(1)}, bf16[2,64,2048]{2,1,0:T(8,128)(2,1)S(1)}, u32[]{:S(2)}, u32[]{:S(2)}) collective-permute-start(bf16[2,64,2048]{2,1,0:T(8,128)(2,1)S(1)} %pad_maximum_fusion.20), channel_id=1, source_target_pairs={{0,4},{1,3},{2,6},{3,1},{4,0},{5,7},{6,2},{7,5},{8,12},{9,11},{10,... | collective-permute-start | bytes 1572872 | tf_op jit(solution)/shard_map/ppermute | solution.py:168
  109.2 26.2 %collective-permute-start.2 = (bf16[4,64,2048]{2,1,0:T(8,128)(2,1)S(1)}, bf16[4,64,2048]{2,1,0:T(8,128)(2,1)S(1)}, u32[]{:S(2)}, u32[]{:S(2)}) collective-permute-start(bf16[4,64,2048]{2,1,0:T(8,128)(2,1)S(1)} %pad_maximum_fusion.7.mine_ref), channel_id=1, source_target_pairs={{0,1},{1,0},{2,3},{3,2},{4,5},{5,4},{6,7},{7,6},{8,9},{9,8},{10,11... | collective-permute-start | bytes 3145736 | tf_op jit(solution)/shard_map/ppermute | solution.py:168
  135.5 23.3 %collective-permute-start.6 = (bf16[4,64,2048]{2,1,0:T(8,128)(2,1)}, bf16[4,64,2048]{2,1,0:T(8,128)(2,1)}, u32[]{:S(2)}, u32[]{:S(2)}) collective-permute-start(bf16[4,64,2048]{2,1,0:T(8,128)(2,1)} %pad_maximum_fusion.8.mine_ref), channel_id=1, source_target_pairs={{0,1},{1,0},{2,3},{3,2},{4,5},{5,4},{6,7},{7,6},{8,9},{9,8},{10,11... | collective-permute-start | bytes 3145736 | tf_op jit(solution)/shard_map/ppermute | solution.py:168
  136.5 27.5 %collective-permute-start.40 = (bf16[4,64,2048]{2,1,0:T(8,128)(2,1)}, bf16[4,64,2048]{2,1,0:T(8,128)(2,1)}, u32[]{:S(2)}, u32[]{:S(2)}) collective-permute-start(bf16[4,64,2048]{2,1,0:T(8,128)(2,1)} %pad_maximum_fusion.13.mine_ref), channel_id=1, source_target_pairs={{0,1},{1,0},{2,3},{3,2},{4,5},{5,4},{6,7},{7,6},{8,9},{9,8},{10,11... | collective-permute-start | bytes 3145736 | tf_op jit(solution)/shard_map/ppermute | solution.py:168
  141.7 30.0 %collective-permute-start.44 = (bf16[4,64,2048]{2,1,0:T(8,128)(2,1)S(1)}, bf16[4,64,2048]{2,1,0:T(8,128)(2,1)S(1)}, u32[]{:S(2)}, u32[]{:S(2)}) collective-permute-start(bf16[4,64,2048]{2,1,0:T(8,128)(2,1)S(1)} %pad_maximum_fusion.14.mine_ref), channel_id=1, source_target_pairs={{0,1},{1,0},{2,3},{3,2},{4,5},{5,4},{6,7},{7,6},{8,9},{9,8},{10,11... | collective-permute-start | bytes 3145736 | tf_op jit(solution)/shard_map/ppermute | solution.py:168
  149.4 33.0 %collective-permute-start.36 = (bf16[4,64,2048]{2,1,0:T(8,128)(2,1)S(1)}, bf16[4,64,2048]{2,1,0:T(8,128)(2,1)S(1)}, u32[]{:S(2)}, u32[]{:S(2)}) collective-permute-start(bf16[4,64,2048]{2,1,0:T(8,128)(2,1)S(1)} %pad_maximum_fusion.12.mine_ref), channel_id=1, source_target_pairs={{0,1},{1,0},{2,3},{3,2},{4,5},{5,4},{6,7},{7,6},{8,9},{9,8},{10,11... | collective-permute-start | bytes 3145736 | tf_op jit(solution)/shard_map/ppermute | solution.py:168
  266.4 23.0 %collective-permute-start.57 = (bf16[4,64,2048]{2,1,0:T(8,128)(2,1)}, bf16[4,64,2048]{2,1,0:T(8,128)(2,1)}, u32[]{:S(2)}, u32[]{:S(2)}) collective-permute-start(bf16[4,64,2048]{2,1,0:T(8,128)(2,1)} %get-tuple-element.61), channel_id=1, source_target_pairs={{0,1},{1,0},{2,3},{3,2},{4,5},{5,4},{6,7},{7,6},{8,9},{9,8},{10,11... | collective-permute-start | bytes 3145736 | tf_op jit(solution)/shard_map/ppermute | solution.py:168
  269.3 21.9 %collective-permute-start.53 = (bf16[4,64,2048]{2,1,0:T(8,128)(2,1)}, bf16[4,64,2048]{2,1,0:T(8,128)(2,1)}, u32[]{:S(2)}, u32[]{:S(2)}) collective-permute-start(bf16[4,64,2048]{2,1,0:T(8,128)(2,1)} %get-tuple-element.59), channel_id=1, source_target_pairs={{0,1},{1,0},{2,3},{3,2},{4,5},{5,4},{6,7},{7,6},{8,9},{9,8},{10,11... | collective-permute-start | bytes 3145736 | tf_op jit(solution)/shard_map/ppermute | solution.py:168
  270.9 22.4 %collective-permute-start.49 = (bf16[4,64,2048]{2,1,0:T(8,128)(2,1)S(1)}, bf16[4,64,2048]{2,1,0:T(8,128)(2,1)}, u32[]{:S(2)}, u32[]{:S(2)}) collective-permute-start(bf16[4,64,2048]{2,1,0:T(8,128)(2,1)S(1)} %get-tuple-element.57), channel_id=1, source_target_pairs={{0,1},{1,0},{2,3},{3,2},{4,5},{5,4},{6,7},{7,6},{8,9},{9,8},{10,11... | collective-permute-start | bytes 3145736 | tf_op jit(solution)/shard_map/ppermute | solution.py:168
  272.7 22.5 %collective-permute-start.45 = (bf16[4,64,2048]{2,1,0:T(8,128)(2,1)S(1)}, bf16[4,64,2048]{2,1,0:T(8,128)(2,1)}, u32[]{:S(2)}, u32[]{:S(2)}) collective-permute-start(bf16[4,64,2048]{2,1,0:T(8,128)(2,1)S(1)} %get-tuple-element.55), channel_id=1, source_target_pairs={{0,1},{1,0},{2,3},{3,2},{4,5},{5,4},{6,7},{7,6},{8,9},{9,8},{10,11... | collective-permute-start | bytes 3145736 | tf_op jit(solution)/shard_map/ppermute | solution.py:168
  303.8 26.0 %collective-permute-start.24 = (bf16[2,64,2048]{2,1,0:T(8,128)(2,1)S(1)}, bf16[2,64,2048]{2,1,0:T(8,128)(2,1)S(1)}, u32[]{:S(2)}, u32[]{:S(2)}) collective-permute-start(bf16[2,64,2048]{2,1,0:T(8,128)(2,1)S(1)} %slice.325), channel_id=1, source_target_pairs={{0,4},{1,3},{2,6},{3,1},{4,0},{5,7},{6,2},{7,5},{8,12},{9,11},{10,... | collective-permute-start | bytes 1572872 | tf_op jit(solution)/shard_map/ppermute | solution.py:168
  304.5 33.7 %collective-permute-start.28 = (bf16[2,64,2048]{2,1,0:T(8,128)(2,1)S(1)}, bf16[2,64,2048]{2,1,0:T(8,128)(2,1)S(1)}, u32[]{:S(2)}, u32[]{:S(2)}) collective-permute-start(bf16[2,64,2048]{2,1,0:T(8,128)(2,1)S(1)} %slice.331), channel_id=1, source_target_pairs={{0,4},{1,3},{2,6},{3,1},{4,0},{5,7},{6,2},{7,5},{8,12},{9,11},{10,... | collective-permute-start | bytes 1572872 | tf_op jit(solution)/shard_map/ppermute | solution.py:168
  310.1 36.5 %collective-permute-start.20 = (bf16[2,64,2048]{2,1,0:T(8,128)(2,1)S(1)}, bf16[2,64,2048]{2,1,0:T(8,128)(2,1)S(1)}, u32[]{:S(2)}, u32[]{:S(2)}) collective-permute-start(bf16[2,64,2048]{2,1,0:T(8,128)(2,1)S(1)} %slice.319), channel_id=1, source_target_pairs={{0,4},{1,3},{2,6},{3,1},{4,0},{5,7},{6,2},{7,5},{8,12},{9,11},{10,... | collective-permute-start | bytes 1572872 | tf_op jit(solution)/shard_map/ppermute | solution.py:168
  315.7 39.3 %collective-permute-start.16 = (bf16[2,64,2048]{2,1,0:T(8,128)(2,1)S(1)}, bf16[2,64,2048]{2,1,0:T(8,128)(2,1)S(1)}, u32[]{:S(2)}, u32[]{:S(2)}) collective-permute-start(bf16[2,64,2048]{2,1,0:T(8,128)(2,1)S(1)} %slice.313), channel_id=1, source_target_pairs={{0,4},{1,3},{2,6},{3,1},{4,0},{5,7},{6,2},{7,5},{8,12},{9,11},{10,... | collective-permute-start | bytes 1572872 | tf_op jit(solution)/shard_map/ppermute | solution.py:168
  321.3 48.6 %collective-permute-start.59 = (bf16[64,2048]{1,0:T(8,128)(2,1)S(1)}, bf16[64,2048]{1,0:T(8,128)(2,1)S(1)}, u32[]{:S(2)}, u32[]{:S(2)}) collective-permute-start(bf16[64,2048]{1,0:T(8,128)(2,1)S(1)} %slice_bitcast_fusion), channel_id=1, source_target_pairs={{0,2},{1,5},{2,0},{3,7},{4,6},{5,1},{6,4},{7,3},{8,10},{9,13},{10,... | collective-permute-start | bytes 786440 | tf_op jit(solution)/shard_map/ppermute | solution.py:168
  329.7 25.5 %collective-permute-start.55 = (bf16[64,2048]{1,0:T(8,128)(2,1)S(1)}, bf16[64,2048]{1,0:T(8,128)(2,1)S(1)}, u32[]{:S(2)}, u32[]{:S(2)}) collective-permute-start(bf16[64,2048]{1,0:T(8,128)(2,1)S(1)} %slice_bitcast_fusion.2), channel_id=1, source_target_pairs={{0,2},{1,5},{2,0},{3,7},{4,6},{5,1},{6,4},{7,3},{8,10},{9,13},{10,... | collective-permute-start | bytes 786440 | tf_op jit(solution)/shard_map/ppermute | solution.py:168
  355.2 30.8 %collective-permute-start.29 = (bf16[64,2048]{1,0:T(8,128)(2,1)S(1)}, bf16[64,2048]{1,0:T(8,128)(2,1)S(1)}, u32[]{:S(2)}, u32[]{:S(2)}) collective-permute-start(bf16[64,2048]{1,0:T(8,128)(2,1)S(1)} %slice_bitcast_fusion.8), channel_id=1, source_target_pairs={{0,2},{1,5},{2,0},{3,7},{4,6},{5,1},{6,4},{7,3},{8,10},{9,13},{10,... | collective-permute-start | bytes 786440 | tf_op jit(solution)/shard_map/ppermute | solution.py:168
  373.8 30.2 %collective-permute-start.22 = (bf16[64,2048]{1,0:T(8,128)(2,1)S(1)}, bf16[64,2048]{1,0:T(8,128)(2,1)S(1)}, u32[]{:S(2)}, u32[]{:S(2)}) collective-permute-start(bf16[64,2048]{1,0:T(8,128)(2,1)S(1)} %fusion.29), channel_id=1, source_target_pairs={{0,16},{1,17},{2,18},{3,19},{4,20},{5,21},{6,22},{7,23},{8,24},{9,... | collective-permute-start | bytes 786440 | tf_op jit(solution)/shard_map/ppermute | solution.py:168
  (69 other events, 1163.7 us)

commit v2 on v0

--- a/solution.py
+++ b/solution.py
@@ -1,10 +1,15 @@
+import functools
+
 import jax
 import jax.numpy as jnp
 from jax import lax
+from jax.experimental import pallas as pl
+from jax.experimental.pallas import tpu as pltpu
 from jax.sharding import PartitionSpec as P
 
 TOP = 8
 EXP_DEV = 2
+VMEM_LIMIT = 48 * 1024 * 1024
 
 
 def normalize(rows):
@@ -24,28 +29,31 @@
     return (gate_pre, up_pre, sigmoid_gate, hidden, block_out)
 
 
-def expert_backward(rows, slot_grads, gate_up, down_proj, gate_pre, up_pre, sigmoid_gate, hidden):
-    hidden_grad = lax.dot_general(
-        slot_grads, down_proj, (((1,), (1,)), ((), ())), preferred_element_type=jnp.float32
-    )
+def times_transposed(left, right):
+    return lax.dot_general(left, right, (((1,), (1,)), ((), ())), preferred_element_type=jnp.float32)
+
+
+def outer_sum(left, right):
+    product = lax.dot_general(left, right, (((0,), (0,)), ((), ())), preferred_element_type=jnp.float32)
+    return product.astype(jnp.bfloat16)
+
+
+def backward_inner(slot_grads, down_proj, gate_pre, up_pre, sigmoid_gate):
+    hidden_grad = times_transposed(slot_grads, down_proj)
     gate_grad = (
         hidden_grad * up_pre * sigmoid_gate * (1.0 + gate_pre * (1.0 - sigmoid_gate))
     ).astype(jnp.bfloat16)
     up_grad = (hidden_grad * gate_pre * sigmoid_gate).astype(jnp.bfloat16)
-    joined_grad = jnp.concatenate([gate_grad, up_grad], axis=1)
-    down_part = lax.dot_general(
-        hidden, slot_grads, (((0,), (0,)), ((), ())), preferred_element_type=jnp.float32
-    ).astype(jnp.bfloat16)
-    gate_up_part = lax.dot_general(
-        rows, joined_grad, (((0,), (0,)), ((), ())), preferred_element_type=jnp.float32
-    ).astype(jnp.bfloat16)
-    input_grad = lax.dot_general(
-        joined_grad, gate_up, (((1,), (1,)), ((), ())), preferred_element_type=jnp.float32
-    ).astype(jnp.bfloat16)
-    return (input_grad, gate_up_part, down_part)
-
-
-def shards(tokens, cotangent, gain, expert_ids, gate_probs, gate_up_weight, down_weight):
+    return jnp.concatenate([gate_grad, up_grad], axis=1)
+
+
+def expert_backward(rows, slot_grads, gate_up, down_proj, gate_pre, up_pre, sigmoid_gate, hidden):
+    joined_grad = backward_inner(slot_grads, down_proj, gate_pre, up_pre, sigmoid_gate)
+    input_grad = times_transposed(joined_grad, gate_up).astype(jnp.bfloat16)
+    return (input_grad, outer_sum(rows, joined_grad), outer_sum(hidden, slot_grads))
+
+
+def routed_shards(tokens, cotangent, gain, expert_ids, gate_probs, gate_up_weight, down_weight):
     tensor_size = lax.axis_size("tensor")
     expert_size = lax.axis_size("expert")
     my_rank = lax.axis_index("tensor")
@@ -143,6 +151,300 @@
     return (mixed, token_grad, prob_grad, gain_grad, gate_up_part[None], down_part[None])
 
 
+BOTH = ("expert", "tensor")
+
+
+def flip_first(expert, core):
+    return expert ^ (2 if core == 0 else 1)
+
+
+def flip_second(expert, core):
+    return expert ^ (1 if core == 0 else 2)
+
+
+def send(array, place):
+    pairs = []
+    for expert in range(lax.axis_size("expert")):
+        for core in range(2):
+            to_expert, to_core = place(expert, core)
+            pairs.append((expert * 2 + core, to_expert * 2 + to_core))
+    return lax.ppermute(array, BOTH, pairs)
+
+
+def send_first(array):
+    return send(array, lambda e, c: (flip_first(e, c), c))
+
+
+def send_second(array):
+    return send(array, lambda e, c: (flip_second(e, c), c))
+
+
+def send_bit(array, bit):
+    return send(array, lambda e, c: (e ^ bit, c))
+
+
+def send_core(array):
+    return send(array, lambda e, c: (e, 1 - c))
+
+
+def send_along(array, step):
+    size = lax.axis_size("expert")
+    return send(array, lambda e, c: ((e + 4 * step) % size, c))
+
+
+def after(array, *others):
+    return lax.optimization_barrier((array,) + others)[0]
+
+
+def gather_plane(block):
+    pair = jnp.concatenate([block, send_second(block)])
+    quad = jnp.concatenate([pair, send_first(pair)])
+    return quad, send_core(quad)
+
+
+def add_half(left, right):
+    return (left.astype(jnp.float32) + right.astype(jnp.float32)).astype(jnp.bfloat16)
+
+
+def fold(array, sender):
+    half = array.shape[0] // 2
+    return add_half(array[:half], sender(array[half:]))
+
+
+def gather_tables(table):
+    steps = lax.axis_size("expert") // 4
+    planes = jnp.stack([table] + [send_along(table, -step) for step in range(1, steps)])
+    pair = jnp.stack([planes, send_second(planes)])
+    return jnp.stack([pair, send_first(pair)])
+
+
+def far_first(array):
+    far = array[:, :, 1:].reshape((-1,) + array.shape[3:])
+    return jnp.concatenate([far, array[:, :, 0].reshape((-1,) + array.shape[3:])])
+
+
+def from_far_first(array, steps):
+    far = array[:4 * (steps - 1)].reshape((2, 2, steps - 1) + array.shape[1:])
+    return jnp.concatenate([array[4 * (steps - 1):].reshape((2, 2, 1) + array.shape[1:]), far], axis=2)
+
+
+def swapped(index, count):
+    bits = index // count
+    return ((bits % 2) * 2 + bits // 2) * count + index % count
+
+
+def chosen_rows(pick_ref, mine_ref, other_ref):
+    half = mine_ref.shape[1]
+    rows = jnp.dot(pick_ref[0][:, :half], mine_ref[0], preferred_element_type=jnp.float32)
+    return rows + jnp.dot(pick_ref[0][:, half:], other_ref[0], preferred_element_type=jnp.float32)
+
+
+def select_norm_kernel(pick_ref, mine_ref, other_ref, gain_ref, *refs):
+    normed_ref = refs[-1]
+    rows = chosen_rows(pick_ref, mine_ref, other_ref)
+    inv_rms = lax.rsqrt(jnp.mean(rows * rows, axis=1, keepdims=True) + 1e-06)
+    normed_ref[0] = (rows * inv_rms * gain_ref[...]).astype(jnp.bfloat16)
+
+
+def select_grad_kernel(pick_ref, mine_ref, other_ref, prob_ref, *refs):
+    cot_ref, grad_ref = refs[-2:]
+    rows = chosen_rows(pick_ref, mine_ref, other_ref)
+    cot_ref[0] = rows.astype(jnp.bfloat16)
+    grad_ref[0] = (rows * prob_ref[0]).astype(jnp.bfloat16)
+
+
+def select(kernel, outputs, pick, blocks, extra, count, arrays, which, first_group, held):
+    groups, capacity, group_rows = pick.shape
+    mine, other = blocks
+    half, features = mine.shape[1:]
+    out = jax.ShapeDtypeStruct((groups, capacity, features), jnp.bfloat16)
+
+    def group_spec(*shape):
+        return pl.BlockSpec((1,) + shape, lambda i: (first_group + i, 0, 0))
+
+    if extra.ndim == 2:
+        extra_spec = pl.BlockSpec(extra.shape, lambda i: (0, 0))
+    else:
+        extra_spec = group_spec(capacity, 1)
+    return pl.pallas_call(
+        kernel,
+        grid=(4 * count,),
+        in_specs=[
+            group_spec(capacity, group_rows),
+            pl.BlockSpec((1, half, features), lambda i: (i * arrays + which, 0, 0)),
+            pl.BlockSpec((1, half, features), lambda i: (swapped(i, count) * arrays + which, 0, 0)),
+            extra_spec,
+        ] + [pl.BlockSpec(memory_space=pl.ANY)] * len(held),
+        out_specs=[group_spec(capacity, features)] * outputs,
+        out_shape=[out] * outputs,
+        input_output_aliases={4 + n: n for n in range(len(held))},
+        compiler_params=pltpu.CompilerParams(vmem_limit_bytes=VMEM_LIMIT),
+        cost_estimate=pl.CostEstimate(
+            flops=8 * count * capacity * group_rows * features,
+            bytes_accessed=16 * count * half * features + 8 * outputs * count * capacity * features,
+            transcendentals=0,
+        ),
+    )(pick, mine, other, extra, *held)
+
+
+def expand_kernel(weighted, pick_ref, prob_ref, *refs):
+    sources, (mine_ref, other_ref) = refs[:-2], refs[-2:]
+    half = mine_ref.shape[1]
+    pick = pick_ref[0]
+    for place, (source_ref, by_prob) in enumerate(zip(sources, weighted)):
+        rows = source_ref[0]
+        if by_prob:
+            rows = (rows.astype(jnp.float32) * prob_ref[0]).astype(jnp.bfloat16)
+        for columns, out_ref in ((pick[:, :half], mine_ref), (pick[:, half:], other_ref)):
+            out_ref[place] = lax.dot_general(
+                columns, rows, (((0,), (0,)), ((), ())), preferred_element_type=jnp.float32
+            ).astype(jnp.bfloat16)
+
+
+def expand(pick, prob, slots, weighted, count, first_group):
+    _, capacity, group_rows = pick.shape
+    half, features, arrays = group_rows // 2, slots[0].shape[2], len(slots)
+    out = jax.ShapeDtypeStruct((4 * count * arrays, half, features), jnp.bfloat16)
+
+    def group_spec(*shape):
+        return pl.BlockSpec((1,) + shape, lambda i: (first_group + i, 0, 0))
+
+    return pl.pallas_call(
+        functools.partial(expand_kernel, weighted),
+        grid=(4 * count,),
+        in_specs=[group_spec(capacity, group_rows), group_spec(capacity, 1)]
+        + [group_spec(capacity, features)] * arrays,
+        out_specs=[
+            pl.BlockSpec((arrays, half, features), lambda i: (i, 0, 0)),
+            pl.BlockSpec((arrays, half, features), lambda i: (swapped(i, count), 0, 0)),
+        ],
+        out_shape=[out, out],
+        compiler_params=pltpu.CompilerParams(vmem_limit_bytes=VMEM_LIMIT),
+        cost_estimate=pl.CostEstimate(
+            flops=8 * arrays * count * capacity * group_rows * features,
+            bytes_accessed=8 * arrays * count * features * (group_rows + capacity),
+            transcendentals=0,
+        ),
+    )(pick, prob, *slots)
+
+
+def home_terms(columns, gain_term):
+    steps, top, rows = columns.shape[2:]
+    half = rows // 2
+    gain_rows = gain_term.reshape(-1, 128)
+    count = gain_rows.shape[0]
+
+    def exchange(part, gains, sender):
+        got = sender(jnp.concatenate([part.reshape(-1, 128), gains]))
+        return got[:-count].reshape(part.shape), got[-count:]
+
+    got, gains = exchange(columns[..., half:], gain_rows, send_core)
+    columns, gain_rows = columns[..., :half] + got, gain_rows + gains
+    for bit in (2, 1):
+        got, gains = exchange(columns[1], gain_rows, functools.partial(send_bit, bit=bit))
+        columns, gain_rows = columns[0] + got, gain_rows + gains
+    total, all_gains = columns[0], [gain_rows]
+    for step in range(1, steps):
+        got, gains = exchange(columns[step], gain_rows, functools.partial(send_along, step=step))
+        total = total + got
+        all_gains.append(gains)
+    order = (lax.axis_index("expert") // 4 - jnp.arange(steps)) % steps
+    gains = jnp.take(jnp.stack(all_gains), order, axis=0)
+    gain_sum = gains[0]
+    for step in range(1, steps):
+        gain_sum = gain_sum + gains[step]
+    return total, gain_sum.reshape(-1)
+
+
+def broadcast_shards(tokens, cotangent, gain, expert_ids, gate_probs, gate_up_weight, down_weight):
+    expert_size = lax.axis_size("expert")
+    steps = expert_size // 4
+    far = 4 * (steps - 1)
+    expert, core = lax.axis_index("expert"), lax.axis_index("tensor")
+    my_expert = expert * EXP_DEV + core
+    group_rows = expert_ids.shape[0]
+    half = group_rows // 2
+    features = tokens.shape[1]
+    capacity = 3 * group_rows * TOP // (2 * EXP_DEV * expert_size)
+    gate_up, down_proj = gate_up_weight[0], down_weight[0]
+
+    tables = gather_tables(jnp.concatenate([expert_ids.T.astype(jnp.float32), gate_probs.T]))
+    near_blocks = gather_plane(jnp.stack([tokens, cotangent]))
+    token_far = jnp.stack([send_along(tokens, -step) for step in range(1, steps)])
+    far_tokens = gather_plane(token_far)
+    late_cot = after(cotangent, token_far)
+    far_cots = gather_plane(
+        after(jnp.stack([send_along(late_cot, -step) for step in range(1, steps)]), far_tokens[0])
+    )
+
+    tables = far_first(tables)
+    tables = jnp.where(core == 0, tables, jnp.roll(tables, half, axis=2))
+    matches = tables[:, :TOP] == my_expert.astype(jnp.float32)
+    chosen = jnp.any(matches, axis=1)
+    weight_of = jnp.sum(jnp.where(matches, tables[:, TOP:], 0.0), axis=1)
+    row_ids = jnp.arange(group_rows, dtype=jnp.int32)
+    earlier = (row_ids[:, None] < row_ids[None, :]).astype(jnp.bfloat16)
+    rank_in = jnp.dot(chosen.astype(jnp.bfloat16), earlier, preferred_element_type=jnp.float32)
+    placed = chosen[:, None, :] & (
+        rank_in.astype(jnp.int32)[:, None, :] == jnp.arange(capacity, dtype=jnp.int32)[None, :, None]
+    )
+    pick = placed.astype(jnp.bfloat16)
+    slot_prob = jnp.sum(jnp.where(placed, weight_of[:, None, :], 0.0), axis=2, keepdims=True)
+
+    held = select(select_norm_kernel, 1, pick, near_blocks, gain[None, :], 1, 2, 0, far, ())
+    rows, = select(
+        select_norm_kernel, 1, pick, far_tokens, gain[None, :], steps - 1, 1, 0, 0, tuple(held)
+    )
+    held = select(select_grad_kernel, 2, pick, near_blocks, slot_prob, 1, 2, 1, far, ())
+    rows = rows.reshape(-1, features)
+    gate_pre, up_pre, sigmoid_gate, hidden, block_out = expert_forward(rows, gate_up, down_proj)
+    out_slots = block_out.reshape(expert_size, capacity, features)
+    out_mine, out_other = expand(pick, slot_prob, (out_slots,), (True,), steps - 1, 0)
+
+    cots, grads = select(
+        select_grad_kernel, 2, pick, far_cots, slot_prob, steps - 1, 1, 0, 0, tuple(held)
+    )
+    grads = after(grads.reshape(-1, features), out_other)
+    joined_grad = backward_inner(grads, down_proj, gate_pre, up_pre, sigmoid_gate)
+    out_quad = add_half(out_mine, send_core(out_other))
+    input_grad = times_transposed(after(joined_grad, out_quad), gate_up).astype(jnp.bfloat16)
+    input_slots = input_grad.reshape(expert_size, capacity, features)
+    in_mine, in_other = expand(pick, slot_prob, (input_slots,), (False,), steps - 1, 0)
+    out_pair = fold(out_quad, send_first)
+    near_mine, near_other = expand(
+        pick, slot_prob, (out_slots, after(input_slots, in_other, out_pair)), (True, False), 1, far
+    )
+    in_quad = add_half(in_mine, send_core(in_other))
+    down_part = outer_sum(after(hidden, near_other, in_quad), grads)
+    near_quad = add_half(near_mine, send_core(near_other))
+    out_far = fold(out_pair, send_second)
+    gate_up_part = outer_sum(after(rows, in_quad, near_quad, out_far), joined_grad)
+
+    out_far = [send_along(out_far[step - 1], step) for step in range(1, steps)]
+    in_far = fold(fold(in_quad, send_first), send_second)
+    in_far = [send_along(in_far[step - 1], step) for step in range(1, steps)]
+    near_sum = fold(fold(near_quad, send_first), send_second).astype(jnp.float32)
+    out_sum = near_sum[0] + sum(block.astype(jnp.float32) for block in out_far)
+    normed_grad = near_sum[1] + sum(block.astype(jnp.float32) for block in in_far)
+
+    gain_term = jnp.sum(input_grad.astype(jnp.float32) * rows.astype(jnp.float32), axis=0) / gain
+    prob_value = jnp.sum(cots.astype(jnp.float32) * out_slots.astype(jnp.float32), axis=2)
+    prob_rows = jnp.sum(jnp.where(placed, prob_value[:, :, None], 0.0), axis=1)
+    columns = from_far_first(jnp.where(matches, prob_rows[:, None, :], 0.0), steps)
+    columns = jnp.where(core == 0, columns, jnp.swapaxes(columns, 0, 1))
+    prob_sum, gain_grad = home_terms(after(columns, near_quad), after(gain_term, near_quad))
+
+    scaled_own, inv_own = normalize(tokens)
+    mixed = (tokens.astype(jnp.float32) + out_sum).astype(jnp.bfloat16)
+    gain_side = normed_grad * gain[None, :]
+    token_grad = (
+        cotangent.astype(jnp.float32)
+        + inv_own
+        * (gain_side - scaled_own * jnp.mean(gain_side * scaled_own, axis=1, keepdims=True))
+    ).astype(jnp.bfloat16)
+    return (mixed, token_grad, prob_sum.T, gain_grad, gate_up_part[None], down_part[None])
+
+
 def solution(mesh):
     in_specs = (
         P(("expert", "tensor"), None),
@@ -161,4 +463,7 @@
         P(("expert", "tensor"), None, None),
         P(("expert", "tensor"), None, None),
     )
+    expert_size, tensor_size = mesh.shape["expert"], mesh.shape["tensor"]
+    few = tensor_size == EXP_DEV and expert_size % 4 == 0 and expert_size <= 4 * TOP
+    shards = broadcast_shards if few else routed_shards
     return jax.shard_map(shards, mesh=mesh, in_specs=in_specs, out_specs=out_specs, check_vma=False)

time: 420 us -> 322 us (0.77)
  waiting for transfers between devices: 200 us -> 86.6 us
  blocking collectives: 54.2 us -> 0 us
  Pallas kernels: 0 us -> 52.1 us
  starting transfers between devices: 52.7 us -> 79.7 us
  other arithmetic: 20.6 us -> 34.7 us
  matrix products: 53.8 us -> 40.7 us
  between operations: 13.9 us -> 1.31 us
    all_to_all x4 -> x0, waiting for transfers between devices: 200 us -> none  [the longest x1 51.6 us: shards(): lax.all_to_all(out_slots, 'expert', split_axis=0, concat_axis=0, tiled=True)]
    ppermute x0 -> x41, waiting for transfers between devices: none -> 86.6 us  [send(): return lax.ppermute(array, BOTH, pairs)]
    ppermute x0 -> x41, starting transfers between devices: none -> 79.7 us  [send(): return lax.ppermute(array, BOTH, pairs)]
    all_to_all x4 -> x0, starting transfers between devices: 52.4 us -> none  [the longest x1 15.7 us: shards(): lax.all_to_all(sent_grads, 'expert', split_axis=0, concat_axis=0, tiled=T...]
    pallas_call x0 -> x7, Pallas kernels: none -> 52.1 us  [the longest x4 28.6 us: select(): pl.pallas_call(kernel, grid=(4 * count,), in_specs=[group_spec(capacity,...]
    psum x1 -> x0, blocking collectives: 49.5 us -> none  [shards(): lax.psum(jnp.sum(normed_grad * scaled_own, axis=0), ('expert', 'tensor'))]
    gather x3 -> x1, local copies, waits for them, and re-layouts: 20.7 us -> 0.55 us  [home_terms(): gains = jnp.take(jnp.stack(all_gains), order, axis=0)]
    convert_element_type x3 -> x13, other arithmetic: 7.78 us -> 23.9 us  [the longest x8 19.3 us: add_half(): (left.astype(jnp.float32) + right.astype(jnp.float32)).astype(jnp.bfloat16)]
  transfers between devices with their start and end apart: 7 -> 41, of which waited for: 4 -> 19; matrix products, arithmetic and copies ran while one was open for 16% -> 27% of each run, Pallas kernels for 0% -> 15%
where the time goes in v2:
time: 322 us; the launch traced here: 320 us
  waiting for transfers between devices  86.6 us (27%)
  starting transfers between devices  79.7 us (25%)
  Pallas kernels  52.1 us (16%)
  matrix products  40.7 us (13%)
  other arithmetic  34.7 us (11%)
  local copies, waits for them, and re-layouts  25.2 us (8%)
    ppermute x41, waiting for transfers between devices, send(): return lax.ppermute(array, BOTH, pairs)  86.6 us
    ppermute x41, starting transfers between devices, send(): return lax.ppermute(array, BOTH, pairs)  79.7 us
    pallas_call x4, Pallas kernels, select(): pl.pallas_call(kernel, grid=(4 * count,), in_specs=[group_spec(capacity,...  28.6 us
    pallas_call x3, Pallas kernels, expand(): pl.pallas_call(functools.partial(expand_kernel, weighted), grid=(4 * coun...  23.4 us
    convert_element_type x8, other arithmetic, add_half(): (left.astype(jnp.float32) + right.astype(jnp.float32)).astype(jnp.bfloat16)  19.3 us
    dot_general x2, matrix products, outer_sum(): lax.dot_general(left, right, (((0,), (0,)), ((), ())), preferred_element_...  15.2 us
    unnamed x82, local copies, waits for them, and re-layouts  13.8 us
    dot_general x2, matrix products, times_transposed(): lax.dot_general(left, right, (((1,), (1,)), ((), ())), preferred_element_...  13 us
  transfers between devices with their start and end apart: 41, of which 19 were waited for; matrix products, arithmetic and copies ran while one was open for 27% of the time, Pallas kernels for 15%

profile of v2, /device:TPU:0, one launch (start us, length us, event | category | flops | bytes accessed | tf_op | source)
XLA Modules:
  0.0 320.2 jit_solution(11122993834099910491)
XLA Ops:
  6.8 11.9 %collective-permute-done.6 = bf16[64,2048]{1,0:T(8,128)(2,1)S(1)} collective-permute-done((bf16[64,2048]{1,0:T(8,128)(2,1)}, bf16[64,2048]{1,0:T(8,128)(2,1)S(1)}, u32[]{:S(2)}, u32[]{:S(2)}) %collective-permute-start.6) | collective-permute-done | bytes 262176 | tf_op jit(solution)/shard_map/ppermute | solution.py:171
  18.6 5.1 %collective-permute-done.7 = bf16[64,2048]{1,0:T(8,128)(2,1)S(1)} collective-permute-done((bf16[64,2048]{1,0:T(8,128)(2,1)}, bf16[64,2048]{1,0:T(8,128)(2,1)S(1)}, u32[]{:S(2)}, u32[]{:S(2)}) %collective-permute-start.7) | collective-permute-done | bytes 262176 | tf_op jit(solution)/shard_map/ppermute | solution.py:171
  27.7 5.3 %collective-permute-start.16 = (bf16[64,2048]{1,0:T(8,128)(2,1)}, bf16[64,2048]{1,0:T(8,128)(2,1)S(1)}, u32[]{:S(2)}, u32[]{:S(2)}) collective-permute-start(bf16[64,2048]{1,0:T(8,128)(2,1)} %param.8), channel_id=1, source_target_pairs={{0,8},{1,9},{2,10},{3,11},{4,12},{5,13},{6,14},{7,15},{8,16},{9,17... | collective-permute-start | bytes 786440 | tf_op jit(solution)/shard_map/ppermute | solution.py:171
  47.1 11.3 %collective-permute-done.9 = bf16[6,64,2048]{2,1,0:T(8,128)(2,1)S(1)} collective-permute-done((bf16[6,64,2048]{2,1,0:T(8,128)(2,1)S(1)}, bf16[6,64,2048]{2,1,0:T(8,128)(2,1)S(1)}, u32[]{:S(2)}, u32[]{:S(2)}) %collective-permute-start.9) | collective-permute-done | bytes 1572896 | tf_op jit(solution)/shard_map/ppermute | solution.py:171
  62.2 7.1 %collective-permute-start.1 = (f32[16,128]{1,0:T(8,128)S(1)}, f32[16,128]{1,0:T(8,128)S(1)}, u32[]{:S(2)}, u32[]{:S(2)}) collective-permute-start(f32[16,128]{1,0:T(8,128)S(1)} %get-tuple-element.71), channel_id=1, source_target_pairs={{0,16},{1,17},{2,18},{3,19},{4,20},{5,21},{6,22},{7,23},{8,24},{9,... | collective-permute-start | bytes 24584 | tf_op jit(solution)/shard_map/ppermute | solution.py:171
  96.0 4.5 %shard_map.118.refs_0_ = bf16[16,48,2048]{2,1,0:T(8,128)(2,1)} custom-call(bf16[16,48,128]{2,1,0:T(8,128)(2,1)S(1)} %fusion.26.pick_ref, bf16[8,64,2048]{2,1,0:T(8,128)(2,1)} %pad_maximum_fusion.1.mine_ref, bf16[8,64,2048]{2,1,0:T(8,128)(2,1)} %collective-permute-done.13.other_ref, f32[1,2048]{1,0:T(1,128)S(1)} %bitcast.139), custom_call_target="tpu_custom_call" | custom-call | flops 100663296 | bytes 2883584 | tf_op jit(solution)/shard_map/pallas_call | solution.py:269
  100.5 7.5 %collective-permute-done.18 = bf16[6,64,2048]{2,1,0:T(8,128)(2,1)} collective-permute-done((bf16[6,64,2048]{2,1,0:T(8,128)(2,1)}, bf16[6,64,2048]{2,1,0:T(8,128)(2,1)}, u32[]{:S(2)}, u32[]{:S(2)}) %collective-permute-start.18) | collective-permute-done | bytes 1572896 | tf_op jit(solution)/shard_map/ppermute | solution.py:171
  110.9 9.6 %shard_map.119 = bf16[16,48,2048]{2,1,0:T(8,128)(2,1)S(1)} custom-call(bf16[16,48,128]{2,1,0:T(8,128)(2,1)S(1)} %fusion.26.pick_ref, bf16[12,64,2048]{2,1,0:T(8,128)(2,1)} %constant_dynamic-update-slice_fusion.mine_ref, bf16[12,64,2048]{2,1,0:T(8,128)(2,1)} %collective-permute-done.10.other_ref, ...), custom_call_target="tpu_custom_call", output_to_operand_aliasing={{}: (4, {})} | custom-call | flops 301989888 | bytes 8650752 | tf_op jit(solution)/shard_map/pallas_call | solution.py:269
  120.5 8.3 %fusion.3 = f32[768,1536]{1,0:T(8,128)S(1)} fusion(bf16[768,2048]{1,0:T(8,128)(2,1)S(1)} %bitcast.137, bf16[1,2048,1536]{2,1,0:T(8,128)(2,1)} %param.12), kind=kOutput, calls=%fused_computation.5 | convolution fusion | flops 4831838208 | bytes 14155776 | tf_op jit(solution)/shard_map/dot_general | solution.py:22
  133.6 9.7 %shard_map.122 = (bf16[12,64,2048]{2,1,0:T(8,128)(2,1)S(1)}, bf16[12,64,2048]{2,1,0:T(8,128)(2,1)}) custom-call(bf16[16,48,128]{2,1,0:T(8,128)(2,1)S(1)} %fusion.26.pick_ref, f32[16,48,1]{2,1,0:T(8,128)S(1)} %copy.25.prob_ref, bf16[16,48,2048]{2,1,0:T(8,128)(2,1)} %bitcast.141), custom_call_target="tpu_custom_call" | custom-call | flops 301989888 | bytes 8650752 | tf_op jit(solution)/shard_map/pallas_call | solution.py:312
  152.6 10.3 %shard_map.121 = (bf16[16,48,2048]{2,1,0:T(8,128)(2,1)S(1)}, bf16[16,48,2048]{2,1,0:T(8,128)(2,1)}) custom-call(bf16[16,48,128]{2,1,0:T(8,128)(2,1)S(1)} %copy-done.3, bf16[12,64,2048]{2,1,0:T(8,128)(2,1)} %constant_dynamic-update-slice_fusion.5.mine_ref, ...), custom_call_target="tpu_custom_call", output_to_operand_aliasing={{0}: (4, {}), {1}: (5, {})} | custom-call | flops 301989888 | bytes 11010048 | tf_op jit(solution)/shard_map/pallas_call | solution.py:269
  162.9 6.4 %multiply_convert_fusion.1 = (bf16[768,768]{1,0:T(8,128)(2,1)S(1)}, bf16[768,768]{1,0:T(8,128)(2,1)S(1)}) fusion(f32[768,1536]{1,0:T(8,128)S(1)} %copy-done.24, bf16[768,2048]{1,0:T(8,128)(2,1)} %bitcast.152, bf16[1,768,2048]{2,1,0:T(8,128)(2,1)S(1)} %copy-done), kind=kOutput, calls=%fused_computation.23 | convolution fusion | flops 2423586816 | bytes 13369344 | tf_op jit(solution)/shard_map/dot_general | solution.py:33
  175.4 6.7 %multiply_reduce_fusion = (f32[2048]{0:T(1024)S(1)}, bf16[768,2048]{1,0:T(8,128)(2,1)}) fusion(bf16[16,48,2048]{2,1,0:T(8,128)(2,1)S(1)} %copy-done.6, bf16[768,1536]{1,0:T(8,128)(2,1)S(1)} %pad_maximum_fusion, bf16[1,2048,1536]{2,1,0:T(8,128)(2,1)S(1)} %bitcast.180), kind=kOutput, calls=%fused_computation.7 | convolution fusion | flops 4839700480 | bytes 14950400 | tf_op jit(solution)/shard_map/dot_general | solution.py:33
  182.1 9.5 %shard_map.123 = (bf16[12,64,2048]{2,1,0:T(8,128)(2,1)S(1)}, bf16[12,64,2048]{2,1,0:T(8,128)(2,1)}) custom-call(bf16[16,48,128]{2,1,0:T(8,128)(2,1)S(1)} %copy-done.3, f32[16,48,1]{2,1,0:T(8,128)S(1)} %copy.25.prob_ref, bf16[16,48,2048]{2,1,0:T(8,128)(2,1)} %bitcast.144), custom_call_target="tpu_custom_call" | custom-call | flops 301989888 | bytes 8650752 | tf_op jit(solution)/shard_map/pallas_call | solution.py:312
  194.6 4.3 %shard_map.124 = (bf16[8,64,2048]{2,1,0:T(8,128)(2,1)S(1)}, bf16[8,64,2048]{2,1,0:T(8,128)(2,1)S(1)}) custom-call(bf16[16,48,128]{2,1,0:T(8,128)(2,1)S(1)} %copy-done.3, f32[16,48,1]{2,1,0:T(8,128)S(1)} %copy.25.prob_ref, bf16[16,48,2048]{2,1,0:T(8,128)(2,1)} %bitcast.142, bf16[16,48,2048]{2,1,0:T(8,128)(2,1)} %bitcast.145), custom_call_target="tpu_custom_call" | custom-call | flops 201326592 | bytes 5767168 | tf_op jit(solution)/shard_map/pallas_call | solution.py:312
  201.6 10.2 %collective-permute-done.25 = bf16[3,64,2048]{2,1,0:T(8,128)(2,1)S(1)} collective-permute-done((bf16[3,64,2048]{2,1,0:T(8,128)(2,1)S(1)}, bf16[3,64,2048]{2,1,0:T(8,128)(2,1)S(1)}, u32[]{:S(2)}, u32[]{:S(2)}) %collective-permute-start.25) | collective-permute-done | bytes 786464 | tf_op jit(solution)/shard_map/ppermute | solution.py:171
  223.0 6.1 %add_convert_fusion = bf16[12,64,2048]{2,1,0:T(8,128)(2,1)} fusion(bf16[12,64,2048]{2,1,0:T(8,128)(2,1)} %collective-permute-done.29, bf16[12,64,2048]{2,1,0:T(8,128)(2,1)} %copy-done.10), kind=kLoop, calls=%fused_computation.9 | loop fusion | flops 6291456 | bytes 9437184 | tf_op jit(solution)/shard_map/convert_element_type | solution.py:206
  230.3 6.6 %fusion.11 = bf16[1,768,2048]{2,1,0:T(8,128)(2,1)} fusion(bf16[768,768]{1,0:T(8,128)(2,1)} %copy-done.27, bf16[768,2048]{1,0:T(8,128)(2,1)} %bitcast.153), kind=kOutput, calls=%fused_computation.20 | convolution fusion | flops 2417491968 | bytes 7471104 | tf_op jit(solution)/shard_map/dot_general | solution.py:37
  244.1 8.6 %fusion = bf16[1,2048,1536]{2,1,0:T(8,128)(2,1)} fusion(bf16[768,2048]{1,0:T(8,128)(2,1)S(1)} %bitcast.138, bf16[768,768]{1,0:T(8,128)(2,1)} %copy-done.29, bf16[768,768]{1,0:T(8,128)(2,1)} %copy-done.28), kind=kOutput, calls=%fused_computation.2 | convolution fusion | flops 4839702528 | bytes 11796480 | tf_op jit(solution)/shard_map/dot_general | solution.py:37
  267.9 7.2 %collective-permute-done.23 = bf16[4,64,2048]{2,1,0:T(8,128)(2,1)} collective-permute-done((bf16[4,64,2048]{2,1,0:T(8,128)(2,1)}, bf16[4,64,2048]{2,1,0:T(8,128)(2,1)}, u32[]{:S(2)}, u32[]{:S(2)}) %collective-permute-start.23) | collective-permute-done | bytes 1048608 | tf_op jit(solution)/shard_map/ppermute | solution.py:171
  285.9 5.1 %collective-permute-start.33 = (bf16[64,2048]{1,0:T(8,128)(2,1)S(1)}, bf16[64,2048]{1,0:T(8,128)(2,1)S(1)}, u32[]{:S(2)}, u32[]{:S(2)}) collective-permute-start(bf16[64,2048]{1,0:T(8,128)(2,1)S(1)} %get-tuple-element.52), channel_id=1, source_target_pairs={{0,16},{1,17},{2,18},{3,19},{4,20},{5,21},{6,22},{7,23},{8,24},{9,... | collective-permute-start | bytes 786440 | tf_op jit(solution)/shard_map/ppermute | solution.py:171
  291.2 16.4 %collective-permute-start.27 = (bf16[64,2048]{1,0:T(8,128)(2,1)S(1)}, bf16[64,2048]{1,0:T(8,128)(2,1)S(1)}, u32[]{:S(2)}, u32[]{:S(2)}) collective-permute-start(bf16[64,2048]{1,0:T(8,128)(2,1)S(1)} %copy-done.30), channel_id=1, source_target_pairs={{0,16},{1,17},{2,18},{3,19},{4,20},{5,21},{6,22},{7,23},{8,24},{9,... | collective-permute-start | bytes 786440 | tf_op jit(solution)/shard_map/ppermute | solution.py:171
  307.6 4.9 %collective-permute-done.33 = bf16[64,2048]{1,0:T(8,128)(2,1)S(1)} collective-permute-done((bf16[64,2048]{1,0:T(8,128)(2,1)S(1)}, bf16[64,2048]{1,0:T(8,128)(2,1)S(1)}, u32[]{:S(2)}, u32[]{:S(2)}) %collective-permute-start.33) | collective-permute-done | bytes 262176 | tf_op jit(solution)/shard_map/ppermute | solution.py:171
  312.8 5.2 %collective-permute-done.27 = bf16[64,2048]{1,0:T(8,128)(2,1)S(1)} collective-permute-done((bf16[64,2048]{1,0:T(8,128)(2,1)S(1)}, bf16[64,2048]{1,0:T(8,128)(2,1)S(1)}, u32[]{:S(2)}, u32[]{:S(2)}) %collective-permute-start.27) | collective-permute-done | bytes 262176 | tf_op jit(solution)/shard_map/ppermute | solution.py:171
  (251 shorter events, 131.5 us)
Async XLA Ops:
  0.6 18.0 %collective-permute-start.6 = (bf16[64,2048]{1,0:T(8,128)(2,1)}, bf16[64,2048]{1,0:T(8,128)(2,1)S(1)}, u32[]{:S(2)}, u32[]{:S(2)}) collective-permute-start(bf16[64,2048]{1,0:T(8,128)(2,1)} %param.7), channel_id=1, source_target_pairs={{0,16},{1,17},{2,18},{3,19},{4,20},{5,21},{6,22},{7,23},{8,24},{9,... | collective-permute-start | bytes 786440 | tf_op jit(solution)/shard_map/ppermute | solution.py:171
  6.1 17.6 %collective-permute-start.7 = (bf16[64,2048]{1,0:T(8,128)(2,1)}, bf16[64,2048]{1,0:T(8,128)(2,1)S(1)}, u32[]{:S(2)}, u32[]{:S(2)}) collective-permute-start(bf16[64,2048]{1,0:T(8,128)(2,1)} %param.7), channel_id=1, source_target_pairs={{0,8},{1,9},{2,10},{3,11},{4,12},{5,13},{6,14},{7,15},{8,16},{9,17... | collective-permute-start | bytes 786440 | tf_op jit(solution)/shard_map/ppermute | solution.py:171
  26.5 17.2 %collective-permute-start.11 = (bf16[2,64,2048]{2,1,0:T(8,128)(2,1)S(1)}, bf16[2,64,2048]{2,1,0:T(8,128)(2,1)S(1)}, u32[]{:S(2)}, u32[]{:S(2)}) collective-permute-start(bf16[2,64,2048]{2,1,0:T(8,128)(2,1)S(1)} %pad_maximum_fusion.7), channel_id=1, source_target_pairs={{0,2},{1,5},{2,0},{3,7},{4,6},{5,1},{6,4},{7,3},{8,10},{9,13},{10,... | collective-permute-start | bytes 1572872 | tf_op jit(solution)/shard_map/ppermute | solution.py:171
  27.7 32.0 %collective-permute-start.16 = (bf16[64,2048]{1,0:T(8,128)(2,1)}, bf16[64,2048]{1,0:T(8,128)(2,1)S(1)}, u32[]{:S(2)}, u32[]{:S(2)}) collective-permute-start(bf16[64,2048]{1,0:T(8,128)(2,1)} %param.8), channel_id=1, source_target_pairs={{0,8},{1,9},{2,10},{3,11},{4,12},{5,13},{6,14},{7,15},{8,16},{9,17... | collective-permute-start | bytes 786440 | tf_op jit(solution)/shard_map/ppermute | solution.py:171
  33.0 26.7 %collective-permute-start.15 = (bf16[64,2048]{1,0:T(8,128)(2,1)}, bf16[64,2048]{1,0:T(8,128)(2,1)S(1)}, u32[]{:S(2)}, u32[]{:S(2)}) collective-permute-start(bf16[64,2048]{1,0:T(8,128)(2,1)} %param.8), channel_id=1, source_target_pairs={{0,16},{1,17},{2,18},{3,19},{4,20},{5,21},{6,22},{7,23},{8,24},{9,... | collective-permute-start | bytes 786440 | tf_op jit(solution)/shard_map/ppermute | solution.py:171
  34.8 24.9 %collective-permute-start.14 = (bf16[64,2048]{1,0:T(8,128)(2,1)}, bf16[64,2048]{1,0:T(8,128)(2,1)S(1)}, u32[]{:S(2)}, u32[]{:S(2)}) collective-permute-start(bf16[64,2048]{1,0:T(8,128)(2,1)} %param.8), channel_id=1, source_target_pairs={{0,24},{1,25},{2,26},{3,27},{4,28},{5,29},{6,30},{7,31},{8,0},{9,1... | collective-permute-start | bytes 786440 | tf_op jit(solution)/shard_map/ppermute | solution.py:171
  37.9 20.5 %collective-permute-start.9 = (bf16[6,64,2048]{2,1,0:T(8,128)(2,1)S(1)}, bf16[6,64,2048]{2,1,0:T(8,128)(2,1)S(1)}, u32[]{:S(2)}, u32[]{:S(2)}) collective-permute-start(bf16[6,64,2048]{2,1,0:T(8,128)(2,1)S(1)} %pad_maximum_fusion.2), channel_id=1, source_target_pairs={{0,4},{1,3},{2,6},{3,1},{4,0},{5,7},{6,2},{7,5},{8,12},{9,11},{10,... | collective-permute-start | bytes 4718600 | tf_op jit(solution)/shard_map/ppermute | solution.py:171
  43.8 33.1 %collective-permute-start.12 = (bf16[4,64,2048]{2,1,0:T(8,128)(2,1)S(1)}, bf16[4,64,2048]{2,1,0:T(8,128)(2,1)S(1)}, u32[]{:S(2)}, u32[]{:S(2)}) collective-permute-start(bf16[4,64,2048]{2,1,0:T(8,128)(2,1)S(1)} %pad_maximum_fusion.4), channel_id=1, source_target_pairs={{0,4},{1,3},{2,6},{3,1},{4,0},{5,7},{6,2},{7,5},{8,12},{9,11},{10,... | collective-permute-start | bytes 3145736 | tf_op jit(solution)/shard_map/ppermute | solution.py:171
  59.7 51.2 %collective-permute-start.10 = (bf16[12,64,2048]{2,1,0:T(8,128)(2,1)}, bf16[12,64,2048]{2,1,0:T(8,128)(2,1)}, u32[]{:S(2)}, u32[]{:S(2)}) collective-permute-start(bf16[12,64,2048]{2,1,0:T(8,128)(2,1)} %constant_dynamic-update-slice_fusion.mine_ref), channel_id=1, source_target_pairs={{0,1},{1,0},{2,3},{3,2},{4,5},{5,4},{6,7},{7,6},{8,9},{9,8},{10,11... | collective-permute-start | bytes 9437192 | tf_op jit(solution)/shard_map/ppermute | solution.py:171
  60.7 23.9 %collective-permute-start.17 = (bf16[3,64,2048]{2,1,0:T(8,128)(2,1)}, bf16[3,64,2048]{2,1,0:T(8,128)(2,1)}, u32[]{:S(2)}, u32[]{:S(2)}) collective-permute-start(bf16[3,64,2048]{2,1,0:T(8,128)(2,1)} %pad_maximum_fusion.6), channel_id=1, source_target_pairs={{0,2},{1,5},{2,0},{3,7},{4,6},{5,1},{6,4},{7,3},{8,10},{9,13},{10,... | collective-permute-start | bytes 2359304 | tf_op jit(solution)/shard_map/ppermute | solution.py:171
  78.5 17.6 %collective-permute-start.13 = (bf16[8,64,2048]{2,1,0:T(8,128)(2,1)}, bf16[8,64,2048]{2,1,0:T(8,128)(2,1)}, u32[]{:S(2)}, u32[]{:S(2)}) collective-permute-start(bf16[8,64,2048]{2,1,0:T(8,128)(2,1)} %pad_maximum_fusion.1.mine_ref), channel_id=1, source_target_pairs={{0,1},{1,0},{2,3},{3,2},{4,5},{5,4},{6,7},{7,6},{8,9},{9,8},{10,11... | collective-permute-start | bytes 6291464 | tf_op jit(solution)/shard_map/ppermute | solution.py:171
  87.3 20.7 %collective-permute-start.18 = (bf16[6,64,2048]{2,1,0:T(8,128)(2,1)}, bf16[6,64,2048]{2,1,0:T(8,128)(2,1)}, u32[]{:S(2)}, u32[]{:S(2)}) collective-permute-start(bf16[6,64,2048]{2,1,0:T(8,128)(2,1)} %pad_maximum_fusion.3), channel_id=1, source_target_pairs={{0,4},{1,3},{2,6},{3,1},{4,0},{5,7},{6,2},{7,5},{8,12},{9,11},{10,... | collective-permute-start | bytes 4718600 | tf_op jit(solution)/shard_map/ppermute | solution.py:171
  110.9 39.8 %collective-permute-start.19 = (bf16[12,64,2048]{2,1,0:T(8,128)(2,1)}, bf16[12,64,2048]{2,1,0:T(8,128)(2,1)}, u32[]{:S(2)}, u32[]{:S(2)}) collective-permute-start(bf16[12,64,2048]{2,1,0:T(8,128)(2,1)} %constant_dynamic-update-slice_fusion.5.mine_ref), channel_id=1, source_target_pairs={{0,1},{1,0},{2,3},{3,2},{4,5},{5,4},{6,7},{7,6},{8,9},{9,8},{10,11... | collective-permute-start | bytes 9437192 | tf_op jit(solution)/shard_map/ppermute | solution.py:171
  145.0 24.3 %collective-permute-start.20 = (bf16[12,64,2048]{2,1,0:T(8,128)(2,1)}, bf16[12,64,2048]{2,1,0:T(8,128)(2,1)}, u32[]{:S(2)}, u32[]{:S(2)}) collective-permute-start(bf16[12,64,2048]{2,1,0:T(8,128)(2,1)} %get-tuple-element.30), channel_id=1, source_target_pairs={{0,1},{1,0},{2,3},{3,2},{4,5},{5,4},{6,7},{7,6},{8,9},{9,8},{10,11... | collective-permute-start | bytes 9437192 | tf_op jit(solution)/shard_map/ppermute | solution.py:171
  173.4 20.5 %collective-permute-start.21 = (bf16[6,64,2048]{2,1,0:T(8,128)(2,1)S(1)}, bf16[6,64,2048]{2,1,0:T(8,128)(2,1)S(1)}, u32[]{:S(2)}, u32[]{:S(2)}) collective-permute-start(bf16[6,64,2048]{2,1,0:T(8,128)(2,1)S(1)} %slice.239), channel_id=1, source_target_pairs={{0,4},{1,3},{2,6},{3,1},{4,0},{5,7},{6,2},{7,5},{8,12},{9,11},{10,... | collective-permute-start | bytes 4718600 | tf_op jit(solution)/shard_map/ppermute | solution.py:171
  198.9 14.1 %collective-permute-start.22 = (bf16[8,64,2048]{2,1,0:T(8,128)(2,1)S(1)}, bf16[8,64,2048]{2,1,0:T(8,128)(2,1)S(1)}, u32[]{:S(2)}, u32[]{:S(2)}) collective-permute-start(bf16[8,64,2048]{2,1,0:T(8,128)(2,1)S(1)} %get-tuple-element.37), channel_id=1, source_target_pairs={{0,1},{1,0},{2,3},{3,2},{4,5},{5,4},{6,7},{7,6},{8,9},{9,8},{10,11... | collective-permute-start | bytes 6291464 | tf_op jit(solution)/shard_map/ppermute | solution.py:171
  199.2 23.8 %collective-permute-start.29 = (bf16[12,64,2048]{2,1,0:T(8,128)(2,1)}, bf16[12,64,2048]{2,1,0:T(8,128)(2,1)}, u32[]{:S(2)}, u32[]{:S(2)}) collective-permute-start(bf16[12,64,2048]{2,1,0:T(8,128)(2,1)} %get-tuple-element.34), channel_id=1, source_target_pairs={{0,1},{1,0},{2,3},{3,2},{4,5},{5,4},{6,7},{7,6},{8,9},{9,8},{10,11... | collective-permute-start | bytes 9437192 | tf_op jit(solution)/shard_map/ppermute | solution.py:171
  217.3 95.4 %collective-permute-start.26 = (bf16[64,2048]{1,0:T(8,128)(2,1)}, bf16[64,2048]{1,0:T(8,128)(2,1)}, u32[]{:S(2)}, u32[]{:S(2)}) collective-permute-start(bf16[64,2048]{1,0:T(8,128)(2,1)} %get-tuple-element.53), channel_id=1, source_target_pairs={{0,8},{1,9},{2,10},{3,11},{4,12},{5,13},{6,14},{7,15},{8,16},{9,17... | collective-permute-start | bytes 786440 | tf_op jit(solution)/shard_map/ppermute | solution.py:171
  220.7 92.1 %collective-permute-start.28 = (bf16[64,2048]{1,0:T(8,128)(2,1)}, bf16[64,2048]{1,0:T(8,128)(2,1)}, u32[]{:S(2)}, u32[]{:S(2)}) collective-permute-start(bf16[64,2048]{1,0:T(8,128)(2,1)} %get-tuple-element.54), channel_id=1, source_target_pairs={{0,24},{1,25},{2,26},{3,27},{4,28},{5,29},{6,30},{7,31},{8,0},{9,1... | collective-permute-start | bytes 786440 | tf_op jit(solution)/shard_map/ppermute | solution.py:171
  238.2 23.4 %collective-permute-start.30 = (bf16[6,64,2048]{2,1,0:T(8,128)(2,1)}, bf16[6,64,2048]{2,1,0:T(8,128)(2,1)}, u32[]{:S(2)}, u32[]{:S(2)}) collective-permute-start(bf16[6,64,2048]{2,1,0:T(8,128)(2,1)} %slice.252), channel_id=1, source_target_pairs={{0,4},{1,3},{2,6},{3,1},{4,0},{5,7},{6,2},{7,5},{8,12},{9,11},{10,... | collective-permute-start | bytes 4718600 | tf_op jit(solution)/shard_map/ppermute | solution.py:171
  240.2 34.9 %collective-permute-start.23 = (bf16[4,64,2048]{2,1,0:T(8,128)(2,1)}, bf16[4,64,2048]{2,1,0:T(8,128)(2,1)}, u32[]{:S(2)}, u32[]{:S(2)}) collective-permute-start(bf16[4,64,2048]{2,1,0:T(8,128)(2,1)} %slice.241), channel_id=1, source_target_pairs={{0,4},{1,3},{2,6},{3,1},{4,0},{5,7},{6,2},{7,5},{8,12},{9,11},{10,... | collective-permute-start | bytes 3145736 | tf_op jit(solution)/shard_map/ppermute | solution.py:171
  281.8 25.8 %collective-permute-start.34 = (bf16[64,2048]{1,0:T(8,128)(2,1)S(1)}, bf16[64,2048]{1,0:T(8,128)(2,1)S(1)}, u32[]{:S(2)}, u32[]{:S(2)}) collective-permute-start(bf16[64,2048]{1,0:T(8,128)(2,1)S(1)} %get-tuple-element.51), channel_id=1, source_target_pairs={{0,24},{1,25},{2,26},{3,27},{4,28},{5,29},{6,30},{7,31},{8,0},{9,1... | collective-permute-start | bytes 786440 | tf_op jit(solution)/shard_map/ppermute | solution.py:171
  285.9 26.6 %collective-permute-start.33 = (bf16[64,2048]{1,0:T(8,128)(2,1)S(1)}, bf16[64,2048]{1,0:T(8,128)(2,1)S(1)}, u32[]{:S(2)}, u32[]{:S(2)}) collective-permute-start(bf16[64,2048]{1,0:T(8,128)(2,1)S(1)} %get-tuple-element.52), channel_id=1, source_target_pairs={{0,16},{1,17},{2,18},{3,19},{4,20},{5,21},{6,22},{7,23},{8,24},{9,... | collective-permute-start | bytes 786440 | tf_op jit(solution)/shard_map/ppermute | solution.py:171
  291.2 26.8 %collective-permute-start.27 = (bf16[64,2048]{1,0:T(8,128)(2,1)S(1)}, bf16[64,2048]{1,0:T(8,128)(2,1)S(1)}, u32[]{:S(2)}, u32[]{:S(2)}) collective-permute-start(bf16[64,2048]{1,0:T(8,128)(2,1)S(1)} %copy-done.30), channel_id=1, source_target_pairs={{0,16},{1,17},{2,18},{3,19},{4,20},{5,21},{6,22},{7,23},{8,24},{9,... | collective-permute-start | bytes 786440 | tf_op jit(solution)/shard_map/ppermute | solution.py:171
  (55 other events, 636.5 us)

commit v3 on v2

--- a/solution.py
+++ b/solution.py
@@ -196,26 +196,24 @@
     return lax.optimization_barrier((array,) + others)[0]
 
 
-def gather_plane(block):
-    pair = jnp.concatenate([block, send_second(block)])
-    quad = jnp.concatenate([pair, send_first(pair)])
-    return quad, send_core(quad)
-
-
-def add_half(left, right):
-    return (left.astype(jnp.float32) + right.astype(jnp.float32)).astype(jnp.bfloat16)
-
-
-def fold(array, sender):
-    half = array.shape[0] // 2
-    return add_half(array[:half], sender(array[half:]))
+def together(*arrays):
+    return lax.optimization_barrier(arrays)
+
+
+def add_up(*terms):
+    return sum(term.astype(jnp.float32) for term in terms)
+
+
+def narrow(value):
+    return value.astype(jnp.bfloat16)
 
 
 def gather_tables(table):
     steps = lax.axis_size("expert") // 4
     planes = jnp.stack([table] + [send_along(table, -step) for step in range(1, steps)])
     pair = jnp.stack([planes, send_second(planes)])
-    return jnp.stack([pair, send_first(pair)])
+    last = send_first(pair)
+    return jnp.stack([pair, last]), last
 
 
 def far_first(array):
@@ -228,95 +226,110 @@
     return jnp.concatenate([array[4 * (steps - 1):].reshape((2, 2, 1) + array.shape[1:]), far], axis=2)
 
 
-def swapped(index, count):
-    bits = index // count
-    return ((bits % 2) * 2 + bits // 2) * count + index % count
-
-
-def chosen_rows(pick_ref, mine_ref, other_ref):
-    half = mine_ref.shape[1]
-    rows = jnp.dot(pick_ref[0][:, :half], mine_ref[0], preferred_element_type=jnp.float32)
-    return rows + jnp.dot(pick_ref[0][:, half:], other_ref[0], preferred_element_type=jnp.float32)
-
-
-def select_norm_kernel(pick_ref, mine_ref, other_ref, gain_ref, *refs):
-    normed_ref = refs[-1]
-    rows = chosen_rows(pick_ref, mine_ref, other_ref)
-    inv_rms = lax.rsqrt(jnp.mean(rows * rows, axis=1, keepdims=True) + 1e-06)
-    normed_ref[0] = (rows * inv_rms * gain_ref[...]).astype(jnp.bfloat16)
-
-
-def select_grad_kernel(pick_ref, mine_ref, other_ref, prob_ref, *refs):
-    cot_ref, grad_ref = refs[-2:]
-    rows = chosen_rows(pick_ref, mine_ref, other_ref)
-    cot_ref[0] = rows.astype(jnp.bfloat16)
-    grad_ref[0] = (rows * prob_ref[0]).astype(jnp.bfloat16)
-
-
-def select(kernel, outputs, pick, blocks, extra, count, arrays, which, first_group, held):
+def swapped(index):
+    return (index % 2) * 2 + index // 2
+
+
+def chosen_rows(pick, mine, other):
+    half = mine.shape[0]
+    rows = jnp.dot(pick[:, :half], mine, preferred_element_type=jnp.float32)
+    return rows + jnp.dot(pick[:, half:], other, preferred_element_type=jnp.float32)
+
+
+def select_kernel(kinds, count, *refs):
+    pick_ref, prob_ref, gain_ref, pieces = refs[0], refs[1], refs[2], refs[3:7]
+    outputs = refs[len(refs) - sum(1 if kind == "norm" else 2 for kind in kinds):]
+
+    def work(mine_ref, other_ref):
+        for group in range(count):
+            places = iter(outputs)
+            for number, kind in enumerate(kinds):
+                block = group * len(kinds) + number
+                rows = chosen_rows(pick_ref[group], mine_ref[block], other_ref[block])
+                if kind == "norm":
+                    inv_rms = lax.rsqrt(jnp.mean(rows * rows, axis=1, keepdims=True) + 1e-06)
+                    next(places)[group] = (rows * inv_rms * gain_ref[...]).astype(jnp.bfloat16)
+                else:
+                    next(places)[group] = rows.astype(jnp.bfloat16)
+                    next(places)[group] = (rows * prob_ref[group]).astype(jnp.bfloat16)
+
+    for first in range(2):
+        for second in range(2):
+            pl.when(pl.program_id(0) == first * 2 + second)(
+                functools.partial(work, pieces[first], pieces[2 + second])
+            )
+
+
+def select(kinds, pick, prob, gain, pieces, count, first_group, held):
     groups, capacity, group_rows = pick.shape
-    mine, other = blocks
-    half, features = mine.shape[1:]
+    blocks = count * len(kinds)
+    half, features = pieces[0].shape[1:]
+    outputs = sum(1 if kind == "norm" else 2 for kind in kinds)
     out = jax.ShapeDtypeStruct((groups, capacity, features), jnp.bfloat16)
+    first_block = first_group // count
 
     def group_spec(*shape):
-        return pl.BlockSpec((1,) + shape, lambda i: (first_group + i, 0, 0))
-
-    if extra.ndim == 2:
-        extra_spec = pl.BlockSpec(extra.shape, lambda i: (0, 0))
-    else:
-        extra_spec = group_spec(capacity, 1)
+        return pl.BlockSpec((count,) + shape, lambda i: (first_block + i, 0, 0))
+
+    def piece_spec(place):
+        return pl.BlockSpec((blocks, half, features), lambda i: (place(i), 0, 0))
+
     return pl.pallas_call(
-        kernel,
-        grid=(4 * count,),
+        functools.partial(select_kernel, kinds, count),
+        grid=(4,),
         in_specs=[
             group_spec(capacity, group_rows),
-            pl.BlockSpec((1, half, features), lambda i: (i * arrays + which, 0, 0)),
-            pl.BlockSpec((1, half, features), lambda i: (swapped(i, count) * arrays + which, 0, 0)),
-            extra_spec,
+            group_spec(capacity, 1),
+            pl.BlockSpec((1, features), lambda i: (0, 0)),
+            piece_spec(lambda i: jnp.minimum(i, 1)),
+            piece_spec(lambda i: jnp.maximum(i - 2, 0)),
+            piece_spec(lambda i: i // 2),
+            piece_spec(lambda i: jnp.maximum(i - 2, 0)),
         ] + [pl.BlockSpec(memory_space=pl.ANY)] * len(held),
         out_specs=[group_spec(capacity, features)] * outputs,
         out_shape=[out] * outputs,
-        input_output_aliases={4 + n: n for n in range(len(held))},
+        input_output_aliases={7 + n: n for n in range(len(held))},
         compiler_params=pltpu.CompilerParams(vmem_limit_bytes=VMEM_LIMIT),
         cost_estimate=pl.CostEstimate(
-            flops=8 * count * capacity * group_rows * features,
-            bytes_accessed=16 * count * half * features + 8 * outputs * count * capacity * features,
+            flops=8 * blocks * capacity * group_rows * features,
+            bytes_accessed=16 * blocks * half * features + 8 * outputs * count * capacity * features,
             transcendentals=0,
         ),
-    )(pick, mine, other, extra, *held)
-
-
-def expand_kernel(weighted, pick_ref, prob_ref, *refs):
+    )(pick, prob, gain, *pieces, *held)
+
+
+def expand_kernel(weighted, count, pick_ref, prob_ref, *refs):
     sources, (mine_ref, other_ref) = refs[:-2], refs[-2:]
     half = mine_ref.shape[1]
-    pick = pick_ref[0]
-    for place, (source_ref, by_prob) in enumerate(zip(sources, weighted)):
-        rows = source_ref[0]
-        if by_prob:
-            rows = (rows.astype(jnp.float32) * prob_ref[0]).astype(jnp.bfloat16)
-        for columns, out_ref in ((pick[:, :half], mine_ref), (pick[:, half:], other_ref)):
-            out_ref[place] = lax.dot_general(
-                columns, rows, (((0,), (0,)), ((), ())), preferred_element_type=jnp.float32
-            ).astype(jnp.bfloat16)
+    for group in range(count):
+        pick = pick_ref[group]
+        for number, (source_ref, by_prob) in enumerate(zip(sources, weighted)):
+            rows = source_ref[group]
+            if by_prob:
+                rows = (rows.astype(jnp.float32) * prob_ref[group]).astype(jnp.bfloat16)
+            for columns, out_ref in ((pick[:, :half], mine_ref), (pick[:, half:], other_ref)):
+                out_ref[group * len(sources) + number] = lax.dot_general(
+                    columns, rows, (((0,), (0,)), ((), ())), preferred_element_type=jnp.float32
+                ).astype(jnp.bfloat16)
 
 
 def expand(pick, prob, slots, weighted, count, first_group):
     _, capacity, group_rows = pick.shape
     half, features, arrays = group_rows // 2, slots[0].shape[2], len(slots)
     out = jax.ShapeDtypeStruct((4 * count * arrays, half, features), jnp.bfloat16)
+    first_block = first_group // count
 
     def group_spec(*shape):
-        return pl.BlockSpec((1,) + shape, lambda i: (first_group + i, 0, 0))
+        return pl.BlockSpec((count,) + shape, lambda i: (first_block + i, 0, 0))
 
     return pl.pallas_call(
-        functools.partial(expand_kernel, weighted),
-        grid=(4 * count,),
+        functools.partial(expand_kernel, weighted, count),
+        grid=(4,),
         in_specs=[group_spec(capacity, group_rows), group_spec(capacity, 1)]
         + [group_spec(capacity, features)] * arrays,
         out_specs=[
-            pl.BlockSpec((arrays, half, features), lambda i: (i, 0, 0)),
-            pl.BlockSpec((arrays, half, features), lambda i: (swapped(i, count), 0, 0)),
+            pl.BlockSpec((count * arrays, half, features), lambda i: (i, 0, 0)),
+            pl.BlockSpec((count * arrays, half, features), lambda i: (swapped(i), 0, 0)),
         ],
         out_shape=[out, out],
         compiler_params=pltpu.CompilerParams(vmem_limit_bytes=VMEM_LIMIT),
@@ -368,14 +381,28 @@
     capacity = 3 * group_rows * TOP // (2 * EXP_DEV * expert_size)
     gate_up, down_proj = gate_up_weight[0], down_weight[0]
 
-    tables = gather_tables(jnp.concatenate([expert_ids.T.astype(jnp.float32), gate_probs.T]))
-    near_blocks = gather_plane(jnp.stack([tokens, cotangent]))
+    near_own = jnp.stack([tokens, cotangent])
+    near_pair = jnp.concatenate([near_own, send_second(near_own)])
+    near_far_pair = send_first(near_pair)
+    tables, tables_last = gather_tables(
+        jnp.concatenate([expert_ids.T.astype(jnp.float32), gate_probs.T])
+    )
     token_far = jnp.stack([send_along(tokens, -step) for step in range(1, steps)])
-    far_tokens = gather_plane(token_far)
+    token_far = after(token_far, tables_last)
     late_cot = after(cotangent, token_far)
-    far_cots = gather_plane(
-        after(jnp.stack([send_along(late_cot, -step) for step in range(1, steps)]), far_tokens[0])
-    )
+    cot_steps = [send_along(late_cot, -step) for step in range(1, steps)]
+    token_second = after(send_second(token_far), near_far_pair, cot_steps[0])
+    token_pair = jnp.concatenate([token_far, token_second])
+    token_far_pair = after(send_first(token_pair), *cot_steps)
+    near_pieces = (near_pair, near_far_pair, send_core(near_pair), send_core(near_far_pair))
+    cot_far = after(jnp.stack(cot_steps), token_far_pair)
+    cot_second = send_second(cot_far)
+    token_pieces = (
+        token_pair, token_far_pair, send_core(token_pair), after(send_core(token_far_pair), cot_second)
+    )
+    cot_pair = jnp.concatenate([cot_far, cot_second])
+    cot_far_pair = send_first(cot_pair)
+    cot_pieces = (cot_pair, cot_far_pair, send_core(cot_pair), send_core(cot_far_pair))
 
     tables = far_first(tables)
     tables = jnp.where(core == 0, tables, jnp.roll(tables, half, axis=2))
@@ -391,48 +418,68 @@
     pick = placed.astype(jnp.bfloat16)
     slot_prob = jnp.sum(jnp.where(placed, weight_of[:, None, :], 0.0), axis=2, keepdims=True)
 
-    held = select(select_norm_kernel, 1, pick, near_blocks, gain[None, :], 1, 2, 0, far, ())
-    rows, = select(
-        select_norm_kernel, 1, pick, far_tokens, gain[None, :], steps - 1, 1, 0, 0, tuple(held)
-    )
-    held = select(select_grad_kernel, 2, pick, near_blocks, slot_prob, 1, 2, 1, far, ())
+    gain_row = gain[None, :]
+    rows, cots, grads = select(("norm", "grad"), pick, slot_prob, gain_row, near_pieces, 1, far, ())
+    rows, = select(("norm",), pick, slot_prob, gain_row, token_pieces, steps - 1, 0, (rows,))
     rows = rows.reshape(-1, features)
     gate_pre, up_pre, sigmoid_gate, hidden, block_out = expert_forward(rows, gate_up, down_proj)
     out_slots = block_out.reshape(expert_size, capacity, features)
     out_mine, out_other = expand(pick, slot_prob, (out_slots,), (True,), steps - 1, 0)
 
+    half_far, one_far = 2 * (steps - 1), steps - 1
+    out_core = send_core(out_other)
+    out_upper = narrow(add_up(out_mine[half_far:], out_core[half_far:]))
+    out_first = send_first(out_upper)
     cots, grads = select(
-        select_grad_kernel, 2, pick, far_cots, slot_prob, steps - 1, 1, 0, 0, tuple(held)
-    )
-    grads = after(grads.reshape(-1, features), out_other)
+        ("grad",), after(pick, out_upper), slot_prob, gain_row, cot_pieces, steps - 1, 0, (cots, grads)
+    )
+    grads = grads.reshape(-1, features)
     joined_grad = backward_inner(grads, down_proj, gate_pre, up_pre, sigmoid_gate)
-    out_quad = add_half(out_mine, send_core(out_other))
-    input_grad = times_transposed(after(joined_grad, out_quad), gate_up).astype(jnp.bfloat16)
+    input_grad = times_transposed(joined_grad, gate_up).astype(jnp.bfloat16)
     input_slots = input_grad.reshape(expert_size, capacity, features)
     in_mine, in_other = expand(pick, slot_prob, (input_slots,), (False,), steps - 1, 0)
-    out_pair = fold(out_quad, send_first)
+    in_core = send_core(in_other)
+    out_middle = narrow(
+        add_up(out_mine[one_far:half_far], out_core[one_far:half_far], after(out_first, in_other)[one_far:])
+    )
+    out_second = send_second(out_middle)
     near_mine, near_other = expand(
-        pick, slot_prob, (out_slots, after(input_slots, in_other, out_pair)), (True, False), 1, far
-    )
-    in_quad = add_half(in_mine, send_core(in_other))
-    down_part = outer_sum(after(hidden, near_other, in_quad), grads)
-    near_quad = add_half(near_mine, send_core(near_other))
-    out_far = fold(out_pair, send_second)
-    gate_up_part = outer_sum(after(rows, in_quad, near_quad, out_far), joined_grad)
-
-    out_far = [send_along(out_far[step - 1], step) for step in range(1, steps)]
-    in_far = fold(fold(in_quad, send_first), send_second)
-    in_far = [send_along(in_far[step - 1], step) for step in range(1, steps)]
-    near_sum = fold(fold(near_quad, send_first), send_second).astype(jnp.float32)
-    out_sum = near_sum[0] + sum(block.astype(jnp.float32) for block in out_far)
-    normed_grad = near_sum[1] + sum(block.astype(jnp.float32) for block in in_far)
-
+        pick, slot_prob, (out_slots, after(input_slots, in_other)), (True, False), 1, far
+    )
+    near_core = send_core(near_other)
+    in_upper = narrow(add_up(in_mine[half_far:], after(in_core, out_middle, near_other)[half_far:]))
+    in_first = send_first(in_upper)
+    down_part = outer_sum(after(hidden, in_upper), grads)
     gain_term = jnp.sum(input_grad.astype(jnp.float32) * rows.astype(jnp.float32), axis=0) / gain
     prob_value = jnp.sum(cots.astype(jnp.float32) * out_slots.astype(jnp.float32), axis=2)
     prob_rows = jnp.sum(jnp.where(placed, prob_value[:, :, None], 0.0), axis=1)
     columns = from_far_first(jnp.where(matches, prob_rows[:, None, :], 0.0), steps)
     columns = jnp.where(core == 0, columns, jnp.swapaxes(columns, 0, 1))
-    prob_sum, gain_grad = home_terms(after(columns, near_quad), after(gain_term, near_quad))
+    prob_sum, gain_grad = home_terms(after(columns, in_upper), after(gain_term, in_upper))
+
+    def own_plane(mine, core_part, first_part, second_part, count):
+        return add_up(mine[:count], core_part[:count], first_part[:count], second_part[:count])
+
+    out_second, down_part = together(out_second, down_part)
+    out_planes = narrow(own_plane(out_mine, out_core, out_first, out_second, one_far))
+    out_far = [send_along(out_planes[step - 1], step) for step in range(1, steps)]
+    in_first, near_core, prob_sum, gain_grad = together(
+        in_first, near_core, prob_sum, gain_grad, *out_far[:2]
+    )[:4]
+    in_middle = narrow(
+        add_up(in_mine[one_far:half_far], in_core[one_far:half_far], in_first[one_far:])
+    )
+    in_second = send_second(in_middle)
+    in_planes = narrow(own_plane(in_mine, in_core, in_first, after(in_second, *out_far), one_far))
+    in_far = [send_along(in_planes[step - 1], step) for step in range(1, steps)]
+    gate_up_part = outer_sum(after(rows, in_far[0]), joined_grad)
+    near_upper = narrow(add_up(near_mine[4:], after(near_core, in_planes)[4:]))
+    near_first = send_first(near_upper)
+    near_middle = narrow(add_up(near_mine[2:4], near_core[2:4], near_first[2:]))
+    near_second = send_second(near_middle)
+    near_sum = own_plane(near_mine, near_core, near_first, near_second, 2)
+    out_sum = near_sum[0] + add_up(*out_far)
+    normed_grad = near_sum[1] + add_up(*in_far)
 
     scaled_own, inv_own = normalize(tokens)
     mixed = (tokens.astype(jnp.float32) + out_sum).astype(jnp.bfloat16)

time: 322 us -> 311 us (0.966)
  waiting for transfers between devices: 86.6 us -> 108 us
  Pallas kernels: 52.1 us -> 30.8 us
  local copies, waits for them, and re-layouts: 25.2 us -> 16.5 us
  starting transfers between devices: 79.7 us -> 73.8 us
    pallas_call x7 -> x6, Pallas kernels: 52.1 us -> 30.8 us  [the longest x3 16.6 us: select(): pl.pallas_call(functools.partial(select_kernel, kinds, count), grid=(4,),...]
    ppermute x41 -> x44, waiting for transfers between devices: 86.6 us -> 108 us  [send(): return lax.ppermute(array, BOTH, pairs)]
    ppermute x41 -> x44, starting transfers between devices: 79.7 us -> 73.8 us  [send(): return lax.ppermute(array, BOTH, pairs)]
    unnamed x82 -> x72, local copies, waits for them, and re-layouts: 13.8 us -> 9.62 us
    concatenate x5 -> x1, other arithmetic: 4.62 us -> 1.13 us  [broadcast_shards(): near_pair = jnp.concatenate([near_own, send_second(near_own)])]
    convert_element_type x9 -> x8, other arithmetic: 19.5 us -> 17.9 us  [narrow(): return value.astype(jnp.bfloat16)]
  transfers between devices with their start and end apart: 41 -> 44, of which waited for: 19 -> 21; matrix products, arithmetic and copies ran while one was open for 27% -> 15% of each run, Pallas kernels for 15% -> 3%
where the time goes in v3:
time: 311 us; the launch traced here: 309 us
  waiting for transfers between devices  108 us (35%)
  starting transfers between devices  73.8 us (24%)
  matrix products  42.1 us (14%)
  other arithmetic  36.9 us (12%)
  Pallas kernels  30.8 us (10%)
  local copies, waits for them, and re-layouts  16.5 us (5%)
    ppermute x44, waiting for transfers between devices, send(): return lax.ppermute(array, BOTH, pairs)  108 us
    ppermute x44, starting transfers between devices, send(): return lax.ppermute(array, BOTH, pairs)  73.8 us
    convert_element_type x8, other arithmetic, narrow(): return value.astype(jnp.bfloat16)  17.9 us
    pallas_call x3, Pallas kernels, select(): pl.pallas_call(functools.partial(select_kernel, kinds, count), grid=(4,),...  16.6 us
    dot_general x2, matrix products, times_transposed(): lax.dot_general(left, right, (((1,), (1,)), ((), ())), preferred_element_...  16.1 us
    pallas_call x3, Pallas kernels, expand(): pl.pallas_call(functools.partial(expand_kernel, weighted, count), grid=(4...  14.1 us
    dot_general x2, matrix products, outer_sum(): lax.dot_general(left, right, (((0,), (0,)), ((), ())), preferred_element_...  13.8 us
    unnamed x72, local copies, waits for them, and re-layouts  9.62 us
  transfers between devices with their start and end apart: 44, of which 21 were waited for; matrix products, arithmetic and copies ran while one was open for 15% of the time, Pallas kernels for 3%

profile of v3, /device:TPU:0, one launch (start us, length us, event | category | flops | bytes accessed | tf_op | source)
XLA Modules:
  0.0 308.8 jit_solution(9695782225707244128)
XLA Ops:
  23.1 8.4 %collective-permute-done.6 = bf16[64,2048]{1,0:T(8,128)(2,1)S(1)} collective-permute-done((bf16[64,2048]{1,0:T(8,128)(2,1)}, bf16[64,2048]{1,0:T(8,128)(2,1)S(1)}, u32[]{:S(2)}, u32[]{:S(2)}) %collective-permute-start.6) | collective-permute-done | bytes 262176 | tf_op jit(solution)/shard_map/ppermute | solution.py:171
  38.7 4.3 %collective-permute-done.11 = bf16[64,2048]{1,0:T(8,128)(2,1)S(1)} collective-permute-done((bf16[64,2048]{1,0:T(8,128)(2,1)S(1)}, bf16[64,2048]{1,0:T(8,128)(2,1)S(1)}, u32[]{:S(2)}, u32[]{:S(2)}) %collective-permute-start.11) | collective-permute-done | bytes 262176 | tf_op jit(solution)/shard_map/ppermute | solution.py:171
  51.7 9.1 %collective-permute-start.13 = (bf16[64,2048]{1,0:T(8,128)(2,1)S(1)}, bf16[64,2048]{1,0:T(8,128)(2,1)S(1)}, u32[]{:S(2)}, u32[]{:S(2)}) collective-permute-start(bf16[64,2048]{1,0:T(8,128)(2,1)S(1)} %copy-done.19), channel_id=1, source_target_pairs={{0,16},{1,17},{2,18},{3,19},{4,20},{5,21},{6,22},{7,23},{8,24},{9,... | collective-permute-start | bytes 786440 | tf_op jit(solution)/shard_map/ppermute | solution.py:171
  60.8 4.3 %collective-permute-done.13 = bf16[64,2048]{1,0:T(8,128)(2,1)S(1)} collective-permute-done((bf16[64,2048]{1,0:T(8,128)(2,1)S(1)}, bf16[64,2048]{1,0:T(8,128)(2,1)S(1)}, u32[]{:S(2)}, u32[]{:S(2)}) %collective-permute-start.13) | collective-permute-done | bytes 262176 | tf_op jit(solution)/shard_map/ppermute | solution.py:171
  65.1 4.6 %collective-permute-done.12.refs_4_ = bf16[6,64,2048]{2,1,0:T(8,128)(2,1)} collective-permute-done((bf16[6,64,2048]{2,1,0:T(8,128)(2,1)}, bf16[6,64,2048]{2,1,0:T(8,128)(2,1)}, u32[]{:S(2)}, u32[]{:S(2)}) %collective-permute-start.12) | collective-permute-done | bytes 1572896 | tf_op jit(solution)/shard_map/ppermute | solution.py:171
  81.2 4.8 %shard_map.118 = (bf16[16,48,2048]{2,1,0:T(8,128)(2,1)}, bf16[16,48,2048]{2,1,0:T(8,128)(2,1)}, bf16[16,48,2048]{2,1,0:T(8,128)(2,1)}) custom-call(bf16[16,48,128]{2,1,0:T(8,128)(2,1)S(1)} %fusion.24.refs_0_.pick_ref, f32[16,48,1]{2,1,0:T(8,128)S(1)} %copy.26.refs_1_.prob_ref, f32[1,2048]{1,0:T(1,128)S(1)} %bitcast.129, bf16[4,64,2048]{2,1,0:T(8,128)(2,1)S(1)} %copy-done.5, ...), custom_call_target="tpu_custom_call" | custom-call | flops 201326592 | bytes 6553600 | tf_op jit(solution)/shard_map/pallas_call | solution.py:277
  86.0 6.5 %shard_map.119 = bf16[16,48,2048]{2,1,0:T(8,128)(2,1)} custom-call(bf16[16,48,128]{2,1,0:T(8,128)(2,1)S(1)} %fusion.24.refs_0_.pick_ref, f32[16,48,1]{2,1,0:T(8,128)S(1)} %copy.26.refs_1_.prob_ref, f32[1,2048]{1,0:T(1,128)S(1)} %bitcast.130, bf16[6,64,2048]{2,1,0:T(8,128)(2,1)} %constant_dynamic-update-slice_fusion.refs_3_, ...), custom_call_target="tpu_custom_call", output_to_operand_aliasing={{}: (7, {})} | custom-call | flops 301989888 | bytes 8650752 | tf_op jit(solution)/shard_map/pallas_call | solution.py:277
  92.5 8.1 %fusion.3 = f32[768,1536]{1,0:T(8,128)S(1)} fusion(bf16[768,2048]{1,0:T(8,128)(2,1)} %bitcast.141, bf16[1,2048,1536]{2,1,0:T(8,128)(2,1)} %param.12), kind=kOutput, calls=%fused_computation.5 | convolution fusion | flops 4831838208 | bytes 14155776 | tf_op jit(solution)/shard_map/dot_general | solution.py:22
  105.4 5.3 %shard_map.120 = (bf16[12,64,2048]{2,1,0:T(8,128)(2,1)S(1)}, bf16[12,64,2048]{2,1,0:T(8,128)(2,1)}) custom-call(bf16[16,48,128]{2,1,0:T(8,128)(2,1)S(1)} %fusion.24.refs_0_.pick_ref, f32[16,48,1]{2,1,0:T(8,128)S(1)} %copy.26.refs_1_.prob_ref, bf16[16,48,2048]{2,1,0:T(8,128)(2,1)} %bitcast.132), custom_call_target="tpu_custom_call" | custom-call | flops 301989888 | bytes 8650752 | tf_op jit(solution)/shard_map/pallas_call | solution.py:325
  116.2 18.0 %collective-permute-done.21.refs_4_ = bf16[6,64,2048]{2,1,0:T(8,128)(2,1)S(1)} collective-permute-done((bf16[6,64,2048]{2,1,0:T(8,128)(2,1)S(1)}, bf16[6,64,2048]{2,1,0:T(8,128)(2,1)S(1)}, u32[]{:S(2)}, u32[]{:S(2)}) %collective-permute-start.21) | collective-permute-done | bytes 1572896 | tf_op jit(solution)/shard_map/ppermute | solution.py:171
  138.9 5.4 %shard_map.121 = (bf16[16,48,2048]{2,1,0:T(8,128)(2,1)}, bf16[16,48,2048]{2,1,0:T(8,128)(2,1)}) custom-call(bf16[16,48,128]{2,1,0:T(8,128)(2,1)S(1)} %fusion.24.refs_0_.pick_ref, f32[16,48,1]{2,1,0:T(8,128)S(1)} %copy.26.refs_1_.prob_ref, f32[1,2048]{1,0:T(1,128)S(1)} %bitcast.131, ...), custom_call_target="tpu_custom_call", output_to_operand_aliasing={{0}: (7, {}), {1}: (8, {})} | custom-call | flops 301989888 | bytes 11010048 | tf_op jit(solution)/shard_map/pallas_call | solution.py:277
  144.3 5.3 %multiply_convert_fusion.1 = (bf16[768,768]{1,0:T(8,128)(2,1)S(1)}, bf16[768,768]{1,0:T(8,128)(2,1)S(1)}) fusion(f32[768,1536]{1,0:T(8,128)S(1)} %fusion.3, bf16[768,2048]{1,0:T(8,128)(2,1)} %bitcast.139, bf16[1,768,2048]{2,1,0:T(8,128)(2,1)S(1)} %copy-done), kind=kOutput, calls=%fused_computation.19 | convolution fusion | flops 2423586816 | bytes 13369344 | tf_op jit(solution)/shard_map/dot_general | solution.py:33
  149.7 10.7 %multiply_reduce_fusion = (f32[2048]{0:T(1024)}, bf16[768,2048]{1,0:T(8,128)(2,1)}) fusion(bf16[16,48,2048]{2,1,0:T(8,128)(2,1)S(1)} %copy-done.16, bf16[1,2048,1536]{2,1,0:T(8,128)(2,1)} %param.12, bf16[768,768]{1,0:T(8,128)(2,1)S(1)} %get-tuple-element.75, bf16[768,768]{1,0:T(8,128)(2,1)S(1)} %get-tuple-element.74), kind=kOutput, calls=%fused_computation.7 | convolution fusion | flops 4844419072 | bytes 14950400 | tf_op jit(solution)/shard_map/dot_general | solution.py:33
  160.4 5.2 %shard_map.122 = (bf16[12,64,2048]{2,1,0:T(8,128)(2,1)S(1)}, bf16[12,64,2048]{2,1,0:T(8,128)(2,1)}) custom-call(bf16[16,48,128]{2,1,0:T(8,128)(2,1)S(1)} %fusion.24.refs_0_.pick_ref, f32[16,48,1]{2,1,0:T(8,128)S(1)} %copy.26.refs_1_.prob_ref, bf16[16,48,2048]{2,1,0:T(8,128)(2,1)} %bitcast.135), custom_call_target="tpu_custom_call" | custom-call | flops 301989888 | bytes 8650752 | tf_op jit(solution)/shard_map/pallas_call | solution.py:325
  179.1 9.1 %collective-permute-done.25 = bf16[6,64,2048]{2,1,0:T(8,128)(2,1)} collective-permute-done((bf16[6,64,2048]{2,1,0:T(8,128)(2,1)}, bf16[6,64,2048]{2,1,0:T(8,128)(2,1)}, u32[]{:S(2)}, u32[]{:S(2)}) %collective-permute-start.25) | collective-permute-done | bytes 1572896 | tf_op jit(solution)/shard_map/ppermute | solution.py:171
  200.1 6.6 %convolution_convert_fusion.1 = bf16[768,2048]{1,0:T(8,128)(2,1)} fusion(bf16[768,768]{1,0:T(8,128)(2,1)} %copy-done.22, bf16[768,2048]{1,0:T(8,128)(2,1)} %bitcast.140), kind=kOutput, calls=%fused_computation.9 | convolution fusion | flops 2417491968 | bytes 7471104 | tf_op jit(solution)/shard_map/dot_general | solution.py:37
  206.6 8.9 %collective-permute-done.34 = bf16[3,64,2048]{2,1,0:T(8,128)(2,1)} collective-permute-done((bf16[3,64,2048]{2,1,0:T(8,128)(2,1)}, bf16[3,64,2048]{2,1,0:T(8,128)(2,1)}, u32[]{:S(2)}, u32[]{:S(2)}) %collective-permute-start.34) | collective-permute-done | bytes 786464 | tf_op jit(solution)/shard_map/ppermute | solution.py:171
  215.5 9.0 %collective-permute-done.29 = f32[48,128]{1,0:T(8,128)S(1)} collective-permute-done((f32[48,128]{1,0:T(8,128)S(1)}, f32[48,128]{1,0:T(8,128)S(1)}, u32[]{:S(2)}, u32[]{:S(2)}) %collective-permute-start.29) | collective-permute-done | bytes 24608 | tf_op jit(solution)/shard_map/ppermute | solution.py:171
  233.3 7.1 %collective-permute-start.36 = (bf16[64,2048]{1,0:T(8,128)(2,1)}, bf16[64,2048]{1,0:T(8,128)(2,1)}, u32[]{:S(2)}, u32[]{:S(2)}) collective-permute-start(bf16[64,2048]{1,0:T(8,128)(2,1)} %get-tuple-element.82), channel_id=1, source_target_pairs={{0,16},{1,17},{2,18},{3,19},{4,20},{5,21},{6,22},{7,23},{8,24},{9,... | collective-permute-start | bytes 786440 | tf_op jit(solution)/shard_map/ppermute | solution.py:171
  243.9 11.2 %collective-permute-done.32 = f32[20,128]{1,0:T(8,128)S(1)} collective-permute-done((f32[20,128]{1,0:T(8,128)S(1)}, f32[20,128]{1,0:T(8,128)S(1)}, u32[]{:S(2)}, u32[]{:S(2)}) %collective-permute-start.32) | collective-permute-done | bytes 10272 | tf_op jit(solution)/shard_map/ppermute | solution.py:171
  263.3 4.1 %collective-permute-start.38 = (bf16[64,2048]{1,0:T(8,128)(2,1)S(1)}, bf16[64,2048]{1,0:T(8,128)(2,1)S(1)}, u32[]{:S(2)}, u32[]{:S(2)}) collective-permute-start(bf16[64,2048]{1,0:T(8,128)(2,1)S(1)} %get-tuple-element.81), channel_id=1, source_target_pairs={{0,24},{1,25},{2,26},{3,27},{4,28},{5,29},{6,30},{7,31},{8,0},{9,1... | collective-permute-start | bytes 786440 | tf_op jit(solution)/shard_map/ppermute | solution.py:171
  280.5 4.1 %collective-permute-start.43 = (bf16[64,2048]{1,0:T(8,128)(2,1)S(1)}, bf16[64,2048]{1,0:T(8,128)(2,1)S(1)}, u32[]{:S(2)}, u32[]{:S(2)}) collective-permute-start(bf16[64,2048]{1,0:T(8,128)(2,1)S(1)} %get-tuple-element.79), channel_id=1, source_target_pairs={{0,24},{1,25},{2,26},{3,27},{4,28},{5,29},{6,30},{7,31},{8,0},{9,1... | collective-permute-start | bytes 786440 | tf_op jit(solution)/shard_map/ppermute | solution.py:171
  285.3 5.9 %collective-permute-done.41 = bf16[64,2048]{1,0:T(8,128)(2,1)S(1)} collective-permute-done((bf16[64,2048]{1,0:T(8,128)(2,1)S(1)}, bf16[64,2048]{1,0:T(8,128)(2,1)S(1)}, u32[]{:S(2)}, u32[]{:S(2)}) %collective-permute-start.41) | collective-permute-done | bytes 262176 | tf_op jit(solution)/shard_map/ppermute | solution.py:171
  295.6 7.2 %fusion = bf16[1,2048,1536]{2,1,0:T(8,128)(2,1)} fusion(bf16[768,2048]{1,0:T(8,128)(2,1)S(1)} %bitcast.142, bf16[768,768]{1,0:T(8,128)(2,1)S(1)} %copy-done.34, bf16[768,768]{1,0:T(8,128)(2,1)S(1)} %copy-done.32), kind=kOutput, calls=%fused_computation.2 | convolution fusion | flops 4839702528 | bytes 11796480 | tf_op jit(solution)/shard_map/dot_general | solution.py:37
  (235 shorter events, 134.4 us)
Async XLA Ops:
  1.9 14.5 %collective-permute-start.9 = (bf16[2,64,2048]{2,1,0:T(8,128)(2,1)S(1)}, bf16[2,64,2048]{2,1,0:T(8,128)(2,1)S(1)}, u32[]{:S(2)}, u32[]{:S(2)}) collective-permute-start(bf16[2,64,2048]{2,1,0:T(8,128)(2,1)S(1)} %pad_maximum_fusion.6), channel_id=1, source_target_pairs={{0,2},{1,5},{2,0},{3,7},{4,6},{5,1},{6,4},{7,3},{8,10},{9,13},{10,... | collective-permute-start | bytes 1572872 | tf_op jit(solution)/shard_map/ppermute | solution.py:171
  10.9 20.6 %collective-permute-start.6 = (bf16[64,2048]{1,0:T(8,128)(2,1)}, bf16[64,2048]{1,0:T(8,128)(2,1)S(1)}, u32[]{:S(2)}, u32[]{:S(2)}) collective-permute-start(bf16[64,2048]{1,0:T(8,128)(2,1)} %param.7), channel_id=1, source_target_pairs={{0,16},{1,17},{2,18},{3,19},{4,20},{5,21},{6,22},{7,23},{8,24},{9,... | collective-permute-start | bytes 786440 | tf_op jit(solution)/shard_map/ppermute | solution.py:171
  11.9 19.5 %collective-permute-start.5 = (bf16[64,2048]{1,0:T(8,128)(2,1)}, bf16[64,2048]{1,0:T(8,128)(2,1)S(1)}, u32[]{:S(2)}, u32[]{:S(2)}) collective-permute-start(bf16[64,2048]{1,0:T(8,128)(2,1)} %param.7), channel_id=1, source_target_pairs={{0,24},{1,25},{2,26},{3,27},{4,28},{5,29},{6,30},{7,31},{8,0},{9,1... | collective-permute-start | bytes 786440 | tf_op jit(solution)/shard_map/ppermute | solution.py:171
  14.8 16.6 %collective-permute-start.7 = (bf16[64,2048]{1,0:T(8,128)(2,1)}, bf16[64,2048]{1,0:T(8,128)(2,1)S(1)}, u32[]{:S(2)}, u32[]{:S(2)}) collective-permute-start(bf16[64,2048]{1,0:T(8,128)(2,1)} %param.7), channel_id=1, source_target_pairs={{0,8},{1,9},{2,10},{3,11},{4,12},{5,13},{6,14},{7,15},{8,16},{9,17... | collective-permute-start | bytes 786440 | tf_op jit(solution)/shard_map/ppermute | solution.py:171
  17.5 29.5 %collective-permute-start.10 = (bf16[4,64,2048]{2,1,0:T(8,128)(2,1)S(1)}, bf16[4,64,2048]{2,1,0:T(8,128)(2,1)S(1)}, u32[]{:S(2)}, u32[]{:S(2)}) collective-permute-start(bf16[4,64,2048]{2,1,0:T(8,128)(2,1)S(1)} %pad_maximum_fusion.3.refs_3_), channel_id=1, source_target_pairs={{0,4},{1,3},{2,6},{3,1},{4,0},{5,7},{6,2},{7,5},{8,12},{9,11},{10,... | collective-permute-start | bytes 3145736 | tf_op jit(solution)/shard_map/ppermute | solution.py:171
  20.2 13.9 %collective-permute-start.4 = (f32[2,4,16,128]{3,2,1,0:T(8,128)S(1)}, f32[2,4,16,128]{3,2,1,0:T(8,128)S(1)}, u32[]{:S(2)}, u32[]{:S(2)}) collective-permute-start(f32[2,4,16,128]{3,2,1,0:T(8,128)S(1)} %get-tuple-element.87), channel_id=1, source_target_pairs={{0,4},{1,3},{2,6},{3,1},{4,0},{5,7},{6,2},{7,5},{8,12},{9,11},{10,... | collective-permute-start | bytes 196616 | tf_op jit(solution)/shard_map/ppermute | solution.py:171
  48.1 21.7 %collective-permute-start.12 = (bf16[6,64,2048]{2,1,0:T(8,128)(2,1)}, bf16[6,64,2048]{2,1,0:T(8,128)(2,1)}, u32[]{:S(2)}, u32[]{:S(2)}) collective-permute-start(bf16[6,64,2048]{2,1,0:T(8,128)(2,1)} %constant_dynamic-update-slice_fusion.refs_3_), channel_id=1, source_target_pairs={{0,4},{1,3},{2,6},{3,1},{4,0},{5,7},{6,2},{7,5},{8,12},{9,11},{10,... | collective-permute-start | bytes 4718600 | tf_op jit(solution)/shard_map/ppermute | solution.py:171
  69.7 16.3 %collective-permute-start.16 = (bf16[6,64,2048]{2,1,0:T(8,128)(2,1)}, bf16[6,64,2048]{2,1,0:T(8,128)(2,1)}, u32[]{:S(2)}, u32[]{:S(2)}) collective-permute-start(bf16[6,64,2048]{2,1,0:T(8,128)(2,1)} %collective-permute-done.12.refs_4_), channel_id=1, source_target_pairs={{0,1},{1,0},{2,3},{3,2},{4,5},{5,4},{6,7},{7,6},{8,9},{9,8},{10,11... | collective-permute-start | bytes 4718600 | tf_op jit(solution)/shard_map/ppermute | solution.py:171
  69.7 16.3 %collective-permute-start.15 = (bf16[6,64,2048]{2,1,0:T(8,128)(2,1)}, bf16[6,64,2048]{2,1,0:T(8,128)(2,1)}, u32[]{:S(2)}, u32[]{:S(2)}) collective-permute-start(bf16[6,64,2048]{2,1,0:T(8,128)(2,1)} %constant_dynamic-update-slice_fusion.refs_3_), channel_id=1, source_target_pairs={{0,1},{1,0},{2,3},{3,2},{4,5},{5,4},{6,7},{7,6},{8,9},{9,8},{10,11... | collective-permute-start | bytes 4718600 | tf_op jit(solution)/shard_map/ppermute | solution.py:171
  110.6 23.7 %collective-permute-start.20 = (bf16[12,64,2048]{2,1,0:T(8,128)(2,1)}, bf16[12,64,2048]{2,1,0:T(8,128)(2,1)S(1)}, u32[]{:S(2)}, u32[]{:S(2)}) collective-permute-start(bf16[12,64,2048]{2,1,0:T(8,128)(2,1)} %get-tuple-element.47), channel_id=1, source_target_pairs={{0,1},{1,0},{2,3},{3,2},{4,5},{5,4},{6,7},{7,6},{8,9},{9,8},{10,11... | collective-permute-start | bytes 9437192 | tf_op jit(solution)/shard_map/ppermute | solution.py:171
  113.8 20.5 %collective-permute-start.21 = (bf16[6,64,2048]{2,1,0:T(8,128)(2,1)S(1)}, bf16[6,64,2048]{2,1,0:T(8,128)(2,1)S(1)}, u32[]{:S(2)}, u32[]{:S(2)}) collective-permute-start(bf16[6,64,2048]{2,1,0:T(8,128)(2,1)S(1)} %constant_dynamic-update-slice_fusion.2.refs_3_), channel_id=1, source_target_pairs={{0,4},{1,3},{2,6},{3,1},{4,0},{5,7},{6,2},{7,5},{8,12},{9,11},{10,... | collective-permute-start | bytes 4718600 | tf_op jit(solution)/shard_map/ppermute | solution.py:171
  115.8 20.7 %collective-permute-start.22 = (bf16[6,64,2048]{2,1,0:T(8,128)(2,1)S(1)}, bf16[6,64,2048]{2,1,0:T(8,128)(2,1)S(1)}, u32[]{:S(2)}, u32[]{:S(2)}) collective-permute-start(bf16[6,64,2048]{2,1,0:T(8,128)(2,1)S(1)} %constant_dynamic-update-slice_fusion.2.refs_3_), channel_id=1, source_target_pairs={{0,1},{1,0},{2,3},{3,2},{4,5},{5,4},{6,7},{7,6},{8,9},{9,8},{10,11... | collective-permute-start | bytes 4718600 | tf_op jit(solution)/shard_map/ppermute | solution.py:171
  167.4 23.8 %collective-permute-start.24 = (bf16[12,64,2048]{2,1,0:T(8,128)(2,1)}, bf16[12,64,2048]{2,1,0:T(8,128)(2,1)}, u32[]{:S(2)}, u32[]{:S(2)}) collective-permute-start(bf16[12,64,2048]{2,1,0:T(8,128)(2,1)} %get-tuple-element.52), channel_id=1, source_target_pairs={{0,1},{1,0},{2,3},{3,2},{4,5},{5,4},{6,7},{7,6},{8,9},{9,8},{10,11... | collective-permute-start | bytes 9437192 | tf_op jit(solution)/shard_map/ppermute | solution.py:171
  167.5 20.7 %collective-permute-start.25 = (bf16[6,64,2048]{2,1,0:T(8,128)(2,1)}, bf16[6,64,2048]{2,1,0:T(8,128)(2,1)}, u32[]{:S(2)}, u32[]{:S(2)}) collective-permute-start(bf16[6,64,2048]{2,1,0:T(8,128)(2,1)} %add_convert_fusion.1), channel_id=1, source_target_pairs={{0,4},{1,3},{2,6},{3,1},{4,0},{5,7},{6,2},{7,5},{8,12},{9,11},{10,... | collective-permute-start | bytes 4718600 | tf_op jit(solution)/shard_map/ppermute | solution.py:171
  195.0 66.4 %collective-permute-start.27 = (bf16[8,64,2048]{2,1,0:T(8,128)(2,1)}, bf16[8,64,2048]{2,1,0:T(8,128)(2,1)}, u32[]{:S(2)}, u32[]{:S(2)}) collective-permute-start(bf16[8,64,2048]{2,1,0:T(8,128)(2,1)} %copy-done.14), channel_id=1, source_target_pairs={{0,1},{1,0},{2,3},{3,2},{4,5},{5,4},{6,7},{7,6},{8,9},{9,8},{10,11... | collective-permute-start | bytes 6291464 | tf_op jit(solution)/shard_map/ppermute | solution.py:171
  195.5 20.0 %collective-permute-start.34 = (bf16[3,64,2048]{2,1,0:T(8,128)(2,1)}, bf16[3,64,2048]{2,1,0:T(8,128)(2,1)}, u32[]{:S(2)}, u32[]{:S(2)}) collective-permute-start(bf16[3,64,2048]{2,1,0:T(8,128)(2,1)} %add_convert_fusion.6), channel_id=1, source_target_pairs={{0,2},{1,5},{2,0},{3,7},{4,6},{5,1},{6,4},{7,3},{8,10},{9,13},{10,... | collective-permute-start | bytes 2359304 | tf_op jit(solution)/shard_map/ppermute | solution.py:171
  197.8 63.7 %collective-permute-start.26 = (bf16[6,64,2048]{2,1,0:T(8,128)(2,1)}, bf16[6,64,2048]{2,1,0:T(8,128)(2,1)}, u32[]{:S(2)}, u32[]{:S(2)}) collective-permute-start(bf16[6,64,2048]{2,1,0:T(8,128)(2,1)} %add_convert_fusion), channel_id=1, source_target_pairs={{0,4},{1,3},{2,6},{3,1},{4,0},{5,7},{6,2},{7,5},{8,12},{9,11},{10,... | collective-permute-start | bytes 4718600 | tf_op jit(solution)/shard_map/ppermute | solution.py:171
  200.0 24.4 %collective-permute-start.29 = (f32[48,128]{1,0:T(8,128)S(1)}, f32[48,128]{1,0:T(8,128)S(1)}, u32[]{:S(2)}, u32[]{:S(2)}) collective-permute-start(f32[48,128]{1,0:T(8,128)S(1)} %pad_maximum_fusion.14), channel_id=1, source_target_pairs={{0,4},{1,5},{2,6},{3,7},{4,0},{5,1},{6,2},{7,3},{8,12},{9,13},{10,... | collective-permute-start | bytes 73736 | tf_op jit(solution)/shard_map/ppermute | solution.py:171
  233.3 28.1 %collective-permute-start.36 = (bf16[64,2048]{1,0:T(8,128)(2,1)}, bf16[64,2048]{1,0:T(8,128)(2,1)}, u32[]{:S(2)}, u32[]{:S(2)}) collective-permute-start(bf16[64,2048]{1,0:T(8,128)(2,1)} %get-tuple-element.82), channel_id=1, source_target_pairs={{0,16},{1,17},{2,18},{3,19},{4,20},{5,21},{6,22},{7,23},{8,24},{9,... | collective-permute-start | bytes 786440 | tf_op jit(solution)/shard_map/ppermute | solution.py:171
  240.4 21.0 %collective-permute-start.35 = (bf16[64,2048]{1,0:T(8,128)(2,1)}, bf16[64,2048]{1,0:T(8,128)(2,1)}, u32[]{:S(2)}, u32[]{:S(2)}) collective-permute-start(bf16[64,2048]{1,0:T(8,128)(2,1)} %get-tuple-element.83), channel_id=1, source_target_pairs={{0,8},{1,9},{2,10},{3,11},{4,12},{5,13},{6,14},{7,15},{8,16},{9,17... | collective-permute-start | bytes 786440 | tf_op jit(solution)/shard_map/ppermute | solution.py:171
  241.0 14.1 %collective-permute-start.32 = (f32[20,128]{1,0:T(8,128)S(1)}, f32[20,128]{1,0:T(8,128)S(1)}, u32[]{:S(2)}, u32[]{:S(2)}) collective-permute-start(f32[20,128]{1,0:T(8,128)S(1)} %get-tuple-element.96), channel_id=1, source_target_pairs={{0,16},{1,17},{2,18},{3,19},{4,20},{5,21},{6,22},{7,23},{8,24},{9,... | collective-permute-start | bytes 30728 | tf_op jit(solution)/shard_map/ppermute | solution.py:171
  278.7 15.5 %collective-permute-start.39 = (bf16[4,64,2048]{2,1,0:T(8,128)(2,1)S(1)}, bf16[4,64,2048]{2,1,0:T(8,128)(2,1)S(1)}, u32[]{:S(2)}, u32[]{:S(2)}) collective-permute-start(bf16[4,64,2048]{2,1,0:T(8,128)(2,1)S(1)} %add_convert_fusion.2), channel_id=1, source_target_pairs={{0,4},{1,3},{2,6},{3,1},{4,0},{5,7},{6,2},{7,5},{8,12},{9,11},{10,... | collective-permute-start | bytes 3145736 | tf_op jit(solution)/shard_map/ppermute | solution.py:171
  280.5 25.7 %collective-permute-start.43 = (bf16[64,2048]{1,0:T(8,128)(2,1)S(1)}, bf16[64,2048]{1,0:T(8,128)(2,1)S(1)}, u32[]{:S(2)}, u32[]{:S(2)}) collective-permute-start(bf16[64,2048]{1,0:T(8,128)(2,1)S(1)} %get-tuple-element.79), channel_id=1, source_target_pairs={{0,24},{1,25},{2,26},{3,27},{4,28},{5,29},{6,30},{7,31},{8,0},{9,1... | collective-permute-start | bytes 786440 | tf_op jit(solution)/shard_map/ppermute | solution.py:171
  284.6 21.6 %collective-permute-start.42 = (bf16[64,2048]{1,0:T(8,128)(2,1)S(1)}, bf16[64,2048]{1,0:T(8,128)(2,1)S(1)}, u32[]{:S(2)}, u32[]{:S(2)}) collective-permute-start(bf16[64,2048]{1,0:T(8,128)(2,1)S(1)} %get-tuple-element.80), channel_id=1, source_target_pairs={{0,16},{1,17},{2,18},{3,19},{4,20},{5,21},{6,22},{7,23},{8,24},{9,... | collective-permute-start | bytes 786440 | tf_op jit(solution)/shard_map/ppermute | solution.py:171
  (55 other events, 689.5 us)

commit v4 on v3

--- a/solution.py
+++ b/solution.py
@@ -9,7 +9,9 @@
 
 TOP = 8
 EXP_DEV = 2
-VMEM_LIMIT = 48 * 1024 * 1024
+SMALL_VMEM = 24 * 1024 * 1024
+LARGE_VMEM = 48 * 1024 * 1024
+LITTLE = pl.CostEstimate(flops=1000000, bytes_accessed=100000, transcendentals=0)
 
 
 def normalize(rows):
@@ -212,8 +214,7 @@
     steps = lax.axis_size("expert") // 4
     planes = jnp.stack([table] + [send_along(table, -step) for step in range(1, steps)])
     pair = jnp.stack([planes, send_second(planes)])
-    last = send_first(pair)
-    return jnp.stack([pair, last]), last
+    return jnp.stack([pair, send_first(pair)])
 
 
 def far_first(array):
@@ -231,28 +232,34 @@
 
 
 def chosen_rows(pick, mine, other):
-    half = mine.shape[0]
-    rows = jnp.dot(pick[:, :half], mine, preferred_element_type=jnp.float32)
-    return rows + jnp.dot(pick[:, half:], other, preferred_element_type=jnp.float32)
-
-
-def select_kernel(kinds, count, *refs):
-    pick_ref, prob_ref, gain_ref, pieces = refs[0], refs[1], refs[2], refs[3:7]
-    outputs = refs[len(refs) - sum(1 if kind == "norm" else 2 for kind in kinds):]
+    return jnp.dot(pick, jnp.concatenate([mine, other]), preferred_element_type=jnp.float32)
+
+
+def norm_kernel(count, pick_ref, *refs):
+    pieces, gain_ref, normed_ref = refs[:4], refs[4], refs[-1]
 
     def work(mine_ref, other_ref):
         for group in range(count):
-            places = iter(outputs)
-            for number, kind in enumerate(kinds):
-                block = group * len(kinds) + number
-                rows = chosen_rows(pick_ref[group], mine_ref[block], other_ref[block])
-                if kind == "norm":
-                    inv_rms = lax.rsqrt(jnp.mean(rows * rows, axis=1, keepdims=True) + 1e-06)
-                    next(places)[group] = (rows * inv_rms * gain_ref[...]).astype(jnp.bfloat16)
-                else:
-                    next(places)[group] = rows.astype(jnp.bfloat16)
-                    next(places)[group] = (rows * prob_ref[group]).astype(jnp.bfloat16)
-
+            rows = chosen_rows(pick_ref[group], mine_ref[group], other_ref[group])
+            inv_rms = lax.rsqrt(jnp.mean(rows * rows, axis=1, keepdims=True) + 1e-06)
+            normed_ref[group] = (rows * inv_rms * gain_ref[...]).astype(jnp.bfloat16)
+
+    by_place(work, pieces)
+
+
+def grad_kernel(count, pick_ref, *refs):
+    pieces, prob_ref, out_ref, (grad_ref, value_ref) = refs[:4], refs[4], refs[5], refs[-2:]
+
+    def work(mine_ref, other_ref):
+        for group in range(count):
+            rows = chosen_rows(pick_ref[group], mine_ref[group], other_ref[group])
+            grad_ref[group] = (rows * prob_ref[group]).astype(jnp.bfloat16)
+            value_ref[group] = jnp.sum(rows * out_ref[group].astype(jnp.float32), axis=1, keepdims=True)
+
+    by_place(work, pieces)
+
+
+def by_place(work, pieces):
     for first in range(2):
         for second in range(2):
             pl.when(pl.program_id(0) == first * 2 + second)(
@@ -260,113 +267,162 @@
             )
 
 
-def select(kinds, pick, prob, gain, pieces, count, first_group, held):
-    groups, capacity, group_rows = pick.shape
-    blocks = count * len(kinds)
+def group_spec(count, first_group, *shape):
+    first_block = first_group // count
+    return pl.BlockSpec((count,) + shape, lambda i: (first_block + i, 0, 0))
+
+
+def select(kernel, pick, pieces, extras, extra_specs, out_shapes, count, arrays, which, first_group, held):
+    _, capacity, group_rows = pick.shape
     half, features = pieces[0].shape[1:]
-    outputs = sum(1 if kind == "norm" else 2 for kind in kinds)
-    out = jax.ShapeDtypeStruct((groups, capacity, features), jnp.bfloat16)
-    first_block = first_group // count
-
-    def group_spec(*shape):
-        return pl.BlockSpec((count,) + shape, lambda i: (first_block + i, 0, 0))
 
     def piece_spec(place):
-        return pl.BlockSpec((blocks, half, features), lambda i: (place(i), 0, 0))
+        return pl.BlockSpec((count, half, features), lambda i: (place(i) * arrays + which, 0, 0))
 
     return pl.pallas_call(
-        functools.partial(select_kernel, kinds, count),
+        functools.partial(kernel, count),
         grid=(4,),
         in_specs=[
-            group_spec(capacity, group_rows),
-            group_spec(capacity, 1),
-            pl.BlockSpec((1, features), lambda i: (0, 0)),
+            group_spec(count, first_group, capacity, group_rows),
             piece_spec(lambda i: jnp.minimum(i, 1)),
             piece_spec(lambda i: jnp.maximum(i - 2, 0)),
             piece_spec(lambda i: i // 2),
             piece_spec(lambda i: jnp.maximum(i - 2, 0)),
-        ] + [pl.BlockSpec(memory_space=pl.ANY)] * len(held),
-        out_specs=[group_spec(capacity, features)] * outputs,
-        out_shape=[out] * outputs,
-        input_output_aliases={7 + n: n for n in range(len(held))},
-        compiler_params=pltpu.CompilerParams(vmem_limit_bytes=VMEM_LIMIT),
-        cost_estimate=pl.CostEstimate(
-            flops=8 * blocks * capacity * group_rows * features,
-            bytes_accessed=16 * blocks * half * features + 8 * outputs * count * capacity * features,
-            transcendentals=0,
-        ),
-    )(pick, prob, gain, *pieces, *held)
-
-
-def expand_kernel(weighted, count, pick_ref, prob_ref, *refs):
+        ] + extra_specs + [pl.BlockSpec(memory_space=pl.ANY)] * len(held),
+        out_specs=[group_spec(count, first_group, *out.shape[1:]) for out in out_shapes],
+        out_shape=out_shapes,
+        input_output_aliases={5 + len(extras) + n: n for n in range(len(held))},
+        compiler_params=pltpu.CompilerParams(vmem_limit_bytes=SMALL_VMEM),
+        cost_estimate=LITTLE,
+    )(pick, *pieces, *extras, *held)
+
+
+def select_normed(pick, gain, pieces, count, arrays, first_group, held):
+    groups, capacity, _ = pick.shape
+    features = pieces[0].shape[2]
+    return select(
+        norm_kernel, pick, pieces, [gain], [pl.BlockSpec((1, features), lambda i: (0, 0))],
+        [jax.ShapeDtypeStruct((groups, capacity, features), jnp.bfloat16)],
+        count, arrays, 0, first_group, held,
+    )
+
+
+def select_grads(pick, prob, out_slots, pieces, count, arrays, which, first_group, held):
+    groups, capacity, _ = pick.shape
+    features = pieces[0].shape[2]
+    return select(
+        grad_kernel, pick, pieces, [prob, out_slots],
+        [group_spec(count, first_group, capacity, 1), group_spec(count, first_group, capacity, features)],
+        [
+            jax.ShapeDtypeStruct((groups, capacity, features), jnp.bfloat16),
+            jax.ShapeDtypeStruct((groups, capacity, 1), jnp.float32),
+        ],
+        count, arrays, which, first_group, held,
+    )
+
+
+def expand_kernel(weighted, count, back_ref, prob_ref, *refs):
     sources, (mine_ref, other_ref) = refs[:-2], refs[-2:]
     half = mine_ref.shape[1]
     for group in range(count):
-        pick = pick_ref[group]
         for number, (source_ref, by_prob) in enumerate(zip(sources, weighted)):
             rows = source_ref[group]
             if by_prob:
                 rows = (rows.astype(jnp.float32) * prob_ref[group]).astype(jnp.bfloat16)
-            for columns, out_ref in ((pick[:, :half], mine_ref), (pick[:, half:], other_ref)):
-                out_ref[group * len(sources) + number] = lax.dot_general(
-                    columns, rows, (((0,), (0,)), ((), ())), preferred_element_type=jnp.float32
-                ).astype(jnp.bfloat16)
-
-
-def expand(pick, prob, slots, weighted, count, first_group):
-    _, capacity, group_rows = pick.shape
+            spread = jnp.dot(back_ref[group], rows, preferred_element_type=jnp.float32)
+            place = group * len(sources) + number
+            mine_ref[place] = spread[:half].astype(jnp.bfloat16)
+            other_ref[place] = spread[half:].astype(jnp.bfloat16)
+
+
+def expand(back, prob, slots, weighted, count, first_group):
+    _, group_rows, capacity = back.shape
     half, features, arrays = group_rows // 2, slots[0].shape[2], len(slots)
     out = jax.ShapeDtypeStruct((4 * count * arrays, half, features), jnp.bfloat16)
-    first_block = first_group // count
-
-    def group_spec(*shape):
-        return pl.BlockSpec((count,) + shape, lambda i: (first_block + i, 0, 0))
-
     return pl.pallas_call(
         functools.partial(expand_kernel, weighted, count),
         grid=(4,),
-        in_specs=[group_spec(capacity, group_rows), group_spec(capacity, 1)]
-        + [group_spec(capacity, features)] * arrays,
+        in_specs=[
+            group_spec(count, first_group, group_rows, capacity),
+            group_spec(count, first_group, capacity, 1),
+        ] + [group_spec(count, first_group, capacity, features)] * arrays,
         out_specs=[
             pl.BlockSpec((count * arrays, half, features), lambda i: (i, 0, 0)),
             pl.BlockSpec((count * arrays, half, features), lambda i: (swapped(i), 0, 0)),
         ],
         out_shape=[out, out],
-        compiler_params=pltpu.CompilerParams(vmem_limit_bytes=VMEM_LIMIT),
-        cost_estimate=pl.CostEstimate(
-            flops=8 * arrays * count * capacity * group_rows * features,
-            bytes_accessed=8 * arrays * count * features * (group_rows + capacity),
-            transcendentals=0,
-        ),
-    )(pick, prob, *slots)
-
-
-def home_terms(columns, gain_term):
-    steps, top, rows = columns.shape[2:]
-    half = rows // 2
-    gain_rows = gain_term.reshape(-1, 128)
-    count = gain_rows.shape[0]
-
-    def exchange(part, gains, sender):
-        got = sender(jnp.concatenate([part.reshape(-1, 128), gains]))
-        return got[:-count].reshape(part.shape), got[-count:]
-
-    got, gains = exchange(columns[..., half:], gain_rows, send_core)
-    columns, gain_rows = columns[..., :half] + got, gain_rows + gains
-    for bit in (2, 1):
-        got, gains = exchange(columns[1], gain_rows, functools.partial(send_bit, bit=bit))
-        columns, gain_rows = columns[0] + got, gain_rows + gains
-    total, all_gains = columns[0], [gain_rows]
-    for step in range(1, steps):
-        got, gains = exchange(columns[step], gain_rows, functools.partial(send_along, step=step))
-        total = total + got
-        all_gains.append(gains)
+        compiler_params=pltpu.CompilerParams(vmem_limit_bytes=SMALL_VMEM),
+        cost_estimate=LITTLE,
+    )(back, prob, *slots)
+
+
+def forward_kernel(rows_ref, gate_up_ref, down_ref, projected_ref, hidden_ref, out_ref):
+    projected = jnp.dot(rows_ref[...], gate_up_ref[0], preferred_element_type=jnp.float32)
+    projected_ref[...] = projected
+    half_width = hidden_ref.shape[1]
+    gate_pre, up_pre = projected[:, :half_width], projected[:, half_width:]
+    hidden = (gate_pre * jax.nn.sigmoid(gate_pre) * up_pre).astype(jnp.bfloat16)
+    hidden_ref[...] = hidden
+    out_ref[...] = jnp.dot(hidden, down_ref[0], preferred_element_type=jnp.float32).astype(jnp.bfloat16)
+
+
+def backward_kernel(
+    grads_ref, projected_ref, rows_ref, gate_up_ref, down_ref, joined_ref, input_ref, gain_ref
+):
+    half_width = projected_ref.shape[1] // 2
+    hidden_grad = times_transposed(grads_ref[...], down_ref[0])
+    gate_pre, up_pre = projected_ref[:, :half_width], projected_ref[:, half_width:]
+    sigmoid_gate = jax.nn.sigmoid(gate_pre)
+    common = hidden_grad * sigmoid_gate
+    joined_ref[:, :half_width] = (
+        common * up_pre * (1.0 + gate_pre * (1.0 - sigmoid_gate))
+    ).astype(jnp.bfloat16)
+    joined_ref[:, half_width:] = (common * gate_pre).astype(jnp.bfloat16)
+    input_grad = times_transposed(joined_ref[...], gate_up_ref[0]).astype(jnp.bfloat16)
+    input_ref[...] = input_grad
+
+    @pl.when(pl.program_id(0) == 0)
+    def _():
+        gain_ref[...] = jnp.zeros_like(gain_ref)
+
+    terms = input_grad.astype(jnp.float32) * rows_ref[...].astype(jnp.float32)
+    gain_ref[...] += jnp.sum(terms, axis=0, keepdims=True)
+
+
+def by_rows(kernel, inputs, weights, outputs, sums):
+    block = inputs[0].shape[0] // 2
+
+    def row_spec(array):
+        return pl.BlockSpec((block,) + array.shape[1:], lambda i: (i, 0))
+
+    def whole_spec(array):
+        return pl.BlockSpec(array.shape, lambda i: (0,) * array.ndim)
+
+    return pl.pallas_call(
+        kernel,
+        grid=(2,),
+        in_specs=[row_spec(array) for array in inputs] + [whole_spec(array) for array in weights],
+        out_specs=[row_spec(array) for array in outputs] + [whole_spec(array) for array in sums],
+        out_shape=outputs + sums,
+        compiler_params=pltpu.CompilerParams(vmem_limit_bytes=LARGE_VMEM),
+        cost_estimate=LITTLE,
+    )(*inputs, *weights)
+
+
+def pack(columns, gains):
+    return jnp.concatenate([columns.reshape(-1, 128), gains])
+
+
+def unpack_add(columns, gains, got):
+    count = gains.shape[0]
+    return columns + got[:-count].reshape(columns.shape), gains + got[-count:]
+
+
+def planes_in_order(gains):
+    steps = len(gains)
     order = (lax.axis_index("expert") // 4 - jnp.arange(steps)) % steps
-    gains = jnp.take(jnp.stack(all_gains), order, axis=0)
-    gain_sum = gains[0]
-    for step in range(1, steps):
-        gain_sum = gain_sum + gains[step]
-    return total, gain_sum.reshape(-1)
+    ordered = jnp.take(jnp.stack(gains), order, axis=0)
+    return functools.reduce(jnp.add, [ordered[step] for step in range(steps)]).reshape(-1)
 
 
 def broadcast_shards(tokens, cotangent, gain, expert_ids, gate_probs, gate_up_weight, down_weight):
@@ -379,16 +435,13 @@
     half = group_rows // 2
     features = tokens.shape[1]
     capacity = 3 * group_rows * TOP // (2 * EXP_DEV * expert_size)
-    gate_up, down_proj = gate_up_weight[0], down_weight[0]
-
     near_own = jnp.stack([tokens, cotangent])
     near_pair = jnp.concatenate([near_own, send_second(near_own)])
     near_far_pair = send_first(near_pair)
-    tables, tables_last = gather_tables(
-        jnp.concatenate([expert_ids.T.astype(jnp.float32), gate_probs.T])
-    )
     token_far = jnp.stack([send_along(tokens, -step) for step in range(1, steps)])
-    token_far = after(token_far, tables_last)
+    tables = gather_tables(
+        after(jnp.concatenate([expert_ids.T.astype(jnp.float32), gate_probs.T]), token_far)
+    )
     late_cot = after(cotangent, token_far)
     cot_steps = [send_along(late_cot, -step) for step in range(1, steps)]
     token_second = after(send_second(token_far), near_far_pair, cot_steps[0])
@@ -402,7 +455,6 @@
     )
     cot_pair = jnp.concatenate([cot_far, cot_second])
     cot_far_pair = send_first(cot_pair)
-    cot_pieces = (cot_pair, cot_far_pair, send_core(cot_pair), send_core(cot_far_pair))
 
     tables = far_first(tables)
     tables = jnp.where(core == 0, tables, jnp.roll(tables, half, axis=2))
@@ -416,63 +468,90 @@
         rank_in.astype(jnp.int32)[:, None, :] == jnp.arange(capacity, dtype=jnp.int32)[None, :, None]
     )
     pick = placed.astype(jnp.bfloat16)
+    back = jnp.swapaxes(pick, 1, 2)
     slot_prob = jnp.sum(jnp.where(placed, weight_of[:, None, :], 0.0), axis=2, keepdims=True)
 
     gain_row = gain[None, :]
-    rows, cots, grads = select(("norm", "grad"), pick, slot_prob, gain_row, near_pieces, 1, far, ())
-    rows, = select(("norm",), pick, slot_prob, gain_row, token_pieces, steps - 1, 0, (rows,))
+    rows = select_normed(pick, gain_row, near_pieces, 1, 2, far, ())
+    rows, = select_normed(pick, gain_row, token_pieces, steps - 1, 1, 0, tuple(rows))
     rows = rows.reshape(-1, features)
-    gate_pre, up_pre, sigmoid_gate, hidden, block_out = expert_forward(rows, gate_up, down_proj)
+    slots, width = rows.shape[0], down_weight.shape[1]
+    projected, hidden, block_out = by_rows(
+        forward_kernel, [rows], [gate_up_weight, down_weight],
+        [
+            jax.ShapeDtypeStruct((slots, 2 * width), jnp.float32),
+            jax.ShapeDtypeStruct((slots, width), jnp.bfloat16),
+            jax.ShapeDtypeStruct((slots, features), jnp.bfloat16),
+        ], [],
+    )
+    block_out, cot_far_pair = together(block_out, cot_far_pair)
+    cot_pieces = (cot_pair, cot_far_pair, send_core(cot_pair), send_core(cot_far_pair))
     out_slots = block_out.reshape(expert_size, capacity, features)
-    out_mine, out_other = expand(pick, slot_prob, (out_slots,), (True,), steps - 1, 0)
+    out_mine, out_other = expand(back, slot_prob, (out_slots,), (True,), steps - 1, 0)
 
     half_far, one_far = 2 * (steps - 1), steps - 1
     out_core = send_core(out_other)
     out_upper = narrow(add_up(out_mine[half_far:], out_core[half_far:]))
     out_first = send_first(out_upper)
-    cots, grads = select(
-        ("grad",), after(pick, out_upper), slot_prob, gain_row, cot_pieces, steps - 1, 0, (cots, grads)
+    held = select_grads(
+        after(pick, out_other), slot_prob, out_slots, near_pieces, 1, 2, 1, far, ()
+    )
+    grads, prob_value = select_grads(
+        after(pick, out_upper), slot_prob, out_slots, cot_pieces, steps - 1, 1, 0, 0, tuple(held)
     )
     grads = grads.reshape(-1, features)
-    joined_grad = backward_inner(grads, down_proj, gate_pre, up_pre, sigmoid_gate)
-    input_grad = times_transposed(joined_grad, gate_up).astype(jnp.bfloat16)
+    joined_grad, input_grad, gain_term = by_rows(
+        backward_kernel, [grads, projected, rows], [gate_up_weight, down_weight],
+        [
+            jax.ShapeDtypeStruct((slots, 2 * width), jnp.bfloat16),
+            jax.ShapeDtypeStruct((slots, features), jnp.bfloat16),
+        ],
+        [jax.ShapeDtypeStruct((1, features), jnp.float32)],
+    )
+    input_grad, out_first = together(input_grad, out_first)
     input_slots = input_grad.reshape(expert_size, capacity, features)
-    in_mine, in_other = expand(pick, slot_prob, (input_slots,), (False,), steps - 1, 0)
+    in_mine, in_other = expand(back, slot_prob, (input_slots,), (False,), steps - 1, 0)
     in_core = send_core(in_other)
     out_middle = narrow(
         add_up(out_mine[one_far:half_far], out_core[one_far:half_far], after(out_first, in_other)[one_far:])
     )
     out_second = send_second(out_middle)
     near_mine, near_other = expand(
-        pick, slot_prob, (out_slots, after(input_slots, in_other)), (True, False), 1, far
+        back, after(slot_prob, in_other), (out_slots, input_slots), (True, False), 1, far
     )
     near_core = send_core(near_other)
     in_upper = narrow(add_up(in_mine[half_far:], after(in_core, out_middle, near_other)[half_far:]))
     in_first = send_first(in_upper)
-    down_part = outer_sum(after(hidden, in_upper), grads)
-    gain_term = jnp.sum(input_grad.astype(jnp.float32) * rows.astype(jnp.float32), axis=0) / gain
-    prob_value = jnp.sum(cots.astype(jnp.float32) * out_slots.astype(jnp.float32), axis=2)
-    prob_rows = jnp.sum(jnp.where(placed, prob_value[:, :, None], 0.0), axis=1)
+    gains = (gain_term[0] / gain).reshape(-1, 128)
+    prob_rows = jnp.sum(jnp.where(placed, prob_value, 0.0), axis=1)
     columns = from_far_first(jnp.where(matches, prob_rows[:, None, :], 0.0), steps)
     columns = jnp.where(core == 0, columns, jnp.swapaxes(columns, 0, 1))
-    prob_sum, gain_grad = home_terms(after(columns, in_upper), after(gain_term, in_upper))
+    got = send_core(after(pack(columns[..., half:], gains), in_upper))
+    down_part = outer_sum(after(hidden, in_upper), grads)
 
     def own_plane(mine, core_part, first_part, second_part, count):
         return add_up(mine[:count], core_part[:count], first_part[:count], second_part[:count])
 
-    out_second, down_part = together(out_second, down_part)
+    out_second, down_part, got = together(out_second, down_part, got)
+    columns, gains = unpack_add(columns[..., :half], gains, got)
+    got = send_bit(pack(columns[1], gains), 2)
     out_planes = narrow(own_plane(out_mine, out_core, out_first, out_second, one_far))
     out_far = [send_along(out_planes[step - 1], step) for step in range(1, steps)]
-    in_first, near_core, prob_sum, gain_grad = together(
-        in_first, near_core, prob_sum, gain_grad, *out_far[:2]
+    gate_up_part = outer_sum(after(rows, out_planes), joined_grad)
+    in_first, near_core, gate_up_part, got = together(
+        in_first, near_core, gate_up_part, got, *out_far[:2]
     )[:4]
+    columns, gains = unpack_add(columns[0], gains, got)
     in_middle = narrow(
         add_up(in_mine[one_far:half_far], in_core[one_far:half_far], in_first[one_far:])
     )
     in_second = send_second(in_middle)
-    in_planes = narrow(own_plane(in_mine, in_core, in_first, after(in_second, *out_far), one_far))
+    got = send_bit(pack(columns[1], gains), 1)
+    in_second, got = together(in_second, got, *out_far)[:2]
+    columns, gains = unpack_add(columns[0], gains, got)
+    in_planes = narrow(own_plane(in_mine, in_core, in_first, in_second, one_far))
+    messages = [send_along(pack(columns[step], gains), step) for step in range(1, steps)]
     in_far = [send_along(in_planes[step - 1], step) for step in range(1, steps)]
-    gate_up_part = outer_sum(after(rows, in_far[0]), joined_grad)
     near_upper = narrow(add_up(near_mine[4:], after(near_core, in_planes)[4:]))
     near_first = send_first(near_upper)
     near_middle = narrow(add_up(near_mine[2:4], near_core[2:4], near_first[2:]))
@@ -480,6 +559,12 @@
     near_sum = own_plane(near_mine, near_core, near_first, near_second, 2)
     out_sum = near_sum[0] + add_up(*out_far)
     normed_grad = near_sum[1] + add_up(*in_far)
+
+    prob_sum, all_gains = columns[0], [gains]
+    for message in messages:
+        prob_sum = prob_sum + message[:-gains.shape[0]].reshape(prob_sum.shape)
+        all_gains.append(message[-gains.shape[0]:])
+    gain_grad = planes_in_order(all_gains)
 
     scaled_own, inv_own = normalize(tokens)
     mixed = (tokens.astype(jnp.float32) + out_sum).astype(jnp.bfloat16)

time: 311 us -> 290 us (0.932)
  matrix products: 42.1 us -> 11.2 us
  Pallas kernels: 30.8 us -> 54.4 us
  starting transfers between devices: 73.8 us -> 53.3 us
  local copies, waits for them, and re-layouts: 16.5 us -> 22.9 us
    dot_general x4 -> x0, matrix products: 28.2 us -> none  [the longest x2 16.1 us: times_transposed(): lax.dot_general(left, right, (((1,), (1,)), ((), ())), preferred_element_...]
    pallas_call x3 -> x6, Pallas kernels: 16.6 us -> 44.8 us  [the longest x2 29.4 us: by_rows(): pl.pallas_call(kernel, grid=(2,), in_specs=[row_spec(array) for array in...]
    ppermute x44, starting transfers between devices: 73.8 us -> 53.3 us  [send(): return lax.ppermute(array, BOTH, pairs)]
    unnamed x72 -> x101, local copies, waits for them, and re-layouts: 9.62 us -> 17.5 us
    pallas_call x3, Pallas kernels: 14.1 us -> 9.59 us  [expand(): pl.pallas_call(functools.partial(expand_kernel, weighted, count), grid=(4...]
  transfers between devices with their start and end apart: 44 -> 44, of which waited for: 21 -> 16; matrix products, arithmetic and copies ran while one was open for 15% -> 16% of each run, Pallas kernels for 3% -> 17%
where the time goes in v4:
time: 290 us; the launch traced here: 289 us
  waiting for transfers between devices  107 us (37%)
  Pallas kernels  54.4 us (19%)
  starting transfers between devices  53.3 us (18%)
  other arithmetic  39 us (13%)
  local copies, waits for them, and re-layouts  22.9 us (8%)
  matrix products  11.2 us (4%)
    ppermute x44, waiting for transfers between devices, send(): return lax.ppermute(array, BOTH, pairs)  107 us
    ppermute x44, starting transfers between devices, send(): return lax.ppermute(array, BOTH, pairs)  53.3 us
    pallas_call x2, Pallas kernels, by_rows(): pl.pallas_call(kernel, grid=(2,), in_specs=[row_spec(array) for array in...  29.4 us
    convert_element_type x8, other arithmetic, narrow(): return value.astype(jnp.bfloat16)  18.1 us
    unnamed x101, local copies, waits for them, and re-layouts  17.5 us
    pallas_call x4, Pallas kernels, select(): pl.pallas_call(functools.partial(kernel, count), grid=(4,), in_specs=[gro...  15.4 us
    dot_general x2, matrix products, outer_sum(): lax.dot_general(left, right, (((0,), (0,)), ((), ())), preferred_element_...  11.1 us
    pallas_call x3, Pallas kernels, expand(): pl.pallas_call(functools.partial(expand_kernel, weighted, count), grid=(4...  9.59 us
  transfers between devices with their start and end apart: 44, of which 16 were waited for; matrix products, arithmetic and copies ran while one was open for 16% of the time, Pallas kernels for 17%

profile of v4, /device:TPU:0, one launch (start us, length us, event | category | flops | bytes accessed | tf_op | source)
XLA Modules:
  0.0 288.8 jit_solution(17099265358083038322)
XLA Ops:
  4.7 3.6 %collective-permute-start = (bf16[64,2048]{1,0:T(8,128)(2,1)}, bf16[64,2048]{1,0:T(8,128)(2,1)S(1)}, u32[]{:S(2)}, u32[]{:S(2)}) collective-permute-start(bf16[64,2048]{1,0:T(8,128)(2,1)} %param.7), channel_id=1, source_target_pairs={{0,24},{1,25},{2,26},{3,27},{4,28},{5,29},{6,30},{7,31},{8,0},{9,1... | collective-permute-start | bytes 786440 | tf_op jit(solution)/shard_map/ppermute | solution.py:173
  15.4 15.2 %collective-permute-done.1 = bf16[64,2048]{1,0:T(8,128)(2,1)S(1)} collective-permute-done((bf16[64,2048]{1,0:T(8,128)(2,1)}, bf16[64,2048]{1,0:T(8,128)(2,1)S(1)}, u32[]{:S(2)}, u32[]{:S(2)}) %collective-permute-start.1) | collective-permute-done | bytes 262176 | tf_op jit(solution)/shard_map/ppermute | solution.py:173
  32.3 6.4 %collective-permute-done.11 = bf16[64,2048]{1,0:T(8,128)(2,1)S(1)} collective-permute-done((bf16[64,2048]{1,0:T(8,128)(2,1)S(1)}, bf16[64,2048]{1,0:T(8,128)(2,1)S(1)}, u32[]{:S(2)}, u32[]{:S(2)}) %collective-permute-start.11) | collective-permute-done | bytes 262176 | tf_op jit(solution)/shard_map/ppermute | solution.py:173
  38.6 4.1 %collective-permute-done.8 = bf16[3,64,2048]{2,1,0:T(8,128)(2,1)S(1)} collective-permute-done((bf16[3,64,2048]{2,1,0:T(8,128)(2,1)S(1)}, bf16[3,64,2048]{2,1,0:T(8,128)(2,1)S(1)}, u32[]{:S(2)}, u32[]{:S(2)}) %collective-permute-start.8) | collective-permute-done | bytes 786464 | tf_op jit(solution)/shard_map/ppermute | solution.py:173
  44.7 5.2 %collective-permute-start.13 = (bf16[64,2048]{1,0:T(8,128)(2,1)S(1)}, bf16[64,2048]{1,0:T(8,128)(2,1)S(1)}, u32[]{:S(2)}, u32[]{:S(2)}) collective-permute-start(bf16[64,2048]{1,0:T(8,128)(2,1)S(1)} %copy-done.32), channel_id=1, source_target_pairs={{0,16},{1,17},{2,18},{3,19},{4,20},{5,21},{6,22},{7,23},{8,24},{9,... | collective-permute-start | bytes 786440 | tf_op jit(solution)/shard_map/ppermute | solution.py:173
  49.9 14.8 %collective-permute-done.13 = bf16[64,2048]{1,0:T(8,128)(2,1)S(1)} collective-permute-done((bf16[64,2048]{1,0:T(8,128)(2,1)S(1)}, bf16[64,2048]{1,0:T(8,128)(2,1)S(1)}, u32[]{:S(2)}, u32[]{:S(2)}) %collective-permute-start.13) | collective-permute-done | bytes 262176 | tf_op jit(solution)/shard_map/ppermute | solution.py:173
  66.5 6.7 %collective-permute-start.4 = (f32[16,128]{1,0:T(8,128)S(1)}, f32[16,128]{1,0:T(8,128)S(1)}, u32[]{:S(2)}, u32[]{:S(2)}) collective-permute-start(f32[16,128]{1,0:T(8,128)S(1)} %pad_maximum_fusion.17), channel_id=1, source_target_pairs={{0,16},{1,17},{2,18},{3,19},{4,20},{5,21},{6,22},{7,23},{8,24},{9,... | collective-permute-start | bytes 24584 | tf_op jit(solution)/shard_map/ppermute | solution.py:173
  75.2 3.5 %collective-permute-done.5 = f32[16,128]{1,0:T(8,128)S(1)} collective-permute-done((f32[16,128]{1,0:T(8,128)S(1)}, f32[16,128]{1,0:T(8,128)S(1)}, u32[]{:S(2)}, u32[]{:S(2)}) %collective-permute-start.5) | collective-permute-done | bytes 8224 | tf_op jit(solution)/shard_map/ppermute | solution.py:173
  85.3 19.2 %collective-permute-done.7 = f32[2,4,16,128]{3,2,1,0:T(8,128)S(1)} collective-permute-done((f32[2,4,16,128]{3,2,1,0:T(8,128)S(1)}, f32[2,4,16,128]{3,2,1,0:T(8,128)S(1)}, u32[]{:S(2)}, u32[]{:S(2)}) %collective-permute-start.7) | collective-permute-done | bytes 65568 | tf_op jit(solution)/shard_map/ppermute | solution.py:173
  117.2 5.1 %shard_map.119 = bf16[16,48,2048]{2,1,0:T(8,128)(2,1)S(1)} custom-call(bf16[16,48,128]{2,1,0:T(8,128)(2,1)S(1)} %fusion.15.pick_ref, bf16[6,64,2048]{2,1,0:T(8,128)(2,1)} %pad_maximum_fusion.refs_0_, bf16[6,64,2048]{2,1,0:T(8,128)(2,1)} %collective-permute-done.12.refs_1_, ...), custom_call_target="tpu_custom_call", output_to_operand_aliasing={{}: (6, {})} | custom-call | flops 1000000 | bytes 100000 | tf_op jit(solution)/shard_map/pallas_call | solution.py:282
  123.9 12.0 %shard_map.120 = (f32[768,1536]{1,0:T(8,128)}, bf16[768,768]{1,0:T(8,128)(2,1)S(1)}, bf16[768,2048]{1,0:T(8,128)(2,1)S(1)}) custom-call(bf16[768,2048]{1,0:T(8,128)(2,1)} %bitcast.112, bf16[1,2048,1536]{2,1,0:T(8,128)(2,1)} %gate_up_ref.3, bf16[1,768,2048]{2,1,0:T(8,128)(2,1)} %down_ref.3), custom_call_target="tpu_custom_call" | custom-call | flops 1000000 | bytes 100000 | tf_op jit(solution)/shard_map/pallas_call | solution.py:401
  140.2 8.7 %collective-permute-done.21 = bf16[12,64,2048]{2,1,0:T(8,128)(2,1)S(1)} collective-permute-done((bf16[12,64,2048]{2,1,0:T(8,128)(2,1)S(1)}, bf16[12,64,2048]{2,1,0:T(8,128)(2,1)S(1)}, u32[]{:S(2)}, u32[]{:S(2)}) %collective-permute-start.21) | collective-permute-done | bytes 3145760 | tf_op jit(solution)/shard_map/ppermute | solution.py:173
  155.5 4.4 %shard_map.123 = (bf16[16,48,2048]{2,1,0:T(8,128)(2,1)S(1)}, f32[16,48,1]{2,1,0:T(8,128)S(1)}) custom-call(bf16[16,48,128]{2,1,0:T(8,128)(2,1)S(1)} %fusion.15.pick_ref, bf16[6,64,2048]{2,1,0:T(8,128)(2,1)} %constant_dynamic-update-slice_fusion.refs_0_, ...), custom_call_target="tpu_custom_call", output_to_operand_aliasing={{0}: (7, {}), {1}: (8, {})} | custom-call | flops 1000000 | bytes 100000 | tf_op jit(solution)/shard_map/pallas_call | solution.py:282
  161.5 17.4 %shard_map.124 = (bf16[768,1536]{1,0:T(8,128)(2,1)S(1)}, bf16[768,2048]{1,0:T(8,128)(2,1)S(1)}, f32[1,2048]{1,0:T(1,128)S(1)}) custom-call(bf16[768,2048]{1,0:T(8,128)(2,1)} %bitcast.121, f32[768,1536]{1,0:T(8,128)} %get-tuple-element.66.projected_ref, bf16[768,2048]{1,0:T(8,128)(2,1)} %bitcast.113, bf16[1,2048,1536]{2,1,0:T(8,128)(2,1)} %gate_up_ref.3, ...), custom_call_target="tpu_custom_call" | custom-call | flops 1000000 | bytes 100000 | tf_op jit(solution)/shard_map/pallas_call | solution.py:401
  180.4 3.9 %shard_map.125 = (bf16[12,64,2048]{2,1,0:T(8,128)(2,1)S(1)}, bf16[12,64,2048]{2,1,0:T(8,128)(2,1)}) custom-call(bf16[16,128,48]{2,1,0:T(8,128)(2,1)S(1)} %fusion.1.back_ref, f32[16,48,1]{2,1,0:T(8,128)S(1)} %copy.20.prob_ref.refs_4_, bf16[16,48,2048]{2,1,0:T(8,128)(2,1)S(1)} %bitcast.119), custom_call_target="tpu_custom_call" | custom-call | flops 1000000 | bytes 100000 | tf_op jit(solution)/shard_map/pallas_call | solution.py:342
  197.5 3.1 %shard_map.126 = (bf16[8,64,2048]{2,1,0:T(8,128)(2,1)S(1)}, bf16[8,64,2048]{2,1,0:T(8,128)(2,1)}) custom-call(bf16[16,128,48]{2,1,0:T(8,128)(2,1)S(1)} %copy-done.10, f32[16,48,1]{2,1,0:T(8,128)S(1)} %copy.21.prob_ref, bf16[16,48,2048]{2,1,0:T(8,128)(2,1)S(1)} %bitcast.118, bf16[16,48,2048]{2,1,0:T(8,128)(2,1)S(1)} %bitcast.120), custom_call_target="tpu_custom_call" | custom-call | flops 1000000 | bytes 100000 | tf_op jit(solution)/shard_map/pallas_call | solution.py:342
  201.0 3.6 %add_convert_fusion = bf16[6,64,2048]{2,1,0:T(8,128)(2,1)} fusion(bf16[12,64,2048]{2,1,0:T(8,128)(2,1)} %collective-permute-done.25, bf16[12,64,2048]{2,1,0:T(8,128)(2,1)S(1)} %copy-done.18), kind=kLoop, calls=%fused_computation.3 | loop fusion | flops 3145728 | bytes 4718592 | tf_op jit(solution)/shard_map/convert_element_type | solution.py:210
  205.7 4.0 %convolution_convert_fusion.1 = bf16[768,2048]{1,0:T(8,128)(2,1)} fusion(bf16[768,768]{1,0:T(8,128)(2,1)S(1)} %copy-done.29, bf16[768,2048]{1,0:T(8,128)(2,1)S(1)} %bitcast.122), kind=kOutput, calls=%fused_computation.2 | convolution fusion | flops 2417491968 | bytes 7471104 | tf_op jit(solution)/shard_map/dot_general | solution.py:39
  217.5 7.1 %convolution_convert_fusion = bf16[2048,1536]{1,0:T(8,128)(2,1)} fusion(bf16[768,2048]{1,0:T(8,128)(2,1)S(1)} %bitcast.114, bf16[768,1536]{1,0:T(8,128)(2,1)S(1)} %copy-done.27), kind=kOutput, calls=%fused_computation.1 | convolution fusion | flops 4834983936 | bytes 11796480 | tf_op jit(solution)/shard_map/dot_general | solution.py:39
  225.8 9.6 %collective-permute-done.32 = bf16[64,2048]{1,0:T(8,128)(2,1)S(1)} collective-permute-done((bf16[64,2048]{1,0:T(8,128)(2,1)S(1)}, bf16[64,2048]{1,0:T(8,128)(2,1)S(1)}, u32[]{:S(2)}, u32[]{:S(2)}) %collective-permute-start.32) | collective-permute-done | bytes 262176 | tf_op jit(solution)/shard_map/ppermute | solution.py:173
  244.3 3.0 %collective-permute-done.35 = bf16[64,2048]{1,0:T(8,128)(2,1)} collective-permute-done((bf16[64,2048]{1,0:T(8,128)(2,1)S(1)}, bf16[64,2048]{1,0:T(8,128)(2,1)}, u32[]{:S(2)}, u32[]{:S(2)}) %collective-permute-start.35) | collective-permute-done | bytes 262176 | tf_op jit(solution)/shard_map/ppermute | solution.py:173
  247.3 3.4 %collective-permute-done.34 = f32[32,128]{1,0:T(8,128)S(1)} collective-permute-done((f32[32,128]{1,0:T(8,128)S(1)}, f32[32,128]{1,0:T(8,128)S(1)}, u32[]{:S(2)}, u32[]{:S(2)}) %collective-permute-start.34) | collective-permute-done | bytes 16416 | tf_op jit(solution)/shard_map/ppermute | solution.py:173
  263.8 8.1 %collective-permute-done.42 = f32[20,128]{1,0:T(8,128)S(1)} collective-permute-done((f32[20,128]{1,0:T(8,128)S(1)}, f32[20,128]{1,0:T(8,128)S(1)}, u32[]{:S(2)}, u32[]{:S(2)}) %collective-permute-start.42) | collective-permute-done | bytes 10272 | tf_op jit(solution)/shard_map/ppermute | solution.py:173
  277.0 6.4 %collective-permute-done.37 = bf16[2,64,2048]{2,1,0:T(8,128)(2,1)S(1)} collective-permute-done((bf16[2,64,2048]{2,1,0:T(8,128)(2,1)S(1)}, bf16[2,64,2048]{2,1,0:T(8,128)(2,1)S(1)}, u32[]{:S(2)}, u32[]{:S(2)}) %collective-permute-start.37) | collective-permute-done | bytes 524320 | tf_op jit(solution)/shard_map/ppermute | solution.py:173
  (264 shorter events, 108.9 us)
Async XLA Ops:
  8.3 22.3 %collective-permute-start.1 = (bf16[64,2048]{1,0:T(8,128)(2,1)}, bf16[64,2048]{1,0:T(8,128)(2,1)S(1)}, u32[]{:S(2)}, u32[]{:S(2)}) collective-permute-start(bf16[64,2048]{1,0:T(8,128)(2,1)} %param.7), channel_id=1, source_target_pairs={{0,16},{1,17},{2,18},{3,19},{4,20},{5,21},{6,22},{7,23},{8,24},{9,... | collective-permute-start | bytes 786440 | tf_op jit(solution)/shard_map/ppermute | solution.py:173
  8.3 22.3 %collective-permute-start.2 = (bf16[64,2048]{1,0:T(8,128)(2,1)}, bf16[64,2048]{1,0:T(8,128)(2,1)S(1)}, u32[]{:S(2)}, u32[]{:S(2)}) collective-permute-start(bf16[64,2048]{1,0:T(8,128)(2,1)} %param.7), channel_id=1, source_target_pairs={{0,8},{1,9},{2,10},{3,11},{4,12},{5,13},{6,14},{7,15},{8,16},{9,17... | collective-permute-start | bytes 786440 | tf_op jit(solution)/shard_map/ppermute | solution.py:173
  13.0 29.7 %collective-permute-start.10 = (bf16[4,64,2048]{2,1,0:T(8,128)(2,1)S(1)}, bf16[4,64,2048]{2,1,0:T(8,128)(2,1)S(1)}, u32[]{:S(2)}, u32[]{:S(2)}) collective-permute-start(bf16[4,64,2048]{2,1,0:T(8,128)(2,1)S(1)} %pad_maximum_fusion.1.refs_0_), channel_id=1, source_target_pairs={{0,4},{1,3},{2,6},{3,1},{4,0},{5,7},{6,2},{7,5},{8,12},{9,11},{10,... | collective-permute-start | bytes 3145736 | tf_op jit(solution)/shard_map/ppermute | solution.py:173
  44.2 20.7 %collective-permute-start.12 = (bf16[6,64,2048]{2,1,0:T(8,128)(2,1)}, bf16[6,64,2048]{2,1,0:T(8,128)(2,1)}, u32[]{:S(2)}, u32[]{:S(2)}) collective-permute-start(bf16[6,64,2048]{2,1,0:T(8,128)(2,1)} %pad_maximum_fusion.refs_0_), channel_id=1, source_target_pairs={{0,4},{1,3},{2,6},{3,1},{4,0},{5,7},{6,2},{7,5},{8,12},{9,11},{10,... | collective-permute-start | bytes 4718600 | tf_op jit(solution)/shard_map/ppermute | solution.py:173
  44.7 20.0 %collective-permute-start.13 = (bf16[64,2048]{1,0:T(8,128)(2,1)S(1)}, bf16[64,2048]{1,0:T(8,128)(2,1)S(1)}, u32[]{:S(2)}, u32[]{:S(2)}) collective-permute-start(bf16[64,2048]{1,0:T(8,128)(2,1)S(1)} %copy-done.32), channel_id=1, source_target_pairs={{0,16},{1,17},{2,18},{3,19},{4,20},{5,21},{6,22},{7,23},{8,24},{9,... | collective-permute-start | bytes 786440 | tf_op jit(solution)/shard_map/ppermute | solution.py:173
  49.9 14.8 %collective-permute-start.14 = (bf16[64,2048]{1,0:T(8,128)(2,1)S(1)}, bf16[64,2048]{1,0:T(8,128)(2,1)S(1)}, u32[]{:S(2)}, u32[]{:S(2)}) collective-permute-start(bf16[64,2048]{1,0:T(8,128)(2,1)S(1)} %copy-done.32), channel_id=1, source_target_pairs={{0,8},{1,9},{2,10},{3,11},{4,12},{5,13},{6,14},{7,15},{8,16},{9,17... | collective-permute-start | bytes 786440 | tf_op jit(solution)/shard_map/ppermute | solution.py:173
  65.0 17.3 %collective-permute-start.17 = (bf16[3,64,2048]{2,1,0:T(8,128)(2,1)S(1)}, bf16[3,64,2048]{2,1,0:T(8,128)(2,1)S(1)}, u32[]{:S(2)}, u32[]{:S(2)}) collective-permute-start(bf16[3,64,2048]{2,1,0:T(8,128)(2,1)S(1)} %pad_maximum_fusion.3), channel_id=1, source_target_pairs={{0,2},{1,5},{2,0},{3,7},{4,6},{5,1},{6,4},{7,3},{8,10},{9,13},{10,... | collective-permute-start | bytes 2359304 | tf_op jit(solution)/shard_map/ppermute | solution.py:173
  80.7 36.5 %collective-permute-start.15 = (bf16[6,64,2048]{2,1,0:T(8,128)(2,1)}, bf16[6,64,2048]{2,1,0:T(8,128)(2,1)}, u32[]{:S(2)}, u32[]{:S(2)}) collective-permute-start(bf16[6,64,2048]{2,1,0:T(8,128)(2,1)} %pad_maximum_fusion.refs_0_), channel_id=1, source_target_pairs={{0,1},{1,0},{2,3},{3,2},{4,5},{5,4},{6,7},{7,6},{8,9},{9,8},{10,11... | collective-permute-start | bytes 4718600 | tf_op jit(solution)/shard_map/ppermute | solution.py:173
  80.7 36.5 %collective-permute-start.16 = (bf16[6,64,2048]{2,1,0:T(8,128)(2,1)}, bf16[6,64,2048]{2,1,0:T(8,128)(2,1)}, u32[]{:S(2)}, u32[]{:S(2)}) collective-permute-start(bf16[6,64,2048]{2,1,0:T(8,128)(2,1)} %collective-permute-done.12.refs_1_), channel_id=1, source_target_pairs={{0,1},{1,0},{2,3},{3,2},{4,5},{5,4},{6,7},{7,6},{8,9},{9,8},{10,11... | collective-permute-start | bytes 4718600 | tf_op jit(solution)/shard_map/ppermute | solution.py:173
  83.2 53.8 %collective-permute-start.20 = (bf16[6,64,2048]{2,1,0:T(8,128)(2,1)}, bf16[6,64,2048]{2,1,0:T(8,128)(2,1)}, u32[]{:S(2)}, u32[]{:S(2)}) collective-permute-start(bf16[6,64,2048]{2,1,0:T(8,128)(2,1)} %constant_dynamic-update-slice_fusion.refs_0_), channel_id=1, source_target_pairs={{0,4},{1,3},{2,6},{3,1},{4,0},{5,7},{6,2},{7,5},{8,12},{9,11},{10,... | collective-permute-start | bytes 4718600 | tf_op jit(solution)/shard_map/ppermute | solution.py:173
  83.2 21.3 %collective-permute-start.7 = (f32[2,4,16,128]{3,2,1,0:T(8,128)S(1)}, f32[2,4,16,128]{3,2,1,0:T(8,128)S(1)}, u32[]{:S(2)}, u32[]{:S(2)}) collective-permute-start(f32[2,4,16,128]{3,2,1,0:T(8,128)S(1)} %get-tuple-element.107), channel_id=1, source_target_pairs={{0,4},{1,3},{2,6},{3,1},{4,0},{5,7},{6,2},{7,5},{8,12},{9,11},{10,... | collective-permute-start | bytes 196616 | tf_op jit(solution)/shard_map/ppermute | solution.py:173
  139.7 15.7 %collective-permute-start.22 = (bf16[6,64,2048]{2,1,0:T(8,128)(2,1)}, bf16[6,64,2048]{2,1,0:T(8,128)(2,1)S(1)}, u32[]{:S(2)}, u32[]{:S(2)}) collective-permute-start(bf16[6,64,2048]{2,1,0:T(8,128)(2,1)} %constant_dynamic-update-slice_fusion.refs_0_), channel_id=1, source_target_pairs={{0,1},{1,0},{2,3},{3,2},{4,5},{5,4},{6,7},{7,6},{8,9},{9,8},{10,11... | collective-permute-start | bytes 4718600 | tf_op jit(solution)/shard_map/ppermute | solution.py:173
  140.1 15.3 %collective-permute-start.23 = (bf16[6,64,2048]{2,1,0:T(8,128)(2,1)}, bf16[6,64,2048]{2,1,0:T(8,128)(2,1)S(1)}, u32[]{:S(2)}, u32[]{:S(2)}) collective-permute-start(bf16[6,64,2048]{2,1,0:T(8,128)(2,1)} %collective-permute-done.20.refs_1_), channel_id=1, source_target_pairs={{0,1},{1,0},{2,3},{3,2},{4,5},{5,4},{6,7},{7,6},{8,9},{9,8},{10,11... | collective-permute-start | bytes 4718600 | tf_op jit(solution)/shard_map/ppermute | solution.py:173
  151.3 29.1 %collective-permute-start.24 = (bf16[6,64,2048]{2,1,0:T(8,128)(2,1)}, bf16[6,64,2048]{2,1,0:T(8,128)(2,1)}, u32[]{:S(2)}, u32[]{:S(2)}) collective-permute-start(bf16[6,64,2048]{2,1,0:T(8,128)(2,1)} %add_convert_fusion.1), channel_id=1, source_target_pairs={{0,4},{1,3},{2,6},{3,1},{4,0},{5,7},{6,2},{7,5},{8,12},{9,11},{10,... | collective-permute-start | bytes 4718600 | tf_op jit(solution)/shard_map/ppermute | solution.py:173
  186.0 15.0 %collective-permute-start.25 = (bf16[12,64,2048]{2,1,0:T(8,128)(2,1)}, bf16[12,64,2048]{2,1,0:T(8,128)(2,1)}, u32[]{:S(2)}, u32[]{:S(2)}) collective-permute-start(bf16[12,64,2048]{2,1,0:T(8,128)(2,1)} %get-tuple-element.69), channel_id=1, source_target_pairs={{0,1},{1,0},{2,3},{3,2},{4,5},{5,4},{6,7},{7,6},{8,9},{9,8},{10,11... | collective-permute-start | bytes 9437192 | tf_op jit(solution)/shard_map/ppermute | solution.py:173
  195.8 13.9 %collective-permute-start.28 = (bf16[3,64,2048]{2,1,0:T(8,128)(2,1)S(1)}, bf16[3,64,2048]{2,1,0:T(8,128)(2,1)S(1)}, u32[]{:S(2)}, u32[]{:S(2)}) collective-permute-start(bf16[3,64,2048]{2,1,0:T(8,128)(2,1)S(1)} %add_convert_fusion.6), channel_id=1, source_target_pairs={{0,2},{1,5},{2,0},{3,7},{4,6},{5,1},{6,4},{7,3},{8,10},{9,13},{10,... | collective-permute-start | bytes 2359304 | tf_op jit(solution)/shard_map/ppermute | solution.py:173
  200.6 24.0 %collective-permute-start.27 = (bf16[8,64,2048]{2,1,0:T(8,128)(2,1)}, bf16[8,64,2048]{2,1,0:T(8,128)(2,1)}, u32[]{:S(2)}, u32[]{:S(2)}) collective-permute-start(bf16[8,64,2048]{2,1,0:T(8,128)(2,1)} %get-tuple-element.75), channel_id=1, source_target_pairs={{0,1},{1,0},{2,3},{3,2},{4,5},{5,4},{6,7},{7,6},{8,9},{9,8},{10,11... | collective-permute-start | bytes 6291464 | tf_op jit(solution)/shard_map/ppermute | solution.py:173
  204.6 30.8 %collective-permute-start.26 = (bf16[6,64,2048]{2,1,0:T(8,128)(2,1)}, bf16[6,64,2048]{2,1,0:T(8,128)(2,1)}, u32[]{:S(2)}, u32[]{:S(2)}) collective-permute-start(bf16[6,64,2048]{2,1,0:T(8,128)(2,1)} %add_convert_fusion), channel_id=1, source_target_pairs={{0,4},{1,3},{2,6},{3,1},{4,0},{5,7},{6,2},{7,5},{8,12},{9,11},{10,... | collective-permute-start | bytes 4718600 | tf_op jit(solution)/shard_map/ppermute | solution.py:173
  210.8 15.0 %collective-permute-start.30 = (f32[48,128]{1,0:T(8,128)S(1)}, f32[48,128]{1,0:T(8,128)S(1)}, u32[]{:S(2)}, u32[]{:S(2)}) collective-permute-start(f32[48,128]{1,0:T(8,128)S(1)} %pad_maximum_fusion.12), channel_id=1, source_target_pairs={{0,4},{1,5},{2,6},{3,7},{4,0},{5,1},{6,2},{7,3},{8,12},{9,13},{10,... | collective-permute-start | bytes 73736 | tf_op jit(solution)/shard_map/ppermute | solution.py:173
  214.7 20.7 %collective-permute-start.32 = (bf16[64,2048]{1,0:T(8,128)(2,1)S(1)}, bf16[64,2048]{1,0:T(8,128)(2,1)S(1)}, u32[]{:S(2)}, u32[]{:S(2)}) collective-permute-start(bf16[64,2048]{1,0:T(8,128)(2,1)S(1)} %get-tuple-element.102), channel_id=1, source_target_pairs={{0,16},{1,17},{2,18},{3,19},{4,20},{5,21},{6,22},{7,23},{8,24},{9,... | collective-permute-start | bytes 786440 | tf_op jit(solution)/shard_map/ppermute | solution.py:173
  257.5 15.1 %collective-permute-start.36 = (bf16[4,64,2048]{2,1,0:T(8,128)(2,1)S(1)}, bf16[4,64,2048]{2,1,0:T(8,128)(2,1)}, u32[]{:S(2)}, u32[]{:S(2)}) collective-permute-start(bf16[4,64,2048]{2,1,0:T(8,128)(2,1)S(1)} %add_convert_fusion.2), channel_id=1, source_target_pairs={{0,4},{1,3},{2,6},{3,1},{4,0},{5,7},{6,2},{7,5},{8,12},{9,11},{10,... | collective-permute-start | bytes 3145736 | tf_op jit(solution)/shard_map/ppermute | solution.py:173
  260.1 24.9 %collective-permute-start.38 = (bf16[64,2048]{1,0:T(8,128)(2,1)}, bf16[64,2048]{1,0:T(8,128)(2,1)S(1)}, u32[]{:S(2)}, u32[]{:S(2)}) collective-permute-start(bf16[64,2048]{1,0:T(8,128)(2,1)} %get-tuple-element.98), channel_id=1, source_target_pairs={{0,8},{1,9},{2,10},{3,11},{4,12},{5,13},{6,14},{7,15},{8,16},{9,17... | collective-permute-start | bytes 786440 | tf_op jit(solution)/shard_map/ppermute | solution.py:173
  262.9 22.1 %collective-permute-start.39 = (bf16[64,2048]{1,0:T(8,128)(2,1)}, bf16[64,2048]{1,0:T(8,128)(2,1)}, u32[]{:S(2)}, u32[]{:S(2)}) collective-permute-start(bf16[64,2048]{1,0:T(8,128)(2,1)} %get-tuple-element.100), channel_id=1, source_target_pairs={{0,16},{1,17},{2,18},{3,19},{4,20},{5,21},{6,22},{7,23},{8,24},{9,... | collective-permute-start | bytes 786440 | tf_op jit(solution)/shard_map/ppermute | solution.py:173
  272.0 13.1 %collective-permute-start.40 = (bf16[64,2048]{1,0:T(8,128)(2,1)}, bf16[64,2048]{1,0:T(8,128)(2,1)}, u32[]{:S(2)}, u32[]{:S(2)}) collective-permute-start(bf16[64,2048]{1,0:T(8,128)(2,1)} %get-tuple-element.99), channel_id=1, source_target_pairs={{0,24},{1,25},{2,26},{3,27},{4,28},{5,29},{6,30},{7,31},{8,0},{9,1... | collective-permute-start | bytes 786440 | tf_op jit(solution)/shard_map/ppermute | solution.py:173
  (70 other events, 712.0 us)

commit v5 on v4

--- a/solution.py
+++ b/solution.py
@@ -210,10 +210,8 @@
     return value.astype(jnp.bfloat16)
 
 
-def gather_tables(table):
-    steps = lax.axis_size("expert") // 4
-    planes = jnp.stack([table] + [send_along(table, -step) for step in range(1, steps)])
-    pair = jnp.stack([planes, send_second(planes)])
+def plane_tables(table):
+    pair = jnp.stack([table, send_second(table)])
     return jnp.stack([pair, send_first(pair)])
 
 
@@ -225,10 +223,6 @@
 def from_far_first(array, steps):
     far = array[:4 * (steps - 1)].reshape((2, 2, steps - 1) + array.shape[1:])
     return jnp.concatenate([array[4 * (steps - 1):].reshape((2, 2, 1) + array.shape[1:]), far], axis=2)
-
-
-def swapped(index):
-    return (index % 2) * 2 + index // 2
 
 
 def chosen_rows(pick, mine, other):
@@ -322,7 +316,7 @@
 
 
 def expand_kernel(weighted, count, back_ref, prob_ref, *refs):
-    sources, (mine_ref, other_ref) = refs[:-2], refs[-2:]
+    sources, (mine_ref, low_ref, high_ref) = refs[:-3], refs[-3:]
     half = mine_ref.shape[1]
     for group in range(count):
         for number, (source_ref, by_prob) in enumerate(zip(sources, weighted)):
@@ -332,13 +326,17 @@
             spread = jnp.dot(back_ref[group], rows, preferred_element_type=jnp.float32)
             place = group * len(sources) + number
             mine_ref[place] = spread[:half].astype(jnp.bfloat16)
-            other_ref[place] = spread[half:].astype(jnp.bfloat16)
+            for second, out_ref in ((0, low_ref), (1, high_ref)):
+                @pl.when(lax.rem(pl.program_id(0), 2) == second)
+                def _(out_ref=out_ref, place=place, spread=spread):
+                    out_ref[place] = spread[half:].astype(jnp.bfloat16)
 
 
 def expand(back, prob, slots, weighted, count, first_group):
     _, group_rows, capacity = back.shape
     half, features, arrays = group_rows // 2, slots[0].shape[2], len(slots)
-    out = jax.ShapeDtypeStruct((4 * count * arrays, half, features), jnp.bfloat16)
+    blocks = count * arrays
+    piece = jax.ShapeDtypeStruct((2 * blocks, half, features), jnp.bfloat16)
     return pl.pallas_call(
         functools.partial(expand_kernel, weighted, count),
         grid=(4,),
@@ -346,67 +344,120 @@
             group_spec(count, first_group, group_rows, capacity),
             group_spec(count, first_group, capacity, 1),
         ] + [group_spec(count, first_group, capacity, features)] * arrays,
-        out_specs=[
-            pl.BlockSpec((count * arrays, half, features), lambda i: (i, 0, 0)),
-            pl.BlockSpec((count * arrays, half, features), lambda i: (swapped(i), 0, 0)),
-        ],
-        out_shape=[out, out],
+        out_specs=[pl.BlockSpec((blocks, half, features), lambda i: (i, 0, 0))]
+        + [pl.BlockSpec((blocks, half, features), lambda i: (i // 2, 0, 0))] * 2,
+        out_shape=[jax.ShapeDtypeStruct((4 * blocks, half, features), jnp.bfloat16), piece, piece],
         compiler_params=pltpu.CompilerParams(vmem_limit_bytes=SMALL_VMEM),
         cost_estimate=LITTLE,
     )(back, prob, *slots)
 
 
-def forward_kernel(rows_ref, gate_up_ref, down_ref, projected_ref, hidden_ref, out_ref):
-    projected = jnp.dot(rows_ref[...], gate_up_ref[0], preferred_element_type=jnp.float32)
-    projected_ref[...] = projected
-    half_width = hidden_ref.shape[1]
-    gate_pre, up_pre = projected[:, :half_width], projected[:, half_width:]
-    hidden = (gate_pre * jax.nn.sigmoid(gate_pre) * up_pre).astype(jnp.bfloat16)
-    hidden_ref[...] = hidden
-    out_ref[...] = jnp.dot(hidden, down_ref[0], preferred_element_type=jnp.float32).astype(jnp.bfloat16)
-
-
-def backward_kernel(
-    grads_ref, projected_ref, rows_ref, gate_up_ref, down_ref, joined_ref, input_ref, gain_ref
-):
-    half_width = projected_ref.shape[1] // 2
-    hidden_grad = times_transposed(grads_ref[...], down_ref[0])
-    gate_pre, up_pre = projected_ref[:, :half_width], projected_ref[:, half_width:]
-    sigmoid_gate = jax.nn.sigmoid(gate_pre)
-    common = hidden_grad * sigmoid_gate
-    joined_ref[:, :half_width] = (
-        common * up_pre * (1.0 + gate_pre * (1.0 - sigmoid_gate))
-    ).astype(jnp.bfloat16)
-    joined_ref[:, half_width:] = (common * gate_pre).astype(jnp.bfloat16)
-    input_grad = times_transposed(joined_ref[...], gate_up_ref[0]).astype(jnp.bfloat16)
-    input_ref[...] = input_grad
-
-    @pl.when(pl.program_id(0) == 0)
+def forward_kernel(units, rows_ref, gate_ref, up_ref, down_ref, gate_pre_ref, up_pre_ref, hidden_ref, out_ref):
+    step = pl.program_id(0)
+    block = gate_pre_ref.shape[1]
+
+    @pl.when(step < units)
     def _():
-        gain_ref[...] = jnp.zeros_like(gain_ref)
-
-    terms = input_grad.astype(jnp.float32) * rows_ref[...].astype(jnp.float32)
-    gain_ref[...] += jnp.sum(terms, axis=0, keepdims=True)
-
-
-def by_rows(kernel, inputs, weights, outputs, sums):
-    block = inputs[0].shape[0] // 2
-
-    def row_spec(array):
-        return pl.BlockSpec((block,) + array.shape[1:], lambda i: (i, 0))
-
-    def whole_spec(array):
-        return pl.BlockSpec(array.shape, lambda i: (0,) * array.ndim)
-
+        gate_pre = jnp.dot(rows_ref[...], gate_ref[0], preferred_element_type=jnp.float32)
+        up_pre = jnp.dot(rows_ref[...], up_ref[0], preferred_element_type=jnp.float32)
+        gate_pre_ref[...] = gate_pre
+        up_pre_ref[...] = up_pre
+        columns = pl.ds(pl.multiple_of(step * block, block), block)
+        hidden_ref[:, columns] = (gate_pre * jax.nn.sigmoid(gate_pre) * up_pre).astype(jnp.bfloat16)
+
+    @pl.when(step >= units)
+    def _():
+        out_ref[...] = jnp.dot(
+            hidden_ref[...], down_ref[0], preferred_element_type=jnp.float32
+        ).astype(jnp.bfloat16)
+
+
+def forward(rows, gate_up_weight, down_weight):
+    slots, features = rows.shape
+    width = down_weight.shape[1]
+    block, units, wide = 256, width // 256, features // 2
+    early = lambda i: jnp.minimum(i, units - 1)
+    late = lambda i: jnp.maximum(i - units, 0)
     return pl.pallas_call(
-        kernel,
-        grid=(2,),
-        in_specs=[row_spec(array) for array in inputs] + [whole_spec(array) for array in weights],
-        out_specs=[row_spec(array) for array in outputs] + [whole_spec(array) for array in sums],
-        out_shape=outputs + sums,
+        functools.partial(forward_kernel, units),
+        grid=(units + 2,),
+        in_specs=[
+            pl.BlockSpec((slots, features), lambda i: (0, 0)),
+            pl.BlockSpec((1, features, block), lambda i: (0, 0, early(i))),
+            pl.BlockSpec((1, features, block), lambda i: (0, 0, units + early(i))),
+            pl.BlockSpec((1, width, wide), lambda i: (0, 0, late(i))),
+        ],
+        out_specs=[
+            pl.BlockSpec((slots, block), lambda i: (0, early(i))),
+            pl.BlockSpec((slots, block), lambda i: (0, early(i))),
+            pl.BlockSpec((slots, width), lambda i: (0, 0)),
+            pl.BlockSpec((slots, wide), lambda i: (0, late(i))),
+        ],
+        out_shape=[
+            jax.ShapeDtypeStruct((slots, width), jnp.float32),
+            jax.ShapeDtypeStruct((slots, width), jnp.float32),
+            jax.ShapeDtypeStruct((slots, width), jnp.bfloat16),
+            jax.ShapeDtypeStruct((slots, features), jnp.bfloat16),
+        ],
         compiler_params=pltpu.CompilerParams(vmem_limit_bytes=LARGE_VMEM),
         cost_estimate=LITTLE,
-    )(*inputs, *weights)
+    )(rows, gate_up_weight, gate_up_weight, down_weight)
+
+
+def backward_kernel(
+    units, grads_ref, gate_pre_ref, up_pre_ref, down_ref, gate_up_ref, rows_ref, joined_ref, input_ref, gain_ref
+):
+    step = pl.program_id(0)
+    block = gate_pre_ref.shape[1]
+
+    @pl.when(step < units)
+    def _():
+        gate_pre, up_pre = gate_pre_ref[...], up_pre_ref[...]
+        sigmoid_gate = jax.nn.sigmoid(gate_pre)
+        common = times_transposed(grads_ref[...], down_ref[0]) * sigmoid_gate
+        gate_grad = common * up_pre * (1.0 + gate_pre * (1.0 - sigmoid_gate))
+        start = pl.multiple_of(step * block, block)
+        joined_ref[:, pl.ds(start, block)] = gate_grad.astype(jnp.bfloat16)
+        joined_ref[:, pl.ds(units * block + start, block)] = (common * gate_pre).astype(jnp.bfloat16)
+
+    @pl.when(step >= units)
+    def _():
+        input_grad = times_transposed(joined_ref[...], gate_up_ref[0]).astype(jnp.bfloat16)
+        input_ref[...] = input_grad
+        terms = input_grad.astype(jnp.float32) * rows_ref[...].astype(jnp.float32)
+        gain_ref[...] = jnp.sum(terms, axis=0, keepdims=True)
+
+
+def backward(grads, gate_pre, up_pre, rows, gate_up_weight, down_weight):
+    slots, features = rows.shape
+    width = down_weight.shape[1]
+    block, units, wide = 256, width // 256, features // 4
+    early = lambda i: jnp.minimum(i, units - 1)
+    late = lambda i: jnp.maximum(i - units, 0)
+    return pl.pallas_call(
+        functools.partial(backward_kernel, units),
+        grid=(units + 4,),
+        in_specs=[
+            pl.BlockSpec((slots, features), lambda i: (0, 0)),
+            pl.BlockSpec((slots, block), lambda i: (0, early(i))),
+            pl.BlockSpec((slots, block), lambda i: (0, early(i))),
+            pl.BlockSpec((1, block, features), lambda i: (0, early(i), 0)),
+            pl.BlockSpec((1, wide, 2 * width), lambda i: (0, late(i), 0)),
+            pl.BlockSpec((slots, wide), lambda i: (0, late(i))),
+        ],
+        out_specs=[
+            pl.BlockSpec((slots, 2 * width), lambda i: (0, 0)),
+            pl.BlockSpec((slots, wide), lambda i: (0, late(i))),
+            pl.BlockSpec((1, wide), lambda i: (0, late(i))),
+        ],
+        out_shape=[
+            jax.ShapeDtypeStruct((slots, 2 * width), jnp.bfloat16),
+            jax.ShapeDtypeStruct((slots, features), jnp.bfloat16),
+            jax.ShapeDtypeStruct((1, features), jnp.float32),
+        ],
+        compiler_params=pltpu.CompilerParams(vmem_limit_bytes=LARGE_VMEM),
+        cost_estimate=LITTLE,
+    )(grads, gate_pre, up_pre, down_weight, gate_up_weight, rows)
 
 
 def pack(columns, gains):
@@ -438,13 +489,15 @@
     near_own = jnp.stack([tokens, cotangent])
     near_pair = jnp.concatenate([near_own, send_second(near_own)])
     near_far_pair = send_first(near_pair)
+    tables = plane_tables(
+        after(jnp.concatenate([expert_ids.T.astype(jnp.float32), gate_probs.T]), near_pair)
+    )
     token_far = jnp.stack([send_along(tokens, -step) for step in range(1, steps)])
-    tables = gather_tables(
-        after(jnp.concatenate([expert_ids.T.astype(jnp.float32), gate_probs.T]), token_far)
-    )
+    late_tables = after(tables, token_far)
+    far_tables = [send_along(late_tables, -step) for step in range(1, steps)]
     late_cot = after(cotangent, token_far)
     cot_steps = [send_along(late_cot, -step) for step in range(1, steps)]
-    token_second = after(send_second(token_far), near_far_pair, cot_steps[0])
+    token_second = after(send_second(token_far), near_far_pair, cot_steps[0], *far_tables)
     token_pair = jnp.concatenate([token_far, token_second])
     token_far_pair = after(send_first(token_pair), *cot_steps)
     near_pieces = (near_pair, near_far_pair, send_core(near_pair), send_core(near_far_pair))
@@ -456,7 +509,7 @@
     cot_pair = jnp.concatenate([cot_far, cot_second])
     cot_far_pair = send_first(cot_pair)
 
-    tables = far_first(tables)
+    tables = far_first(jnp.stack([tables] + far_tables, axis=2))
     tables = jnp.where(core == 0, tables, jnp.roll(tables, half, axis=2))
     matches = tables[:, :TOP] == my_expert.astype(jnp.float32)
     chosen = jnp.any(matches, axis=1)
@@ -475,52 +528,42 @@
     rows = select_normed(pick, gain_row, near_pieces, 1, 2, far, ())
     rows, = select_normed(pick, gain_row, token_pieces, steps - 1, 1, 0, tuple(rows))
     rows = rows.reshape(-1, features)
-    slots, width = rows.shape[0], down_weight.shape[1]
-    projected, hidden, block_out = by_rows(
-        forward_kernel, [rows], [gate_up_weight, down_weight],
-        [
-            jax.ShapeDtypeStruct((slots, 2 * width), jnp.float32),
-            jax.ShapeDtypeStruct((slots, width), jnp.bfloat16),
-            jax.ShapeDtypeStruct((slots, features), jnp.bfloat16),
-        ], [],
-    )
+    gate_pre, up_pre, hidden, block_out = forward(rows, gate_up_weight, down_weight)
     block_out, cot_far_pair = together(block_out, cot_far_pair)
     cot_pieces = (cot_pair, cot_far_pair, send_core(cot_pair), send_core(cot_far_pair))
     out_slots = block_out.reshape(expert_size, capacity, features)
-    out_mine, out_other = expand(back, slot_prob, (out_slots,), (True,), steps - 1, 0)
+    out_mine, out_low, out_high = expand(back, slot_prob, (out_slots,), (True,), steps - 1, 0)
 
     half_far, one_far = 2 * (steps - 1), steps - 1
-    out_core = send_core(out_other)
-    out_upper = narrow(add_up(out_mine[half_far:], out_core[half_far:]))
+    out_core_high = send_core(out_high)
+    out_core = send_core(out_low)
+    out_upper = narrow(add_up(out_mine[half_far:], out_core_high))
     out_first = send_first(out_upper)
     held = select_grads(
-        after(pick, out_other), slot_prob, out_slots, near_pieces, 1, 2, 1, far, ()
+        after(pick, out_high), slot_prob, out_slots, near_pieces, 1, 2, 1, far, ()
     )
     grads, prob_value = select_grads(
         after(pick, out_upper), slot_prob, out_slots, cot_pieces, steps - 1, 1, 0, 0, tuple(held)
     )
     grads = grads.reshape(-1, features)
-    joined_grad, input_grad, gain_term = by_rows(
-        backward_kernel, [grads, projected, rows], [gate_up_weight, down_weight],
-        [
-            jax.ShapeDtypeStruct((slots, 2 * width), jnp.bfloat16),
-            jax.ShapeDtypeStruct((slots, features), jnp.bfloat16),
-        ],
-        [jax.ShapeDtypeStruct((1, features), jnp.float32)],
+    joined_grad, input_grad, gain_term = backward(
+        grads, gate_pre, up_pre, rows, gate_up_weight, down_weight
     )
     input_grad, out_first = together(input_grad, out_first)
     input_slots = input_grad.reshape(expert_size, capacity, features)
-    in_mine, in_other = expand(back, slot_prob, (input_slots,), (False,), steps - 1, 0)
-    in_core = send_core(in_other)
+    in_mine, in_low, in_high = expand(back, slot_prob, (input_slots,), (False,), steps - 1, 0)
+    in_core_high = send_core(in_high)
+    in_core = send_core(in_low)
     out_middle = narrow(
-        add_up(out_mine[one_far:half_far], out_core[one_far:half_far], after(out_first, in_other)[one_far:])
+        add_up(out_mine[one_far:half_far], out_core[one_far:half_far], after(out_first, in_high)[one_far:])
     )
     out_second = send_second(out_middle)
-    near_mine, near_other = expand(
-        back, after(slot_prob, in_other), (out_slots, input_slots), (True, False), 1, far
-    )
-    near_core = send_core(near_other)
-    in_upper = narrow(add_up(in_mine[half_far:], after(in_core, out_middle, near_other)[half_far:]))
+    near_mine, near_low, near_high = expand(
+        back, after(slot_prob, in_high), (out_slots, input_slots), (True, False), 1, far
+    )
+    near_core_high = send_core(near_high)
+    near_core = send_core(near_low)
+    in_upper = narrow(add_up(in_mine[half_far:], after(in_core_high, out_middle, near_high)))
     in_first = send_first(in_upper)
     gains = (gain_term[0] / gain).reshape(-1, 128)
     prob_rows = jnp.sum(jnp.where(placed, prob_value, 0.0), axis=1)
@@ -539,7 +582,7 @@
     out_far = [send_along(out_planes[step - 1], step) for step in range(1, steps)]
     gate_up_part = outer_sum(after(rows, out_planes), joined_grad)
     in_first, near_core, gate_up_part, got = together(
-        in_first, near_core, gate_up_part, got, *out_far[:2]
+        in_first, near_core, gate_up_part, got, out_far[len(out_far) // 2]
     )[:4]
     columns, gains = unpack_add(columns[0], gains, got)
     in_middle = narrow(
@@ -552,7 +595,7 @@
     in_planes = narrow(own_plane(in_mine, in_core, in_first, in_second, one_far))
     messages = [send_along(pack(columns[step], gains), step) for step in range(1, steps)]
     in_far = [send_along(in_planes[step - 1], step) for step in range(1, steps)]
-    near_upper = narrow(add_up(near_mine[4:], after(near_core, in_planes)[4:]))
+    near_upper = narrow(add_up(near_mine[4:], after(near_core_high, in_planes)))
     near_first = send_first(near_upper)
     near_middle = narrow(add_up(near_mine[2:4], near_core[2:4], near_first[2:]))
     near_second = send_second(near_middle)

time: 290 us -> 288 us (level)
  waiting for transfers between devices: 107 us -> 95 us
  local copies, waits for them, and re-layouts: 22.9 us -> 34.4 us
  starting transfers between devices: 53.3 us -> 47.4 us
  Pallas kernels: 54.4 us -> 58.5 us
    ppermute x44 -> x47, waiting for transfers between devices: 107 us -> 95 us  [send(): return lax.ppermute(array, BOTH, pairs)]
    unnamed x101 -> x117, local copies, waits for them, and re-layouts: 17.5 us -> 28.2 us
    ppermute x44 -> x47, starting transfers between devices: 53.3 us -> 47.4 us  [send(): return lax.ppermute(array, BOTH, pairs)]
    pallas_call x3, Pallas kernels: 9.59 us -> 14 us  [expand(): pl.pallas_call(functools.partial(expand_kernel, weighted, count), grid=(4...]
  transfers between devices with their start and end apart: 44 -> 47, of which waited for: 16 -> 20; matrix products, arithmetic and copies ran while one was open for 16% -> 17% of each run, Pallas kernels for 17% -> 18%
where the time goes in v5:
time: 288 us; the launch traced here: 287 us
  waiting for transfers between devices  95 us (33%)
  Pallas kernels  58.5 us (20%)
  starting transfers between devices  47.4 us (16%)
  other arithmetic  39 us (14%)
  local copies, waits for them, and re-layouts  34.4 us (12%)
  matrix products  11.2 us (4%)
    ppermute x47, waiting for transfers between devices, send(): return lax.ppermute(array, BOTH, pairs)  95 us
    ppermute x47, starting transfers between devices, send(): return lax.ppermute(array, BOTH, pairs)  47.4 us
    unnamed x117, local copies, waits for them, and re-layouts  28.2 us
    convert_element_type x8, other arithmetic, narrow(): return value.astype(jnp.bfloat16)  18 us
    pallas_call x4, Pallas kernels, select(): pl.pallas_call(functools.partial(kernel, count), grid=(4,), in_specs=[gro...  16.4 us
    pallas_call x1, Pallas kernels, backward(): pl.pallas_call(functools.partial(backward_kernel, units), grid=(units + 4...  14.8 us
    pallas_call x3, Pallas kernels, expand(): pl.pallas_call(functools.partial(expand_kernel, weighted, count), grid=(4...  14 us
    pallas_call x1, Pallas kernels, forward(): pl.pallas_call(functools.partial(forward_kernel, units), grid=(units + 2,...  13.3 us
  transfers between devices with their start and end apart: 47, of which 20 were waited for; matrix products, arithmetic and copies ran while one was open for 17% of the time, Pallas kernels for 18%

profile of v5, /device:TPU:0, one launch (start us, length us, event | category | flops | bytes accessed | tf_op | source)
XLA Modules:
  0.0 286.8 jit_solution(3013435782531330196)
XLA Ops:
  1.8 3.0 %collective-permute-start = (bf16[2,64,2048]{2,1,0:T(8,128)(2,1)S(1)}, bf16[2,64,2048]{2,1,0:T(8,128)(2,1)S(1)}, u32[]{:S(2)}, u32[]{:S(2)}) collective-permute-start(bf16[2,64,2048]{2,1,0:T(8,128)(2,1)S(1)} %pad_maximum_fusion.4), channel_id=1, source_target_pairs={{0,2},{1,5},{2,0},{3,7},{4,6},{5,1},{6,4},{7,3},{8,10},{9,13},{10,... | collective-permute-start | bytes 1572872 | tf_op jit(solution)/shard_map/ppermute | solution.py:173
  16.0 3.6 %collective-permute-done.3 = bf16[64,2048]{1,0:T(8,128)(2,1)S(1)} collective-permute-done((bf16[64,2048]{1,0:T(8,128)(2,1)}, bf16[64,2048]{1,0:T(8,128)(2,1)S(1)}, u32[]{:S(2)}, u32[]{:S(2)}) %collective-permute-start.3) | collective-permute-done | bytes 262176 | tf_op jit(solution)/shard_map/ppermute | solution.py:173
  19.7 11.8 %collective-permute-done.4 = bf16[64,2048]{1,0:T(8,128)(2,1)S(1)} collective-permute-done((bf16[64,2048]{1,0:T(8,128)(2,1)}, bf16[64,2048]{1,0:T(8,128)(2,1)S(1)}, u32[]{:S(2)}, u32[]{:S(2)}) %collective-permute-start.4) | collective-permute-done | bytes 262176 | tf_op jit(solution)/shard_map/ppermute | solution.py:173
  35.3 8.4 %collective-permute-done.1 = f32[16,128]{1,0:T(8,128)S(1)} collective-permute-done((f32[16,128]{1,0:T(8,128)S(1)}, f32[16,128]{1,0:T(8,128)S(1)}, u32[]{:S(2)}, u32[]{:S(2)}) %collective-permute-start.1) | collective-permute-done | bytes 8224 | tf_op jit(solution)/shard_map/ppermute | solution.py:173
  44.2 3.2 %collective-permute-done.2 = f32[2,16,128]{2,1,0:T(8,128)S(1)} collective-permute-done((f32[2,16,128]{2,1,0:T(8,128)S(1)}, f32[2,16,128]{2,1,0:T(8,128)S(1)}, u32[]{:S(2)}, u32[]{:S(2)}) %collective-permute-start.2) | collective-permute-done | bytes 16416 | tf_op jit(solution)/shard_map/ppermute | solution.py:173
  58.4 15.2 %collective-permute-done.13 = bf16[64,2048]{1,0:T(8,128)(2,1)S(1)} collective-permute-done((bf16[64,2048]{1,0:T(8,128)(2,1)S(1)}, bf16[64,2048]{1,0:T(8,128)(2,1)S(1)}, u32[]{:S(2)}, u32[]{:S(2)}) %collective-permute-start.13) | collective-permute-done | bytes 262176 | tf_op jit(solution)/shard_map/ppermute | solution.py:173
  73.6 4.0 %collective-permute-done.12.refs_1_ = bf16[6,64,2048]{2,1,0:T(8,128)(2,1)} collective-permute-done((bf16[6,64,2048]{2,1,0:T(8,128)(2,1)}, bf16[6,64,2048]{2,1,0:T(8,128)(2,1)}, u32[]{:S(2)}, u32[]{:S(2)}) %collective-permute-start.12) | collective-permute-done | bytes 1572896 | tf_op jit(solution)/shard_map/ppermute | solution.py:173
  81.7 9.4 %collective-permute-done.17 = bf16[3,64,2048]{2,1,0:T(8,128)(2,1)S(1)} collective-permute-done((bf16[3,64,2048]{2,1,0:T(8,128)(2,1)S(1)}, bf16[3,64,2048]{2,1,0:T(8,128)(2,1)S(1)}, u32[]{:S(2)}, u32[]{:S(2)}) %collective-permute-start.17) | collective-permute-done | bytes 786464 | tf_op jit(solution)/shard_map/ppermute | solution.py:173
  102.4 3.0 %shard_map.118.refs_5_ = bf16[16,48,2048]{2,1,0:T(8,128)(2,1)S(1)} custom-call(bf16[16,48,128]{2,1,0:T(8,128)(2,1)S(1)} %fusion.15.pick_ref, bf16[4,64,2048]{2,1,0:T(8,128)(2,1)S(1)} %copy-done.9, bf16[4,64,2048]{2,1,0:T(8,128)(2,1)S(1)} %copy-done.17, bf16[4,64,2048]{2,1,0:T(8,128)(2,1)S(1)} %copy-done.20, ...), custom_call_target="tpu_custom_call" | custom-call | flops 1000000 | bytes 100000 | tf_op jit(solution)/shard_map/pallas_call | solution.py:276
  105.4 5.1 %shard_map.119 = bf16[16,48,2048]{2,1,0:T(8,128)(2,1)S(1)} custom-call(bf16[16,48,128]{2,1,0:T(8,128)(2,1)S(1)} %fusion.15.pick_ref, bf16[6,64,2048]{2,1,0:T(8,128)(2,1)} %pad_maximum_fusion.refs_0_, bf16[6,64,2048]{2,1,0:T(8,128)(2,1)} %collective-permute-done.12.refs_1_, ...), custom_call_target="tpu_custom_call", output_to_operand_aliasing={{}: (6, {})} | custom-call | flops 1000000 | bytes 100000 | tf_op jit(solution)/shard_map/pallas_call | solution.py:276
  112.2 13.3 %shard_map.120 = (f32[768,768]{1,0:T(8,128)S(1)}, f32[768,768]{1,0:T(8,128)S(1)}, bf16[768,768]{1,0:T(8,128)(2,1)S(1)}, bf16[768,2048]{1,0:T(8,128)(2,1)}) custom-call(bf16[768,2048]{1,0:T(8,128)(2,1)} %bitcast.114, bf16[1,2048,1536]{2,1,0:T(8,128)(2,1)} %gate_up_ref.1, bf16[1,2048,1536]{2,1,0:T(8,128)(2,1)} %gate_up_ref.1, bf16[1,768,2048]{2,1,0:T(8,128)(2,1)} %down_ref.3), custom_call_target="tpu_custom_call" | custom-call | flops 1000000 | bytes 100000 | tf_op jit(solution)/shard_map/pallas_call | solution.py:381
  131.4 5.4 %shard_map.121 = (bf16[12,64,2048]{2,1,0:T(8,128)(2,1)S(1)}, bf16[6,64,2048]{2,1,0:T(8,128)(2,1)}, bf16[6,64,2048]{2,1,0:T(8,128)(2,1)S(1)}) custom-call(bf16[16,128,48]{2,1,0:T(8,128)(2,1)S(1)} %fusion.1.back_ref, f32[16,48,1]{2,1,0:T(8,128)S(1)} %copy.22.prob_ref.refs_4_, bf16[16,48,2048]{2,1,0:T(8,128)(2,1)S(1)} %bitcast.117), custom_call_target="tpu_custom_call" | custom-call | flops 1000000 | bytes 100000 | tf_op jit(solution)/shard_map/pallas_call | solution.py:340
  137.4 4.8 %collective-permute-done.21 = bf16[6,64,2048]{2,1,0:T(8,128)(2,1)S(1)} collective-permute-done((bf16[6,64,2048]{2,1,0:T(8,128)(2,1)S(1)}, bf16[6,64,2048]{2,1,0:T(8,128)(2,1)S(1)}, u32[]{:S(2)}, u32[]{:S(2)}) %collective-permute-start.21) | collective-permute-done | bytes 1572896 | tf_op jit(solution)/shard_map/ppermute | solution.py:173
  155.7 5.3 %shard_map.123 = (bf16[16,48,2048]{2,1,0:T(8,128)(2,1)S(1)}, f32[16,48,1]{2,1,0:T(8,128)S(1)}) custom-call(bf16[16,48,128]{2,1,0:T(8,128)(2,1)S(1)} %copy-done.15, bf16[6,64,2048]{2,1,0:T(8,128)(2,1)} %constant_dynamic-update-slice_fusion.refs_0_, ...), custom_call_target="tpu_custom_call", output_to_operand_aliasing={{0}: (7, {}), {1}: (8, {})} | custom-call | flops 1000000 | bytes 100000 | tf_op jit(solution)/shard_map/pallas_call | solution.py:276
  162.7 14.8 %shard_map.124 = (bf16[768,1536]{1,0:T(8,128)(2,1)S(1)}, bf16[768,2048]{1,0:T(8,128)(2,1)}, f32[1,2048]{1,0:T(1,128)S(1)}) custom-call(bf16[768,2048]{1,0:T(8,128)(2,1)} %bitcast.123, f32[768,768]{1,0:T(8,128)S(1)} %copy-done.27, f32[768,768]{1,0:T(8,128)} %copy-done.28, bf16[1,768,2048]{2,1,0:T(8,128)(2,1)} %down_ref.3, bf16[1,2048,1536]{2,1,0:T(8,128)(2,1)} %gate_up_ref.1, ...), custom_call_target="tpu_custom_call" | custom-call | flops 1000000 | bytes 100000 | tf_op jit(solution)/shard_map/pallas_call | solution.py:437
  180.9 5.0 %shard_map.125 = (bf16[12,64,2048]{2,1,0:T(8,128)(2,1)S(1)}, bf16[6,64,2048]{2,1,0:T(8,128)(2,1)}, bf16[6,64,2048]{2,1,0:T(8,128)(2,1)}) custom-call(bf16[16,128,48]{2,1,0:T(8,128)(2,1)S(1)} %copy-done.12, f32[16,48,1]{2,1,0:T(8,128)S(1)} %copy.22.prob_ref.refs_4_, bf16[16,48,2048]{2,1,0:T(8,128)(2,1)S(1)} %bitcast.121), custom_call_target="tpu_custom_call" | custom-call | flops 1000000 | bytes 100000 | tf_op jit(solution)/shard_map/pallas_call | solution.py:340
  198.7 3.6 %shard_map.126 = (bf16[8,64,2048]{2,1,0:T(8,128)(2,1)S(1)}, bf16[4,64,2048]{2,1,0:T(8,128)(2,1)}, bf16[4,64,2048]{2,1,0:T(8,128)(2,1)S(1)}) custom-call(bf16[16,128,48]{2,1,0:T(8,128)(2,1)S(1)} %copy-done.13, f32[16,48,1]{2,1,0:T(8,128)S(1)} %copy.23.prob_ref, bf16[16,48,2048]{2,1,0:T(8,128)(2,1)S(1)} %bitcast.120, bf16[16,48,2048]{2,1,0:T(8,128)(2,1)S(1)} %bitcast.122), custom_call_target="tpu_custom_call" | custom-call | flops 1000000 | bytes 100000 | tf_op jit(solution)/shard_map/pallas_call | solution.py:340
  203.9 3.5 %add_convert_fusion = bf16[6,64,2048]{2,1,0:T(8,128)(2,1)} fusion(bf16[6,64,2048]{2,1,0:T(8,128)(2,1)} %collective-permute-done.25, bf16[12,64,2048]{2,1,0:T(8,128)(2,1)S(1)} %copy-done.23), kind=kLoop, calls=%fused_computation.3 | loop fusion | flops 3145728 | bytes 4718592 | tf_op jit(solution)/shard_map/convert_element_type | solution.py:210
  207.8 4.0 %convolution_convert_fusion.1 = bf16[768,2048]{1,0:T(8,128)(2,1)} fusion(bf16[768,768]{1,0:T(8,128)(2,1)S(1)} %copy-done.37, bf16[768,2048]{1,0:T(8,128)(2,1)S(1)} %bitcast.124), kind=kOutput, calls=%fused_computation.2 | convolution fusion | flops 2417491968 | bytes 7471104 | tf_op jit(solution)/shard_map/dot_general | solution.py:39
  219.8 7.1 %convolution_convert_fusion = bf16[2048,1536]{1,0:T(8,128)(2,1)} fusion(bf16[768,2048]{1,0:T(8,128)(2,1)S(1)} %bitcast.116, bf16[768,1536]{1,0:T(8,128)(2,1)S(1)} %copy-done.35), kind=kOutput, calls=%fused_computation.1 | convolution fusion | flops 4834983936 | bytes 11796480 | tf_op jit(solution)/shard_map/dot_general | solution.py:39
  235.5 3.8 %collective-permute-start.38 = (bf16[64,2048]{1,0:T(8,128)(2,1)S(1)}, bf16[64,2048]{1,0:T(8,128)(2,1)}, u32[]{:S(2)}, u32[]{:S(2)}) collective-permute-start(bf16[64,2048]{1,0:T(8,128)(2,1)S(1)} %get-tuple-element.111), channel_id=1, source_target_pairs={{0,24},{1,25},{2,26},{3,27},{4,28},{5,29},{6,30},{7,31},{8,0},{9,1... | collective-permute-start | bytes 786440 | tf_op jit(solution)/shard_map/ppermute | solution.py:173
  241.6 5.3 %collective-permute-done.37 = bf16[64,2048]{1,0:T(8,128)(2,1)} collective-permute-done((bf16[64,2048]{1,0:T(8,128)(2,1)}, bf16[64,2048]{1,0:T(8,128)(2,1)}, u32[]{:S(2)}, u32[]{:S(2)}) %collective-permute-start.37) | collective-permute-done | bytes 262176 | tf_op jit(solution)/shard_map/ppermute | solution.py:173
  262.8 6.7 %collective-permute-done.45 = f32[20,128]{1,0:T(8,128)S(1)} collective-permute-done((f32[20,128]{1,0:T(8,128)S(1)}, f32[20,128]{1,0:T(8,128)S(1)}, u32[]{:S(2)}, u32[]{:S(2)}) %collective-permute-start.45) | collective-permute-done | bytes 10272 | tf_op jit(solution)/shard_map/ppermute | solution.py:173
  274.3 7.0 %collective-permute-done.40 = bf16[2,64,2048]{2,1,0:T(8,128)(2,1)S(1)} collective-permute-done((bf16[2,64,2048]{2,1,0:T(8,128)(2,1)S(1)}, bf16[2,64,2048]{2,1,0:T(8,128)(2,1)S(1)}, u32[]{:S(2)}, u32[]{:S(2)}) %collective-permute-start.40) | collective-permute-done | bytes 524320 | tf_op jit(solution)/shard_map/ppermute | solution.py:173
  (285 shorter events, 129.2 us)
Async XLA Ops:
  8.6 22.9 %collective-permute-start.4 = (bf16[64,2048]{1,0:T(8,128)(2,1)}, bf16[64,2048]{1,0:T(8,128)(2,1)S(1)}, u32[]{:S(2)}, u32[]{:S(2)}) collective-permute-start(bf16[64,2048]{1,0:T(8,128)(2,1)} %param.7), channel_id=1, source_target_pairs={{0,16},{1,17},{2,18},{3,19},{4,20},{5,21},{6,22},{7,23},{8,24},{9,... | collective-permute-start | bytes 786440 | tf_op jit(solution)/shard_map/ppermute | solution.py:173
  13.1 41.7 %collective-permute-start.10 = (bf16[4,64,2048]{2,1,0:T(8,128)(2,1)S(1)}, bf16[4,64,2048]{2,1,0:T(8,128)(2,1)S(1)}, u32[]{:S(2)}, u32[]{:S(2)}) collective-permute-start(bf16[4,64,2048]{2,1,0:T(8,128)(2,1)S(1)} %pad_maximum_fusion.1.refs_0_), channel_id=1, source_target_pairs={{0,4},{1,3},{2,6},{3,1},{4,0},{5,7},{6,2},{7,5},{8,12},{9,11},{10,... | collective-permute-start | bytes 3145736 | tf_op jit(solution)/shard_map/ppermute | solution.py:173
  31.6 23.2 %collective-permute-start.9 = (bf16[3,64,2048]{2,1,0:T(8,128)(2,1)S(1)}, bf16[3,64,2048]{2,1,0:T(8,128)(2,1)S(1)}, u32[]{:S(2)}, u32[]{:S(2)}) collective-permute-start(bf16[3,64,2048]{2,1,0:T(8,128)(2,1)S(1)} %pad_maximum_fusion.2), channel_id=1, source_target_pairs={{0,2},{1,5},{2,0},{3,7},{4,6},{5,1},{6,4},{7,3},{8,10},{9,13},{10,... | collective-permute-start | bytes 2359304 | tf_op jit(solution)/shard_map/ppermute | solution.py:173
  33.1 16.0 %collective-permute-start.11 = (bf16[64,2048]{1,0:T(8,128)(2,1)S(1)}, bf16[64,2048]{1,0:T(8,128)(2,1)S(1)}, u32[]{:S(2)}, u32[]{:S(2)}) collective-permute-start(bf16[64,2048]{1,0:T(8,128)(2,1)S(1)} %copy-done.40), channel_id=1, source_target_pairs={{0,24},{1,25},{2,26},{3,27},{4,28},{5,29},{6,30},{7,31},{8,0},{9,1... | collective-permute-start | bytes 786440 | tf_op jit(solution)/shard_map/ppermute | solution.py:173
  56.3 21.3 %collective-permute-start.12 = (bf16[6,64,2048]{2,1,0:T(8,128)(2,1)}, bf16[6,64,2048]{2,1,0:T(8,128)(2,1)}, u32[]{:S(2)}, u32[]{:S(2)}) collective-permute-start(bf16[6,64,2048]{2,1,0:T(8,128)(2,1)} %pad_maximum_fusion.refs_0_), channel_id=1, source_target_pairs={{0,4},{1,3},{2,6},{3,1},{4,0},{5,7},{6,2},{7,5},{8,12},{9,11},{10,... | collective-permute-start | bytes 4718600 | tf_op jit(solution)/shard_map/ppermute | solution.py:173
  56.8 16.7 %collective-permute-start.13 = (bf16[64,2048]{1,0:T(8,128)(2,1)S(1)}, bf16[64,2048]{1,0:T(8,128)(2,1)S(1)}, u32[]{:S(2)}, u32[]{:S(2)}) collective-permute-start(bf16[64,2048]{1,0:T(8,128)(2,1)S(1)} %copy-done.40), channel_id=1, source_target_pairs={{0,16},{1,17},{2,18},{3,19},{4,20},{5,21},{6,22},{7,23},{8,24},{9,... | collective-permute-start | bytes 786440 | tf_op jit(solution)/shard_map/ppermute | solution.py:173
  58.0 15.6 %collective-permute-start.14 = (bf16[64,2048]{1,0:T(8,128)(2,1)S(1)}, bf16[64,2048]{1,0:T(8,128)(2,1)S(1)}, u32[]{:S(2)}, u32[]{:S(2)}) collective-permute-start(bf16[64,2048]{1,0:T(8,128)(2,1)S(1)} %copy-done.40), channel_id=1, source_target_pairs={{0,8},{1,9},{2,10},{3,11},{4,12},{5,13},{6,14},{7,15},{8,16},{9,17... | collective-permute-start | bytes 786440 | tf_op jit(solution)/shard_map/ppermute | solution.py:173
  80.2 25.2 %collective-permute-start.15 = (bf16[6,64,2048]{2,1,0:T(8,128)(2,1)}, bf16[6,64,2048]{2,1,0:T(8,128)(2,1)}, u32[]{:S(2)}, u32[]{:S(2)}) collective-permute-start(bf16[6,64,2048]{2,1,0:T(8,128)(2,1)} %pad_maximum_fusion.refs_0_), channel_id=1, source_target_pairs={{0,1},{1,0},{2,3},{3,2},{4,5},{5,4},{6,7},{7,6},{8,9},{9,8},{10,11... | collective-permute-start | bytes 4718600 | tf_op jit(solution)/shard_map/ppermute | solution.py:173
  80.2 25.2 %collective-permute-start.16 = (bf16[6,64,2048]{2,1,0:T(8,128)(2,1)}, bf16[6,64,2048]{2,1,0:T(8,128)(2,1)}, u32[]{:S(2)}, u32[]{:S(2)}) collective-permute-start(bf16[6,64,2048]{2,1,0:T(8,128)(2,1)} %collective-permute-done.12.refs_1_), channel_id=1, source_target_pairs={{0,1},{1,0},{2,3},{3,2},{4,5},{5,4},{6,7},{7,6},{8,9},{9,8},{10,11... | collective-permute-start | bytes 4718600 | tf_op jit(solution)/shard_map/ppermute | solution.py:173
  92.0 37.5 %collective-permute-start.20 = (bf16[6,64,2048]{2,1,0:T(8,128)(2,1)}, bf16[6,64,2048]{2,1,0:T(8,128)(2,1)}, u32[]{:S(2)}, u32[]{:S(2)}) collective-permute-start(bf16[6,64,2048]{2,1,0:T(8,128)(2,1)} %constant_dynamic-update-slice_fusion.refs_0_), channel_id=1, source_target_pairs={{0,4},{1,3},{2,6},{3,1},{4,0},{5,7},{6,2},{7,5},{8,12},{9,11},{10,... | collective-permute-start | bytes 4718600 | tf_op jit(solution)/shard_map/ppermute | solution.py:173
  136.9 18.9 %collective-permute-start.22 = (bf16[6,64,2048]{2,1,0:T(8,128)(2,1)}, bf16[6,64,2048]{2,1,0:T(8,128)(2,1)}, u32[]{:S(2)}, u32[]{:S(2)}) collective-permute-start(bf16[6,64,2048]{2,1,0:T(8,128)(2,1)} %constant_dynamic-update-slice_fusion.refs_0_), channel_id=1, source_target_pairs={{0,1},{1,0},{2,3},{3,2},{4,5},{5,4},{6,7},{7,6},{8,9},{9,8},{10,11... | collective-permute-start | bytes 4718600 | tf_op jit(solution)/shard_map/ppermute | solution.py:173
  137.3 18.4 %collective-permute-start.23 = (bf16[6,64,2048]{2,1,0:T(8,128)(2,1)}, bf16[6,64,2048]{2,1,0:T(8,128)(2,1)}, u32[]{:S(2)}, u32[]{:S(2)}) collective-permute-start(bf16[6,64,2048]{2,1,0:T(8,128)(2,1)} %collective-permute-done.20.refs_1_), channel_id=1, source_target_pairs={{0,1},{1,0},{2,3},{3,2},{4,5},{5,4},{6,7},{7,6},{8,9},{9,8},{10,11... | collective-permute-start | bytes 4718600 | tf_op jit(solution)/shard_map/ppermute | solution.py:173
  144.0 35.0 %collective-permute-start.24 = (bf16[6,64,2048]{2,1,0:T(8,128)(2,1)}, bf16[6,64,2048]{2,1,0:T(8,128)(2,1)}, u32[]{:S(2)}, u32[]{:S(2)}) collective-permute-start(bf16[6,64,2048]{2,1,0:T(8,128)(2,1)} %add_convert_fusion.1), channel_id=1, source_target_pairs={{0,4},{1,3},{2,6},{3,1},{4,0},{5,7},{6,2},{7,5},{8,12},{9,11},{10,... | collective-permute-start | bytes 4718600 | tf_op jit(solution)/shard_map/ppermute | solution.py:173
  145.7 47.4 %collective-permute-start.26 = (bf16[6,64,2048]{2,1,0:T(8,128)(2,1)}, bf16[6,64,2048]{2,1,0:T(8,128)(2,1)}, u32[]{:S(2)}, u32[]{:S(2)}) collective-permute-start(bf16[6,64,2048]{2,1,0:T(8,128)(2,1)} %get-tuple-element.80), channel_id=1, source_target_pairs={{0,1},{1,0},{2,3},{3,2},{4,5},{5,4},{6,7},{7,6},{8,9},{9,8},{10,11... | collective-permute-start | bytes 4718600 | tf_op jit(solution)/shard_map/ppermute | solution.py:173
  187.5 16.4 %collective-permute-start.25 = (bf16[6,64,2048]{2,1,0:T(8,128)(2,1)}, bf16[6,64,2048]{2,1,0:T(8,128)(2,1)}, u32[]{:S(2)}, u32[]{:S(2)}) collective-permute-start(bf16[6,64,2048]{2,1,0:T(8,128)(2,1)} %get-tuple-element.76), channel_id=1, source_target_pairs={{0,1},{1,0},{2,3},{3,2},{4,5},{5,4},{6,7},{7,6},{8,9},{9,8},{10,11... | collective-permute-start | bytes 4718600 | tf_op jit(solution)/shard_map/ppermute | solution.py:173
  195.3 16.6 %collective-permute-start.29 = (bf16[3,64,2048]{2,1,0:T(8,128)(2,1)S(1)}, bf16[3,64,2048]{2,1,0:T(8,128)(2,1)S(1)}, u32[]{:S(2)}, u32[]{:S(2)}) collective-permute-start(bf16[3,64,2048]{2,1,0:T(8,128)(2,1)S(1)} %add_convert_fusion.6), channel_id=1, source_target_pairs={{0,2},{1,5},{2,0},{3,7},{4,6},{5,1},{6,4},{7,3},{8,10},{9,13},{10,... | collective-permute-start | bytes 2359304 | tf_op jit(solution)/shard_map/ppermute | solution.py:173
  203.4 23.5 %collective-permute-start.28 = (bf16[4,64,2048]{2,1,0:T(8,128)(2,1)}, bf16[4,64,2048]{2,1,0:T(8,128)(2,1)}, u32[]{:S(2)}, u32[]{:S(2)}) collective-permute-start(bf16[4,64,2048]{2,1,0:T(8,128)(2,1)} %get-tuple-element.85), channel_id=1, source_target_pairs={{0,1},{1,0},{2,3},{3,2},{4,5},{5,4},{6,7},{7,6},{8,9},{9,8},{10,11... | collective-permute-start | bytes 3145736 | tf_op jit(solution)/shard_map/ppermute | solution.py:173
  203.4 27.9 %collective-permute-start.34 = (bf16[6,64,2048]{2,1,0:T(8,128)(2,1)}, bf16[6,64,2048]{2,1,0:T(8,128)(2,1)}, u32[]{:S(2)}, u32[]{:S(2)}) collective-permute-start(bf16[6,64,2048]{2,1,0:T(8,128)(2,1)} %get-tuple-element.96), channel_id=1, source_target_pairs={{0,1},{1,0},{2,3},{3,2},{4,5},{5,4},{6,7},{7,6},{8,9},{9,8},{10,11... | collective-permute-start | bytes 4718600 | tf_op jit(solution)/shard_map/ppermute | solution.py:173
  207.4 23.9 %collective-permute-start.27 = (bf16[6,64,2048]{2,1,0:T(8,128)(2,1)}, bf16[6,64,2048]{2,1,0:T(8,128)(2,1)}, u32[]{:S(2)}, u32[]{:S(2)}) collective-permute-start(bf16[6,64,2048]{2,1,0:T(8,128)(2,1)} %add_convert_fusion), channel_id=1, source_target_pairs={{0,4},{1,3},{2,6},{3,1},{4,0},{5,7},{6,2},{7,5},{8,12},{9,11},{10,... | collective-permute-start | bytes 4718600 | tf_op jit(solution)/shard_map/ppermute | solution.py:173
  234.1 15.0 %collective-permute-start.35 = (bf16[3,64,2048]{2,1,0:T(8,128)(2,1)}, bf16[3,64,2048]{2,1,0:T(8,128)(2,1)}, u32[]{:S(2)}, u32[]{:S(2)}) collective-permute-start(bf16[3,64,2048]{2,1,0:T(8,128)(2,1)} %add_convert_fusion.4), channel_id=1, source_target_pairs={{0,2},{1,5},{2,0},{3,7},{4,6},{5,1},{6,4},{7,3},{8,10},{9,13},{10,... | collective-permute-start | bytes 2359304 | tf_op jit(solution)/shard_map/ppermute | solution.py:173
  235.5 13.6 %collective-permute-start.38 = (bf16[64,2048]{1,0:T(8,128)(2,1)S(1)}, bf16[64,2048]{1,0:T(8,128)(2,1)}, u32[]{:S(2)}, u32[]{:S(2)}) collective-permute-start(bf16[64,2048]{1,0:T(8,128)(2,1)S(1)} %get-tuple-element.111), channel_id=1, source_target_pairs={{0,24},{1,25},{2,26},{3,27},{4,28},{5,29},{6,30},{7,31},{8,0},{9,1... | collective-permute-start | bytes 786440 | tf_op jit(solution)/shard_map/ppermute | solution.py:173
  255.6 15.0 %collective-permute-start.39 = (bf16[4,64,2048]{2,1,0:T(8,128)(2,1)S(1)}, bf16[4,64,2048]{2,1,0:T(8,128)(2,1)}, u32[]{:S(2)}, u32[]{:S(2)}) collective-permute-start(bf16[4,64,2048]{2,1,0:T(8,128)(2,1)S(1)} %add_convert_fusion.2), channel_id=1, source_target_pairs={{0,4},{1,3},{2,6},{3,1},{4,0},{5,7},{6,2},{7,5},{8,12},{9,11},{10,... | collective-permute-start | bytes 3145736 | tf_op jit(solution)/shard_map/ppermute | solution.py:173
  260.3 22.6 %collective-permute-start.41 = (bf16[64,2048]{1,0:T(8,128)(2,1)}, bf16[64,2048]{1,0:T(8,128)(2,1)S(1)}, u32[]{:S(2)}, u32[]{:S(2)}) collective-permute-start(bf16[64,2048]{1,0:T(8,128)(2,1)} %get-tuple-element.108), channel_id=1, source_target_pairs={{0,8},{1,9},{2,10},{3,11},{4,12},{5,13},{6,14},{7,15},{8,16},{9,17... | collective-permute-start | bytes 786440 | tf_op jit(solution)/shard_map/ppermute | solution.py:173
  261.5 21.5 %collective-permute-start.42 = (bf16[64,2048]{1,0:T(8,128)(2,1)}, bf16[64,2048]{1,0:T(8,128)(2,1)}, u32[]{:S(2)}, u32[]{:S(2)}) collective-permute-start(bf16[64,2048]{1,0:T(8,128)(2,1)} %get-tuple-element.110), channel_id=1, source_target_pairs={{0,16},{1,17},{2,18},{3,19},{4,20},{5,21},{6,22},{7,23},{8,24},{9,... | collective-permute-start | bytes 786440 | tf_op jit(solution)/shard_map/ppermute | solution.py:173
  (81 other events, 700.7 us)

commit v6 on v5

--- a/solution.py
+++ b/solution.py
@@ -9,8 +9,7 @@
 
 TOP = 8
 EXP_DEV = 2
-SMALL_VMEM = 24 * 1024 * 1024
-LARGE_VMEM = 48 * 1024 * 1024
+VMEM_LIMIT = 63 * 1024 * 1024
 LITTLE = pl.CostEstimate(flops=1000000, bytes_accessed=100000, transcendentals=0)
 
 
@@ -286,7 +285,7 @@
         out_specs=[group_spec(count, first_group, *out.shape[1:]) for out in out_shapes],
         out_shape=out_shapes,
         input_output_aliases={5 + len(extras) + n: n for n in range(len(held))},
-        compiler_params=pltpu.CompilerParams(vmem_limit_bytes=SMALL_VMEM),
+        compiler_params=pltpu.CompilerParams(vmem_limit_bytes=VMEM_LIMIT),
         cost_estimate=LITTLE,
     )(pick, *pieces, *extras, *held)
 
@@ -347,61 +346,48 @@
         out_specs=[pl.BlockSpec((blocks, half, features), lambda i: (i, 0, 0))]
         + [pl.BlockSpec((blocks, half, features), lambda i: (i // 2, 0, 0))] * 2,
         out_shape=[jax.ShapeDtypeStruct((4 * blocks, half, features), jnp.bfloat16), piece, piece],
-        compiler_params=pltpu.CompilerParams(vmem_limit_bytes=SMALL_VMEM),
+        compiler_params=pltpu.CompilerParams(vmem_limit_bytes=VMEM_LIMIT),
         cost_estimate=LITTLE,
     )(back, prob, *slots)
 
 
-def forward_kernel(units, rows_ref, gate_ref, up_ref, down_ref, gate_pre_ref, up_pre_ref, hidden_ref, out_ref):
-    step = pl.program_id(0)
-    block = gate_pre_ref.shape[1]
-
-    @pl.when(step < units)
-    def _():
-        gate_pre = jnp.dot(rows_ref[...], gate_ref[0], preferred_element_type=jnp.float32)
-        up_pre = jnp.dot(rows_ref[...], up_ref[0], preferred_element_type=jnp.float32)
-        gate_pre_ref[...] = gate_pre
-        up_pre_ref[...] = up_pre
-        columns = pl.ds(pl.multiple_of(step * block, block), block)
-        hidden_ref[:, columns] = (gate_pre * jax.nn.sigmoid(gate_pre) * up_pre).astype(jnp.bfloat16)
-
-    @pl.when(step >= units)
-    def _():
-        out_ref[...] = jnp.dot(
-            hidden_ref[...], down_ref[0], preferred_element_type=jnp.float32
-        ).astype(jnp.bfloat16)
+def forward_kernel(rows_ref, gate_up_ref, down_ref, gate_pre_ref, up_pre_ref, hidden_ref, out_ref):
+    projected = jnp.dot(rows_ref[...], gate_up_ref[0], preferred_element_type=jnp.float32)
+    half_width = hidden_ref.shape[1]
+    gate_pre, up_pre = projected[:, :half_width], projected[:, half_width:]
+    gate_pre_ref[...] = gate_pre
+    up_pre_ref[...] = up_pre
+    hidden = (gate_pre * jax.nn.sigmoid(gate_pre) * up_pre).astype(jnp.bfloat16)
+    hidden_ref[...] = hidden
+    out_ref[...] = jnp.dot(hidden, down_ref[0], preferred_element_type=jnp.float32).astype(jnp.bfloat16)
 
 
 def forward(rows, gate_up_weight, down_weight):
     slots, features = rows.shape
     width = down_weight.shape[1]
-    block, units, wide = 256, width // 256, features // 2
-    early = lambda i: jnp.minimum(i, units - 1)
-    late = lambda i: jnp.maximum(i - units, 0)
+    block = slots // 2
+
+    def row_spec(columns):
+        return pl.BlockSpec((block, columns), lambda i: (i, 0))
+
     return pl.pallas_call(
-        functools.partial(forward_kernel, units),
-        grid=(units + 2,),
+        forward_kernel,
+        grid=(2,),
         in_specs=[
-            pl.BlockSpec((slots, features), lambda i: (0, 0)),
-            pl.BlockSpec((1, features, block), lambda i: (0, 0, early(i))),
-            pl.BlockSpec((1, features, block), lambda i: (0, 0, units + early(i))),
-            pl.BlockSpec((1, width, wide), lambda i: (0, 0, late(i))),
+            row_spec(features),
+            pl.BlockSpec((1, features, 2 * width), lambda i: (0, 0, 0)),
+            pl.BlockSpec((1, width, features), lambda i: (0, 0, 0)),
         ],
-        out_specs=[
-            pl.BlockSpec((slots, block), lambda i: (0, early(i))),
-            pl.BlockSpec((slots, block), lambda i: (0, early(i))),
-            pl.BlockSpec((slots, width), lambda i: (0, 0)),
-            pl.BlockSpec((slots, wide), lambda i: (0, late(i))),
-        ],
+        out_specs=[row_spec(width), row_spec(width), row_spec(width), row_spec(features)],
         out_shape=[
             jax.ShapeDtypeStruct((slots, width), jnp.float32),
             jax.ShapeDtypeStruct((slots, width), jnp.float32),
             jax.ShapeDtypeStruct((slots, width), jnp.bfloat16),
             jax.ShapeDtypeStruct((slots, features), jnp.bfloat16),
         ],
-        compiler_params=pltpu.CompilerParams(vmem_limit_bytes=LARGE_VMEM),
+        compiler_params=pltpu.CompilerParams(vmem_limit_bytes=VMEM_LIMIT),
         cost_estimate=LITTLE,
-    )(rows, gate_up_weight, gate_up_weight, down_weight)
+    )(rows, gate_up_weight, down_weight)
 
 
 def backward_kernel(
@@ -455,7 +441,7 @@
             jax.ShapeDtypeStruct((slots, features), jnp.bfloat16),
             jax.ShapeDtypeStruct((1, features), jnp.float32),
         ],
-        compiler_params=pltpu.CompilerParams(vmem_limit_bytes=LARGE_VMEM),
+        compiler_params=pltpu.CompilerParams(vmem_limit_bytes=VMEM_LIMIT),
         cost_estimate=LITTLE,
     )(grads, gate_pre, up_pre, down_weight, gate_up_weight, rows)
 
@@ -492,23 +478,13 @@
     tables = plane_tables(
         after(jnp.concatenate([expert_ids.T.astype(jnp.float32), gate_probs.T]), near_pair)
     )
-    token_far = jnp.stack([send_along(tokens, -step) for step in range(1, steps)])
+    token_far = after(jnp.stack([send_along(tokens, -step) for step in range(1, steps)]), tables)
     late_tables = after(tables, token_far)
     far_tables = [send_along(late_tables, -step) for step in range(1, steps)]
     late_cot = after(cotangent, token_far)
     cot_steps = [send_along(late_cot, -step) for step in range(1, steps)]
     token_second = after(send_second(token_far), near_far_pair, cot_steps[0], *far_tables)
     token_pair = jnp.concatenate([token_far, token_second])
-    token_far_pair = after(send_first(token_pair), *cot_steps)
-    near_pieces = (near_pair, near_far_pair, send_core(near_pair), send_core(near_far_pair))
-    cot_far = after(jnp.stack(cot_steps), token_far_pair)
-    cot_second = send_second(cot_far)
-    token_pieces = (
-        token_pair, token_far_pair, send_core(token_pair), after(send_core(token_far_pair), cot_second)
-    )
-    cot_pair = jnp.concatenate([cot_far, cot_second])
-    cot_far_pair = send_first(cot_pair)
-
     tables = far_first(jnp.stack([tables] + far_tables, axis=2))
     tables = jnp.where(core == 0, tables, jnp.roll(tables, half, axis=2))
     matches = tables[:, :TOP] == my_expert.astype(jnp.float32)
@@ -525,8 +501,18 @@
     slot_prob = jnp.sum(jnp.where(placed, weight_of[:, None, :], 0.0), axis=2, keepdims=True)
 
     gain_row = gain[None, :]
-    rows = select_normed(pick, gain_row, near_pieces, 1, 2, far, ())
-    rows, = select_normed(pick, gain_row, token_pieces, steps - 1, 1, 0, tuple(rows))
+    near_pieces = (near_pair, near_far_pair, send_core(near_pair), send_core(near_far_pair))
+    rows, = select_normed(pick, gain_row, near_pieces, 1, 2, far, ())
+    token_far_pair, rows = together(send_first(token_pair), rows, *cot_steps)[:2]
+    cot_far = after(jnp.stack(cot_steps), token_far_pair)
+    cot_second = send_second(cot_far)
+    token_pieces = (
+        token_pair, token_far_pair, send_core(token_pair), after(send_core(token_far_pair), cot_second)
+    )
+    cot_pair = jnp.concatenate([cot_far, cot_second])
+    cot_far_pair = send_first(cot_pair)
+
+    rows, = select_normed(pick, gain_row, token_pieces, steps - 1, 1, 0, (rows,))
     rows = rows.reshape(-1, features)
     gate_pre, up_pre, hidden, block_out = forward(rows, gate_up_weight, down_weight)
     block_out, cot_far_pair = together(block_out, cot_far_pair)

time: 288 us -> 257 us (0.89)
  local copies, waits for them, and re-layouts: 34.4 us -> 10.4 us
  waiting for transfers between devices: 95 us -> 77 us
  Pallas kernels: 58.5 us -> 71.8 us
  other arithmetic: 39 us -> 34.1 us
    unnamed x117 -> x46, local copies, waits for them, and re-layouts: 28.2 us -> 3.87 us
    ppermute x47, waiting for transfers between devices: 95 us -> 77 us  [send(): return lax.ppermute(array, BOTH, pairs)]
    pallas_call x3, Pallas kernels: 14 us -> 21 us  [expand(): pl.pallas_call(functools.partial(expand_kernel, weighted, count), grid=(4...]
    pallas_call x4, Pallas kernels: 16.4 us -> 21.5 us  [select(): pl.pallas_call(functools.partial(kernel, count), grid=(4,), in_specs=[gro...]
  transfers between devices with their start and end apart: 47 -> 47, of which waited for: 20 -> 17; matrix products, arithmetic and copies ran while one was open for 17% -> 19% of each run, Pallas kernels for 18% -> 25%
where the time goes in v6:
time: 257 us; the launch traced here: 256 us
  waiting for transfers between devices  77 us (30%)
  Pallas kernels  71.8 us (28%)
  starting transfers between devices  50 us (19%)
  other arithmetic  34.1 us (13%)
  matrix products  11.2 us (4%)
  local copies, waits for them, and re-layouts  10.4 us (4%)
    ppermute x47, waiting for transfers between devices, send(): return lax.ppermute(array, BOTH, pairs)  77 us
    ppermute x47, starting transfers between devices, send(): return lax.ppermute(array, BOTH, pairs)  50 us
    pallas_call x4, Pallas kernels, select(): pl.pallas_call(functools.partial(kernel, count), grid=(4,), in_specs=[gro...  21.5 us
    pallas_call x3, Pallas kernels, expand(): pl.pallas_call(functools.partial(expand_kernel, weighted, count), grid=(4...  21 us
    convert_element_type x8, other arithmetic, narrow(): return value.astype(jnp.bfloat16)  20.6 us
    pallas_call x1, Pallas kernels, backward(): pl.pallas_call(functools.partial(backward_kernel, units), grid=(units + 4...  16.3 us
    pallas_call x1, Pallas kernels, forward(): pl.pallas_call(forward_kernel, grid=(2,), in_specs=[row_spec(features), p...  13 us
    dot_general x2, matrix products, outer_sum(): lax.dot_general(left, right, (((0,), (0,)), ((), ())), preferred_element_...  11.1 us
  transfers between devices with their start and end apart: 47, of which 17 were waited for; matrix products, arithmetic and copies ran while one was open for 19% of the time, Pallas kernels for 25%

profile of v6, /device:TPU:0, one launch (start us, length us, event | category | flops | bytes accessed | tf_op | source)
XLA Modules:
  0.0 255.6 jit_solution(15507184039798315190)
XLA Ops:
  1.7 3.0 %collective-permute-start = (bf16[2,64,2048]{2,1,0:T(8,128)(2,1)S(1)}, bf16[2,64,2048]{2,1,0:T(8,128)(2,1)S(1)}, u32[]{:S(2)}, u32[]{:S(2)}) collective-permute-start(bf16[2,64,2048]{2,1,0:T(8,128)(2,1)S(1)} %pad_maximum_fusion.3), channel_id=1, source_target_pairs={{0,2},{1,5},{2,0},{3,7},{4,6},{5,1},{6,4},{7,3},{8,10},{9,13},{10,... | collective-permute-start | bytes 1572872 | tf_op jit(solution)/shard_map/ppermute | solution.py:172
  19.6 11.8 %collective-permute-done.4 = bf16[64,2048]{1,0:T(8,128)(2,1)S(1)} collective-permute-done((bf16[64,2048]{1,0:T(8,128)(2,1)}, bf16[64,2048]{1,0:T(8,128)(2,1)S(1)}, u32[]{:S(2)}, u32[]{:S(2)}) %collective-permute-start.4) | collective-permute-done | bytes 262176 | tf_op jit(solution)/shard_map/ppermute | solution.py:172
  38.4 5.0 %collective-permute-done.7 = f32[2,2,16,128]{3,2,1,0:T(8,128)S(1)} collective-permute-done((f32[2,2,16,128]{3,2,1,0:T(8,128)S(1)}, f32[2,2,16,128]{3,2,1,0:T(8,128)S(1)}, u32[]{:S(2)}, u32[]{:S(2)}) %collective-permute-start.7) | collective-permute-done | bytes 32800 | tf_op jit(solution)/shard_map/ppermute | solution.py:172
  50.4 16.5 %collective-permute-done.15 = bf16[64,2048]{1,0:T(8,128)(2,1)} collective-permute-done((bf16[64,2048]{1,0:T(8,128)(2,1)S(1)}, bf16[64,2048]{1,0:T(8,128)(2,1)}, u32[]{:S(2)}, u32[]{:S(2)}) %collective-permute-start.15) | collective-permute-done | bytes 262176 | tf_op jit(solution)/shard_map/ppermute | solution.py:172
  70.0 4.4 %shard_map.118.refs_5_ = bf16[16,48,2048]{2,1,0:T(8,128)(2,1)} custom-call(bf16[16,48,128]{2,1,0:T(8,128)(2,1)} %fusion.15.pick_ref, bf16[4,64,2048]{2,1,0:T(8,128)(2,1)} %copy-done.2, bf16[4,64,2048]{2,1,0:T(8,128)(2,1)} %copy-done.4, bf16[4,64,2048]{2,1,0:T(8,128)(2,1)} %copy-done.5, bf16[4,64,2048]{2,1,0:T(8,128)(2,1)} %collective-permute-done.14.refs_3_, ...), custom_call_target="tpu_custom_call" | custom-call | flops 1000000 | bytes 100000 | tf_op jit(solution)/shard_map/pallas_call | solution.py:275
  77.3 9.1 %collective-permute-done.19 = bf16[3,64,2048]{2,1,0:T(8,128)(2,1)S(1)} collective-permute-done((bf16[3,64,2048]{2,1,0:T(8,128)(2,1)S(1)}, bf16[3,64,2048]{2,1,0:T(8,128)(2,1)S(1)}, u32[]{:S(2)}, u32[]{:S(2)}) %collective-permute-start.19) | collective-permute-done | bytes 786464 | tf_op jit(solution)/shard_map/ppermute | solution.py:172
  90.2 6.0 %shard_map.119 = bf16[16,48,2048]{2,1,0:T(8,128)(2,1)} custom-call(bf16[16,48,128]{2,1,0:T(8,128)(2,1)} %fusion.15.pick_ref, bf16[6,64,2048]{2,1,0:T(8,128)(2,1)} %constant_dynamic-update-slice_fusion.refs_0_, bf16[6,64,2048]{2,1,0:T(8,128)(2,1)} %collective-permute-done.12.refs_1_, ...), custom_call_target="tpu_custom_call", output_to_operand_aliasing={{}: (6, {})} | custom-call | flops 1000000 | bytes 100000 | tf_op jit(solution)/shard_map/pallas_call | solution.py:275
  96.2 13.0 %shard_map.120 = (f32[768,768]{1,0:T(8,128)}, f32[768,768]{1,0:T(8,128)}, bf16[768,768]{1,0:T(8,128)(2,1)}, bf16[768,2048]{1,0:T(8,128)(2,1)}) custom-call(bf16[768,2048]{1,0:T(8,128)(2,1)} %bitcast.114, bf16[1,2048,1536]{2,1,0:T(8,128)(2,1)} %gate_up_ref.3, bf16[1,768,2048]{2,1,0:T(8,128)(2,1)} %down_ref.3), custom_call_target="tpu_custom_call" | custom-call | flops 1000000 | bytes 100000 | tf_op jit(solution)/shard_map/pallas_call | solution.py:373
  109.2 7.8 %shard_map.121 = (bf16[12,64,2048]{2,1,0:T(8,128)(2,1)}, bf16[6,64,2048]{2,1,0:T(8,128)(2,1)}, bf16[6,64,2048]{2,1,0:T(8,128)(2,1)}) custom-call(bf16[16,128,48]{2,1,0:T(8,128)(2,1)} %fusion.1.back_ref, f32[16,48,1]{2,1,0:T(8,128)} %copy.22.prob_ref.refs_4_, bf16[16,48,2048]{2,1,0:T(8,128)(2,1)} %bitcast.117), custom_call_target="tpu_custom_call" | custom-call | flops 1000000 | bytes 100000 | tf_op jit(solution)/shard_map/pallas_call | solution.py:339
  117.7 4.5 %collective-permute-done.21 = bf16[6,64,2048]{2,1,0:T(8,128)(2,1)S(1)} collective-permute-done((bf16[6,64,2048]{2,1,0:T(8,128)(2,1)}, bf16[6,64,2048]{2,1,0:T(8,128)(2,1)S(1)}, u32[]{:S(2)}, u32[]{:S(2)}) %collective-permute-start.21) | collective-permute-done | bytes 1572896 | tf_op jit(solution)/shard_map/ppermute | solution.py:172
  122.1 3.2 %add_convert_fusion.1 = bf16[6,64,2048]{2,1,0:T(8,128)(2,1)} fusion(bf16[6,64,2048]{2,1,0:T(8,128)(2,1)S(1)} %collective-permute-done.21, bf16[12,64,2048]{2,1,0:T(8,128)(2,1)} %get-tuple-element.68), kind=kLoop, calls=%fused_computation.4 | loop fusion | flops 3145728 | bytes 4718592 | tf_op jit(solution)/shard_map/convert_element_type | solution.py:209
  128.1 4.5 %shard_map.122 = (bf16[16,48,2048]{2,1,0:T(8,128)(2,1)}, f32[16,48,1]{2,1,0:T(8,128)}) custom-call(bf16[16,48,128]{2,1,0:T(8,128)(2,1)} %fusion.15.pick_ref, bf16[4,64,2048]{2,1,0:T(8,128)(2,1)} %copy-done.2, bf16[4,64,2048]{2,1,0:T(8,128)(2,1)} %copy-done.4, bf16[4,64,2048]{2,1,0:T(8,128)(2,1)} %copy-done.5, ...), custom_call_target="tpu_custom_call" | custom-call | flops 1000000 | bytes 100000 | tf_op jit(solution)/shard_map/pallas_call | solution.py:275
  132.7 6.6 %shard_map.123 = (bf16[16,48,2048]{2,1,0:T(8,128)(2,1)}, f32[16,48,1]{2,1,0:T(8,128)}) custom-call(bf16[16,48,128]{2,1,0:T(8,128)(2,1)} %fusion.15.pick_ref, bf16[6,64,2048]{2,1,0:T(8,128)(2,1)} %constant_dynamic-update-slice_fusion.2.refs_0_, bf16[6,64,2048]{2,1,0:T(8,128)(2,1)} %collective-permute-done.20.refs_1_, ...), custom_call_target="tpu_custom_call", output_to_operand_aliasing={{0}: (7, {}), {1}: (8, {})} | custom-call | flops 1000000 | bytes 100000 | tf_op jit(solution)/shard_map/pallas_call | solution.py:275
  139.3 16.3 %shard_map.124 = (bf16[768,1536]{1,0:T(8,128)(2,1)}, bf16[768,2048]{1,0:T(8,128)(2,1)}, f32[1,2048]{1,0:T(1,128)}) custom-call(bf16[768,2048]{1,0:T(8,128)(2,1)} %bitcast.123, f32[768,768]{1,0:T(8,128)} %get-tuple-element.76.gate_pre_ref, f32[768,768]{1,0:T(8,128)} %get-tuple-element.77.up_pre_ref, bf16[1,768,2048]{2,1,0:T(8,128)(2,1)} %down_ref.3, ...), custom_call_target="tpu_custom_call" | custom-call | flops 1000000 | bytes 100000 | tf_op jit(solution)/shard_map/pallas_call | solution.py:423
  155.6 7.2 %shard_map.125 = (bf16[12,64,2048]{2,1,0:T(8,128)(2,1)}, bf16[6,64,2048]{2,1,0:T(8,128)(2,1)}, bf16[6,64,2048]{2,1,0:T(8,128)(2,1)}) custom-call(bf16[16,128,48]{2,1,0:T(8,128)(2,1)} %fusion.1.back_ref, f32[16,48,1]{2,1,0:T(8,128)} %copy.22.prob_ref.refs_4_, bf16[16,48,2048]{2,1,0:T(8,128)(2,1)} %bitcast.121), custom_call_target="tpu_custom_call" | custom-call | flops 1000000 | bytes 100000 | tf_op jit(solution)/shard_map/pallas_call | solution.py:339
  164.9 2.9 %add_convert_fusion.6 = bf16[3,64,2048]{2,1,0:T(8,128)(2,1)} fusion(bf16[6,64,2048]{2,1,0:T(8,128)(2,1)} %collective-permute-done.26, bf16[6,64,2048]{2,1,0:T(8,128)(2,1)} %collective-permute-done.24, bf16[12,64,2048]{2,1,0:T(8,128)(2,1)} %get-tuple-element.68), kind=kLoop, calls=%fused_computation.9 | loop fusion | flops 2359296 | bytes 3145728 | tf_op jit(solution)/shard_map/convert_element_type | solution.py:209
  169.1 6.0 %shard_map.126 = (bf16[8,64,2048]{2,1,0:T(8,128)(2,1)}, bf16[4,64,2048]{2,1,0:T(8,128)(2,1)}, bf16[4,64,2048]{2,1,0:T(8,128)(2,1)}) custom-call(bf16[16,128,48]{2,1,0:T(8,128)(2,1)} %fusion.1.back_ref, f32[16,48,1]{2,1,0:T(8,128)} %copy.23.prob_ref, bf16[16,48,2048]{2,1,0:T(8,128)(2,1)} %bitcast.120, bf16[16,48,2048]{2,1,0:T(8,128)(2,1)} %bitcast.122), custom_call_target="tpu_custom_call" | custom-call | flops 1000000 | bytes 100000 | tf_op jit(solution)/shard_map/pallas_call | solution.py:339
  178.8 4.0 %convolution_convert_fusion.1 = bf16[768,2048]{1,0:T(8,128)(2,1)} fusion(bf16[768,768]{1,0:T(8,128)(2,1)S(1)} %copy-done.21, bf16[768,2048]{1,0:T(8,128)(2,1)S(1)} %bitcast.124), kind=kOutput, calls=%fused_computation.2 | convolution fusion | flops 2417491968 | bytes 7471104 | tf_op jit(solution)/shard_map/dot_general | solution.py:38
  188.6 7.1 %convolution_convert_fusion = bf16[2048,1536]{1,0:T(8,128)(2,1)} fusion(bf16[768,2048]{1,0:T(8,128)(2,1)S(1)} %bitcast.116, bf16[768,1536]{1,0:T(8,128)(2,1)S(1)} %copy-done.20), kind=kOutput, calls=%fused_computation.1 | convolution fusion | flops 4834983936 | bytes 11796480 | tf_op jit(solution)/shard_map/dot_general | solution.py:38
  195.7 3.6 %collective-permute-done.31 = f32[48,128]{1,0:T(8,128)S(1)} collective-permute-done((f32[48,128]{1,0:T(8,128)S(1)}, f32[48,128]{1,0:T(8,128)S(1)}, u32[]{:S(2)}, u32[]{:S(2)}) %collective-permute-start.31) | collective-permute-done | bytes 24608 | tf_op jit(solution)/shard_map/ppermute | solution.py:172
  203.8 3.8 %collective-permute-start.38 = (bf16[64,2048]{1,0:T(8,128)(2,1)S(1)}, bf16[64,2048]{1,0:T(8,128)(2,1)S(1)}, u32[]{:S(2)}, u32[]{:S(2)}) collective-permute-start(bf16[64,2048]{1,0:T(8,128)(2,1)S(1)} %get-tuple-element.115), channel_id=1, source_target_pairs={{0,24},{1,25},{2,26},{3,27},{4,28},{5,29},{6,30},{7,31},{8,0},{9,1... | collective-permute-start | bytes 786440 | tf_op jit(solution)/shard_map/ppermute | solution.py:172
  209.3 5.5 %collective-permute-done.37 = bf16[64,2048]{1,0:T(8,128)(2,1)S(1)} collective-permute-done((bf16[64,2048]{1,0:T(8,128)(2,1)S(1)}, bf16[64,2048]{1,0:T(8,128)(2,1)S(1)}, u32[]{:S(2)}, u32[]{:S(2)}) %collective-permute-start.37) | collective-permute-done | bytes 262176 | tf_op jit(solution)/shard_map/ppermute | solution.py:172
  232.0 6.5 %collective-permute-done.45 = f32[20,128]{1,0:T(8,128)S(1)} collective-permute-done((f32[20,128]{1,0:T(8,128)S(1)}, f32[20,128]{1,0:T(8,128)S(1)}, u32[]{:S(2)}, u32[]{:S(2)}) %collective-permute-start.45) | collective-permute-done | bytes 10272 | tf_op jit(solution)/shard_map/ppermute | solution.py:172
  244.7 6.7 %collective-permute-done.40 = bf16[2,64,2048]{2,1,0:T(8,128)(2,1)} collective-permute-done((bf16[2,64,2048]{2,1,0:T(8,128)(2,1)}, bf16[2,64,2048]{2,1,0:T(8,128)(2,1)}, u32[]{:S(2)}, u32[]{:S(2)}) %collective-permute-start.40) | collective-permute-done | bytes 524320 | tf_op jit(solution)/shard_map/ppermute | solution.py:172
  (214 shorter events, 89.6 us)
Async XLA Ops:
  4.7 14.2 %collective-permute-start.5 = (bf16[64,2048]{1,0:T(8,128)(2,1)}, bf16[64,2048]{1,0:T(8,128)(2,1)S(1)}, u32[]{:S(2)}, u32[]{:S(2)}) collective-permute-start(bf16[64,2048]{1,0:T(8,128)(2,1)} %param.7), channel_id=1, source_target_pairs={{0,8},{1,9},{2,10},{3,11},{4,12},{5,13},{6,14},{7,15},{8,16},{9,17... | collective-permute-start | bytes 786440 | tf_op jit(solution)/shard_map/ppermute | solution.py:172
  8.5 22.9 %collective-permute-start.4 = (bf16[64,2048]{1,0:T(8,128)(2,1)}, bf16[64,2048]{1,0:T(8,128)(2,1)S(1)}, u32[]{:S(2)}, u32[]{:S(2)}) collective-permute-start(bf16[64,2048]{1,0:T(8,128)(2,1)} %param.7), channel_id=1, source_target_pairs={{0,16},{1,17},{2,18},{3,19},{4,20},{5,21},{6,22},{7,23},{8,24},{9,... | collective-permute-start | bytes 786440 | tf_op jit(solution)/shard_map/ppermute | solution.py:172
  15.1 28.5 %collective-permute-start.10 = (bf16[4,64,2048]{2,1,0:T(8,128)(2,1)S(1)}, bf16[4,64,2048]{2,1,0:T(8,128)(2,1)S(1)}, u32[]{:S(2)}, u32[]{:S(2)}) collective-permute-start(bf16[4,64,2048]{2,1,0:T(8,128)(2,1)S(1)} %pad_maximum_fusion.refs_0_), channel_id=1, source_target_pairs={{0,4},{1,3},{2,6},{3,1},{4,0},{5,7},{6,2},{7,5},{8,12},{9,11},{10,... | collective-permute-start | bytes 3145736 | tf_op jit(solution)/shard_map/ppermute | solution.py:172
  16.8 14.7 %collective-permute-start.2 = (f32[2,16,128]{2,1,0:T(8,128)S(1)}, f32[2,16,128]{2,1,0:T(8,128)S(1)}, u32[]{:S(2)}, u32[]{:S(2)}) collective-permute-start(f32[2,16,128]{2,1,0:T(8,128)S(1)} %get-tuple-element.126), channel_id=1, source_target_pairs={{0,4},{1,3},{2,6},{3,1},{4,0},{5,7},{6,2},{7,5},{8,12},{9,11},{10,... | collective-permute-start | bytes 49160 | tf_op jit(solution)/shard_map/ppermute | solution.py:172
  44.6 29.8 %collective-permute-start.12 = (bf16[6,64,2048]{2,1,0:T(8,128)(2,1)}, bf16[6,64,2048]{2,1,0:T(8,128)(2,1)}, u32[]{:S(2)}, u32[]{:S(2)}) collective-permute-start(bf16[6,64,2048]{2,1,0:T(8,128)(2,1)} %constant_dynamic-update-slice_fusion.refs_0_), channel_id=1, source_target_pairs={{0,4},{1,3},{2,6},{3,1},{4,0},{5,7},{6,2},{7,5},{8,12},{9,11},{10,... | collective-permute-start | bytes 4718600 | tf_op jit(solution)/shard_map/ppermute | solution.py:172
  46.0 23.1 %collective-permute-start.13 = (bf16[4,64,2048]{2,1,0:T(8,128)(2,1)S(1)}, bf16[4,64,2048]{2,1,0:T(8,128)(2,1)S(1)}, u32[]{:S(2)}, u32[]{:S(2)}) collective-permute-start(bf16[4,64,2048]{2,1,0:T(8,128)(2,1)S(1)} %pad_maximum_fusion.refs_0_), channel_id=1, source_target_pairs={{0,1},{1,0},{2,3},{3,2},{4,5},{5,4},{6,7},{7,6},{8,9},{9,8},{10,11... | collective-permute-start | bytes 3145736 | tf_op jit(solution)/shard_map/ppermute | solution.py:172
  46.0 21.0 %collective-permute-start.15 = (bf16[64,2048]{1,0:T(8,128)(2,1)S(1)}, bf16[64,2048]{1,0:T(8,128)(2,1)}, u32[]{:S(2)}, u32[]{:S(2)}) collective-permute-start(bf16[64,2048]{1,0:T(8,128)(2,1)S(1)} %copy-done.7), channel_id=1, source_target_pairs={{0,16},{1,17},{2,18},{3,19},{4,20},{5,21},{6,22},{7,23},{8,24},{9,... | collective-permute-start | bytes 786440 | tf_op jit(solution)/shard_map/ppermute | solution.py:172
  47.3 19.6 %collective-permute-start.16 = (bf16[64,2048]{1,0:T(8,128)(2,1)S(1)}, bf16[64,2048]{1,0:T(8,128)(2,1)}, u32[]{:S(2)}, u32[]{:S(2)}) collective-permute-start(bf16[64,2048]{1,0:T(8,128)(2,1)S(1)} %copy-done.7), channel_id=1, source_target_pairs={{0,8},{1,9},{2,10},{3,11},{4,12},{5,13},{6,14},{7,15},{8,16},{9,17... | collective-permute-start | bytes 786440 | tf_op jit(solution)/shard_map/ppermute | solution.py:172
  49.2 19.8 %collective-permute-start.14 = (bf16[4,64,2048]{2,1,0:T(8,128)(2,1)S(1)}, bf16[4,64,2048]{2,1,0:T(8,128)(2,1)}, u32[]{:S(2)}, u32[]{:S(2)}) collective-permute-start(bf16[4,64,2048]{2,1,0:T(8,128)(2,1)S(1)} %collective-permute-done.10.refs_1_), channel_id=1, source_target_pairs={{0,1},{1,0},{2,3},{3,2},{4,5},{5,4},{6,7},{7,6},{8,9},{9,8},{10,11... | collective-permute-start | bytes 3145736 | tf_op jit(solution)/shard_map/ppermute | solution.py:172
  75.8 14.4 %collective-permute-start.17 = (bf16[6,64,2048]{2,1,0:T(8,128)(2,1)}, bf16[6,64,2048]{2,1,0:T(8,128)(2,1)}, u32[]{:S(2)}, u32[]{:S(2)}) collective-permute-start(bf16[6,64,2048]{2,1,0:T(8,128)(2,1)} %constant_dynamic-update-slice_fusion.refs_0_), channel_id=1, source_target_pairs={{0,1},{1,0},{2,3},{3,2},{4,5},{5,4},{6,7},{7,6},{8,9},{9,8},{10,11... | collective-permute-start | bytes 4718600 | tf_op jit(solution)/shard_map/ppermute | solution.py:172
  75.8 14.4 %collective-permute-start.18 = (bf16[6,64,2048]{2,1,0:T(8,128)(2,1)}, bf16[6,64,2048]{2,1,0:T(8,128)(2,1)}, u32[]{:S(2)}, u32[]{:S(2)}) collective-permute-start(bf16[6,64,2048]{2,1,0:T(8,128)(2,1)} %collective-permute-done.12.refs_1_), channel_id=1, source_target_pairs={{0,1},{1,0},{2,3},{3,2},{4,5},{5,4},{6,7},{7,6},{8,9},{9,8},{10,11... | collective-permute-start | bytes 4718600 | tf_op jit(solution)/shard_map/ppermute | solution.py:172
  87.5 21.7 %collective-permute-start.20 = (bf16[6,64,2048]{2,1,0:T(8,128)(2,1)}, bf16[6,64,2048]{2,1,0:T(8,128)(2,1)}, u32[]{:S(2)}, u32[]{:S(2)}) collective-permute-start(bf16[6,64,2048]{2,1,0:T(8,128)(2,1)} %constant_dynamic-update-slice_fusion.2.refs_0_), channel_id=1, source_target_pairs={{0,4},{1,3},{2,6},{3,1},{4,0},{5,7},{6,2},{7,5},{8,12},{9,11},{10,... | collective-permute-start | bytes 4718600 | tf_op jit(solution)/shard_map/ppermute | solution.py:172
  117.2 15.5 %collective-permute-start.22 = (bf16[6,64,2048]{2,1,0:T(8,128)(2,1)}, bf16[6,64,2048]{2,1,0:T(8,128)(2,1)}, u32[]{:S(2)}, u32[]{:S(2)}) collective-permute-start(bf16[6,64,2048]{2,1,0:T(8,128)(2,1)} %constant_dynamic-update-slice_fusion.2.refs_0_), channel_id=1, source_target_pairs={{0,1},{1,0},{2,3},{3,2},{4,5},{5,4},{6,7},{7,6},{8,9},{9,8},{10,11... | collective-permute-start | bytes 4718600 | tf_op jit(solution)/shard_map/ppermute | solution.py:172
  117.6 15.1 %collective-permute-start.23 = (bf16[6,64,2048]{2,1,0:T(8,128)(2,1)}, bf16[6,64,2048]{2,1,0:T(8,128)(2,1)}, u32[]{:S(2)}, u32[]{:S(2)}) collective-permute-start(bf16[6,64,2048]{2,1,0:T(8,128)(2,1)} %collective-permute-done.20.refs_1_), channel_id=1, source_target_pairs={{0,1},{1,0},{2,3},{3,2},{4,5},{5,4},{6,7},{7,6},{8,9},{9,8},{10,11... | collective-permute-start | bytes 4718600 | tf_op jit(solution)/shard_map/ppermute | solution.py:172
  125.3 30.2 %collective-permute-start.24 = (bf16[6,64,2048]{2,1,0:T(8,128)(2,1)}, bf16[6,64,2048]{2,1,0:T(8,128)(2,1)}, u32[]{:S(2)}, u32[]{:S(2)}) collective-permute-start(bf16[6,64,2048]{2,1,0:T(8,128)(2,1)} %add_convert_fusion.1), channel_id=1, source_target_pairs={{0,4},{1,3},{2,6},{3,1},{4,0},{5,7},{6,2},{7,5},{8,12},{9,11},{10,... | collective-permute-start | bytes 4718600 | tf_op jit(solution)/shard_map/ppermute | solution.py:172
  128.0 36.9 %collective-permute-start.26 = (bf16[6,64,2048]{2,1,0:T(8,128)(2,1)}, bf16[6,64,2048]{2,1,0:T(8,128)(2,1)}, u32[]{:S(2)}, u32[]{:S(2)}) collective-permute-start(bf16[6,64,2048]{2,1,0:T(8,128)(2,1)} %get-tuple-element.84), channel_id=1, source_target_pairs={{0,1},{1,0},{2,3},{3,2},{4,5},{5,4},{6,7},{7,6},{8,9},{9,8},{10,11... | collective-permute-start | bytes 4718600 | tf_op jit(solution)/shard_map/ppermute | solution.py:172
  167.8 15.0 %collective-permute-start.29 = (bf16[3,64,2048]{2,1,0:T(8,128)(2,1)}, bf16[3,64,2048]{2,1,0:T(8,128)(2,1)}, u32[]{:S(2)}, u32[]{:S(2)}) collective-permute-start(bf16[3,64,2048]{2,1,0:T(8,128)(2,1)} %add_convert_fusion.6), channel_id=1, source_target_pairs={{0,2},{1,5},{2,0},{3,7},{4,6},{5,1},{6,4},{7,3},{8,10},{9,13},{10,... | collective-permute-start | bytes 2359304 | tf_op jit(solution)/shard_map/ppermute | solution.py:172
  175.1 20.6 %collective-permute-start.28 = (bf16[4,64,2048]{2,1,0:T(8,128)(2,1)}, bf16[4,64,2048]{2,1,0:T(8,128)(2,1)}, u32[]{:S(2)}, u32[]{:S(2)}) collective-permute-start(bf16[4,64,2048]{2,1,0:T(8,128)(2,1)} %get-tuple-element.89), channel_id=1, source_target_pairs={{0,1},{1,0},{2,3},{3,2},{4,5},{5,4},{6,7},{7,6},{8,9},{9,8},{10,11... | collective-permute-start | bytes 3145736 | tf_op jit(solution)/shard_map/ppermute | solution.py:172
  175.1 25.9 %collective-permute-start.34 = (bf16[6,64,2048]{2,1,0:T(8,128)(2,1)}, bf16[6,64,2048]{2,1,0:T(8,128)(2,1)}, u32[]{:S(2)}, u32[]{:S(2)}) collective-permute-start(bf16[6,64,2048]{2,1,0:T(8,128)(2,1)} %get-tuple-element.100), channel_id=1, source_target_pairs={{0,1},{1,0},{2,3},{3,2},{4,5},{5,4},{6,7},{7,6},{8,9},{9,8},{10,11... | collective-permute-start | bytes 4718600 | tf_op jit(solution)/shard_map/ppermute | solution.py:172
  178.2 22.7 %collective-permute-start.27 = (bf16[6,64,2048]{2,1,0:T(8,128)(2,1)S(1)}, bf16[6,64,2048]{2,1,0:T(8,128)(2,1)}, u32[]{:S(2)}, u32[]{:S(2)}) collective-permute-start(bf16[6,64,2048]{2,1,0:T(8,128)(2,1)S(1)} %add_convert_fusion), channel_id=1, source_target_pairs={{0,4},{1,3},{2,6},{3,1},{4,0},{5,7},{6,2},{7,5},{8,12},{9,11},{10,... | collective-permute-start | bytes 4718600 | tf_op jit(solution)/shard_map/ppermute | solution.py:172
  224.6 15.1 %collective-permute-start.39 = (bf16[4,64,2048]{2,1,0:T(8,128)(2,1)}, bf16[4,64,2048]{2,1,0:T(8,128)(2,1)}, u32[]{:S(2)}, u32[]{:S(2)}) collective-permute-start(bf16[4,64,2048]{2,1,0:T(8,128)(2,1)} %add_convert_fusion.2), channel_id=1, source_target_pairs={{0,4},{1,3},{2,6},{3,1},{4,0},{5,7},{6,2},{7,5},{8,12},{9,11},{10,... | collective-permute-start | bytes 3145736 | tf_op jit(solution)/shard_map/ppermute | solution.py:172
  229.5 23.7 %collective-permute-start.41 = (bf16[64,2048]{1,0:T(8,128)(2,1)}, bf16[64,2048]{1,0:T(8,128)(2,1)S(1)}, u32[]{:S(2)}, u32[]{:S(2)}) collective-permute-start(bf16[64,2048]{1,0:T(8,128)(2,1)} %get-tuple-element.112), channel_id=1, source_target_pairs={{0,8},{1,9},{2,10},{3,11},{4,12},{5,13},{6,14},{7,15},{8,16},{9,17... | collective-permute-start | bytes 786440 | tf_op jit(solution)/shard_map/ppermute | solution.py:172
  230.7 22.5 %collective-permute-start.42 = (bf16[64,2048]{1,0:T(8,128)(2,1)}, bf16[64,2048]{1,0:T(8,128)(2,1)S(1)}, u32[]{:S(2)}, u32[]{:S(2)}) collective-permute-start(bf16[64,2048]{1,0:T(8,128)(2,1)} %get-tuple-element.114), channel_id=1, source_target_pairs={{0,16},{1,17},{2,18},{3,19},{4,20},{5,21},{6,22},{7,23},{8,24},{9,... | collective-permute-start | bytes 786440 | tf_op jit(solution)/shard_map/ppermute | solution.py:172
  238.5 14.7 %collective-permute-start.43 = (bf16[64,2048]{1,0:T(8,128)(2,1)}, bf16[64,2048]{1,0:T(8,128)(2,1)S(1)}, u32[]{:S(2)}, u32[]{:S(2)}) collective-permute-start(bf16[64,2048]{1,0:T(8,128)(2,1)} %get-tuple-element.113), channel_id=1, source_target_pairs={{0,24},{1,25},{2,26},{3,27},{4,28},{5,29},{6,30},{7,31},{8,0},{9,1... | collective-permute-start | bytes 786440 | tf_op jit(solution)/shard_map/ppermute | solution.py:172
  (45 other events, 390.2 us)

commit v7 on v6

--- a/solution.py
+++ b/solution.py
@@ -224,128 +224,129 @@
     return jnp.concatenate([array[4 * (steps - 1):].reshape((2, 2, 1) + array.shape[1:]), far], axis=2)
 
 
-def chosen_rows(pick, mine, other):
-    return jnp.dot(pick, jnp.concatenate([mine, other]), preferred_element_type=jnp.float32)
-
-
-def norm_kernel(count, pick_ref, *refs):
-    pieces, gain_ref, normed_ref = refs[:4], refs[4], refs[-1]
-
-    def work(mine_ref, other_ref):
-        for group in range(count):
-            rows = chosen_rows(pick_ref[group], mine_ref[group], other_ref[group])
+def start(source, target, semaphore):
+    copy = pltpu.make_async_copy(source, target, semaphore)
+    copy.start()
+    return copy
+
+
+def select_kernel(count, arrays, which, first_group, grads, pick_ref, scale_ref, *refs):
+    pieces, refs = refs[:4], refs[4:]
+    if grads:
+        out_slots, (_, grad_ref, value_ref, loaded, made, loads, stores, outs, out_loads) = refs[0], refs[-9:]
+    else:
+        grad_ref, loaded, made, loads, stores = refs[-5:]
+    half = pieces[0].shape[1]
+    copies, written = [], []
+    for group in range(4 * count):
+        place, inner = divmod(group, count)
+        first, second = divmod(place, 2)
+        mine = pieces[first].at[(second * count + inner) * arrays + which]
+        other = pieces[2 + second].at[(first * count + inner) * arrays + which]
+        both = [
+            start(mine, loaded.at[group, pl.ds(0, half)], loads.at[group, 0]),
+            start(other, loaded.at[group, pl.ds(half, half)], loads.at[group, 1]),
+        ]
+        if grads:
+            both.append(start(out_slots.at[first_group + group], outs.at[group], out_loads.at[group]))
+        copies.append(both)
+    for group in range(4 * count):
+        for copy in copies[group]:
+            copy.wait()
+        rows = jnp.dot(pick_ref[first_group + group], loaded[group], preferred_element_type=jnp.float32)
+        if grads:
+            made[group] = (rows * scale_ref[first_group + group]).astype(jnp.bfloat16)
+            value_ref[group] = jnp.sum(rows * outs[group].astype(jnp.float32), axis=1, keepdims=True)
+        else:
             inv_rms = lax.rsqrt(jnp.mean(rows * rows, axis=1, keepdims=True) + 1e-06)
-            normed_ref[group] = (rows * inv_rms * gain_ref[...]).astype(jnp.bfloat16)
-
-    by_place(work, pieces)
-
-
-def grad_kernel(count, pick_ref, *refs):
-    pieces, prob_ref, out_ref, (grad_ref, value_ref) = refs[:4], refs[4], refs[5], refs[-2:]
-
-    def work(mine_ref, other_ref):
-        for group in range(count):
-            rows = chosen_rows(pick_ref[group], mine_ref[group], other_ref[group])
-            grad_ref[group] = (rows * prob_ref[group]).astype(jnp.bfloat16)
-            value_ref[group] = jnp.sum(rows * out_ref[group].astype(jnp.float32), axis=1, keepdims=True)
-
-    by_place(work, pieces)
-
-
-def by_place(work, pieces):
-    for first in range(2):
-        for second in range(2):
-            pl.when(pl.program_id(0) == first * 2 + second)(
-                functools.partial(work, pieces[first], pieces[2 + second])
-            )
-
-
-def group_spec(count, first_group, *shape):
-    first_block = first_group // count
-    return pl.BlockSpec((count,) + shape, lambda i: (first_block + i, 0, 0))
-
-
-def select(kernel, pick, pieces, extras, extra_specs, out_shapes, count, arrays, which, first_group, held):
-    _, capacity, group_rows = pick.shape
-    half, features = pieces[0].shape[1:]
-
-    def piece_spec(place):
-        return pl.BlockSpec((count, half, features), lambda i: (place(i) * arrays + which, 0, 0))
-
+            made[group] = (rows * inv_rms * scale_ref[...]).astype(jnp.bfloat16)
+        written.append(start(made.at[group], grad_ref.at[first_group + group], stores.at[group]))
+    for copy in written:
+        copy.wait()
+
+
+def select(pick, scale, pieces, count, arrays, which, first_group, held=None, out_slots=None):
+    groups, capacity, group_rows = pick.shape
+    features = pieces[0].shape[2]
+    many, grads = 4 * count, out_slots is not None
+    anywhere, whole = pl.BlockSpec(memory_space=pl.ANY), pl.BlockSpec(memory_space=pltpu.VMEM)
+    operands = [pick, scale, *pieces] + ([out_slots] if grads else []) + ([] if held is None else [held])
+    out_shape = [jax.ShapeDtypeStruct((groups, capacity, features), jnp.bfloat16)]
+    scratch = [
+        pltpu.VMEM((many, group_rows, features), jnp.bfloat16),
+        pltpu.VMEM((many, capacity, features), jnp.bfloat16),
+        pltpu.SemaphoreType.DMA((many, 2)),
+        pltpu.SemaphoreType.DMA((many,)),
+    ]
+    if grads:
+        out_shape.append(jax.ShapeDtypeStruct((many, capacity, 1), jnp.float32))
+        scratch += [
+            pltpu.VMEM((many, capacity, features), jnp.bfloat16), pltpu.SemaphoreType.DMA((many,)),
+        ]
+    kernel = functools.partial(select_kernel, count, arrays, which, first_group, grads)
+    if grads and held is None:
+        inner = kernel
+        kernel = lambda *refs: inner(*refs[:7], None, *refs[7:])
     return pl.pallas_call(
-        functools.partial(kernel, count),
-        grid=(4,),
-        in_specs=[
-            group_spec(count, first_group, capacity, group_rows),
-            piece_spec(lambda i: jnp.minimum(i, 1)),
-            piece_spec(lambda i: jnp.maximum(i - 2, 0)),
-            piece_spec(lambda i: i // 2),
-            piece_spec(lambda i: jnp.maximum(i - 2, 0)),
-        ] + extra_specs + [pl.BlockSpec(memory_space=pl.ANY)] * len(held),
-        out_specs=[group_spec(count, first_group, *out.shape[1:]) for out in out_shapes],
-        out_shape=out_shapes,
-        input_output_aliases={5 + len(extras) + n: n for n in range(len(held))},
+        kernel,
+        in_specs=[whole, whole] + [anywhere] * (len(operands) - 2),
+        out_specs=[anywhere] + [whole] * (len(out_shape) - 1),
+        out_shape=out_shape,
+        scratch_shapes=scratch,
+        input_output_aliases={} if held is None else {len(operands) - 1: 0},
         compiler_params=pltpu.CompilerParams(vmem_limit_bytes=VMEM_LIMIT),
         cost_estimate=LITTLE,
-    )(pick, *pieces, *extras, *held)
-
-
-def select_normed(pick, gain, pieces, count, arrays, first_group, held):
-    groups, capacity, _ = pick.shape
-    features = pieces[0].shape[2]
-    return select(
-        norm_kernel, pick, pieces, [gain], [pl.BlockSpec((1, features), lambda i: (0, 0))],
-        [jax.ShapeDtypeStruct((groups, capacity, features), jnp.bfloat16)],
-        count, arrays, 0, first_group, held,
-    )
-
-
-def select_grads(pick, prob, out_slots, pieces, count, arrays, which, first_group, held):
-    groups, capacity, _ = pick.shape
-    features = pieces[0].shape[2]
-    return select(
-        grad_kernel, pick, pieces, [prob, out_slots],
-        [group_spec(count, first_group, capacity, 1), group_spec(count, first_group, capacity, features)],
-        [
-            jax.ShapeDtypeStruct((groups, capacity, features), jnp.bfloat16),
-            jax.ShapeDtypeStruct((groups, capacity, 1), jnp.float32),
-        ],
-        count, arrays, which, first_group, held,
-    )
-
-
-def expand_kernel(weighted, count, back_ref, prob_ref, *refs):
-    sources, (mine_ref, low_ref, high_ref) = refs[:-3], refs[-3:]
+    )(*operands)
+
+
+def expand_kernel(weighted, count, first_group, back_ref, prob_ref, *refs):
+    arrays = len(weighted)
+    sources, mine_ref, pieces = refs[:arrays], refs[arrays], refs[arrays + 1:arrays + 3]
+    loaded, spread, loads, stores = refs[arrays + 3:]
     half = mine_ref.shape[1]
-    for group in range(count):
-        for number, (source_ref, by_prob) in enumerate(zip(sources, weighted)):
-            rows = source_ref[group]
+    copies, written = [], []
+    for group in range(4 * count):
+        for number, source in enumerate(sources):
+            place = group * arrays + number
+            copies.append(start(source.at[first_group + group], loaded.at[place], loads.at[place]))
+    for group in range(4 * count):
+        outer, inner = divmod(group, count)
+        first, second = divmod(outer, 2)
+        for number, by_prob in enumerate(weighted):
+            place = group * arrays + number
+            copies[place].wait()
+            rows = loaded[place]
             if by_prob:
-                rows = (rows.astype(jnp.float32) * prob_ref[group]).astype(jnp.bfloat16)
-            spread = jnp.dot(back_ref[group], rows, preferred_element_type=jnp.float32)
-            place = group * len(sources) + number
-            mine_ref[place] = spread[:half].astype(jnp.bfloat16)
-            for second, out_ref in ((0, low_ref), (1, high_ref)):
-                @pl.when(lax.rem(pl.program_id(0), 2) == second)
-                def _(out_ref=out_ref, place=place, spread=spread):
-                    out_ref[place] = spread[half:].astype(jnp.bfloat16)
+                rows = (rows.astype(jnp.float32) * prob_ref[first_group + group]).astype(jnp.bfloat16)
+            spread[place] = jnp.dot(
+                back_ref[first_group + group], rows, preferred_element_type=jnp.float32
+            ).astype(jnp.bfloat16)
+            target = pieces[second].at[(first * count + inner) * arrays + number]
+            written += [
+                start(spread.at[place, pl.ds(half, half)], target, stores.at[place, 0]),
+                start(spread.at[place, pl.ds(0, half)], mine_ref.at[place], stores.at[place, 1]),
+            ]
+    for copy in written:
+        copy.wait()
 
 
 def expand(back, prob, slots, weighted, count, first_group):
     _, group_rows, capacity = back.shape
     half, features, arrays = group_rows // 2, slots[0].shape[2], len(slots)
-    blocks = count * arrays
-    piece = jax.ShapeDtypeStruct((2 * blocks, half, features), jnp.bfloat16)
+    blocks = 4 * count * arrays
+    anywhere, whole = pl.BlockSpec(memory_space=pl.ANY), pl.BlockSpec(memory_space=pltpu.VMEM)
+    piece = jax.ShapeDtypeStruct((blocks // 2, half, features), jnp.bfloat16)
     return pl.pallas_call(
-        functools.partial(expand_kernel, weighted, count),
-        grid=(4,),
-        in_specs=[
-            group_spec(count, first_group, group_rows, capacity),
-            group_spec(count, first_group, capacity, 1),
-        ] + [group_spec(count, first_group, capacity, features)] * arrays,
-        out_specs=[pl.BlockSpec((blocks, half, features), lambda i: (i, 0, 0))]
-        + [pl.BlockSpec((blocks, half, features), lambda i: (i // 2, 0, 0))] * 2,
-        out_shape=[jax.ShapeDtypeStruct((4 * blocks, half, features), jnp.bfloat16), piece, piece],
+        functools.partial(expand_kernel, weighted, count, first_group),
+        in_specs=[whole, whole] + [anywhere] * arrays,
+        out_specs=[anywhere] * 3,
+        out_shape=[jax.ShapeDtypeStruct((blocks, half, features), jnp.bfloat16), piece, piece],
+        scratch_shapes=[
+            pltpu.VMEM((blocks, capacity, features), jnp.bfloat16),
+            pltpu.VMEM((blocks, group_rows, features), jnp.bfloat16),
+            pltpu.SemaphoreType.DMA((blocks,)),
+            pltpu.SemaphoreType.DMA((blocks, 2)),
+        ],
         compiler_params=pltpu.CompilerParams(vmem_limit_bytes=VMEM_LIMIT),
         cost_estimate=LITTLE,
     )(back, prob, *slots)
@@ -483,7 +484,7 @@
     far_tables = [send_along(late_tables, -step) for step in range(1, steps)]
     late_cot = after(cotangent, token_far)
     cot_steps = [send_along(late_cot, -step) for step in range(1, steps)]
-    token_second = after(send_second(token_far), near_far_pair, cot_steps[0], *far_tables)
+    token_second = after(send_second(token_far), near_far_pair, cot_steps[len(cot_steps) // 2], *far_tables)
     token_pair = jnp.concatenate([token_far, token_second])
     tables = far_first(jnp.stack([tables] + far_tables, axis=2))
     tables = jnp.where(core == 0, tables, jnp.roll(tables, half, axis=2))
@@ -502,7 +503,7 @@
 
     gain_row = gain[None, :]
     near_pieces = (near_pair, near_far_pair, send_core(near_pair), send_core(near_far_pair))
-    rows, = select_normed(pick, gain_row, near_pieces, 1, 2, far, ())
+    rows, = select(pick, gain_row, near_pieces, 1, 2, 0, far)
     token_far_pair, rows = together(send_first(token_pair), rows, *cot_steps)[:2]
     cot_far = after(jnp.stack(cot_steps), token_far_pair)
     cot_second = send_second(cot_far)
@@ -512,7 +513,7 @@
     cot_pair = jnp.concatenate([cot_far, cot_second])
     cot_far_pair = send_first(cot_pair)
 
-    rows, = select_normed(pick, gain_row, token_pieces, steps - 1, 1, 0, (rows,))
+    rows, = select(pick, gain_row, token_pieces, steps - 1, 1, 0, 0, rows)
     rows = rows.reshape(-1, features)
     gate_pre, up_pre, hidden, block_out = forward(rows, gate_up_weight, down_weight)
     block_out, cot_far_pair = together(block_out, cot_far_pair)
@@ -521,29 +522,30 @@
     out_mine, out_low, out_high = expand(back, slot_prob, (out_slots,), (True,), steps - 1, 0)
 
     half_far, one_far = 2 * (steps - 1), steps - 1
-    out_core_high = send_core(out_high)
+    grads, near_value = select(
+        after(pick, out_high), slot_prob, near_pieces, 1, 2, 1, far, None, out_slots
+    )
+    out_core_high, grads = together(send_core(out_high), grads)
     out_core = send_core(out_low)
     out_upper = narrow(add_up(out_mine[half_far:], out_core_high))
     out_first = send_first(out_upper)
-    held = select_grads(
-        after(pick, out_high), slot_prob, out_slots, near_pieces, 1, 2, 1, far, ()
-    )
-    grads, prob_value = select_grads(
-        after(pick, out_upper), slot_prob, out_slots, cot_pieces, steps - 1, 1, 0, 0, tuple(held)
-    )
+    grads, prob_value = select(
+        after(pick, out_upper), slot_prob, cot_pieces, steps - 1, 1, 0, 0, grads, out_slots
+    )
+    prob_value = jnp.concatenate([prob_value, near_value])
     grads = grads.reshape(-1, features)
     joined_grad, input_grad, gain_term = backward(
         grads, gate_pre, up_pre, rows, gate_up_weight, down_weight
     )
     input_grad, out_first = together(input_grad, out_first)
     input_slots = input_grad.reshape(expert_size, capacity, features)
-    in_mine, in_low, in_high = expand(back, slot_prob, (input_slots,), (False,), steps - 1, 0)
+    out_middle = narrow(
+        add_up(out_mine[one_far:half_far], out_core[one_far:half_far], out_first[one_far:])
+    )
+    out_second = send_second(out_middle)
+    in_mine, in_low, in_high = expand(back, after(slot_prob, out_middle), (input_slots,), (False,), steps - 1, 0)
     in_core_high = send_core(in_high)
     in_core = send_core(in_low)
-    out_middle = narrow(
-        add_up(out_mine[one_far:half_far], out_core[one_far:half_far], after(out_first, in_high)[one_far:])
-    )
-    out_second = send_second(out_middle)
     near_mine, near_low, near_high = expand(
         back, after(slot_prob, in_high), (out_slots, input_slots), (True, False), 1, far
     )

time: 257 us -> 258 us (level)
  waiting for transfers between devices: 77 us -> 71.5 us
    ppermute x47, waiting for transfers between devices: 77 us -> 71.5 us  [send(): return lax.ppermute(array, BOTH, pairs)]
  transfers between devices with their start and end apart: 47 -> 47, of which waited for: 17 -> 14; matrix products, arithmetic and copies ran while one was open for 19% -> 18% of each run, Pallas kernels for 25% -> 24%
where the time goes in v7:
time: 258 us; the launch traced here: 257 us
  Pallas kernels  74.3 us (29%)
  waiting for transfers between devices  71.5 us (28%)
  starting transfers between devices  51.5 us (20%)
  other arithmetic  34.5 us (13%)
  local copies, waits for them, and re-layouts  12.5 us (5%)
  matrix products  11.2 us (4%)
    ppermute x47, waiting for transfers between devices, send(): return lax.ppermute(array, BOTH, pairs)  71.5 us
    ppermute x47, starting transfers between devices, send(): return lax.ppermute(array, BOTH, pairs)  51.5 us
    pallas_call x4, Pallas kernels, select(): pl.pallas_call(kernel, in_specs=[whole, whole] + [anywhere] * (len(operan...  25.3 us
    convert_element_type x8, other arithmetic, narrow(): return value.astype(jnp.bfloat16)  21 us
    pallas_call x3, Pallas kernels, expand(): pl.pallas_call(functools.partial(expand_kernel, weighted, count, first_gr...  19.4 us
    pallas_call x1, Pallas kernels, backward(): pl.pallas_call(functools.partial(backward_kernel, units), grid=(units + 4...  16.5 us
    pallas_call x1, Pallas kernels, forward(): pl.pallas_call(forward_kernel, grid=(2,), in_specs=[row_spec(features), p...  13 us
    dot_general x2, matrix products, outer_sum(): lax.dot_general(left, right, (((0,), (0,)), ((), ())), preferred_element_...  11.1 us
  transfers between devices with their start and end apart: 47, of which 14 were waited for; matrix products, arithmetic and copies ran while one was open for 18% of the time, Pallas kernels for 24%

profile of v7, /device:TPU:0, one launch (start us, length us, event | category | flops | bytes accessed | tf_op | source)
XLA Modules:
  0.0 256.7 jit_solution(9432676944652271246)
XLA Ops:
  1.7 3.0 %collective-permute-start = (bf16[2,64,2048]{2,1,0:T(8,128)(2,1)S(1)}, bf16[2,64,2048]{2,1,0:T(8,128)(2,1)S(1)}, u32[]{:S(2)}, u32[]{:S(2)}) collective-permute-start(bf16[2,64,2048]{2,1,0:T(8,128)(2,1)S(1)} %pad_maximum_fusion.3), channel_id=1, source_target_pairs={{0,2},{1,5},{2,0},{3,7},{4,6},{5,1},{6,4},{7,3},{8,10},{9,13},{10,... | collective-permute-start | bytes 1572872 | tf_op jit(solution)/shard_map/ppermute | solution.py:172
  19.6 11.8 %collective-permute-done.4 = bf16[64,2048]{1,0:T(8,128)(2,1)S(1)} collective-permute-done((bf16[64,2048]{1,0:T(8,128)(2,1)}, bf16[64,2048]{1,0:T(8,128)(2,1)S(1)}, u32[]{:S(2)}, u32[]{:S(2)}) %collective-permute-start.4) | collective-permute-done | bytes 262176 | tf_op jit(solution)/shard_map/ppermute | solution.py:172
  34.7 2.9 %collective-permute-start.7 = (f32[2,2,16,128]{3,2,1,0:T(8,128)S(1)}, f32[2,2,16,128]{3,2,1,0:T(8,128)S(1)}, u32[]{:S(2)}, u32[]{:S(2)}) collective-permute-start(f32[2,2,16,128]{3,2,1,0:T(8,128)S(1)} %pad_maximum_fusion.8), channel_id=1, source_target_pairs={{0,16},{1,17},{2,18},{3,19},{4,20},{5,21},{6,22},{7,23},{8,24},{9,... | collective-permute-start | bytes 98312 | tf_op jit(solution)/shard_map/ppermute | solution.py:172
  39.0 9.9 %collective-permute-done.7 = f32[2,2,16,128]{3,2,1,0:T(8,128)S(1)} collective-permute-done((f32[2,2,16,128]{3,2,1,0:T(8,128)S(1)}, f32[2,2,16,128]{3,2,1,0:T(8,128)S(1)}, u32[]{:S(2)}, u32[]{:S(2)}) %collective-permute-start.7) | collective-permute-done | bytes 32800 | tf_op jit(solution)/shard_map/ppermute | solution.py:172
  55.0 5.7 %collective-permute-done.15 = bf16[64,2048]{1,0:T(8,128)(2,1)} collective-permute-done((bf16[64,2048]{1,0:T(8,128)(2,1)S(1)}, bf16[64,2048]{1,0:T(8,128)(2,1)}, u32[]{:S(2)}, u32[]{:S(2)}) %collective-permute-start.15) | collective-permute-done | bytes 262176 | tf_op jit(solution)/shard_map/ppermute | solution.py:172
  60.6 5.6 %collective-permute-done.16 = bf16[64,2048]{1,0:T(8,128)(2,1)} collective-permute-done((bf16[64,2048]{1,0:T(8,128)(2,1)S(1)}, bf16[64,2048]{1,0:T(8,128)(2,1)}, u32[]{:S(2)}, u32[]{:S(2)}) %collective-permute-start.16) | collective-permute-done | bytes 262176 | tf_op jit(solution)/shard_map/ppermute | solution.py:172
  69.4 4.2 %shard_map.118.refs_4_ = bf16[16,48,2048]{2,1,0:T(8,128)(2,1)} custom-call(bf16[16,48,128]{2,1,0:T(8,128)(2,1)} %fusion.15.pick_ref.refs_0_, f32[1,2048]{1,0:T(1,128)} %bitcast.135, bf16[4,64,2048]{2,1,0:T(8,128)(2,1)} %copy-done.2, bf16[4,64,2048]{2,1,0:T(8,128)(2,1)} %copy-done.4, bf16[4,64,2048]{2,1,0:T(8,128)(2,1)} %copy-done.5, ...), custom_call_target="tpu_custom_call" | custom-call | flops 1000000 | bytes 100000 | tf_op jit(solution)/shard_map/pallas_call | solution.py:290
  77.4 8.4 %collective-permute-done.19 = bf16[3,64,2048]{2,1,0:T(8,128)(2,1)S(1)} collective-permute-done((bf16[3,64,2048]{2,1,0:T(8,128)(2,1)S(1)}, bf16[3,64,2048]{2,1,0:T(8,128)(2,1)S(1)}, u32[]{:S(2)}, u32[]{:S(2)}) %collective-permute-start.19) | collective-permute-done | bytes 786464 | tf_op jit(solution)/shard_map/ppermute | solution.py:172
  90.6 7.2 %shard_map.119 = bf16[16,48,2048]{2,1,0:T(8,128)(2,1)} custom-call(bf16[16,48,128]{2,1,0:T(8,128)(2,1)} %fusion.15.pick_ref.refs_0_, f32[1,2048]{1,0:T(1,128)} %bitcast.136, bf16[6,64,2048]{2,1,0:T(8,128)(2,1)} %constant_dynamic-update-slice_fusion.refs_0_, bf16[6,64,2048]{2,1,0:T(8,128)(2,1)} %collective-permute-done.12.refs_1_, ...), custom_call_target="tpu_custom_call", output_to_operand_aliasing={{}: (6, {})} | custom-call | flops 1000000 | bytes 100000 | tf_op jit(solution)/shard_map/pallas_call | solution.py:290
  97.8 13.0 %shard_map.120 = (f32[768,768]{1,0:T(8,128)}, f32[768,768]{1,0:T(8,128)}, bf16[768,768]{1,0:T(8,128)(2,1)}, bf16[768,2048]{1,0:T(8,128)(2,1)}) custom-call(bf16[768,2048]{1,0:T(8,128)(2,1)} %bitcast.116, bf16[1,2048,1536]{2,1,0:T(8,128)(2,1)} %gate_up_ref.3, bf16[1,768,2048]{2,1,0:T(8,128)(2,1)} %down_ref.3), custom_call_target="tpu_custom_call" | custom-call | flops 1000000 | bytes 100000 | tf_op jit(solution)/shard_map/pallas_call | solution.py:374
  110.8 7.3 %shard_map.121 = (bf16[12,64,2048]{2,1,0:T(8,128)(2,1)}, bf16[6,64,2048]{2,1,0:T(8,128)(2,1)}, bf16[6,64,2048]{2,1,0:T(8,128)(2,1)}) custom-call(bf16[16,128,48]{2,1,0:T(8,128)(2,1)} %fusion.1.back_ref, f32[16,48,1]{2,1,0:T(8,128)} %copy.27.prob_ref.refs_1_.scale_ref, bf16[16,48,2048]{2,1,0:T(8,128)(2,1)} %bitcast.119), custom_call_target="tpu_custom_call" | custom-call | flops 1000000 | bytes 100000 | tf_op jit(solution)/shard_map/pallas_call | solution.py:339
  118.8 5.1 %shard_map.122 = (bf16[16,48,2048]{2,1,0:T(8,128)(2,1)}, f32[4,48,1]{2,1,0:T(8,128)}) custom-call(bf16[16,48,128]{2,1,0:T(8,128)(2,1)} %fusion.15.pick_ref.refs_0_, f32[16,48,1]{2,1,0:T(8,128)} %copy.27.prob_ref.refs_1_.scale_ref, bf16[4,64,2048]{2,1,0:T(8,128)(2,1)} %copy-done.2, bf16[4,64,2048]{2,1,0:T(8,128)(2,1)} %copy-done.4, ...), custom_call_target="tpu_custom_call" | custom-call | flops 1000000 | bytes 100000 | tf_op jit(solution)/shard_map/pallas_call | solution.py:290
  124.0 3.7 %add_convert_fusion.1 = bf16[6,64,2048]{2,1,0:T(8,128)(2,1)} fusion(bf16[6,64,2048]{2,1,0:T(8,128)(2,1)} %collective-permute-done.22, bf16[12,64,2048]{2,1,0:T(8,128)(2,1)} %get-tuple-element.70), kind=kLoop, calls=%fused_computation.4 | loop fusion | flops 3145728 | bytes 4718592 | tf_op jit(solution)/shard_map/convert_element_type | solution.py:209
  129.0 8.8 %shard_map.123 = (bf16[16,48,2048]{2,1,0:T(8,128)(2,1)}, f32[12,48,1]{2,1,0:T(8,128)}) custom-call(bf16[16,48,128]{2,1,0:T(8,128)(2,1)} %fusion.15.pick_ref.refs_0_, f32[16,48,1]{2,1,0:T(8,128)} %copy.27.prob_ref.refs_1_.scale_ref, bf16[6,64,2048]{2,1,0:T(8,128)(2,1)} %constant_dynamic-update-slice_fusion.2.refs_0_, ...), custom_call_target="tpu_custom_call", output_to_operand_aliasing={{0}: (7, {})} | custom-call | flops 1000000 | bytes 100000 | tf_op jit(solution)/shard_map/pallas_call | solution.py:290
  137.8 16.5 %shard_map.124 = (bf16[768,1536]{1,0:T(8,128)(2,1)}, bf16[768,2048]{1,0:T(8,128)(2,1)}, f32[1,2048]{1,0:T(1,128)}) custom-call(bf16[768,2048]{1,0:T(8,128)(2,1)} %bitcast.125, f32[768,768]{1,0:T(8,128)} %get-tuple-element.80.gate_pre_ref, f32[768,768]{1,0:T(8,128)} %get-tuple-element.81.up_pre_ref, bf16[1,768,2048]{2,1,0:T(8,128)(2,1)} %down_ref.3, ...), custom_call_target="tpu_custom_call" | custom-call | flops 1000000 | bytes 100000 | tf_op jit(solution)/shard_map/pallas_call | solution.py:424
  158.3 6.5 %shard_map.125 = (bf16[12,64,2048]{2,1,0:T(8,128)(2,1)}, bf16[6,64,2048]{2,1,0:T(8,128)(2,1)}, bf16[6,64,2048]{2,1,0:T(8,128)(2,1)}) custom-call(bf16[16,128,48]{2,1,0:T(8,128)(2,1)} %fusion.1.back_ref, f32[16,48,1]{2,1,0:T(8,128)} %copy.30.prob_ref, bf16[16,48,2048]{2,1,0:T(8,128)(2,1)} %bitcast.123), custom_call_target="tpu_custom_call" | custom-call | flops 1000000 | bytes 100000 | tf_op jit(solution)/shard_map/pallas_call | solution.py:339
  168.9 5.6 %shard_map.126 = (bf16[8,64,2048]{2,1,0:T(8,128)(2,1)}, bf16[4,64,2048]{2,1,0:T(8,128)(2,1)}, bf16[4,64,2048]{2,1,0:T(8,128)(2,1)}) custom-call(bf16[16,128,48]{2,1,0:T(8,128)(2,1)} %fusion.1.back_ref, f32[16,48,1]{2,1,0:T(8,128)} %copy.31.prob_ref, bf16[16,48,2048]{2,1,0:T(8,128)(2,1)} %bitcast.122, bf16[16,48,2048]{2,1,0:T(8,128)(2,1)} %bitcast.124), custom_call_target="tpu_custom_call" | custom-call | flops 1000000 | bytes 100000 | tf_op jit(solution)/shard_map/pallas_call | solution.py:339
  178.2 4.0 %convolution_convert_fusion.1 = bf16[768,2048]{1,0:T(8,128)(2,1)} fusion(bf16[768,768]{1,0:T(8,128)(2,1)S(1)} %copy-done.23, bf16[768,2048]{1,0:T(8,128)(2,1)S(1)} %bitcast.126), kind=kOutput, calls=%fused_computation.2 | convolution fusion | flops 2417491968 | bytes 7471104 | tf_op jit(solution)/shard_map/dot_general | solution.py:38
  188.1 7.1 %convolution_convert_fusion = bf16[2048,1536]{1,0:T(8,128)(2,1)} fusion(bf16[768,2048]{1,0:T(8,128)(2,1)S(1)} %bitcast.118, bf16[768,1536]{1,0:T(8,128)(2,1)S(1)} %copy-done.22), kind=kOutput, calls=%fused_computation.1 | convolution fusion | flops 4834983936 | bytes 11796480 | tf_op jit(solution)/shard_map/dot_general | solution.py:38
  195.2 3.5 %collective-permute-done.31 = f32[48,128]{1,0:T(8,128)S(1)} collective-permute-done((f32[48,128]{1,0:T(8,128)S(1)}, f32[48,128]{1,0:T(8,128)S(1)}, u32[]{:S(2)}, u32[]{:S(2)}) %collective-permute-start.31) | collective-permute-done | bytes 24608 | tf_op jit(solution)/shard_map/ppermute | solution.py:172
  203.9 3.8 %collective-permute-start.38 = (bf16[64,2048]{1,0:T(8,128)(2,1)S(1)}, bf16[64,2048]{1,0:T(8,128)(2,1)S(1)}, u32[]{:S(2)}, u32[]{:S(2)}) collective-permute-start(bf16[64,2048]{1,0:T(8,128)(2,1)S(1)} %get-tuple-element.119), channel_id=1, source_target_pairs={{0,24},{1,25},{2,26},{3,27},{4,28},{5,29},{6,30},{7,31},{8,0},{9,1... | collective-permute-start | bytes 786440 | tf_op jit(solution)/shard_map/ppermute | solution.py:172
  209.9 4.9 %collective-permute-done.37 = bf16[64,2048]{1,0:T(8,128)(2,1)S(1)} collective-permute-done((bf16[64,2048]{1,0:T(8,128)(2,1)S(1)}, bf16[64,2048]{1,0:T(8,128)(2,1)S(1)}, u32[]{:S(2)}, u32[]{:S(2)}) %collective-permute-start.37) | collective-permute-done | bytes 262176 | tf_op jit(solution)/shard_map/ppermute | solution.py:172
  233.0 7.2 %collective-permute-done.45 = f32[20,128]{1,0:T(8,128)S(1)} collective-permute-done((f32[20,128]{1,0:T(8,128)S(1)}, f32[20,128]{1,0:T(8,128)S(1)}, u32[]{:S(2)}, u32[]{:S(2)}) %collective-permute-start.45) | collective-permute-done | bytes 10272 | tf_op jit(solution)/shard_map/ppermute | solution.py:172
  245.8 6.8 %collective-permute-done.40 = bf16[2,64,2048]{2,1,0:T(8,128)(2,1)} collective-permute-done((bf16[2,64,2048]{2,1,0:T(8,128)(2,1)}, bf16[2,64,2048]{2,1,0:T(8,128)(2,1)}, u32[]{:S(2)}, u32[]{:S(2)}) %collective-permute-start.40) | collective-permute-done | bytes 524320 | tf_op jit(solution)/shard_map/ppermute | solution.py:172
  (221 shorter events, 92.9 us)
Async XLA Ops:
  4.7 14.2 %collective-permute-start.5 = (bf16[64,2048]{1,0:T(8,128)(2,1)}, bf16[64,2048]{1,0:T(8,128)(2,1)S(1)}, u32[]{:S(2)}, u32[]{:S(2)}) collective-permute-start(bf16[64,2048]{1,0:T(8,128)(2,1)} %param.7), channel_id=1, source_target_pairs={{0,8},{1,9},{2,10},{3,11},{4,12},{5,13},{6,14},{7,15},{8,16},{9,17... | collective-permute-start | bytes 786440 | tf_op jit(solution)/shard_map/ppermute | solution.py:172
  8.5 22.9 %collective-permute-start.4 = (bf16[64,2048]{1,0:T(8,128)(2,1)}, bf16[64,2048]{1,0:T(8,128)(2,1)S(1)}, u32[]{:S(2)}, u32[]{:S(2)}) collective-permute-start(bf16[64,2048]{1,0:T(8,128)(2,1)} %param.7), channel_id=1, source_target_pairs={{0,16},{1,17},{2,18},{3,19},{4,20},{5,21},{6,22},{7,23},{8,24},{9,... | collective-permute-start | bytes 786440 | tf_op jit(solution)/shard_map/ppermute | solution.py:172
  15.1 33.8 %collective-permute-start.10 = (bf16[4,64,2048]{2,1,0:T(8,128)(2,1)S(1)}, bf16[4,64,2048]{2,1,0:T(8,128)(2,1)S(1)}, u32[]{:S(2)}, u32[]{:S(2)}) collective-permute-start(bf16[4,64,2048]{2,1,0:T(8,128)(2,1)S(1)} %pad_maximum_fusion.refs_0_.refs_2_), channel_id=1, source_target_pairs={{0,4},{1,3},{2,6},{3,1},{4,0},{5,7},{6,2},{7,5},{8,12},{9,11},{10,... | collective-permute-start | bytes 3145736 | tf_op jit(solution)/shard_map/ppermute | solution.py:172
  16.8 14.7 %collective-permute-start.2 = (f32[2,16,128]{2,1,0:T(8,128)S(1)}, f32[2,16,128]{2,1,0:T(8,128)S(1)}, u32[]{:S(2)}, u32[]{:S(2)}) collective-permute-start(f32[2,16,128]{2,1,0:T(8,128)S(1)} %get-tuple-element.130), channel_id=1, source_target_pairs={{0,4},{1,3},{2,6},{3,1},{4,0},{5,7},{6,2},{7,5},{8,12},{9,11},{10,... | collective-permute-start | bytes 49160 | tf_op jit(solution)/shard_map/ppermute | solution.py:172
  31.6 17.4 %collective-permute-start.9 = (bf16[3,64,2048]{2,1,0:T(8,128)(2,1)S(1)}, bf16[3,64,2048]{2,1,0:T(8,128)(2,1)S(1)}, u32[]{:S(2)}, u32[]{:S(2)}) collective-permute-start(bf16[3,64,2048]{2,1,0:T(8,128)(2,1)S(1)} %pad_maximum_fusion.1), channel_id=1, source_target_pairs={{0,2},{1,5},{2,0},{3,7},{4,6},{5,1},{6,4},{7,3},{8,10},{9,13},{10,... | collective-permute-start | bytes 2359304 | tf_op jit(solution)/shard_map/ppermute | solution.py:172
  34.7 14.2 %collective-permute-start.11 = (bf16[64,2048]{1,0:T(8,128)(2,1)S(1)}, bf16[64,2048]{1,0:T(8,128)(2,1)S(1)}, u32[]{:S(2)}, u32[]{:S(2)}) collective-permute-start(bf16[64,2048]{1,0:T(8,128)(2,1)S(1)} %copy-done.7), channel_id=1, source_target_pairs={{0,16},{1,17},{2,18},{3,19},{4,20},{5,21},{6,22},{7,23},{8,24},{9,... | collective-permute-start | bytes 786440 | tf_op jit(solution)/shard_map/ppermute | solution.py:172
  34.7 14.2 %collective-permute-start.7 = (f32[2,2,16,128]{3,2,1,0:T(8,128)S(1)}, f32[2,2,16,128]{3,2,1,0:T(8,128)S(1)}, u32[]{:S(2)}, u32[]{:S(2)}) collective-permute-start(f32[2,2,16,128]{3,2,1,0:T(8,128)S(1)} %pad_maximum_fusion.8), channel_id=1, source_target_pairs={{0,16},{1,17},{2,18},{3,19},{4,20},{5,21},{6,22},{7,23},{8,24},{9,... | collective-permute-start | bytes 98312 | tf_op jit(solution)/shard_map/ppermute | solution.py:172
  50.0 23.6 %collective-permute-start.12 = (bf16[6,64,2048]{2,1,0:T(8,128)(2,1)}, bf16[6,64,2048]{2,1,0:T(8,128)(2,1)}, u32[]{:S(2)}, u32[]{:S(2)}) collective-permute-start(bf16[6,64,2048]{2,1,0:T(8,128)(2,1)} %constant_dynamic-update-slice_fusion.refs_0_), channel_id=1, source_target_pairs={{0,4},{1,3},{2,6},{3,1},{4,0},{5,7},{6,2},{7,5},{8,12},{9,11},{10,... | collective-permute-start | bytes 4718600 | tf_op jit(solution)/shard_map/ppermute | solution.py:172
  51.6 16.8 %collective-permute-start.13 = (bf16[4,64,2048]{2,1,0:T(8,128)(2,1)S(1)}, bf16[4,64,2048]{2,1,0:T(8,128)(2,1)S(1)}, u32[]{:S(2)}, u32[]{:S(2)}) collective-permute-start(bf16[4,64,2048]{2,1,0:T(8,128)(2,1)S(1)} %pad_maximum_fusion.refs_0_.refs_2_), channel_id=1, source_target_pairs={{0,1},{1,0},{2,3},{3,2},{4,5},{5,4},{6,7},{7,6},{8,9},{9,8},{10,11... | collective-permute-start | bytes 3145736 | tf_op jit(solution)/shard_map/ppermute | solution.py:172
  53.7 14.7 %collective-permute-start.14 = (bf16[4,64,2048]{2,1,0:T(8,128)(2,1)S(1)}, bf16[4,64,2048]{2,1,0:T(8,128)(2,1)}, u32[]{:S(2)}, u32[]{:S(2)}) collective-permute-start(bf16[4,64,2048]{2,1,0:T(8,128)(2,1)S(1)} %collective-permute-done.10.refs_1_.refs_3_), channel_id=1, source_target_pairs={{0,1},{1,0},{2,3},{3,2},{4,5},{5,4},{6,7},{7,6},{8,9},{9,8},{10,11... | collective-permute-start | bytes 3145736 | tf_op jit(solution)/shard_map/ppermute | solution.py:172
  75.9 14.8 %collective-permute-start.17 = (bf16[6,64,2048]{2,1,0:T(8,128)(2,1)}, bf16[6,64,2048]{2,1,0:T(8,128)(2,1)}, u32[]{:S(2)}, u32[]{:S(2)}) collective-permute-start(bf16[6,64,2048]{2,1,0:T(8,128)(2,1)} %constant_dynamic-update-slice_fusion.refs_0_), channel_id=1, source_target_pairs={{0,1},{1,0},{2,3},{3,2},{4,5},{5,4},{6,7},{7,6},{8,9},{9,8},{10,11... | collective-permute-start | bytes 4718600 | tf_op jit(solution)/shard_map/ppermute | solution.py:172
  75.9 14.7 %collective-permute-start.18 = (bf16[6,64,2048]{2,1,0:T(8,128)(2,1)}, bf16[6,64,2048]{2,1,0:T(8,128)(2,1)}, u32[]{:S(2)}, u32[]{:S(2)}) collective-permute-start(bf16[6,64,2048]{2,1,0:T(8,128)(2,1)} %collective-permute-done.12.refs_1_), channel_id=1, source_target_pairs={{0,1},{1,0},{2,3},{3,2},{4,5},{5,4},{6,7},{7,6},{8,9},{9,8},{10,11... | collective-permute-start | bytes 4718600 | tf_op jit(solution)/shard_map/ppermute | solution.py:172
  86.9 23.9 %collective-permute-start.20 = (bf16[6,64,2048]{2,1,0:T(8,128)(2,1)}, bf16[6,64,2048]{2,1,0:T(8,128)(2,1)}, u32[]{:S(2)}, u32[]{:S(2)}) collective-permute-start(bf16[6,64,2048]{2,1,0:T(8,128)(2,1)} %constant_dynamic-update-slice_fusion.2.refs_0_), channel_id=1, source_target_pairs={{0,4},{1,3},{2,6},{3,1},{4,0},{5,7},{6,2},{7,5},{8,12},{9,11},{10,... | collective-permute-start | bytes 4718600 | tf_op jit(solution)/shard_map/ppermute | solution.py:172
  127.7 26.7 %collective-permute-start.25 = (bf16[6,64,2048]{2,1,0:T(8,128)(2,1)}, bf16[6,64,2048]{2,1,0:T(8,128)(2,1)}, u32[]{:S(2)}, u32[]{:S(2)}) collective-permute-start(bf16[6,64,2048]{2,1,0:T(8,128)(2,1)} %add_convert_fusion.1), channel_id=1, source_target_pairs={{0,4},{1,3},{2,6},{3,1},{4,0},{5,7},{6,2},{7,5},{8,12},{9,11},{10,... | collective-permute-start | bytes 4718600 | tf_op jit(solution)/shard_map/ppermute | solution.py:172
  128.5 25.8 %collective-permute-start.21 = (bf16[6,64,2048]{2,1,0:T(8,128)(2,1)}, bf16[6,64,2048]{2,1,0:T(8,128)(2,1)}, u32[]{:S(2)}, u32[]{:S(2)}) collective-permute-start(bf16[6,64,2048]{2,1,0:T(8,128)(2,1)} %get-tuple-element.71), channel_id=1, source_target_pairs={{0,1},{1,0},{2,3},{3,2},{4,5},{5,4},{6,7},{7,6},{8,9},{9,8},{10,11... | collective-permute-start | bytes 4718600 | tf_op jit(solution)/shard_map/ppermute | solution.py:172
  165.8 16.4 %collective-permute-start.29 = (bf16[3,64,2048]{2,1,0:T(8,128)(2,1)}, bf16[3,64,2048]{2,1,0:T(8,128)(2,1)}, u32[]{:S(2)}, u32[]{:S(2)}) collective-permute-start(bf16[3,64,2048]{2,1,0:T(8,128)(2,1)} %add_convert_fusion.6), channel_id=1, source_target_pairs={{0,2},{1,5},{2,0},{3,7},{4,6},{5,1},{6,4},{7,3},{8,10},{9,13},{10,... | collective-permute-start | bytes 2359304 | tf_op jit(solution)/shard_map/ppermute | solution.py:172
  174.5 20.8 %collective-permute-start.28 = (bf16[4,64,2048]{2,1,0:T(8,128)(2,1)}, bf16[4,64,2048]{2,1,0:T(8,128)(2,1)}, u32[]{:S(2)}, u32[]{:S(2)}) collective-permute-start(bf16[4,64,2048]{2,1,0:T(8,128)(2,1)} %get-tuple-element.92), channel_id=1, source_target_pairs={{0,1},{1,0},{2,3},{3,2},{4,5},{5,4},{6,7},{7,6},{8,9},{9,8},{10,11... | collective-permute-start | bytes 3145736 | tf_op jit(solution)/shard_map/ppermute | solution.py:172
  174.5 27.1 %collective-permute-start.34 = (bf16[6,64,2048]{2,1,0:T(8,128)(2,1)}, bf16[6,64,2048]{2,1,0:T(8,128)(2,1)}, u32[]{:S(2)}, u32[]{:S(2)}) collective-permute-start(bf16[6,64,2048]{2,1,0:T(8,128)(2,1)} %get-tuple-element.104), channel_id=1, source_target_pairs={{0,1},{1,0},{2,3},{3,2},{4,5},{5,4},{6,7},{7,6},{8,9},{9,8},{10,11... | collective-permute-start | bytes 4718600 | tf_op jit(solution)/shard_map/ppermute | solution.py:172
  177.7 23.9 %collective-permute-start.27 = (bf16[6,64,2048]{2,1,0:T(8,128)(2,1)S(1)}, bf16[6,64,2048]{2,1,0:T(8,128)(2,1)}, u32[]{:S(2)}, u32[]{:S(2)}) collective-permute-start(bf16[6,64,2048]{2,1,0:T(8,128)(2,1)S(1)} %add_convert_fusion), channel_id=1, source_target_pairs={{0,4},{1,3},{2,6},{3,1},{4,0},{5,7},{6,2},{7,5},{8,12},{9,11},{10,... | collective-permute-start | bytes 4718600 | tf_op jit(solution)/shard_map/ppermute | solution.py:172
  186.7 14.9 %collective-permute-start.32 = (bf16[64,2048]{1,0:T(8,128)(2,1)S(1)}, bf16[64,2048]{1,0:T(8,128)(2,1)S(1)}, u32[]{:S(2)}, u32[]{:S(2)}) collective-permute-start(bf16[64,2048]{1,0:T(8,128)(2,1)S(1)} %get-tuple-element.121), channel_id=1, source_target_pairs={{0,16},{1,17},{2,18},{3,19},{4,20},{5,21},{6,22},{7,23},{8,24},{9,... | collective-permute-start | bytes 786440 | tf_op jit(solution)/shard_map/ppermute | solution.py:172
  225.6 15.3 %collective-permute-start.39 = (bf16[4,64,2048]{2,1,0:T(8,128)(2,1)}, bf16[4,64,2048]{2,1,0:T(8,128)(2,1)}, u32[]{:S(2)}, u32[]{:S(2)}) collective-permute-start(bf16[4,64,2048]{2,1,0:T(8,128)(2,1)} %add_convert_fusion.2), channel_id=1, source_target_pairs={{0,4},{1,3},{2,6},{3,1},{4,0},{5,7},{6,2},{7,5},{8,12},{9,11},{10,... | collective-permute-start | bytes 3145736 | tf_op jit(solution)/shard_map/ppermute | solution.py:172
  230.5 23.8 %collective-permute-start.41 = (bf16[64,2048]{1,0:T(8,128)(2,1)}, bf16[64,2048]{1,0:T(8,128)(2,1)S(1)}, u32[]{:S(2)}, u32[]{:S(2)}) collective-permute-start(bf16[64,2048]{1,0:T(8,128)(2,1)} %get-tuple-element.116), channel_id=1, source_target_pairs={{0,8},{1,9},{2,10},{3,11},{4,12},{5,13},{6,14},{7,15},{8,16},{9,17... | collective-permute-start | bytes 786440 | tf_op jit(solution)/shard_map/ppermute | solution.py:172
  231.6 22.7 %collective-permute-start.42 = (bf16[64,2048]{1,0:T(8,128)(2,1)}, bf16[64,2048]{1,0:T(8,128)(2,1)S(1)}, u32[]{:S(2)}, u32[]{:S(2)}) collective-permute-start(bf16[64,2048]{1,0:T(8,128)(2,1)} %get-tuple-element.118), channel_id=1, source_target_pairs={{0,16},{1,17},{2,18},{3,19},{4,20},{5,21},{6,22},{7,23},{8,24},{9,... | collective-permute-start | bytes 786440 | tf_op jit(solution)/shard_map/ppermute | solution.py:172
  240.2 14.1 %collective-permute-start.43 = (bf16[64,2048]{1,0:T(8,128)(2,1)}, bf16[64,2048]{1,0:T(8,128)(2,1)S(1)}, u32[]{:S(2)}, u32[]{:S(2)}) collective-permute-start(bf16[64,2048]{1,0:T(8,128)(2,1)} %get-tuple-element.117), channel_id=1, source_target_pairs={{0,24},{1,25},{2,26},{3,27},{4,28},{5,29},{6,30},{7,31},{8,0},{9,1... | collective-permute-start | bytes 786440 | tf_op jit(solution)/shard_map/ppermute | solution.py:172
  (47 other events, 398.5 us)

commit v8 on v6

--- a/solution.py
+++ b/solution.py
@@ -224,6 +224,12 @@
     return jnp.concatenate([array[4 * (steps - 1):].reshape((2, 2, 1) + array.shape[1:]), far], axis=2)
 
 
+def start(source, target, semaphore):
+    copy = pltpu.make_async_copy(source, target, semaphore)
+    copy.start()
+    return copy
+
+
 def chosen_rows(pick, mine, other):
     return jnp.dot(pick, jnp.concatenate([mine, other]), preferred_element_type=jnp.float32)
 
@@ -314,38 +320,54 @@
     )
 
 
-def expand_kernel(weighted, count, back_ref, prob_ref, *refs):
-    sources, (mine_ref, low_ref, high_ref) = refs[:-3], refs[-3:]
+def expand_kernel(weighted, count, first_group, back_ref, prob_ref, *refs):
+    arrays = len(weighted)
+    sources, mine_ref, pieces = refs[:arrays], refs[arrays], refs[arrays + 1:arrays + 3]
+    loaded, spread, loads, stores = refs[arrays + 3:]
     half = mine_ref.shape[1]
-    for group in range(count):
-        for number, (source_ref, by_prob) in enumerate(zip(sources, weighted)):
-            rows = source_ref[group]
+    copies, written = [], []
+    for group in range(4 * count):
+        for number, source in enumerate(sources):
+            place = group * arrays + number
+            copies.append(start(source.at[first_group + group], loaded.at[place], loads.at[place]))
+    for group in range(4 * count):
+        outer, inner = divmod(group, count)
+        first, second = divmod(outer, 2)
+        for number, by_prob in enumerate(weighted):
+            place = group * arrays + number
+            copies[place].wait()
+            rows = loaded[place]
             if by_prob:
-                rows = (rows.astype(jnp.float32) * prob_ref[group]).astype(jnp.bfloat16)
-            spread = jnp.dot(back_ref[group], rows, preferred_element_type=jnp.float32)
-            place = group * len(sources) + number
-            mine_ref[place] = spread[:half].astype(jnp.bfloat16)
-            for second, out_ref in ((0, low_ref), (1, high_ref)):
-                @pl.when(lax.rem(pl.program_id(0), 2) == second)
-                def _(out_ref=out_ref, place=place, spread=spread):
-                    out_ref[place] = spread[half:].astype(jnp.bfloat16)
+                rows = (rows.astype(jnp.float32) * prob_ref[first_group + group]).astype(jnp.bfloat16)
+            spread[place] = jnp.dot(
+                back_ref[first_group + group], rows, preferred_element_type=jnp.float32
+            ).astype(jnp.bfloat16)
+            target = pieces[second].at[(first * count + inner) * arrays + number]
+            written += [
+                start(spread.at[place, pl.ds(half, half)], target, stores.at[place, 0]),
+                start(spread.at[place, pl.ds(0, half)], mine_ref.at[place], stores.at[place, 1]),
+            ]
+    for copy in written:
+        copy.wait()
 
 
 def expand(back, prob, slots, weighted, count, first_group):
     _, group_rows, capacity = back.shape
     half, features, arrays = group_rows // 2, slots[0].shape[2], len(slots)
-    blocks = count * arrays
-    piece = jax.ShapeDtypeStruct((2 * blocks, half, features), jnp.bfloat16)
+    blocks = 4 * count * arrays
+    anywhere, whole = pl.BlockSpec(memory_space=pl.ANY), pl.BlockSpec(memory_space=pltpu.VMEM)
+    piece = jax.ShapeDtypeStruct((blocks // 2, half, features), jnp.bfloat16)
     return pl.pallas_call(
-        functools.partial(expand_kernel, weighted, count),
-        grid=(4,),
-        in_specs=[
-            group_spec(count, first_group, group_rows, capacity),
-            group_spec(count, first_group, capacity, 1),
-        ] + [group_spec(count, first_group, capacity, features)] * arrays,
-        out_specs=[pl.BlockSpec((blocks, half, features), lambda i: (i, 0, 0))]
-        + [pl.BlockSpec((blocks, half, features), lambda i: (i // 2, 0, 0))] * 2,
-        out_shape=[jax.ShapeDtypeStruct((4 * blocks, half, features), jnp.bfloat16), piece, piece],
+        functools.partial(expand_kernel, weighted, count, first_group),
+        in_specs=[whole, whole] + [anywhere] * arrays,
+        out_specs=[anywhere] * 3,
+        out_shape=[jax.ShapeDtypeStruct((blocks, half, features), jnp.bfloat16), piece, piece],
+        scratch_shapes=[
+            pltpu.VMEM((blocks, capacity, features), jnp.bfloat16),
+            pltpu.VMEM((blocks, group_rows, features), jnp.bfloat16),
+            pltpu.SemaphoreType.DMA((blocks,)),
+            pltpu.SemaphoreType.DMA((blocks, 2)),
+        ],
         compiler_params=pltpu.CompilerParams(vmem_limit_bytes=VMEM_LIMIT),
         cost_estimate=LITTLE,
     )(back, prob, *slots)
@@ -483,7 +505,7 @@
     far_tables = [send_along(late_tables, -step) for step in range(1, steps)]
     late_cot = after(cotangent, token_far)
     cot_steps = [send_along(late_cot, -step) for step in range(1, steps)]
-    token_second = after(send_second(token_far), near_far_pair, cot_steps[0], *far_tables)
+    token_second = after(send_second(token_far), near_far_pair, cot_steps[len(cot_steps) // 2], *far_tables)
     token_pair = jnp.concatenate([token_far, token_second])
     tables = far_first(jnp.stack([tables] + far_tables, axis=2))
     tables = jnp.where(core == 0, tables, jnp.roll(tables, half, axis=2))
@@ -503,16 +525,16 @@
     gain_row = gain[None, :]
     near_pieces = (near_pair, near_far_pair, send_core(near_pair), send_core(near_far_pair))
     rows, = select_normed(pick, gain_row, near_pieces, 1, 2, far, ())
-    token_far_pair, rows = together(send_first(token_pair), rows, *cot_steps)[:2]
-    cot_far = after(jnp.stack(cot_steps), token_far_pair)
+    cot_steps = together(*cot_steps, rows)
+    rows, cot_far = cot_steps[-1], jnp.stack(cot_steps[:-1])
+    token_far_pair, cot_far = together(send_first(token_pair), cot_far)
     cot_second = send_second(cot_far)
-    token_pieces = (
-        token_pair, token_far_pair, send_core(token_pair), after(send_core(token_far_pair), cot_second)
-    )
+    token_pieces = (token_pair, token_far_pair, send_core(token_pair), send_core(token_far_pair))
+    rows, = select_normed(pick, gain_row, token_pieces, steps - 1, 1, 0, (rows,))
+    rows, cot_second = together(rows, cot_second)
     cot_pair = jnp.concatenate([cot_far, cot_second])
     cot_far_pair = send_first(cot_pair)
 
-    rows, = select_normed(pick, gain_row, token_pieces, steps - 1, 1, 0, (rows,))
     rows = rows.reshape(-1, features)
     gate_pre, up_pre, hidden, block_out = forward(rows, gate_up_weight, down_weight)
     block_out, cot_far_pair = together(block_out, cot_far_pair)
@@ -521,31 +543,46 @@
     out_mine, out_low, out_high = expand(back, slot_prob, (out_slots,), (True,), steps - 1, 0)
 
     half_far, one_far = 2 * (steps - 1), steps - 1
-    out_core_high = send_core(out_high)
+    own_mine, own_low, own_high = expand(
+        back, after(slot_prob, out_high), (out_slots,), (True,), 1, far
+    )
+    own_core_high = send_core(own_high)
+    own_core = send_core(own_low)
+    held = select_grads(
+        after(pick, out_high), slot_prob, out_slots, near_pieces, 1, 2, 1, far, ()
+    )
+    out_core_high = after(send_core(out_high), own_high, held[1])
     out_core = send_core(out_low)
     out_upper = narrow(add_up(out_mine[half_far:], out_core_high))
     out_first = send_first(out_upper)
-    held = select_grads(
-        after(pick, out_high), slot_prob, out_slots, near_pieces, 1, 2, 1, far, ()
-    )
+    own_upper = narrow(add_up(own_mine[2:], after(own_core_high, out_upper)))
+    own_first = send_first(own_upper)
     grads, prob_value = select_grads(
-        after(pick, out_upper), slot_prob, out_slots, cot_pieces, steps - 1, 1, 0, 0, tuple(held)
+        after(pick, own_upper), slot_prob, out_slots, cot_pieces, steps - 1, 1, 0, 0, tuple(held)
     )
     grads = grads.reshape(-1, features)
     joined_grad, input_grad, gain_term = backward(
         grads, gate_pre, up_pre, rows, gate_up_weight, down_weight
     )
-    input_grad, out_first = together(input_grad, out_first)
+    input_grad, out_first, own_first = together(input_grad, out_first, own_first)
     input_slots = input_grad.reshape(expert_size, capacity, features)
-    in_mine, in_low, in_high = expand(back, slot_prob, (input_slots,), (False,), steps - 1, 0)
+    out_middle = narrow(
+        add_up(out_mine[one_far:half_far], out_core[one_far:half_far], out_first[one_far:])
+    )
+    out_second = send_second(out_middle)
+    in_mine, in_low, in_high = expand(back, after(slot_prob, out_middle), (input_slots,), (False,), steps - 1, 0)
+    own_middle = narrow(add_up(own_mine[1:2], own_core[1:], own_first[1:]))
+    own_second = send_second(own_middle)
+    in_high, out_second, own_second = together(in_high, out_second, own_second)
     in_core_high = send_core(in_high)
     in_core = send_core(in_low)
-    out_middle = narrow(
-        add_up(out_mine[one_far:half_far], out_core[one_far:half_far], after(out_first, in_high)[one_far:])
-    )
-    out_second = send_second(out_middle)
+    def own_plane(mine, core_part, first_part, second_part, count):
+        return add_up(mine[:count], core_part[:count], first_part[:count], second_part[:count])
+
+    out_planes = narrow(own_plane(out_mine, out_core, out_first, out_second, one_far))
+    out_far = [send_along(out_planes[step - 1], step) for step in range(1, steps)]
     near_mine, near_low, near_high = expand(
-        back, after(slot_prob, in_high), (out_slots, input_slots), (True, False), 1, far
+        back, after(slot_prob, in_high), (input_slots,), (False,), 1, far
     )
     near_core_high = send_core(near_high)
     near_core = send_core(near_low)
@@ -558,17 +595,12 @@
     got = send_core(after(pack(columns[..., half:], gains), in_upper))
     down_part = outer_sum(after(hidden, in_upper), grads)
 
-    def own_plane(mine, core_part, first_part, second_part, count):
-        return add_up(mine[:count], core_part[:count], first_part[:count], second_part[:count])
-
-    out_second, down_part, got = together(out_second, down_part, got)
+    down_part, got = together(down_part, got)
     columns, gains = unpack_add(columns[..., :half], gains, got)
     got = send_bit(pack(columns[1], gains), 2)
-    out_planes = narrow(own_plane(out_mine, out_core, out_first, out_second, one_far))
-    out_far = [send_along(out_planes[step - 1], step) for step in range(1, steps)]
-    gate_up_part = outer_sum(after(rows, out_planes), joined_grad)
+    gate_up_part = outer_sum(after(rows, in_upper), joined_grad)
     in_first, near_core, gate_up_part, got = together(
-        in_first, near_core, gate_up_part, got, out_far[len(out_far) // 2]
+        in_first, near_core, gate_up_part, got, *out_far
     )[:4]
     columns, gains = unpack_add(columns[0], gains, got)
     in_middle = narrow(
@@ -576,18 +608,17 @@
     )
     in_second = send_second(in_middle)
     got = send_bit(pack(columns[1], gains), 1)
-    in_second, got = together(in_second, got, *out_far)[:2]
+    in_second, got = together(in_second, got)
     columns, gains = unpack_add(columns[0], gains, got)
     in_planes = narrow(own_plane(in_mine, in_core, in_first, in_second, one_far))
     messages = [send_along(pack(columns[step], gains), step) for step in range(1, steps)]
     in_far = [send_along(in_planes[step - 1], step) for step in range(1, steps)]
-    near_upper = narrow(add_up(near_mine[4:], after(near_core_high, in_planes)))
+    near_upper = narrow(add_up(near_mine[2:], after(near_core_high, in_planes)))
     near_first = send_first(near_upper)
-    near_middle = narrow(add_up(near_mine[2:4], near_core[2:4], near_first[2:]))
+    near_middle = narrow(add_up(near_mine[1:2], near_core[1:], near_first[1:]))
     near_second = send_second(near_middle)
-    near_sum = own_plane(near_mine, near_core, near_first, near_second, 2)
-    out_sum = near_sum[0] + add_up(*out_far)
-    normed_grad = near_sum[1] + add_up(*in_far)
+    out_sum = own_plane(own_mine, own_core, own_first, own_second, 1)[0] + add_up(*out_far)
+    normed_grad = own_plane(near_mine, near_core, near_first, near_second, 1)[0] + add_up(*in_far)
 
     prob_sum, all_gains = columns[0], [gains]
     for message in messages:

time: 257 us -> 269 us (1.047)
  waiting for transfers between devices: 77 us -> 70 us
  local copies, waits for them, and re-layouts: 10.4 us -> 15.6 us
  other arithmetic: 34.1 us -> 39 us
  starting transfers between devices: 50 us -> 53.2 us
    ppermute x47 -> x51, waiting for transfers between devices: 77 us -> 70 us  [send(): return lax.ppermute(array, BOTH, pairs)]
    ppermute x47 -> x51, starting transfers between devices: 50 us -> 53.2 us  [send(): return lax.ppermute(array, BOTH, pairs)]
    pallas_call x3 -> x4, Pallas kernels: 21 us -> 22.3 us  [expand(): pl.pallas_call(functools.partial(expand_kernel, weighted, count, first_gr...]
    convert_element_type x8 -> x10, other arithmetic: 20.6 us -> 21.1 us  [narrow(): return value.astype(jnp.bfloat16)]
  transfers between devices with their start and end apart: 47 -> 51, of which waited for: 17 -> 17; matrix products, arithmetic and copies ran while one was open for 19% -> 21% of each run, Pallas kernels for 25% -> 25%
where the time goes in v8:
time: 269 us; the launch traced here: 265 us
  Pallas kernels  73.1 us (27%)
  waiting for transfers between devices  70 us (26%)
  starting transfers between devices  53.2 us (20%)
  other arithmetic  39 us (14%)
  local copies, waits for them, and re-layouts  15.6 us (6%)
  matrix products  13 us (5%)
    ppermute x51, waiting for transfers between devices, send(): return lax.ppermute(array, BOTH, pairs)  70 us
    ppermute x51, starting transfers between devices, send(): return lax.ppermute(array, BOTH, pairs)  53.2 us
    pallas_call x4, Pallas kernels, expand(): pl.pallas_call(functools.partial(expand_kernel, weighted, count, first_gr...  22.3 us
    pallas_call x4, Pallas kernels, select(): pl.pallas_call(functools.partial(kernel, count), grid=(4,), in_specs=[gro...  21.6 us
    convert_element_type x10, other arithmetic, narrow(): return value.astype(jnp.bfloat16)  21.1 us
    pallas_call x1, Pallas kernels, backward(): pl.pallas_call(functools.partial(backward_kernel, units), grid=(units + 4...  16.3 us
    pallas_call x1, Pallas kernels, forward(): pl.pallas_call(forward_kernel, grid=(2,), in_specs=[row_spec(features), p...  13 us
    dot_general x2, matrix products, outer_sum(): lax.dot_general(left, right, (((0,), (0,)), ((), ())), preferred_element_...  12.9 us
  transfers between devices with their start and end apart: 51, of which 17 were waited for; matrix products, arithmetic and copies ran while one was open for 21% of the time, Pallas kernels for 25%

profile of v8, /device:TPU:0, one launch (start us, length us, event | category | flops | bytes accessed | tf_op | source)
XLA Modules:
  0.0 265.1 jit_solution(17452696812097265452)
XLA Ops:
  19.6 11.8 %collective-permute-done.4 = bf16[64,2048]{1,0:T(8,128)(2,1)S(1)} collective-permute-done((bf16[64,2048]{1,0:T(8,128)(2,1)}, bf16[64,2048]{1,0:T(8,128)(2,1)S(1)}, u32[]{:S(2)}, u32[]{:S(2)}) %collective-permute-start.4) | collective-permute-done | bytes 262176 | tf_op jit(solution)/shard_map/ppermute | solution.py:172
  39.0 9.9 %collective-permute-done.7 = f32[2,2,16,128]{3,2,1,0:T(8,128)S(1)} collective-permute-done((f32[2,2,16,128]{3,2,1,0:T(8,128)S(1)}, f32[2,2,16,128]{3,2,1,0:T(8,128)S(1)}, u32[]{:S(2)}, u32[]{:S(2)}) %collective-permute-start.7) | collective-permute-done | bytes 32800 | tf_op jit(solution)/shard_map/ppermute | solution.py:172
  56.3 4.3 %shard_map.118.refs_5_ = bf16[16,48,2048]{2,1,0:T(8,128)(2,1)} custom-call(bf16[16,48,128]{2,1,0:T(8,128)(2,1)} %fusion.13.pick_ref, bf16[4,64,2048]{2,1,0:T(8,128)(2,1)} %copy-done.2, bf16[4,64,2048]{2,1,0:T(8,128)(2,1)} %copy-done.4, bf16[4,64,2048]{2,1,0:T(8,128)(2,1)} %copy-done.5, bf16[4,64,2048]{2,1,0:T(8,128)(2,1)} %collective-permute-done.16.refs_3_, ...), custom_call_target="tpu_custom_call" | custom-call | flops 1000000 | bytes 100000 | tf_op jit(solution)/shard_map/pallas_call | solution.py:281
  61.3 5.0 %collective-permute-done.14 = bf16[64,2048]{1,0:T(8,128)(2,1)} collective-permute-done((bf16[64,2048]{1,0:T(8,128)(2,1)S(1)}, bf16[64,2048]{1,0:T(8,128)(2,1)}, u32[]{:S(2)}, u32[]{:S(2)}) %collective-permute-start.14) | collective-permute-done | bytes 262176 | tf_op jit(solution)/shard_map/ppermute | solution.py:172
  75.1 6.0 %shard_map.119 = bf16[16,48,2048]{2,1,0:T(8,128)(2,1)} custom-call(bf16[16,48,128]{2,1,0:T(8,128)(2,1)} %fusion.13.pick_ref, bf16[6,64,2048]{2,1,0:T(8,128)(2,1)} %constant_dynamic-update-slice_fusion.refs_0_, bf16[6,64,2048]{2,1,0:T(8,128)(2,1)} %collective-permute-done.12.refs_1_, ...), custom_call_target="tpu_custom_call", output_to_operand_aliasing={{}: (6, {})} | custom-call | flops 1000000 | bytes 100000 | tf_op jit(solution)/shard_map/pallas_call | solution.py:281
  89.6 13.0 %shard_map.120 = (f32[768,768]{1,0:T(8,128)}, f32[768,768]{1,0:T(8,128)}, bf16[768,768]{1,0:T(8,128)(2,1)}, bf16[768,2048]{1,0:T(8,128)(2,1)}) custom-call(bf16[768,2048]{1,0:T(8,128)(2,1)} %bitcast.107, bf16[1,2048,1536]{2,1,0:T(8,128)(2,1)} %gate_up_ref.3, bf16[1,768,2048]{2,1,0:T(8,128)(2,1)} %down_ref.3), custom_call_target="tpu_custom_call" | custom-call | flops 1000000 | bytes 100000 | tf_op jit(solution)/shard_map/pallas_call | solution.py:395
  102.6 3.5 %collective-permute-done.20.refs_1_ = bf16[6,64,2048]{2,1,0:T(8,128)(2,1)} collective-permute-done((bf16[6,64,2048]{2,1,0:T(8,128)(2,1)}, bf16[6,64,2048]{2,1,0:T(8,128)(2,1)}, u32[]{:S(2)}, u32[]{:S(2)}) %collective-permute-start.20) | collective-permute-done | bytes 1572896 | tf_op jit(solution)/shard_map/ppermute | solution.py:172
  106.1 7.3 %shard_map.121 = (bf16[12,64,2048]{2,1,0:T(8,128)(2,1)}, bf16[6,64,2048]{2,1,0:T(8,128)(2,1)}, bf16[6,64,2048]{2,1,0:T(8,128)(2,1)}) custom-call(bf16[16,128,48]{2,1,0:T(8,128)(2,1)} %fusion.1.back_ref, f32[16,48,1]{2,1,0:T(8,128)} %copy.19.prob_ref.refs_4_, bf16[16,48,2048]{2,1,0:T(8,128)(2,1)} %bitcast.110), custom_call_target="tpu_custom_call" | custom-call | flops 1000000 | bytes 100000 | tf_op jit(solution)/shard_map/pallas_call | solution.py:360
  115.0 4.4 %shard_map.122 = (bf16[4,64,2048]{2,1,0:T(8,128)(2,1)}, bf16[2,64,2048]{2,1,0:T(8,128)(2,1)}, bf16[2,64,2048]{2,1,0:T(8,128)(2,1)}) custom-call(bf16[16,128,48]{2,1,0:T(8,128)(2,1)} %fusion.1.back_ref, f32[16,48,1]{2,1,0:T(8,128)} %copy.20.prob_ref, bf16[16,48,2048]{2,1,0:T(8,128)(2,1)} %bitcast.111), custom_call_target="tpu_custom_call" | custom-call | flops 1000000 | bytes 100000 | tf_op jit(solution)/shard_map/pallas_call | solution.py:360
  119.9 4.5 %shard_map.123 = (bf16[16,48,2048]{2,1,0:T(8,128)(2,1)}, f32[16,48,1]{2,1,0:T(8,128)}) custom-call(bf16[16,48,128]{2,1,0:T(8,128)(2,1)} %fusion.13.pick_ref, bf16[4,64,2048]{2,1,0:T(8,128)(2,1)} %copy-done.2, bf16[4,64,2048]{2,1,0:T(8,128)(2,1)} %copy-done.4, bf16[4,64,2048]{2,1,0:T(8,128)(2,1)} %copy-done.5, ...), custom_call_target="tpu_custom_call" | custom-call | flops 1000000 | bytes 100000 | tf_op jit(solution)/shard_map/pallas_call | solution.py:281
  124.5 3.8 %add_convert_fusion.1 = bf16[6,64,2048]{2,1,0:T(8,128)(2,1)} fusion(bf16[6,64,2048]{2,1,0:T(8,128)(2,1)} %collective-permute-done.23, bf16[12,64,2048]{2,1,0:T(8,128)(2,1)} %get-tuple-element.90), kind=kLoop, calls=%fused_computation.4 | loop fusion | flops 3145728 | bytes 4718592 | tf_op jit(solution)/shard_map/convert_element_type | solution.py:209
  134.4 6.7 %shard_map.124 = (bf16[16,48,2048]{2,1,0:T(8,128)(2,1)}, f32[16,48,1]{2,1,0:T(8,128)}) custom-call(bf16[16,48,128]{2,1,0:T(8,128)(2,1)} %fusion.13.pick_ref, bf16[6,64,2048]{2,1,0:T(8,128)(2,1)} %constant_dynamic-update-slice_fusion.2.refs_0_, bf16[6,64,2048]{2,1,0:T(8,128)(2,1)} %collective-permute-done.20.refs_1_, ...), custom_call_target="tpu_custom_call", output_to_operand_aliasing={{0}: (7, {}), {1}: (8, {})} | custom-call | flops 1000000 | bytes 100000 | tf_op jit(solution)/shard_map/pallas_call | solution.py:281
  142.3 16.3 %shard_map.125 = (bf16[768,1536]{1,0:T(8,128)(2,1)}, bf16[768,2048]{1,0:T(8,128)(2,1)}, f32[1,2048]{1,0:T(1,128)}) custom-call(bf16[768,2048]{1,0:T(8,128)(2,1)} %bitcast.114, f32[768,768]{1,0:T(8,128)} %get-tuple-element.99.gate_pre_ref, f32[768,768]{1,0:T(8,128)} %get-tuple-element.100.up_pre_ref, bf16[1,768,2048]{2,1,0:T(8,128)(2,1)} %down_ref.3, ...), custom_call_target="tpu_custom_call" | custom-call | flops 1000000 | bytes 100000 | tf_op jit(solution)/shard_map/pallas_call | solution.py:445
  158.8 3.1 %add_convert_fusion.5 = bf16[3,64,2048]{2,1,0:T(8,128)(2,1)} fusion(bf16[6,64,2048]{2,1,0:T(8,128)(2,1)} %collective-permute-done.28, bf16[6,64,2048]{2,1,0:T(8,128)(2,1)} %collective-permute-done.26, bf16[12,64,2048]{2,1,0:T(8,128)(2,1)} %get-tuple-element.90), kind=kLoop, calls=%fused_computation.8 | loop fusion | flops 2359296 | bytes 3145728 | tf_op jit(solution)/shard_map/convert_element_type | solution.py:209
  166.7 6.5 %shard_map.126 = (bf16[12,64,2048]{2,1,0:T(8,128)(2,1)}, bf16[6,64,2048]{2,1,0:T(8,128)(2,1)}, bf16[6,64,2048]{2,1,0:T(8,128)(2,1)}) custom-call(bf16[16,128,48]{2,1,0:T(8,128)(2,1)} %fusion.1.back_ref, f32[16,48,1]{2,1,0:T(8,128)} %copy.23.prob_ref, bf16[16,48,2048]{2,1,0:T(8,128)(2,1)} %bitcast.116), custom_call_target="tpu_custom_call" | custom-call | flops 1000000 | bytes 100000 | tf_op jit(solution)/shard_map/pallas_call | solution.py:360
  173.2 3.7 %collective-permute-done.30 = bf16[1,64,2048]{2,1,0:T(8,128)(2,1)S(1)} collective-permute-done((bf16[1,64,2048]{2,1,0:T(8,128)(2,1)}, bf16[1,64,2048]{2,1,0:T(8,128)(2,1)S(1)}, u32[]{:S(2)}, u32[]{:S(2)}) %collective-permute-start.30) | collective-permute-done | bytes 262176 | tf_op jit(solution)/shard_map/ppermute | solution.py:172
  185.7 4.1 %shard_map.127 = (bf16[4,64,2048]{2,1,0:T(8,128)(2,1)}, bf16[2,64,2048]{2,1,0:T(8,128)(2,1)}, bf16[2,64,2048]{2,1,0:T(8,128)(2,1)}) custom-call(bf16[16,128,48]{2,1,0:T(8,128)(2,1)} %fusion.1.back_ref, f32[16,48,1]{2,1,0:T(8,128)} %copy.24.prob_ref, bf16[16,48,2048]{2,1,0:T(8,128)(2,1)} %bitcast.117), custom_call_target="tpu_custom_call" | custom-call | flops 1000000 | bytes 100000 | tf_op jit(solution)/shard_map/pallas_call | solution.py:360
  189.9 3.9 %add_convert_fusion = bf16[6,64,2048]{2,1,0:T(8,128)(2,1)} fusion(bf16[6,64,2048]{2,1,0:T(8,128)(2,1)} %collective-permute-done.34, bf16[12,64,2048]{2,1,0:T(8,128)(2,1)} %get-tuple-element.113), kind=kLoop, calls=%fused_computation.3 | loop fusion | flops 3145728 | bytes 4718592 | tf_op jit(solution)/shard_map/convert_element_type | solution.py:209
  193.8 4.2 %convolution_convert_fusion.1 = bf16[768,2048]{1,0:T(8,128)(2,1)} fusion(bf16[768,768]{1,0:T(8,128)(2,1)S(1)} %copy-done.23, bf16[768,2048]{1,0:T(8,128)(2,1)S(1)} %bitcast.115), kind=kOutput, calls=%fused_computation.2 | convolution fusion | flops 2417491968 | bytes 7471104 | tf_op jit(solution)/shard_map/dot_general | solution.py:38
  202.9 8.7 %convolution_convert_fusion = bf16[2048,1536]{1,0:T(8,128)(2,1)} fusion(bf16[768,2048]{1,0:T(8,128)(2,1)S(1)} %bitcast.109, bf16[768,1536]{1,0:T(8,128)(2,1)} %get-tuple-element.118), kind=kOutput, calls=%fused_computation.1 | convolution fusion | flops 4834983936 | bytes 11796480 | tf_op jit(solution)/shard_map/dot_general | solution.py:38
  211.6 7.6 %collective-permute-done.38 = f32[48,128]{1,0:T(8,128)S(1)} collective-permute-done((f32[48,128]{1,0:T(8,128)S(1)}, f32[48,128]{1,0:T(8,128)S(1)}, u32[]{:S(2)}, u32[]{:S(2)}) %collective-permute-start.38) | collective-permute-done | bytes 24608 | tf_op jit(solution)/shard_map/ppermute | solution.py:172
  223.6 9.8 %collective-permute-done.42 = f32[32,128]{1,0:T(8,128)S(1)} collective-permute-done((f32[32,128]{1,0:T(8,128)S(1)}, f32[32,128]{1,0:T(8,128)S(1)}, u32[]{:S(2)}, u32[]{:S(2)}) %collective-permute-start.42) | collective-permute-done | bytes 16416 | tf_op jit(solution)/shard_map/ppermute | solution.py:172
  234.3 3.3 %collective-permute-start.50 = (f32[20,128]{1,0:T(8,128)S(1)}, f32[20,128]{1,0:T(8,128)S(1)}, u32[]{:S(2)}, u32[]{:S(2)}) collective-permute-start(f32[20,128]{1,0:T(8,128)S(1)} %get-tuple-element.157), channel_id=1, source_target_pairs={{0,24},{1,25},{2,26},{3,27},{4,28},{5,29},{6,30},{7,31},{8,0},{9,1... | collective-permute-start | bytes 30728 | tf_op jit(solution)/shard_map/ppermute | solution.py:172
  253.8 7.1 %collective-permute-done.46 = bf16[64,2048]{1,0:T(8,128)(2,1)} collective-permute-done((bf16[64,2048]{1,0:T(8,128)(2,1)}, bf16[64,2048]{1,0:T(8,128)(2,1)}, u32[]{:S(2)}, u32[]{:S(2)}) %collective-permute-start.46) | collective-permute-done | bytes 262176 | tf_op jit(solution)/shard_map/ppermute | solution.py:172
  (230 shorter events, 105.6 us)
Async XLA Ops:
  4.7 14.2 %collective-permute-start.5 = (bf16[64,2048]{1,0:T(8,128)(2,1)}, bf16[64,2048]{1,0:T(8,128)(2,1)S(1)}, u32[]{:S(2)}, u32[]{:S(2)}) collective-permute-start(bf16[64,2048]{1,0:T(8,128)(2,1)} %param.7), channel_id=1, source_target_pairs={{0,8},{1,9},{2,10},{3,11},{4,12},{5,13},{6,14},{7,15},{8,16},{9,17... | collective-permute-start | bytes 786440 | tf_op jit(solution)/shard_map/ppermute | solution.py:172
  8.5 22.9 %collective-permute-start.4 = (bf16[64,2048]{1,0:T(8,128)(2,1)}, bf16[64,2048]{1,0:T(8,128)(2,1)S(1)}, u32[]{:S(2)}, u32[]{:S(2)}) collective-permute-start(bf16[64,2048]{1,0:T(8,128)(2,1)} %param.7), channel_id=1, source_target_pairs={{0,16},{1,17},{2,18},{3,19},{4,20},{5,21},{6,22},{7,23},{8,24},{9,... | collective-permute-start | bytes 786440 | tf_op jit(solution)/shard_map/ppermute | solution.py:172
  15.1 33.8 %collective-permute-start.10 = (bf16[4,64,2048]{2,1,0:T(8,128)(2,1)S(1)}, bf16[4,64,2048]{2,1,0:T(8,128)(2,1)S(1)}, u32[]{:S(2)}, u32[]{:S(2)}) collective-permute-start(bf16[4,64,2048]{2,1,0:T(8,128)(2,1)S(1)} %pad_maximum_fusion.refs_0_), channel_id=1, source_target_pairs={{0,4},{1,3},{2,6},{3,1},{4,0},{5,7},{6,2},{7,5},{8,12},{9,11},{10,... | collective-permute-start | bytes 3145736 | tf_op jit(solution)/shard_map/ppermute | solution.py:172
  16.8 14.7 %collective-permute-start.2 = (f32[2,16,128]{2,1,0:T(8,128)S(1)}, f32[2,16,128]{2,1,0:T(8,128)S(1)}, u32[]{:S(2)}, u32[]{:S(2)}) collective-permute-start(f32[2,16,128]{2,1,0:T(8,128)S(1)} %get-tuple-element.154), channel_id=1, source_target_pairs={{0,4},{1,3},{2,6},{3,1},{4,0},{5,7},{6,2},{7,5},{8,12},{9,11},{10,... | collective-permute-start | bytes 49160 | tf_op jit(solution)/shard_map/ppermute | solution.py:172
  31.6 17.4 %collective-permute-start.9 = (bf16[3,64,2048]{2,1,0:T(8,128)(2,1)S(1)}, bf16[3,64,2048]{2,1,0:T(8,128)(2,1)S(1)}, u32[]{:S(2)}, u32[]{:S(2)}) collective-permute-start(bf16[3,64,2048]{2,1,0:T(8,128)(2,1)S(1)} %pad_maximum_fusion.1), channel_id=1, source_target_pairs={{0,2},{1,5},{2,0},{3,7},{4,6},{5,1},{6,4},{7,3},{8,10},{9,13},{10,... | collective-permute-start | bytes 2359304 | tf_op jit(solution)/shard_map/ppermute | solution.py:172
  50.0 20.7 %collective-permute-start.12 = (bf16[6,64,2048]{2,1,0:T(8,128)(2,1)}, bf16[6,64,2048]{2,1,0:T(8,128)(2,1)}, u32[]{:S(2)}, u32[]{:S(2)}) collective-permute-start(bf16[6,64,2048]{2,1,0:T(8,128)(2,1)} %constant_dynamic-update-slice_fusion.refs_0_), channel_id=1, source_target_pairs={{0,4},{1,3},{2,6},{3,1},{4,0},{5,7},{6,2},{7,5},{8,12},{9,11},{10,... | collective-permute-start | bytes 4718600 | tf_op jit(solution)/shard_map/ppermute | solution.py:172
  55.3 19.8 %collective-permute-start.17 = (bf16[6,64,2048]{2,1,0:T(8,128)(2,1)}, bf16[6,64,2048]{2,1,0:T(8,128)(2,1)}, u32[]{:S(2)}, u32[]{:S(2)}) collective-permute-start(bf16[6,64,2048]{2,1,0:T(8,128)(2,1)} %constant_dynamic-update-slice_fusion.refs_0_), channel_id=1, source_target_pairs={{0,1},{1,0},{2,3},{3,2},{4,5},{5,4},{6,7},{7,6},{8,9},{9,8},{10,11... | collective-permute-start | bytes 4718600 | tf_op jit(solution)/shard_map/ppermute | solution.py:172
  85.4 20.7 %collective-permute-start.20 = (bf16[6,64,2048]{2,1,0:T(8,128)(2,1)}, bf16[6,64,2048]{2,1,0:T(8,128)(2,1)}, u32[]{:S(2)}, u32[]{:S(2)}) collective-permute-start(bf16[6,64,2048]{2,1,0:T(8,128)(2,1)} %constant_dynamic-update-slice_fusion.2.refs_0_), channel_id=1, source_target_pairs={{0,4},{1,3},{2,6},{3,1},{4,0},{5,7},{6,2},{7,5},{8,12},{9,11},{10,... | collective-permute-start | bytes 4718600 | tf_op jit(solution)/shard_map/ppermute | solution.py:172
  113.5 20.4 %collective-permute-start.24 = (bf16[6,64,2048]{2,1,0:T(8,128)(2,1)}, bf16[6,64,2048]{2,1,0:T(8,128)(2,1)}, u32[]{:S(2)}, u32[]{:S(2)}) collective-permute-start(bf16[6,64,2048]{2,1,0:T(8,128)(2,1)} %constant_dynamic-update-slice_fusion.2.refs_0_), channel_id=1, source_target_pairs={{0,1},{1,0},{2,3},{3,2},{4,5},{5,4},{6,7},{7,6},{8,9},{9,8},{10,11... | collective-permute-start | bytes 4718600 | tf_op jit(solution)/shard_map/ppermute | solution.py:172
  119.5 14.9 %collective-permute-start.25 = (bf16[6,64,2048]{2,1,0:T(8,128)(2,1)}, bf16[6,64,2048]{2,1,0:T(8,128)(2,1)}, u32[]{:S(2)}, u32[]{:S(2)}) collective-permute-start(bf16[6,64,2048]{2,1,0:T(8,128)(2,1)} %collective-permute-done.20.refs_1_), channel_id=1, source_target_pairs={{0,1},{1,0},{2,3},{3,2},{4,5},{5,4},{6,7},{7,6},{8,9},{9,8},{10,11... | collective-permute-start | bytes 4718600 | tf_op jit(solution)/shard_map/ppermute | solution.py:172
  128.2 30.5 %collective-permute-start.26 = (bf16[6,64,2048]{2,1,0:T(8,128)(2,1)}, bf16[6,64,2048]{2,1,0:T(8,128)(2,1)}, u32[]{:S(2)}, u32[]{:S(2)}) collective-permute-start(bf16[6,64,2048]{2,1,0:T(8,128)(2,1)} %add_convert_fusion.1), channel_id=1, source_target_pairs={{0,4},{1,3},{2,6},{3,1},{4,0},{5,7},{6,2},{7,5},{8,12},{9,11},{10,... | collective-permute-start | bytes 4718600 | tf_op jit(solution)/shard_map/ppermute | solution.py:172
  129.9 28.8 %collective-permute-start.28 = (bf16[6,64,2048]{2,1,0:T(8,128)(2,1)}, bf16[6,64,2048]{2,1,0:T(8,128)(2,1)}, u32[]{:S(2)}, u32[]{:S(2)}) collective-permute-start(bf16[6,64,2048]{2,1,0:T(8,128)(2,1)} %get-tuple-element.103), channel_id=1, source_target_pairs={{0,1},{1,0},{2,3},{3,2},{4,5},{5,4},{6,7},{7,6},{8,9},{9,8},{10,11... | collective-permute-start | bytes 4718600 | tf_op jit(solution)/shard_map/ppermute | solution.py:172
  131.0 27.7 %collective-permute-start.27 = (bf16[2,64,2048]{2,1,0:T(8,128)(2,1)}, bf16[2,64,2048]{2,1,0:T(8,128)(2,1)S(1)}, u32[]{:S(2)}, u32[]{:S(2)}) collective-permute-start(bf16[2,64,2048]{2,1,0:T(8,128)(2,1)} %add_convert_fusion.7), channel_id=1, source_target_pairs={{0,4},{1,3},{2,6},{3,1},{4,0},{5,7},{6,2},{7,5},{8,12},{9,11},{10,... | collective-permute-start | bytes 1572872 | tf_op jit(solution)/shard_map/ppermute | solution.py:172
  133.9 28.2 %collective-permute-start.21 = (bf16[2,64,2048]{2,1,0:T(8,128)(2,1)}, bf16[2,64,2048]{2,1,0:T(8,128)(2,1)}, u32[]{:S(2)}, u32[]{:S(2)}) collective-permute-start(bf16[2,64,2048]{2,1,0:T(8,128)(2,1)} %get-tuple-element.88), channel_id=1, source_target_pairs={{0,1},{1,0},{2,3},{3,2},{4,5},{5,4},{6,7},{7,6},{8,9},{9,8},{10,11... | collective-permute-start | bytes 1572872 | tf_op jit(solution)/shard_map/ppermute | solution.py:172
  161.9 15.0 %collective-permute-start.29 = (bf16[3,64,2048]{2,1,0:T(8,128)(2,1)}, bf16[3,64,2048]{2,1,0:T(8,128)(2,1)}, u32[]{:S(2)}, u32[]{:S(2)}) collective-permute-start(bf16[3,64,2048]{2,1,0:T(8,128)(2,1)} %add_convert_fusion.5), channel_id=1, source_target_pairs={{0,2},{1,5},{2,0},{3,7},{4,6},{5,1},{6,4},{7,3},{8,10},{9,13},{10,... | collective-permute-start | bytes 2359304 | tf_op jit(solution)/shard_map/ppermute | solution.py:172
  177.1 42.1 %collective-permute-start.40 = (bf16[6,64,2048]{2,1,0:T(8,128)(2,1)}, bf16[6,64,2048]{2,1,0:T(8,128)(2,1)}, u32[]{:S(2)}, u32[]{:S(2)}) collective-permute-start(bf16[6,64,2048]{2,1,0:T(8,128)(2,1)} %get-tuple-element.126), channel_id=1, source_target_pairs={{0,1},{1,0},{2,3},{3,2},{4,5},{5,4},{6,7},{7,6},{8,9},{9,8},{10,11... | collective-permute-start | bytes 4718600 | tf_op jit(solution)/shard_map/ppermute | solution.py:172
  180.9 20.1 %collective-permute-start.31 = (bf16[64,2048]{1,0:T(8,128)(2,1)}, bf16[64,2048]{1,0:T(8,128)(2,1)}, u32[]{:S(2)}, u32[]{:S(2)}) collective-permute-start(bf16[64,2048]{1,0:T(8,128)(2,1)} %get-tuple-element.141), channel_id=1, source_target_pairs={{0,8},{1,9},{2,10},{3,11},{4,12},{5,13},{6,14},{7,15},{8,16},{9,17... | collective-permute-start | bytes 786440 | tf_op jit(solution)/shard_map/ppermute | solution.py:172
  180.9 21.6 %collective-permute-start.32 = (bf16[64,2048]{1,0:T(8,128)(2,1)}, bf16[64,2048]{1,0:T(8,128)(2,1)}, u32[]{:S(2)}, u32[]{:S(2)}) collective-permute-start(bf16[64,2048]{1,0:T(8,128)(2,1)} %get-tuple-element.143), channel_id=1, source_target_pairs={{0,16},{1,17},{2,18},{3,19},{4,20},{5,21},{6,22},{7,23},{8,24},{9,... | collective-permute-start | bytes 786440 | tf_op jit(solution)/shard_map/ppermute | solution.py:172
  182.2 29.4 %collective-permute-start.33 = (bf16[64,2048]{1,0:T(8,128)(2,1)}, bf16[64,2048]{1,0:T(8,128)(2,1)}, u32[]{:S(2)}, u32[]{:S(2)}) collective-permute-start(bf16[64,2048]{1,0:T(8,128)(2,1)} %get-tuple-element.142), channel_id=1, source_target_pairs={{0,24},{1,25},{2,26},{3,27},{4,28},{5,29},{6,30},{7,31},{8,0},{9,1... | collective-permute-start | bytes 786440 | tf_op jit(solution)/shard_map/ppermute | solution.py:172
  198.0 21.2 %collective-permute-start.35 = (bf16[6,64,2048]{2,1,0:T(8,128)(2,1)}, bf16[6,64,2048]{2,1,0:T(8,128)(2,1)}, u32[]{:S(2)}, u32[]{:S(2)}) collective-permute-start(bf16[6,64,2048]{2,1,0:T(8,128)(2,1)} %add_convert_fusion), channel_id=1, source_target_pairs={{0,4},{1,3},{2,6},{3,1},{4,0},{5,7},{6,2},{7,5},{8,12},{9,11},{10,... | collective-permute-start | bytes 4718600 | tf_op jit(solution)/shard_map/ppermute | solution.py:172
  202.6 16.6 %collective-permute-start.38 = (f32[48,128]{1,0:T(8,128)S(1)}, f32[48,128]{1,0:T(8,128)S(1)}, u32[]{:S(2)}, u32[]{:S(2)}) collective-permute-start(f32[48,128]{1,0:T(8,128)S(1)} %pad_maximum_fusion.10), channel_id=1, source_target_pairs={{0,4},{1,5},{2,6},{3,7},{4,0},{5,1},{6,2},{7,3},{8,12},{9,13},{10,... | collective-permute-start | bytes 73736 | tf_op jit(solution)/shard_map/ppermute | solution.py:172
  223.5 17.3 %collective-permute-start.39 = (bf16[2,64,2048]{2,1,0:T(8,128)(2,1)}, bf16[2,64,2048]{2,1,0:T(8,128)(2,1)S(1)}, u32[]{:S(2)}, u32[]{:S(2)}) collective-permute-start(bf16[2,64,2048]{2,1,0:T(8,128)(2,1)} %get-tuple-element.114), channel_id=1, source_target_pairs={{0,1},{1,0},{2,3},{3,2},{4,5},{5,4},{6,7},{7,6},{8,9},{9,8},{10,11... | collective-permute-start | bytes 1572872 | tf_op jit(solution)/shard_map/ppermute | solution.py:172
  242.4 18.5 %collective-permute-start.46 = (bf16[64,2048]{1,0:T(8,128)(2,1)}, bf16[64,2048]{1,0:T(8,128)(2,1)}, u32[]{:S(2)}, u32[]{:S(2)}) collective-permute-start(bf16[64,2048]{1,0:T(8,128)(2,1)} %get-tuple-element.140), channel_id=1, source_target_pairs={{0,16},{1,17},{2,18},{3,19},{4,20},{5,21},{6,22},{7,23},{8,24},{9,... | collective-permute-start | bytes 786440 | tf_op jit(solution)/shard_map/ppermute | solution.py:172
  244.7 16.2 %collective-permute-start.47 = (bf16[64,2048]{1,0:T(8,128)(2,1)}, bf16[64,2048]{1,0:T(8,128)(2,1)}, u32[]{:S(2)}, u32[]{:S(2)}) collective-permute-start(bf16[64,2048]{1,0:T(8,128)(2,1)} %get-tuple-element.139), channel_id=1, source_target_pairs={{0,24},{1,25},{2,26},{3,27},{4,28},{5,29},{6,30},{7,31},{8,0},{9,1... | collective-permute-start | bytes 786440 | tf_op jit(solution)/shard_map/ppermute | solution.py:172
  (51 other events, 483.9 us)

commit v9 on v8

--- a/solution.py
+++ b/solution.py
@@ -412,60 +412,71 @@
     )(rows, gate_up_weight, down_weight)
 
 
-def backward_kernel(
-    units, grads_ref, gate_pre_ref, up_pre_ref, down_ref, gate_up_ref, rows_ref, joined_ref, input_ref, gain_ref
-):
+def inner_kernel(units, grads_ref, gate_pre_ref, up_pre_ref, down_ref, joined_ref):
     step = pl.program_id(0)
     block = gate_pre_ref.shape[1]
-
-    @pl.when(step < units)
-    def _():
-        gate_pre, up_pre = gate_pre_ref[...], up_pre_ref[...]
-        sigmoid_gate = jax.nn.sigmoid(gate_pre)
-        common = times_transposed(grads_ref[...], down_ref[0]) * sigmoid_gate
-        gate_grad = common * up_pre * (1.0 + gate_pre * (1.0 - sigmoid_gate))
-        start = pl.multiple_of(step * block, block)
-        joined_ref[:, pl.ds(start, block)] = gate_grad.astype(jnp.bfloat16)
-        joined_ref[:, pl.ds(units * block + start, block)] = (common * gate_pre).astype(jnp.bfloat16)
-
-    @pl.when(step >= units)
-    def _():
-        input_grad = times_transposed(joined_ref[...], gate_up_ref[0]).astype(jnp.bfloat16)
-        input_ref[...] = input_grad
-        terms = input_grad.astype(jnp.float32) * rows_ref[...].astype(jnp.float32)
-        gain_ref[...] = jnp.sum(terms, axis=0, keepdims=True)
-
-
-def backward(grads, gate_pre, up_pre, rows, gate_up_weight, down_weight):
-    slots, features = rows.shape
+    gate_pre, up_pre = gate_pre_ref[...], up_pre_ref[...]
+    sigmoid_gate = jax.nn.sigmoid(gate_pre)
+    common = times_transposed(grads_ref[...], down_ref[0]) * sigmoid_gate
+    gate_grad = common * up_pre * (1.0 + gate_pre * (1.0 - sigmoid_gate))
+    start = pl.multiple_of(step * block, block)
+    joined_ref[:, pl.ds(start, block)] = gate_grad.astype(jnp.bfloat16)
+    joined_ref[:, pl.ds(units * block + start, block)] = (common * gate_pre).astype(jnp.bfloat16)
+
+
+def backward_hidden(grads, gate_pre, up_pre, down_weight):
+    slots, features = grads.shape
     width = down_weight.shape[1]
-    block, units, wide = 256, width // 256, features // 4
-    early = lambda i: jnp.minimum(i, units - 1)
-    late = lambda i: jnp.maximum(i - units, 0)
+    block, units = 256, width // 256
     return pl.pallas_call(
-        functools.partial(backward_kernel, units),
-        grid=(units + 4,),
+        functools.partial(inner_kernel, units),
+        grid=(units,),
         in_specs=[
             pl.BlockSpec((slots, features), lambda i: (0, 0)),
-            pl.BlockSpec((slots, block), lambda i: (0, early(i))),
-            pl.BlockSpec((slots, block), lambda i: (0, early(i))),
-            pl.BlockSpec((1, block, features), lambda i: (0, early(i), 0)),
-            pl.BlockSpec((1, wide, 2 * width), lambda i: (0, late(i), 0)),
-            pl.BlockSpec((slots, wide), lambda i: (0, late(i))),
+            pl.BlockSpec((slots, block), lambda i: (0, i)),
+            pl.BlockSpec((slots, block), lambda i: (0, i)),
+            pl.BlockSpec((1, block, features), lambda i: (0, i, 0)),
         ],
+        out_specs=pl.BlockSpec((slots, 2 * width), lambda i: (0, 0)),
+        out_shape=jax.ShapeDtypeStruct((slots, 2 * width), jnp.bfloat16),
+        compiler_params=pltpu.CompilerParams(vmem_limit_bytes=VMEM_LIMIT),
+        cost_estimate=LITTLE,
+    )(grads, gate_pre, up_pre, down_weight)
+
+
+def input_kernel(joined_ref, gate_up_ref, rows_ref, *refs):
+    input_ref, gain_ref = refs[-2:]
+    input_grad = times_transposed(joined_ref[...], gate_up_ref[0]).astype(jnp.bfloat16)
+    input_ref[...] = input_grad
+    terms = input_grad.astype(jnp.float32) * rows_ref[...].astype(jnp.float32)
+    gain_ref[...] = jnp.sum(terms, axis=0, keepdims=True)
+
+
+def backward_input(joined_grad, gate_up_weight, rows, part, held):
+    slots, features = rows.shape
+    width = joined_grad.shape[1]
+    wide = features // 4
+    first = 2 * part
+    return pl.pallas_call(
+        input_kernel,
+        grid=(2,),
+        in_specs=[
+            pl.BlockSpec((slots, width), lambda i: (0, 0)),
+            pl.BlockSpec((1, wide, width), lambda i: (0, first + i, 0)),
+            pl.BlockSpec((slots, wide), lambda i: (0, first + i)),
+        ] + [pl.BlockSpec(memory_space=pl.ANY)] * len(held),
         out_specs=[
-            pl.BlockSpec((slots, 2 * width), lambda i: (0, 0)),
-            pl.BlockSpec((slots, wide), lambda i: (0, late(i))),
-            pl.BlockSpec((1, wide), lambda i: (0, late(i))),
+            pl.BlockSpec((slots, wide), lambda i: (0, first + i)),
+            pl.BlockSpec((1, wide), lambda i: (0, i)),
         ],
         out_shape=[
-            jax.ShapeDtypeStruct((slots, 2 * width), jnp.bfloat16),
             jax.ShapeDtypeStruct((slots, features), jnp.bfloat16),
-            jax.ShapeDtypeStruct((1, features), jnp.float32),
+            jax.ShapeDtypeStruct((1, features // 2), jnp.float32),
         ],
+        input_output_aliases={3 + n: n for n in range(len(held))},
         compiler_params=pltpu.CompilerParams(vmem_limit_bytes=VMEM_LIMIT),
         cost_estimate=LITTLE,
-    )(grads, gate_pre, up_pre, down_weight, gate_up_weight, rows)
+    )(joined_grad, gate_up_weight, rows, *held)
 
 
 def pack(columns, gains):
@@ -537,88 +548,84 @@
 
     rows = rows.reshape(-1, features)
     gate_pre, up_pre, hidden, block_out = forward(rows, gate_up_weight, down_weight)
-    block_out, cot_far_pair = together(block_out, cot_far_pair)
-    cot_pieces = (cot_pair, cot_far_pair, send_core(cot_pair), send_core(cot_far_pair))
     out_slots = block_out.reshape(expert_size, capacity, features)
     out_mine, out_low, out_high = expand(back, slot_prob, (out_slots,), (True,), steps - 1, 0)
+    out_high, cot_far_pair = together(out_high, cot_far_pair)
+    cot_pieces = (cot_pair, cot_far_pair, send_core(cot_pair), send_core(cot_far_pair))
 
     half_far, one_far = 2 * (steps - 1), steps - 1
-    own_mine, own_low, own_high = expand(
-        back, after(slot_prob, out_high), (out_slots,), (True,), 1, far
-    )
-    own_core_high = send_core(own_high)
-    own_core = send_core(own_low)
     held = select_grads(
         after(pick, out_high), slot_prob, out_slots, near_pieces, 1, 2, 1, far, ()
     )
-    out_core_high = after(send_core(out_high), own_high, held[1])
+    out_core_high = after(send_core(out_high), held[1])
     out_core = send_core(out_low)
     out_upper = narrow(add_up(out_mine[half_far:], out_core_high))
     out_first = send_first(out_upper)
-    own_upper = narrow(add_up(own_mine[2:], after(own_core_high, out_upper)))
-    own_first = send_first(own_upper)
     grads, prob_value = select_grads(
-        after(pick, own_upper), slot_prob, out_slots, cot_pieces, steps - 1, 1, 0, 0, tuple(held)
+        after(pick, out_upper), slot_prob, out_slots, cot_pieces, steps - 1, 1, 0, 0, tuple(held)
     )
     grads = grads.reshape(-1, features)
-    joined_grad, input_grad, gain_term = backward(
-        grads, gate_pre, up_pre, rows, gate_up_weight, down_weight
-    )
-    input_grad, out_first, own_first = together(input_grad, out_first, own_first)
-    input_slots = input_grad.reshape(expert_size, capacity, features)
+    joined_grad = backward_hidden(grads, gate_pre, up_pre, down_weight)
+    input_grad, gain_low = backward_input(joined_grad, gate_up_weight, rows, 0, ())
+    out_first, gain_low = together(out_first, gain_low)
     out_middle = narrow(
         add_up(out_mine[one_far:half_far], out_core[one_far:half_far], out_first[one_far:])
     )
     out_second = send_second(out_middle)
-    in_mine, in_low, in_high = expand(back, after(slot_prob, out_middle), (input_slots,), (False,), steps - 1, 0)
-    own_middle = narrow(add_up(own_mine[1:2], own_core[1:], own_first[1:]))
-    own_second = send_second(own_middle)
-    in_high, out_second, own_second = together(in_high, out_second, own_second)
+    input_grad, gain_high = backward_input(
+        joined_grad, gate_up_weight, after(rows, out_middle), 1, (input_grad,)
+    )
+    gain_term = jnp.concatenate([gain_low[0], gain_high[0]])
+    input_slots = input_grad.reshape(expert_size, capacity, features)
+    in_mine, in_low, in_high = expand(back, slot_prob, (input_slots,), (False,), steps - 1, 0)
+    in_high, out_second = together(in_high, out_second)
     in_core_high = send_core(in_high)
     in_core = send_core(in_low)
+
     def own_plane(mine, core_part, first_part, second_part, count):
         return add_up(mine[:count], core_part[:count], first_part[:count], second_part[:count])
 
     out_planes = narrow(own_plane(out_mine, out_core, out_first, out_second, one_far))
     out_far = [send_along(out_planes[step - 1], step) for step in range(1, steps)]
+    in_upper = narrow(add_up(in_mine[half_far:], after(in_core_high, out_planes)))
+    in_first = send_first(in_upper)
     near_mine, near_low, near_high = expand(
-        back, after(slot_prob, in_high), (input_slots,), (False,), 1, far
+        back, after(slot_prob, in_upper), (out_slots, input_slots), (True, False), 1, far
     )
     near_core_high = send_core(near_high)
     near_core = send_core(near_low)
-    in_upper = narrow(add_up(in_mine[half_far:], after(in_core_high, out_middle, near_high)))
-    in_first = send_first(in_upper)
-    gains = (gain_term[0] / gain).reshape(-1, 128)
+    gains = (gain_term / gain).reshape(-1, 128)
     prob_rows = jnp.sum(jnp.where(placed, prob_value, 0.0), axis=1)
     columns = from_far_first(jnp.where(matches, prob_rows[:, None, :], 0.0), steps)
     columns = jnp.where(core == 0, columns, jnp.swapaxes(columns, 0, 1))
     got = send_core(after(pack(columns[..., half:], gains), in_upper))
     down_part = outer_sum(after(hidden, in_upper), grads)
 
-    down_part, got = together(down_part, got)
+    middle = len(out_far) // 2
+    down_part, got, out_far[middle] = together(down_part, got, out_far[middle])
     columns, gains = unpack_add(columns[..., :half], gains, got)
     got = send_bit(pack(columns[1], gains), 2)
-    gate_up_part = outer_sum(after(rows, in_upper), joined_grad)
-    in_first, near_core, gate_up_part, got = together(
-        in_first, near_core, gate_up_part, got, *out_far
-    )[:4]
+    gate_up_part = outer_sum(after(rows, near_high, down_part), joined_grad)
+    gate_up_part, got = together(gate_up_part, got)
+    columns, gains = unpack_add(columns[0], gains, got)
+    got = send_bit(pack(columns[1], gains), 1)
+    in_first, near_core, got = together(in_first, near_core, got, *out_far)[:3]
     columns, gains = unpack_add(columns[0], gains, got)
     in_middle = narrow(
         add_up(in_mine[one_far:half_far], in_core[one_far:half_far], in_first[one_far:])
     )
     in_second = send_second(in_middle)
-    got = send_bit(pack(columns[1], gains), 1)
-    in_second, got = together(in_second, got)
-    columns, gains = unpack_add(columns[0], gains, got)
+    messages = [send_along(pack(columns[step], gains), step) for step in range(1, steps)]
+    in_second, *messages = together(in_second, *messages)
     in_planes = narrow(own_plane(in_mine, in_core, in_first, in_second, one_far))
-    messages = [send_along(pack(columns[step], gains), step) for step in range(1, steps)]
     in_far = [send_along(in_planes[step - 1], step) for step in range(1, steps)]
-    near_upper = narrow(add_up(near_mine[2:], after(near_core_high, in_planes)))
+    near_upper = narrow(add_up(near_mine[4:], after(near_core_high, in_planes)))
     near_first = send_first(near_upper)
-    near_middle = narrow(add_up(near_mine[1:2], near_core[1:], near_first[1:]))
+    near_middle = narrow(add_up(near_mine[2:4], near_core[2:], near_first[2:]))
     near_second = send_second(near_middle)
-    out_sum = own_plane(own_mine, own_core, own_first, own_second, 1)[0] + add_up(*out_far)
-    normed_grad = own_plane(near_mine, near_core, near_first, near_second, 1)[0] + add_up(*in_far)
+    near_sum = own_plane(near_mine, near_core, near_first, near_second, 2)
+    out_sum = near_sum[0] + add_up(*out_far)
+    normed_grad = near_sum[1] + add_up(*in_far)
 
     prob_sum, all_gains = columns[0], [gains]
     for message in messages:

time: 269 us -> 251 us (0.933); the launches traced: 265 us -> 250 us
  other arithmetic: 39 us -> 31.7 us
  starting transfers between devices: 53.2 us -> 46.3 us
  local copies, waits for them, and re-layouts: 15.6 us -> 11.9 us
    ppermute x51 -> x47, starting transfers between devices: 53.2 us -> 46.3 us  [send(): return lax.ppermute(array, BOTH, pairs)]
    pallas_call x1 -> x3, Pallas kernels: 16.3 us -> 21.2 us  [the longest x2 12.6 us: backward_input(): pl.pallas_call(input_kernel, grid=(2,), in_specs=[pl.BlockSpec((slots, wi...]
    convert_element_type x10 -> x8, other arithmetic: 21.1 us -> 18.2 us  [narrow(): return value.astype(jnp.bfloat16)]
    pallas_call x4 -> x3, Pallas kernels: 22.3 us -> 19.5 us  [expand(): pl.pallas_call(functools.partial(expand_kernel, weighted, count, first_gr...]
    ppermute x51 -> x47, waiting for transfers between devices: 70 us -> 70.9 us  [send(): return lax.ppermute(array, BOTH, pairs)]
  transfers between devices with their start and end apart: 51 -> 47, of which waited for: 17 -> 18; matrix products, arithmetic and copies ran while one was open for 21% -> 18% of each run, Pallas kernels for 25% -> 30%
where the time goes in v9:
time: 251 us; the launch traced here: 250 us
  Pallas kernels  74.9 us (30%)
  waiting for transfers between devices  70.9 us (28%)
  starting transfers between devices  46.3 us (18%)
  other arithmetic  31.7 us (13%)
  matrix products  13.6 us (5%)
  local copies, waits for them, and re-layouts  11.9 us (5%)
    ppermute x47, waiting for transfers between devices, send(): return lax.ppermute(array, BOTH, pairs)  70.9 us
    ppermute x47, starting transfers between devices, send(): return lax.ppermute(array, BOTH, pairs)  46.3 us
    pallas_call x4, Pallas kernels, select(): pl.pallas_call(functools.partial(kernel, count), grid=(4,), in_specs=[gro...  21.3 us
    pallas_call x3, Pallas kernels, expand(): pl.pallas_call(functools.partial(expand_kernel, weighted, count, first_gr...  19.5 us
    convert_element_type x8, other arithmetic, narrow(): return value.astype(jnp.bfloat16)  18.2 us
    dot_general x2, matrix products, outer_sum(): lax.dot_general(left, right, (((0,), (0,)), ((), ())), preferred_element_...  13.4 us
    pallas_call x1, Pallas kernels, forward(): pl.pallas_call(forward_kernel, grid=(2,), in_specs=[row_spec(features), p...  13 us
    pallas_call x2, Pallas kernels, backward_input(): pl.pallas_call(input_kernel, grid=(2,), in_specs=[pl.BlockSpec((slots, wi...  12.6 us
  transfers between devices with their start and end apart: 47, of which 18 were waited for; matrix products, arithmetic and copies ran while one was open for 18% of the time, Pallas kernels for 30%

profile of v9, /device:TPU:0, one launch (start us, length us, event | category | flops | bytes accessed | tf_op | source)
XLA Modules:
  0.0 250.4 jit_solution(17198529721846472107)
XLA Ops:
  1.7 3.0 %collective-permute-start = (bf16[2,64,2048]{2,1,0:T(8,128)(2,1)S(1)}, bf16[2,64,2048]{2,1,0:T(8,128)(2,1)S(1)}, u32[]{:S(2)}, u32[]{:S(2)}) collective-permute-start(bf16[2,64,2048]{2,1,0:T(8,128)(2,1)S(1)} %pad_maximum_fusion.3), channel_id=1, source_target_pairs={{0,2},{1,5},{2,0},{3,7},{4,6},{5,1},{6,4},{7,3},{8,10},{9,13},{10,... | collective-permute-start | bytes 1572872 | tf_op jit(solution)/shard_map/ppermute | solution.py:172
  19.6 11.8 %collective-permute-done.4 = bf16[64,2048]{1,0:T(8,128)(2,1)S(1)} collective-permute-done((bf16[64,2048]{1,0:T(8,128)(2,1)}, bf16[64,2048]{1,0:T(8,128)(2,1)S(1)}, u32[]{:S(2)}, u32[]{:S(2)}) %collective-permute-start.4) | collective-permute-done | bytes 262176 | tf_op jit(solution)/shard_map/ppermute | solution.py:172
  39.0 9.9 %collective-permute-done.7 = f32[2,2,16,128]{3,2,1,0:T(8,128)S(1)} collective-permute-done((f32[2,2,16,128]{3,2,1,0:T(8,128)S(1)}, f32[2,2,16,128]{3,2,1,0:T(8,128)S(1)}, u32[]{:S(2)}, u32[]{:S(2)}) %collective-permute-start.7) | collective-permute-done | bytes 32800 | tf_op jit(solution)/shard_map/ppermute | solution.py:172
  56.2 4.3 %shard_map.118.refs_5_ = bf16[16,48,2048]{2,1,0:T(8,128)(2,1)} custom-call(bf16[16,48,128]{2,1,0:T(8,128)(2,1)} %fusion.15.pick_ref, bf16[4,64,2048]{2,1,0:T(8,128)(2,1)} %copy-done.1, bf16[4,64,2048]{2,1,0:T(8,128)(2,1)} %copy-done.3, bf16[4,64,2048]{2,1,0:T(8,128)(2,1)} %copy-done.4, bf16[4,64,2048]{2,1,0:T(8,128)(2,1)} %collective-permute-done.16.refs_3_, ...), custom_call_target="tpu_custom_call" | custom-call | flops 1000000 | bytes 100000 | tf_op jit(solution)/shard_map/pallas_call | solution.py:281
  61.2 5.0 %collective-permute-done.14 = bf16[64,2048]{1,0:T(8,128)(2,1)} collective-permute-done((bf16[64,2048]{1,0:T(8,128)(2,1)S(1)}, bf16[64,2048]{1,0:T(8,128)(2,1)}, u32[]{:S(2)}, u32[]{:S(2)}) %collective-permute-start.14) | collective-permute-done | bytes 262176 | tf_op jit(solution)/shard_map/ppermute | solution.py:172
  67.4 3.3 %collective-permute-done.12.refs_1_ = bf16[6,64,2048]{2,1,0:T(8,128)(2,1)} collective-permute-done((bf16[6,64,2048]{2,1,0:T(8,128)(2,1)}, bf16[6,64,2048]{2,1,0:T(8,128)(2,1)}, u32[]{:S(2)}, u32[]{:S(2)}) %collective-permute-start.12) | collective-permute-done | bytes 1572896 | tf_op jit(solution)/shard_map/ppermute | solution.py:172
  74.5 6.0 %shard_map.119 = bf16[16,48,2048]{2,1,0:T(8,128)(2,1)} custom-call(bf16[16,48,128]{2,1,0:T(8,128)(2,1)} %fusion.15.pick_ref, bf16[6,64,2048]{2,1,0:T(8,128)(2,1)} %constant_dynamic-update-slice_fusion.refs_0_, bf16[6,64,2048]{2,1,0:T(8,128)(2,1)} %collective-permute-done.12.refs_1_, ...), custom_call_target="tpu_custom_call", output_to_operand_aliasing={{}: (6, {})} | custom-call | flops 1000000 | bytes 100000 | tf_op jit(solution)/shard_map/pallas_call | solution.py:281
  89.4 13.0 %shard_map.120 = (f32[768,768]{1,0:T(8,128)}, f32[768,768]{1,0:T(8,128)}, bf16[768,768]{1,0:T(8,128)(2,1)}, bf16[768,2048]{1,0:T(8,128)(2,1)}) custom-call(bf16[768,2048]{1,0:T(8,128)(2,1)} %bitcast.115, bf16[1,2048,1536]{2,1,0:T(8,128)(2,1)} %gate_up_ref.5, bf16[1,768,2048]{2,1,0:T(8,128)(2,1)} %down_ref.3), custom_call_target="tpu_custom_call" | custom-call | flops 1000000 | bytes 100000 | tf_op jit(solution)/shard_map/pallas_call | solution.py:395
  102.4 7.4 %shard_map.121 = (bf16[12,64,2048]{2,1,0:T(8,128)(2,1)}, bf16[6,64,2048]{2,1,0:T(8,128)(2,1)}, bf16[6,64,2048]{2,1,0:T(8,128)(2,1)}) custom-call(bf16[16,128,48]{2,1,0:T(8,128)(2,1)} %fusion.1.back_ref, f32[16,48,1]{2,1,0:T(8,128)} %copy.23.prob_ref.refs_4_, bf16[16,48,2048]{2,1,0:T(8,128)(2,1)} %bitcast.119), custom_call_target="tpu_custom_call" | custom-call | flops 1000000 | bytes 100000 | tf_op jit(solution)/shard_map/pallas_call | solution.py:360
  110.4 4.5 %shard_map.122 = (bf16[16,48,2048]{2,1,0:T(8,128)(2,1)}, f32[16,48,1]{2,1,0:T(8,128)}) custom-call(bf16[16,48,128]{2,1,0:T(8,128)(2,1)} %fusion.15.pick_ref, bf16[4,64,2048]{2,1,0:T(8,128)(2,1)} %copy-done.1, bf16[4,64,2048]{2,1,0:T(8,128)(2,1)} %copy-done.3, bf16[4,64,2048]{2,1,0:T(8,128)(2,1)} %copy-done.4, ...), custom_call_target="tpu_custom_call" | custom-call | flops 1000000 | bytes 100000 | tf_op jit(solution)/shard_map/pallas_call | solution.py:281
  114.9 3.7 %add_convert_fusion.1 = bf16[6,64,2048]{2,1,0:T(8,128)(2,1)} fusion(bf16[6,64,2048]{2,1,0:T(8,128)(2,1)} %collective-permute-done.21, bf16[12,64,2048]{2,1,0:T(8,128)(2,1)} %get-tuple-element.81), kind=kLoop, calls=%fused_computation.4 | loop fusion | flops 3145728 | bytes 4718592 | tf_op jit(solution)/shard_map/convert_element_type | solution.py:209
  120.8 6.5 %shard_map.123 = (bf16[16,48,2048]{2,1,0:T(8,128)(2,1)}, f32[16,48,1]{2,1,0:T(8,128)}) custom-call(bf16[16,48,128]{2,1,0:T(8,128)(2,1)} %fusion.15.pick_ref, bf16[6,64,2048]{2,1,0:T(8,128)(2,1)} %constant_dynamic-update-slice_fusion.2.refs_0_, bf16[6,64,2048]{2,1,0:T(8,128)(2,1)} %collective-permute-done.20.refs_1_, ...), custom_call_target="tpu_custom_call", output_to_operand_aliasing={{0}: (7, {}), {1}: (8, {})} | custom-call | flops 1000000 | bytes 100000 | tf_op jit(solution)/shard_map/pallas_call | solution.py:281
  127.3 8.6 %shard_map.124.joined_ref = bf16[768,1536]{1,0:T(8,128)(2,1)} custom-call(bf16[768,2048]{1,0:T(8,128)(2,1)} %bitcast.125, f32[768,768]{1,0:T(8,128)} %get-tuple-element.92.gate_pre_ref, f32[768,768]{1,0:T(8,128)} %get-tuple-element.93.up_pre_ref, bf16[1,768,2048]{2,1,0:T(8,128)(2,1)} %down_ref.3), custom_call_target="tpu_custom_call" | custom-call | flops 1000000 | bytes 100000 | tf_op jit(solution)/shard_map/pallas_call | solution.py:431
  135.9 6.3 %shard_map.125 = (bf16[768,2048]{1,0:T(8,128)(2,1)}, f32[1,1024]{1,0:T(1,128)}) custom-call(bf16[768,1536]{1,0:T(8,128)(2,1)} %shard_map.124.joined_ref, bf16[1,2048,1536]{2,1,0:T(8,128)(2,1)} %gate_up_ref.5, bf16[768,2048]{1,0:T(8,128)(2,1)} %bitcast.116), custom_call_target="tpu_custom_call" | custom-call | flops 1000000 | bytes 100000 | tf_op jit(solution)/shard_map/pallas_call | solution.py:460
  146.1 6.3 %shard_map.126 = (bf16[768,2048]{1,0:T(8,128)(2,1)}, f32[1,1024]{1,0:T(1,128)}) custom-call(bf16[768,1536]{1,0:T(8,128)(2,1)} %shard_map.124.joined_ref, bf16[1,2048,1536]{2,1,0:T(8,128)(2,1)} %gate_up_ref.5, bf16[768,2048]{1,0:T(8,128)(2,1)} %bitcast.117, bf16[768,2048]{1,0:T(8,128)(2,1)} %get-tuple-element.98.refs_0_), custom_call_target="tpu_custom_call", output_to_operand_aliasing={{0}: (3, {})} | custom-call | flops 1000000 | bytes 100000 | tf_op jit(solution)/shard_map/pallas_call | solution.py:460
  152.5 6.5 %shard_map.127 = (bf16[12,64,2048]{2,1,0:T(8,128)(2,1)}, bf16[6,64,2048]{2,1,0:T(8,128)(2,1)}, bf16[6,64,2048]{2,1,0:T(8,128)(2,1)}) custom-call(bf16[16,128,48]{2,1,0:T(8,128)(2,1)} %fusion.1.back_ref, f32[16,48,1]{2,1,0:T(8,128)} %copy.23.prob_ref.refs_4_, bf16[16,48,2048]{2,1,0:T(8,128)(2,1)} %bitcast.123), custom_call_target="tpu_custom_call" | custom-call | flops 1000000 | bytes 100000 | tf_op jit(solution)/shard_map/pallas_call | solution.py:360
  167.7 4.3 %convolution_convert_fusion.1 = bf16[768,2048]{1,0:T(8,128)(2,1)} fusion(bf16[768,768]{1,0:T(8,128)(2,1)S(1)} %copy-done.16, bf16[768,2048]{1,0:T(8,128)(2,1)S(1)} %bitcast.126), kind=kOutput, calls=%fused_computation.2 | convolution fusion | flops 2417491968 | bytes 7471104 | tf_op jit(solution)/shard_map/dot_general | solution.py:38
  173.0 5.6 %shard_map.128 = (bf16[8,64,2048]{2,1,0:T(8,128)(2,1)}, bf16[4,64,2048]{2,1,0:T(8,128)(2,1)}, bf16[4,64,2048]{2,1,0:T(8,128)(2,1)}) custom-call(bf16[16,128,48]{2,1,0:T(8,128)(2,1)} %fusion.1.back_ref, f32[16,48,1]{2,1,0:T(8,128)} %copy.24.prob_ref, bf16[16,48,2048]{2,1,0:T(8,128)(2,1)} %bitcast.122, bf16[16,48,2048]{2,1,0:T(8,128)(2,1)} %bitcast.124), custom_call_target="tpu_custom_call" | custom-call | flops 1000000 | bytes 100000 | tf_op jit(solution)/shard_map/pallas_call | solution.py:360
  178.6 3.3 %collective-permute-done.31 = bf16[64,2048]{1,0:T(8,128)(2,1)} collective-permute-done((bf16[64,2048]{1,0:T(8,128)(2,1)}, bf16[64,2048]{1,0:T(8,128)(2,1)}, u32[]{:S(2)}, u32[]{:S(2)}) %collective-permute-start.31) | collective-permute-done | bytes 262176 | tf_op jit(solution)/shard_map/ppermute | solution.py:172
  183.7 9.1 %convolution_convert_fusion = bf16[2048,1536]{1,0:T(8,128)(2,1)} fusion(bf16[768,2048]{1,0:T(8,128)(2,1)} %bitcast.118, bf16[768,1536]{1,0:T(8,128)(2,1)} %shard_map.124.joined_ref), kind=kOutput, calls=%fused_computation.1 | convolution fusion | flops 4834983936 | bytes 11796480 | tf_op jit(solution)/shard_map/dot_general | solution.py:38
  193.7 7.5 %collective-permute-done.35 = bf16[64,2048]{1,0:T(8,128)(2,1)S(1)} collective-permute-done((bf16[64,2048]{1,0:T(8,128)(2,1)S(1)}, bf16[64,2048]{1,0:T(8,128)(2,1)S(1)}, u32[]{:S(2)}, u32[]{:S(2)}) %collective-permute-start.35) | collective-permute-done | bytes 262176 | tf_op jit(solution)/shard_map/ppermute | solution.py:172
  211.4 4.8 %collective-permute-done.38 = bf16[3,64,2048]{2,1,0:T(8,128)(2,1)} collective-permute-done((bf16[3,64,2048]{2,1,0:T(8,128)(2,1)S(1)}, bf16[3,64,2048]{2,1,0:T(8,128)(2,1)}, u32[]{:S(2)}, u32[]{:S(2)}) %collective-permute-start.38) | collective-permute-done | bytes 786464 | tf_op jit(solution)/shard_map/ppermute | solution.py:172
  225.8 9.1 %collective-permute-done.42 = bf16[4,64,2048]{2,1,0:T(8,128)(2,1)S(1)} collective-permute-done((bf16[4,64,2048]{2,1,0:T(8,128)(2,1)}, bf16[4,64,2048]{2,1,0:T(8,128)(2,1)S(1)}, u32[]{:S(2)}, u32[]{:S(2)}) %collective-permute-start.42) | collective-permute-done | bytes 1048608 | tf_op jit(solution)/shard_map/ppermute | solution.py:172
  238.3 7.3 %collective-permute-done.43 = bf16[2,64,2048]{2,1,0:T(8,128)(2,1)S(1)} collective-permute-done((bf16[2,64,2048]{2,1,0:T(8,128)(2,1)S(1)}, bf16[2,64,2048]{2,1,0:T(8,128)(2,1)S(1)}, u32[]{:S(2)}, u32[]{:S(2)}) %collective-permute-start.43) | collective-permute-done | bytes 524320 | tf_op jit(solution)/shard_map/ppermute | solution.py:172
  (205 shorter events, 92.2 us)
Async XLA Ops:
  4.7 14.2 %collective-permute-start.5 = (bf16[64,2048]{1,0:T(8,128)(2,1)}, bf16[64,2048]{1,0:T(8,128)(2,1)S(1)}, u32[]{:S(2)}, u32[]{:S(2)}) collective-permute-start(bf16[64,2048]{1,0:T(8,128)(2,1)} %param.7), channel_id=1, source_target_pairs={{0,8},{1,9},{2,10},{3,11},{4,12},{5,13},{6,14},{7,15},{8,16},{9,17... | collective-permute-start | bytes 786440 | tf_op jit(solution)/shard_map/ppermute | solution.py:172
  8.5 22.9 %collective-permute-start.4 = (bf16[64,2048]{1,0:T(8,128)(2,1)}, bf16[64,2048]{1,0:T(8,128)(2,1)S(1)}, u32[]{:S(2)}, u32[]{:S(2)}) collective-permute-start(bf16[64,2048]{1,0:T(8,128)(2,1)} %param.7), channel_id=1, source_target_pairs={{0,16},{1,17},{2,18},{3,19},{4,20},{5,21},{6,22},{7,23},{8,24},{9,... | collective-permute-start | bytes 786440 | tf_op jit(solution)/shard_map/ppermute | solution.py:172
  15.1 33.8 %collective-permute-start.10 = (bf16[4,64,2048]{2,1,0:T(8,128)(2,1)S(1)}, bf16[4,64,2048]{2,1,0:T(8,128)(2,1)S(1)}, u32[]{:S(2)}, u32[]{:S(2)}) collective-permute-start(bf16[4,64,2048]{2,1,0:T(8,128)(2,1)S(1)} %pad_maximum_fusion.refs_0_), channel_id=1, source_target_pairs={{0,4},{1,3},{2,6},{3,1},{4,0},{5,7},{6,2},{7,5},{8,12},{9,11},{10,... | collective-permute-start | bytes 3145736 | tf_op jit(solution)/shard_map/ppermute | solution.py:172
  16.8 14.7 %collective-permute-start.2 = (f32[2,16,128]{2,1,0:T(8,128)S(1)}, f32[2,16,128]{2,1,0:T(8,128)S(1)}, u32[]{:S(2)}, u32[]{:S(2)}) collective-permute-start(f32[2,16,128]{2,1,0:T(8,128)S(1)} %get-tuple-element.148), channel_id=1, source_target_pairs={{0,4},{1,3},{2,6},{3,1},{4,0},{5,7},{6,2},{7,5},{8,12},{9,11},{10,... | collective-permute-start | bytes 49160 | tf_op jit(solution)/shard_map/ppermute | solution.py:172
  31.6 17.4 %collective-permute-start.9 = (bf16[3,64,2048]{2,1,0:T(8,128)(2,1)S(1)}, bf16[3,64,2048]{2,1,0:T(8,128)(2,1)S(1)}, u32[]{:S(2)}, u32[]{:S(2)}) collective-permute-start(bf16[3,64,2048]{2,1,0:T(8,128)(2,1)S(1)} %pad_maximum_fusion.1), channel_id=1, source_target_pairs={{0,2},{1,5},{2,0},{3,7},{4,6},{5,1},{6,4},{7,3},{8,10},{9,13},{10,... | collective-permute-start | bytes 2359304 | tf_op jit(solution)/shard_map/ppermute | solution.py:172
  34.7 14.2 %collective-permute-start.11 = (bf16[64,2048]{1,0:T(8,128)(2,1)S(1)}, bf16[64,2048]{1,0:T(8,128)(2,1)S(1)}, u32[]{:S(2)}, u32[]{:S(2)}) collective-permute-start(bf16[64,2048]{1,0:T(8,128)(2,1)S(1)} %copy-done.6), channel_id=1, source_target_pairs={{0,16},{1,17},{2,18},{3,19},{4,20},{5,21},{6,22},{7,23},{8,24},{9,... | collective-permute-start | bytes 786440 | tf_op jit(solution)/shard_map/ppermute | solution.py:172
  34.7 14.2 %collective-permute-start.7 = (f32[2,2,16,128]{3,2,1,0:T(8,128)S(1)}, f32[2,2,16,128]{3,2,1,0:T(8,128)S(1)}, u32[]{:S(2)}, u32[]{:S(2)}) collective-permute-start(f32[2,2,16,128]{3,2,1,0:T(8,128)S(1)} %pad_maximum_fusion.8), channel_id=1, source_target_pairs={{0,16},{1,17},{2,18},{3,19},{4,20},{5,21},{6,22},{7,23},{8,24},{9,... | collective-permute-start | bytes 98312 | tf_op jit(solution)/shard_map/ppermute | solution.py:172
  50.0 20.7 %collective-permute-start.12 = (bf16[6,64,2048]{2,1,0:T(8,128)(2,1)}, bf16[6,64,2048]{2,1,0:T(8,128)(2,1)}, u32[]{:S(2)}, u32[]{:S(2)}) collective-permute-start(bf16[6,64,2048]{2,1,0:T(8,128)(2,1)} %constant_dynamic-update-slice_fusion.refs_0_), channel_id=1, source_target_pairs={{0,4},{1,3},{2,6},{3,1},{4,0},{5,7},{6,2},{7,5},{8,12},{9,11},{10,... | collective-permute-start | bytes 4718600 | tf_op jit(solution)/shard_map/ppermute | solution.py:172
  55.2 18.7 %collective-permute-start.17 = (bf16[6,64,2048]{2,1,0:T(8,128)(2,1)}, bf16[6,64,2048]{2,1,0:T(8,128)(2,1)}, u32[]{:S(2)}, u32[]{:S(2)}) collective-permute-start(bf16[6,64,2048]{2,1,0:T(8,128)(2,1)} %constant_dynamic-update-slice_fusion.refs_0_), channel_id=1, source_target_pairs={{0,1},{1,0},{2,3},{3,2},{4,5},{5,4},{6,7},{7,6},{8,9},{9,8},{10,11... | collective-permute-start | bytes 4718600 | tf_op jit(solution)/shard_map/ppermute | solution.py:172
  85.1 24.6 %collective-permute-start.20 = (bf16[6,64,2048]{2,1,0:T(8,128)(2,1)}, bf16[6,64,2048]{2,1,0:T(8,128)(2,1)}, u32[]{:S(2)}, u32[]{:S(2)}) collective-permute-start(bf16[6,64,2048]{2,1,0:T(8,128)(2,1)} %constant_dynamic-update-slice_fusion.2.refs_0_), channel_id=1, source_target_pairs={{0,4},{1,3},{2,6},{3,1},{4,0},{5,7},{6,2},{7,5},{8,12},{9,11},{10,... | collective-permute-start | bytes 4718600 | tf_op jit(solution)/shard_map/ppermute | solution.py:172
  118.7 23.5 %collective-permute-start.25 = (bf16[6,64,2048]{2,1,0:T(8,128)(2,1)}, bf16[6,64,2048]{2,1,0:T(8,128)(2,1)}, u32[]{:S(2)}, u32[]{:S(2)}) collective-permute-start(bf16[6,64,2048]{2,1,0:T(8,128)(2,1)} %add_convert_fusion.1), channel_id=1, source_target_pairs={{0,4},{1,3},{2,6},{3,1},{4,0},{5,7},{6,2},{7,5},{8,12},{9,11},{10,... | collective-permute-start | bytes 4718600 | tf_op jit(solution)/shard_map/ppermute | solution.py:172
  120.0 22.3 %collective-permute-start.24 = (bf16[6,64,2048]{2,1,0:T(8,128)(2,1)}, bf16[6,64,2048]{2,1,0:T(8,128)(2,1)}, u32[]{:S(2)}, u32[]{:S(2)}) collective-permute-start(bf16[6,64,2048]{2,1,0:T(8,128)(2,1)} %get-tuple-element.94), channel_id=1, source_target_pairs={{0,1},{1,0},{2,3},{3,2},{4,5},{5,4},{6,7},{7,6},{8,9},{9,8},{10,11... | collective-permute-start | bytes 4718600 | tf_op jit(solution)/shard_map/ppermute | solution.py:172
  145.2 13.7 %collective-permute-start.26 = (bf16[3,64,2048]{2,1,0:T(8,128)(2,1)}, bf16[3,64,2048]{2,1,0:T(8,128)(2,1)}, u32[]{:S(2)}, u32[]{:S(2)}) collective-permute-start(bf16[3,64,2048]{2,1,0:T(8,128)(2,1)} %add_convert_fusion.6), channel_id=1, source_target_pairs={{0,2},{1,5},{2,0},{3,7},{4,6},{5,1},{6,4},{7,3},{8,10},{9,13},{10,... | collective-permute-start | bytes 2359304 | tf_op jit(solution)/shard_map/ppermute | solution.py:172
  159.2 42.7 %collective-permute-start.37 = (bf16[6,64,2048]{2,1,0:T(8,128)(2,1)}, bf16[6,64,2048]{2,1,0:T(8,128)(2,1)}, u32[]{:S(2)}, u32[]{:S(2)}) collective-permute-start(bf16[6,64,2048]{2,1,0:T(8,128)(2,1)} %get-tuple-element.121), channel_id=1, source_target_pairs={{0,1},{1,0},{2,3},{3,2},{4,5},{5,4},{6,7},{7,6},{8,9},{9,8},{10,11... | collective-permute-start | bytes 4718600 | tf_op jit(solution)/shard_map/ppermute | solution.py:172
  163.1 18.8 %collective-permute-start.31 = (bf16[64,2048]{1,0:T(8,128)(2,1)}, bf16[64,2048]{1,0:T(8,128)(2,1)}, u32[]{:S(2)}, u32[]{:S(2)}) collective-permute-start(bf16[64,2048]{1,0:T(8,128)(2,1)} %get-tuple-element.139), channel_id=1, source_target_pairs={{0,16},{1,17},{2,18},{3,19},{4,20},{5,21},{6,22},{7,23},{8,24},{9,... | collective-permute-start | bytes 786440 | tf_op jit(solution)/shard_map/ppermute | solution.py:172
  163.3 29.7 %collective-permute-start.34 = (bf16[64,2048]{1,0:T(8,128)(2,1)S(1)}, bf16[64,2048]{1,0:T(8,128)(2,1)}, u32[]{:S(2)}, u32[]{:S(2)}) collective-permute-start(bf16[64,2048]{1,0:T(8,128)(2,1)S(1)} %get-tuple-element.138), channel_id=1, source_target_pairs={{0,8},{1,9},{2,10},{3,11},{4,12},{5,13},{6,14},{7,15},{8,16},{9,17... | collective-permute-start | bytes 786440 | tf_op jit(solution)/shard_map/ppermute | solution.py:172
  166.2 35.1 %collective-permute-start.28 = (bf16[6,64,2048]{2,1,0:T(8,128)(2,1)}, bf16[6,64,2048]{2,1,0:T(8,128)(2,1)}, u32[]{:S(2)}, u32[]{:S(2)}) collective-permute-start(bf16[6,64,2048]{2,1,0:T(8,128)(2,1)} %add_convert_fusion), channel_id=1, source_target_pairs={{0,4},{1,3},{2,6},{3,1},{4,0},{5,7},{6,2},{7,5},{8,12},{9,11},{10,... | collective-permute-start | bytes 4718600 | tf_op jit(solution)/shard_map/ppermute | solution.py:172
  167.7 14.2 %collective-permute-start.30 = (f32[80,128]{1,0:T(8,128)S(1)}, f32[80,128]{1,0:T(8,128)S(1)}, u32[]{:S(2)}, u32[]{:S(2)}) collective-permute-start(f32[80,128]{1,0:T(8,128)S(1)} %pad_maximum_fusion.7), channel_id=1, source_target_pairs={{0,1},{1,0},{2,3},{3,2},{4,5},{5,4},{6,7},{7,6},{8,9},{9,8},{10,11... | collective-permute-start | bytes 122888 | tf_op jit(solution)/shard_map/ppermute | solution.py:172
  181.9 19.4 %collective-permute-start.29 = (bf16[4,64,2048]{2,1,0:T(8,128)(2,1)}, bf16[4,64,2048]{2,1,0:T(8,128)(2,1)}, u32[]{:S(2)}, u32[]{:S(2)}) collective-permute-start(bf16[4,64,2048]{2,1,0:T(8,128)(2,1)} %get-tuple-element.107), channel_id=1, source_target_pairs={{0,1},{1,0},{2,3},{3,2},{4,5},{5,4},{6,7},{7,6},{8,9},{9,8},{10,11... | collective-permute-start | bytes 3145736 | tf_op jit(solution)/shard_map/ppermute | solution.py:172
  201.3 17.2 %collective-permute-start.36 = (bf16[4,64,2048]{2,1,0:T(8,128)(2,1)}, bf16[4,64,2048]{2,1,0:T(8,128)(2,1)S(1)}, u32[]{:S(2)}, u32[]{:S(2)}) collective-permute-start(bf16[4,64,2048]{2,1,0:T(8,128)(2,1)} %get-tuple-element.115), channel_id=1, source_target_pairs={{0,1},{1,0},{2,3},{3,2},{4,5},{5,4},{6,7},{7,6},{8,9},{9,8},{10,11... | collective-permute-start | bytes 3145736 | tf_op jit(solution)/shard_map/ppermute | solution.py:172
  219.9 15.0 %collective-permute-start.42 = (bf16[4,64,2048]{2,1,0:T(8,128)(2,1)}, bf16[4,64,2048]{2,1,0:T(8,128)(2,1)S(1)}, u32[]{:S(2)}, u32[]{:S(2)}) collective-permute-start(bf16[4,64,2048]{2,1,0:T(8,128)(2,1)} %add_convert_fusion.2), channel_id=1, source_target_pairs={{0,4},{1,3},{2,6},{3,1},{4,0},{5,7},{6,2},{7,5},{8,12},{9,11},{10,... | collective-permute-start | bytes 3145736 | tf_op jit(solution)/shard_map/ppermute | solution.py:172
  221.4 25.8 %collective-permute-start.44 = (bf16[64,2048]{1,0:T(8,128)(2,1)}, bf16[64,2048]{1,0:T(8,128)(2,1)S(1)}, u32[]{:S(2)}, u32[]{:S(2)}) collective-permute-start(bf16[64,2048]{1,0:T(8,128)(2,1)} %get-tuple-element.134), channel_id=1, source_target_pairs={{0,8},{1,9},{2,10},{3,11},{4,12},{5,13},{6,14},{7,15},{8,16},{9,17... | collective-permute-start | bytes 786440 | tf_op jit(solution)/shard_map/ppermute | solution.py:172
  221.4 25.8 %collective-permute-start.45 = (bf16[64,2048]{1,0:T(8,128)(2,1)S(1)}, bf16[64,2048]{1,0:T(8,128)(2,1)S(1)}, u32[]{:S(2)}, u32[]{:S(2)}) collective-permute-start(bf16[64,2048]{1,0:T(8,128)(2,1)S(1)} %get-tuple-element.136), channel_id=1, source_target_pairs={{0,16},{1,17},{2,18},{3,19},{4,20},{5,21},{6,22},{7,23},{8,24},{9,... | collective-permute-start | bytes 786440 | tf_op jit(solution)/shard_map/ppermute | solution.py:172
  224.0 23.1 %collective-permute-start.46 = (bf16[64,2048]{1,0:T(8,128)(2,1)S(1)}, bf16[64,2048]{1,0:T(8,128)(2,1)S(1)}, u32[]{:S(2)}, u32[]{:S(2)}) collective-permute-start(bf16[64,2048]{1,0:T(8,128)(2,1)S(1)} %get-tuple-element.135), channel_id=1, source_target_pairs={{0,24},{1,25},{2,26},{3,27},{4,28},{5,29},{6,30},{7,31},{8,0},{9,1... | collective-permute-start | bytes 786440 | tf_op jit(solution)/shard_map/ppermute | solution.py:172
  (40 other events, 307.7 us)

commit v10 on v9

--- a/solution.py
+++ b/solution.py
@@ -516,7 +516,7 @@
     far_tables = [send_along(late_tables, -step) for step in range(1, steps)]
     late_cot = after(cotangent, token_far)
     cot_steps = [send_along(late_cot, -step) for step in range(1, steps)]
-    token_second = after(send_second(token_far), near_far_pair, cot_steps[len(cot_steps) // 2], *far_tables)
+    token_second = after(send_second(token_far), near_far_pair, cot_steps[0], *far_tables)
     token_pair = jnp.concatenate([token_far, token_second])
     tables = far_first(jnp.stack([tables] + far_tables, axis=2))
     tables = jnp.where(core == 0, tables, jnp.roll(tables, half, axis=2))
@@ -601,26 +601,25 @@
     got = send_core(after(pack(columns[..., half:], gains), in_upper))
     down_part = outer_sum(after(hidden, in_upper), grads)
 
-    middle = len(out_far) // 2
-    down_part, got, out_far[middle] = together(down_part, got, out_far[middle])
+    down_part, got = together(down_part, got)
     columns, gains = unpack_add(columns[..., :half], gains, got)
     got = send_bit(pack(columns[1], gains), 2)
     gate_up_part = outer_sum(after(rows, near_high, down_part), joined_grad)
-    gate_up_part, got = together(gate_up_part, got)
+    gate_up_part, got = together(gate_up_part, got, *out_far[:-1])[:2]
     columns, gains = unpack_add(columns[0], gains, got)
     got = send_bit(pack(columns[1], gains), 1)
-    in_first, near_core, got = together(in_first, near_core, got, *out_far)[:3]
+    in_first, near_core, near_core_high, got = together(in_first, near_core, near_core_high, got)
     columns, gains = unpack_add(columns[0], gains, got)
     in_middle = narrow(
         add_up(in_mine[one_far:half_far], in_core[one_far:half_far], in_first[one_far:])
     )
     in_second = send_second(in_middle)
     messages = [send_along(pack(columns[step], gains), step) for step in range(1, steps)]
-    in_second, *messages = together(in_second, *messages)
+    near_upper = narrow(add_up(near_mine[4:], near_core_high))
+    in_second, near_upper, *messages = together(in_second, near_upper, *messages, *out_far[-1:])[:2 + len(messages)]
     in_planes = narrow(own_plane(in_mine, in_core, in_first, in_second, one_far))
     in_far = [send_along(in_planes[step - 1], step) for step in range(1, steps)]
-    near_upper = narrow(add_up(near_mine[4:], after(near_core_high, in_planes)))
-    near_first = send_first(near_upper)
+    near_first = send_first(after(near_upper, in_planes))
     near_middle = narrow(add_up(near_mine[2:4], near_core[2:], near_first[2:]))
     near_second = send_second(near_middle)
     near_sum = own_plane(near_mine, near_core, near_first, near_second, 2)

time: 251 us -> 246 us (0.980)
  waiting for transfers between devices: 70.9 us -> 61.2 us
    ppermute x47, waiting for transfers between devices: 70.9 us -> 61.2 us  [send(): return lax.ppermute(array, BOTH, pairs)]
  transfers between devices with their start and end apart: 47 -> 47, of which waited for: 18 -> 15; matrix products, arithmetic and copies ran while one was open for 18% -> 18% of each run, Pallas kernels for 30% -> 30%
where the time goes in v10:
time: 246 us
  Pallas kernels  74.9 us (30%)
  waiting for transfers between devices  61.2 us (25%)
  starting transfers between devices  47.7 us (19%)
  other arithmetic  34 us (14%)
  matrix products  13.4 us (5%)
  local copies, waits for them, and re-layouts  13.2 us (5%)
    ppermute x47, waiting for transfers between devices, send(): return lax.ppermute(array, BOTH, pairs)  61.2 us
    ppermute x47, starting transfers between devices, send(): return lax.ppermute(array, BOTH, pairs)  47.7 us
    pallas_call x4, Pallas kernels, select(): pl.pallas_call(functools.partial(kernel, count), grid=(4,), in_specs=[gro...  21.3 us
    convert_element_type x8, other arithmetic, narrow(): return value.astype(jnp.bfloat16)  20.5 us
    pallas_call x3, Pallas kernels, expand(): pl.pallas_call(functools.partial(expand_kernel, weighted, count, first_gr...  19.4 us
    dot_general x2, matrix products, outer_sum(): lax.dot_general(left, right, (((0,), (0,)), ((), ())), preferred_element_...  13.2 us
    pallas_call x1, Pallas kernels, forward(): pl.pallas_call(forward_kernel, grid=(2,), in_specs=[row_spec(features), p...  13 us
    pallas_call x2, Pallas kernels, backward_input(): pl.pallas_call(input_kernel, grid=(2,), in_specs=[pl.BlockSpec((slots, wi...  12.6 us
  transfers between devices with their start and end apart: 47, of which 15 were waited for; matrix products, arithmetic and copies ran while one was open for 18% of the time, Pallas kernels for 30%

profile of v10, /device:TPU:0, one launch (start us, length us, event | category | flops | bytes accessed | tf_op | source)
XLA Modules:
  0.0 245.6 jit_solution(2542863886640547033)
XLA Ops:
  19.6 11.8 %collective-permute-done.4 = bf16[64,2048]{1,0:T(8,128)(2,1)S(1)} collective-permute-done((bf16[64,2048]{1,0:T(8,128)(2,1)}, bf16[64,2048]{1,0:T(8,128)(2,1)S(1)}, u32[]{:S(2)}, u32[]{:S(2)}) %collective-permute-start.4) | collective-permute-done | bytes 262176 | tf_op jit(solution)/shard_map/ppermute | solution.py:172
  38.4 5.0 %collective-permute-done.7 = f32[2,2,16,128]{3,2,1,0:T(8,128)S(1)} collective-permute-done((f32[2,2,16,128]{3,2,1,0:T(8,128)S(1)}, f32[2,2,16,128]{3,2,1,0:T(8,128)S(1)}, u32[]{:S(2)}, u32[]{:S(2)}) %collective-permute-start.7) | collective-permute-done | bytes 32800 | tf_op jit(solution)/shard_map/ppermute | solution.py:172
  51.8 4.3 %shard_map.118.refs_5_ = bf16[16,48,2048]{2,1,0:T(8,128)(2,1)} custom-call(bf16[16,48,128]{2,1,0:T(8,128)(2,1)} %fusion.15.pick_ref, bf16[4,64,2048]{2,1,0:T(8,128)(2,1)} %copy-done.1, bf16[4,64,2048]{2,1,0:T(8,128)(2,1)} %copy-done.3, bf16[4,64,2048]{2,1,0:T(8,128)(2,1)} %copy-done.4, bf16[4,64,2048]{2,1,0:T(8,128)(2,1)} %collective-permute-done.16.refs_3_, ...), custom_call_target="tpu_custom_call" | custom-call | flops 1000000 | bytes 100000 | tf_op jit(solution)/shard_map/pallas_call | solution.py:281
  56.1 10.8 %collective-permute-done.13 = bf16[64,2048]{1,0:T(8,128)(2,1)} collective-permute-done((bf16[64,2048]{1,0:T(8,128)(2,1)S(1)}, bf16[64,2048]{1,0:T(8,128)(2,1)}, u32[]{:S(2)}, u32[]{:S(2)}) %collective-permute-start.13) | collective-permute-done | bytes 262176 | tf_op jit(solution)/shard_map/ppermute | solution.py:172
  72.0 6.0 %shard_map.119 = bf16[16,48,2048]{2,1,0:T(8,128)(2,1)} custom-call(bf16[16,48,128]{2,1,0:T(8,128)(2,1)} %fusion.15.pick_ref, bf16[6,64,2048]{2,1,0:T(8,128)(2,1)} %constant_dynamic-update-slice_fusion.refs_0_, bf16[6,64,2048]{2,1,0:T(8,128)(2,1)} %collective-permute-done.12.refs_1_, ...), custom_call_target="tpu_custom_call", output_to_operand_aliasing={{}: (6, {})} | custom-call | flops 1000000 | bytes 100000 | tf_op jit(solution)/shard_map/pallas_call | solution.py:281
  85.7 13.0 %shard_map.120 = (f32[768,768]{1,0:T(8,128)}, f32[768,768]{1,0:T(8,128)}, bf16[768,768]{1,0:T(8,128)(2,1)}, bf16[768,2048]{1,0:T(8,128)(2,1)}) custom-call(bf16[768,2048]{1,0:T(8,128)(2,1)} %bitcast.115, bf16[1,2048,1536]{2,1,0:T(8,128)(2,1)} %gate_up_ref.5, bf16[1,768,2048]{2,1,0:T(8,128)(2,1)} %down_ref.3), custom_call_target="tpu_custom_call" | custom-call | flops 1000000 | bytes 100000 | tf_op jit(solution)/shard_map/pallas_call | solution.py:395
  98.7 7.3 %shard_map.121 = (bf16[12,64,2048]{2,1,0:T(8,128)(2,1)}, bf16[6,64,2048]{2,1,0:T(8,128)(2,1)}, bf16[6,64,2048]{2,1,0:T(8,128)(2,1)}) custom-call(bf16[16,128,48]{2,1,0:T(8,128)(2,1)} %fusion.1.back_ref, f32[16,48,1]{2,1,0:T(8,128)} %copy.23.prob_ref.refs_4_, bf16[16,48,2048]{2,1,0:T(8,128)(2,1)} %bitcast.119), custom_call_target="tpu_custom_call" | custom-call | flops 1000000 | bytes 100000 | tf_op jit(solution)/shard_map/pallas_call | solution.py:360
  106.7 4.5 %shard_map.122 = (bf16[16,48,2048]{2,1,0:T(8,128)(2,1)}, f32[16,48,1]{2,1,0:T(8,128)}) custom-call(bf16[16,48,128]{2,1,0:T(8,128)(2,1)} %fusion.15.pick_ref, bf16[4,64,2048]{2,1,0:T(8,128)(2,1)} %copy-done.1, bf16[4,64,2048]{2,1,0:T(8,128)(2,1)} %copy-done.3, bf16[4,64,2048]{2,1,0:T(8,128)(2,1)} %copy-done.4, ...), custom_call_target="tpu_custom_call" | custom-call | flops 1000000 | bytes 100000 | tf_op jit(solution)/shard_map/pallas_call | solution.py:281
  111.2 3.8 %add_convert_fusion.1 = bf16[6,64,2048]{2,1,0:T(8,128)(2,1)} fusion(bf16[6,64,2048]{2,1,0:T(8,128)(2,1)} %collective-permute-done.21, bf16[12,64,2048]{2,1,0:T(8,128)(2,1)} %get-tuple-element.82), kind=kLoop, calls=%fused_computation.4 | loop fusion | flops 3145728 | bytes 4718592 | tf_op jit(solution)/shard_map/convert_element_type | solution.py:209
  116.6 6.5 %shard_map.123 = (bf16[16,48,2048]{2,1,0:T(8,128)(2,1)}, f32[16,48,1]{2,1,0:T(8,128)}) custom-call(bf16[16,48,128]{2,1,0:T(8,128)(2,1)} %fusion.15.pick_ref, bf16[6,64,2048]{2,1,0:T(8,128)(2,1)} %constant_dynamic-update-slice_fusion.2.refs_0_, bf16[6,64,2048]{2,1,0:T(8,128)(2,1)} %collective-permute-done.20.refs_1_, ...), custom_call_target="tpu_custom_call", output_to_operand_aliasing={{0}: (7, {}), {1}: (8, {})} | custom-call | flops 1000000 | bytes 100000 | tf_op jit(solution)/shard_map/pallas_call | solution.py:281
  123.1 8.6 %shard_map.124.joined_ref = bf16[768,1536]{1,0:T(8,128)(2,1)} custom-call(bf16[768,2048]{1,0:T(8,128)(2,1)} %bitcast.125, f32[768,768]{1,0:T(8,128)} %get-tuple-element.93.gate_pre_ref, f32[768,768]{1,0:T(8,128)} %get-tuple-element.94.up_pre_ref, bf16[1,768,2048]{2,1,0:T(8,128)(2,1)} %down_ref.3), custom_call_target="tpu_custom_call" | custom-call | flops 1000000 | bytes 100000 | tf_op jit(solution)/shard_map/pallas_call | solution.py:431
  131.7 6.3 %shard_map.125 = (bf16[768,2048]{1,0:T(8,128)(2,1)}, f32[1,1024]{1,0:T(1,128)}) custom-call(bf16[768,1536]{1,0:T(8,128)(2,1)} %shard_map.124.joined_ref, bf16[1,2048,1536]{2,1,0:T(8,128)(2,1)} %gate_up_ref.5, bf16[768,2048]{1,0:T(8,128)(2,1)} %bitcast.116), custom_call_target="tpu_custom_call" | custom-call | flops 1000000 | bytes 100000 | tf_op jit(solution)/shard_map/pallas_call | solution.py:460
  142.8 6.3 %shard_map.126 = (bf16[768,2048]{1,0:T(8,128)(2,1)}, f32[1,1024]{1,0:T(1,128)}) custom-call(bf16[768,1536]{1,0:T(8,128)(2,1)} %shard_map.124.joined_ref, bf16[1,2048,1536]{2,1,0:T(8,128)(2,1)} %gate_up_ref.5, bf16[768,2048]{1,0:T(8,128)(2,1)} %bitcast.117, bf16[768,2048]{1,0:T(8,128)(2,1)} %get-tuple-element.99.refs_0_), custom_call_target="tpu_custom_call", output_to_operand_aliasing={{0}: (3, {})} | custom-call | flops 1000000 | bytes 100000 | tf_op jit(solution)/shard_map/pallas_call | solution.py:460
  149.1 6.5 %shard_map.127 = (bf16[12,64,2048]{2,1,0:T(8,128)(2,1)}, bf16[6,64,2048]{2,1,0:T(8,128)(2,1)}, bf16[6,64,2048]{2,1,0:T(8,128)(2,1)}) custom-call(bf16[16,128,48]{2,1,0:T(8,128)(2,1)} %fusion.1.back_ref, f32[16,48,1]{2,1,0:T(8,128)} %copy.23.prob_ref.refs_4_, bf16[16,48,2048]{2,1,0:T(8,128)(2,1)} %bitcast.123), custom_call_target="tpu_custom_call" | custom-call | flops 1000000 | bytes 100000 | tf_op jit(solution)/shard_map/pallas_call | solution.py:360
  163.9 4.1 %convolution_convert_fusion.1 = bf16[768,2048]{1,0:T(8,128)(2,1)} fusion(bf16[768,768]{1,0:T(8,128)(2,1)S(1)} %copy-done.19, bf16[768,2048]{1,0:T(8,128)(2,1)S(1)} %bitcast.126), kind=kOutput, calls=%fused_computation.2 | convolution fusion | flops 2417491968 | bytes 7471104 | tf_op jit(solution)/shard_map/dot_general | solution.py:38
  168.9 5.6 %shard_map.128 = (bf16[8,64,2048]{2,1,0:T(8,128)(2,1)}, bf16[4,64,2048]{2,1,0:T(8,128)(2,1)}, bf16[4,64,2048]{2,1,0:T(8,128)(2,1)}) custom-call(bf16[16,128,48]{2,1,0:T(8,128)(2,1)} %fusion.1.back_ref, f32[16,48,1]{2,1,0:T(8,128)} %copy.24.prob_ref, bf16[16,48,2048]{2,1,0:T(8,128)(2,1)} %bitcast.122, bf16[16,48,2048]{2,1,0:T(8,128)(2,1)} %bitcast.124), custom_call_target="tpu_custom_call" | custom-call | flops 1000000 | bytes 100000 | tf_op jit(solution)/shard_map/pallas_call | solution.py:360
  175.4 4.8 %collective-permute-done.34 = bf16[64,2048]{1,0:T(8,128)(2,1)} collective-permute-done((bf16[64,2048]{1,0:T(8,128)(2,1)S(1)}, bf16[64,2048]{1,0:T(8,128)(2,1)}, u32[]{:S(2)}, u32[]{:S(2)}) %collective-permute-start.34) | collective-permute-done | bytes 262176 | tf_op jit(solution)/shard_map/ppermute | solution.py:172
  181.2 9.1 %convolution_convert_fusion = bf16[2048,1536]{1,0:T(8,128)(2,1)} fusion(bf16[768,2048]{1,0:T(8,128)(2,1)} %bitcast.118, bf16[768,1536]{1,0:T(8,128)(2,1)} %shard_map.124.joined_ref), kind=kOutput, calls=%fused_computation.1 | convolution fusion | flops 4834983936 | bytes 11796480 | tf_op jit(solution)/shard_map/dot_general | solution.py:38
  197.1 3.1 %add_convert_fusion.4 = bf16[3,64,2048]{2,1,0:T(8,128)(2,1)} fusion(bf16[6,64,2048]{2,1,0:T(8,128)(2,1)} %collective-permute-done.36, bf16[6,64,2048]{2,1,0:T(8,128)(2,1)} %collective-permute-done.28, bf16[12,64,2048]{2,1,0:T(8,128)(2,1)} %get-tuple-element.101), kind=kLoop, calls=%fused_computation.7 | loop fusion | flops 2359296 | bytes 3145728 | tf_op jit(solution)/shard_map/convert_element_type | solution.py:209
  202.3 3.3 %collective-permute-start.40 = (f32[20,128]{1,0:T(8,128)S(1)}, f32[20,128]{1,0:T(8,128)S(1)}, u32[]{:S(2)}, u32[]{:S(2)}) collective-permute-start(f32[20,128]{1,0:T(8,128)S(1)} %get-tuple-element.151), channel_id=1, source_target_pairs={{0,24},{1,25},{2,26},{3,27},{4,28},{5,29},{6,30},{7,31},{8,0},{9,1... | collective-permute-start | bytes 30728 | tf_op jit(solution)/shard_map/ppermute | solution.py:172
  208.2 4.2 %collective-permute-done.37 = bf16[3,64,2048]{2,1,0:T(8,128)(2,1)} collective-permute-done((bf16[3,64,2048]{2,1,0:T(8,128)(2,1)}, bf16[3,64,2048]{2,1,0:T(8,128)(2,1)}, u32[]{:S(2)}, u32[]{:S(2)}) %collective-permute-start.37) | collective-permute-done | bytes 786464 | tf_op jit(solution)/shard_map/ppermute | solution.py:172
  217.6 3.3 %collective-permute-start.46 = (bf16[64,2048]{1,0:T(8,128)(2,1)S(1)}, bf16[64,2048]{1,0:T(8,128)(2,1)S(1)}, u32[]{:S(2)}, u32[]{:S(2)}) collective-permute-start(bf16[64,2048]{1,0:T(8,128)(2,1)S(1)} %get-tuple-element.137), channel_id=1, source_target_pairs={{0,24},{1,25},{2,26},{3,27},{4,28},{5,29},{6,30},{7,31},{8,0},{9,1... | collective-permute-start | bytes 786440 | tf_op jit(solution)/shard_map/ppermute | solution.py:172
  221.4 8.6 %collective-permute-done.42 = bf16[4,64,2048]{2,1,0:T(8,128)(2,1)} collective-permute-done((bf16[4,64,2048]{2,1,0:T(8,128)(2,1)}, bf16[4,64,2048]{2,1,0:T(8,128)(2,1)}, u32[]{:S(2)}, u32[]{:S(2)}) %collective-permute-start.42) | collective-permute-done | bytes 1048608 | tf_op jit(solution)/shard_map/ppermute | solution.py:172
  234.2 6.5 %collective-permute-done.43 = bf16[2,64,2048]{2,1,0:T(8,128)(2,1)S(1)} collective-permute-done((bf16[2,64,2048]{2,1,0:T(8,128)(2,1)S(1)}, bf16[2,64,2048]{2,1,0:T(8,128)(2,1)S(1)}, u32[]{:S(2)}, u32[]{:S(2)}) %collective-permute-start.43) | collective-permute-done | bytes 524320 | tf_op jit(solution)/shard_map/ppermute | solution.py:172
  (211 shorter events, 91.2 us)
Async XLA Ops:
  4.7 14.2 %collective-permute-start.5 = (bf16[64,2048]{1,0:T(8,128)(2,1)}, bf16[64,2048]{1,0:T(8,128)(2,1)S(1)}, u32[]{:S(2)}, u32[]{:S(2)}) collective-permute-start(bf16[64,2048]{1,0:T(8,128)(2,1)} %param.7), channel_id=1, source_target_pairs={{0,8},{1,9},{2,10},{3,11},{4,12},{5,13},{6,14},{7,15},{8,16},{9,17... | collective-permute-start | bytes 786440 | tf_op jit(solution)/shard_map/ppermute | solution.py:172
  6.3 13.3 %collective-permute-start.3 = (bf16[64,2048]{1,0:T(8,128)(2,1)}, bf16[64,2048]{1,0:T(8,128)(2,1)S(1)}, u32[]{:S(2)}, u32[]{:S(2)}) collective-permute-start(bf16[64,2048]{1,0:T(8,128)(2,1)} %param.7), channel_id=1, source_target_pairs={{0,24},{1,25},{2,26},{3,27},{4,28},{5,29},{6,30},{7,31},{8,0},{9,1... | collective-permute-start | bytes 786440 | tf_op jit(solution)/shard_map/ppermute | solution.py:172
  8.5 22.9 %collective-permute-start.4 = (bf16[64,2048]{1,0:T(8,128)(2,1)}, bf16[64,2048]{1,0:T(8,128)(2,1)S(1)}, u32[]{:S(2)}, u32[]{:S(2)}) collective-permute-start(bf16[64,2048]{1,0:T(8,128)(2,1)} %param.7), channel_id=1, source_target_pairs={{0,16},{1,17},{2,18},{3,19},{4,20},{5,21},{6,22},{7,23},{8,24},{9,... | collective-permute-start | bytes 786440 | tf_op jit(solution)/shard_map/ppermute | solution.py:172
  15.1 28.5 %collective-permute-start.10 = (bf16[4,64,2048]{2,1,0:T(8,128)(2,1)S(1)}, bf16[4,64,2048]{2,1,0:T(8,128)(2,1)S(1)}, u32[]{:S(2)}, u32[]{:S(2)}) collective-permute-start(bf16[4,64,2048]{2,1,0:T(8,128)(2,1)S(1)} %pad_maximum_fusion.refs_0_), channel_id=1, source_target_pairs={{0,4},{1,3},{2,6},{3,1},{4,0},{5,7},{6,2},{7,5},{8,12},{9,11},{10,... | collective-permute-start | bytes 3145736 | tf_op jit(solution)/shard_map/ppermute | solution.py:172
  16.8 14.7 %collective-permute-start.2 = (f32[2,16,128]{2,1,0:T(8,128)S(1)}, f32[2,16,128]{2,1,0:T(8,128)S(1)}, u32[]{:S(2)}, u32[]{:S(2)}) collective-permute-start(f32[2,16,128]{2,1,0:T(8,128)S(1)} %get-tuple-element.150), channel_id=1, source_target_pairs={{0,4},{1,3},{2,6},{3,1},{4,0},{5,7},{6,2},{7,5},{8,12},{9,11},{10,... | collective-permute-start | bytes 49160 | tf_op jit(solution)/shard_map/ppermute | solution.py:172
  44.6 23.5 %collective-permute-start.12 = (bf16[6,64,2048]{2,1,0:T(8,128)(2,1)}, bf16[6,64,2048]{2,1,0:T(8,128)(2,1)}, u32[]{:S(2)}, u32[]{:S(2)}) collective-permute-start(bf16[6,64,2048]{2,1,0:T(8,128)(2,1)} %constant_dynamic-update-slice_fusion.refs_0_), channel_id=1, source_target_pairs={{0,4},{1,3},{2,6},{3,1},{4,0},{5,7},{6,2},{7,5},{8,12},{9,11},{10,... | collective-permute-start | bytes 4718600 | tf_op jit(solution)/shard_map/ppermute | solution.py:172
  46.5 20.5 %collective-permute-start.13 = (bf16[64,2048]{1,0:T(8,128)(2,1)S(1)}, bf16[64,2048]{1,0:T(8,128)(2,1)}, u32[]{:S(2)}, u32[]{:S(2)}) collective-permute-start(bf16[64,2048]{1,0:T(8,128)(2,1)S(1)} %copy-done.6), channel_id=1, source_target_pairs={{0,16},{1,17},{2,18},{3,19},{4,20},{5,21},{6,22},{7,23},{8,24},{9,... | collective-permute-start | bytes 786440 | tf_op jit(solution)/shard_map/ppermute | solution.py:172
  47.7 19.2 %collective-permute-start.14 = (bf16[64,2048]{1,0:T(8,128)(2,1)S(1)}, bf16[64,2048]{1,0:T(8,128)(2,1)}, u32[]{:S(2)}, u32[]{:S(2)}) collective-permute-start(bf16[64,2048]{1,0:T(8,128)(2,1)S(1)} %copy-done.6), channel_id=1, source_target_pairs={{0,8},{1,9},{2,10},{3,11},{4,12},{5,13},{6,14},{7,15},{8,16},{9,17... | collective-permute-start | bytes 786440 | tf_op jit(solution)/shard_map/ppermute | solution.py:172
  50.8 19.8 %collective-permute-start.17 = (bf16[6,64,2048]{2,1,0:T(8,128)(2,1)}, bf16[6,64,2048]{2,1,0:T(8,128)(2,1)}, u32[]{:S(2)}, u32[]{:S(2)}) collective-permute-start(bf16[6,64,2048]{2,1,0:T(8,128)(2,1)} %constant_dynamic-update-slice_fusion.refs_0_), channel_id=1, source_target_pairs={{0,1},{1,0},{2,3},{3,2},{4,5},{5,4},{6,7},{7,6},{8,9},{9,8},{10,11... | collective-permute-start | bytes 4718600 | tf_op jit(solution)/shard_map/ppermute | solution.py:172
  82.6 23.5 %collective-permute-start.20 = (bf16[6,64,2048]{2,1,0:T(8,128)(2,1)}, bf16[6,64,2048]{2,1,0:T(8,128)(2,1)}, u32[]{:S(2)}, u32[]{:S(2)}) collective-permute-start(bf16[6,64,2048]{2,1,0:T(8,128)(2,1)} %constant_dynamic-update-slice_fusion.2.refs_0_), channel_id=1, source_target_pairs={{0,4},{1,3},{2,6},{3,1},{4,0},{5,7},{6,2},{7,5},{8,12},{9,11},{10,... | collective-permute-start | bytes 4718600 | tf_op jit(solution)/shard_map/ppermute | solution.py:172
  115.0 23.0 %collective-permute-start.25 = (bf16[6,64,2048]{2,1,0:T(8,128)(2,1)}, bf16[6,64,2048]{2,1,0:T(8,128)(2,1)}, u32[]{:S(2)}, u32[]{:S(2)}) collective-permute-start(bf16[6,64,2048]{2,1,0:T(8,128)(2,1)} %add_convert_fusion.1), channel_id=1, source_target_pairs={{0,4},{1,3},{2,6},{3,1},{4,0},{5,7},{6,2},{7,5},{8,12},{9,11},{10,... | collective-permute-start | bytes 4718600 | tf_op jit(solution)/shard_map/ppermute | solution.py:172
  116.4 21.6 %collective-permute-start.24 = (bf16[6,64,2048]{2,1,0:T(8,128)(2,1)}, bf16[6,64,2048]{2,1,0:T(8,128)(2,1)}, u32[]{:S(2)}, u32[]{:S(2)}) collective-permute-start(bf16[6,64,2048]{2,1,0:T(8,128)(2,1)} %get-tuple-element.95), channel_id=1, source_target_pairs={{0,1},{1,0},{2,3},{3,2},{4,5},{5,4},{6,7},{7,6},{8,9},{9,8},{10,11... | collective-permute-start | bytes 4718600 | tf_op jit(solution)/shard_map/ppermute | solution.py:172
  141.0 14.6 %collective-permute-start.26 = (bf16[3,64,2048]{2,1,0:T(8,128)(2,1)}, bf16[3,64,2048]{2,1,0:T(8,128)(2,1)}, u32[]{:S(2)}, u32[]{:S(2)}) collective-permute-start(bf16[3,64,2048]{2,1,0:T(8,128)(2,1)} %add_convert_fusion.6), channel_id=1, source_target_pairs={{0,2},{1,5},{2,0},{3,7},{4,6},{5,1},{6,4},{7,3},{8,10},{9,13},{10,... | collective-permute-start | bytes 2359304 | tf_op jit(solution)/shard_map/ppermute | solution.py:172
  155.9 41.2 %collective-permute-start.36 = (bf16[6,64,2048]{2,1,0:T(8,128)(2,1)}, bf16[6,64,2048]{2,1,0:T(8,128)(2,1)}, u32[]{:S(2)}, u32[]{:S(2)}) collective-permute-start(bf16[6,64,2048]{2,1,0:T(8,128)(2,1)} %get-tuple-element.121), channel_id=1, source_target_pairs={{0,1},{1,0},{2,3},{3,2},{4,5},{5,4},{6,7},{7,6},{8,9},{9,8},{10,11... | collective-permute-start | bytes 4718600 | tf_op jit(solution)/shard_map/ppermute | solution.py:172
  159.7 15.3 %collective-permute-start.33 = (bf16[64,2048]{1,0:T(8,128)(2,1)}, bf16[64,2048]{1,0:T(8,128)(2,1)}, u32[]{:S(2)}, u32[]{:S(2)}) collective-permute-start(bf16[64,2048]{1,0:T(8,128)(2,1)} %get-tuple-element.141), channel_id=1, source_target_pairs={{0,8},{1,9},{2,10},{3,11},{4,12},{5,13},{6,14},{7,15},{8,16},{9,17... | collective-permute-start | bytes 786440 | tf_op jit(solution)/shard_map/ppermute | solution.py:172
  159.7 20.5 %collective-permute-start.34 = (bf16[64,2048]{1,0:T(8,128)(2,1)S(1)}, bf16[64,2048]{1,0:T(8,128)(2,1)}, u32[]{:S(2)}, u32[]{:S(2)}) collective-permute-start(bf16[64,2048]{1,0:T(8,128)(2,1)S(1)} %get-tuple-element.140), channel_id=1, source_target_pairs={{0,16},{1,17},{2,18},{3,19},{4,20},{5,21},{6,22},{7,23},{8,24},{9,... | collective-permute-start | bytes 786440 | tf_op jit(solution)/shard_map/ppermute | solution.py:172
  162.8 33.0 %collective-permute-start.28 = (bf16[6,64,2048]{2,1,0:T(8,128)(2,1)}, bf16[6,64,2048]{2,1,0:T(8,128)(2,1)}, u32[]{:S(2)}, u32[]{:S(2)}) collective-permute-start(bf16[6,64,2048]{2,1,0:T(8,128)(2,1)} %add_convert_fusion), channel_id=1, source_target_pairs={{0,4},{1,3},{2,6},{3,1},{4,0},{5,7},{6,2},{7,5},{8,12},{9,11},{10,... | collective-permute-start | bytes 4718600 | tf_op jit(solution)/shard_map/ppermute | solution.py:172
  174.5 21.2 %collective-permute-start.30 = (bf16[4,64,2048]{2,1,0:T(8,128)(2,1)}, bf16[4,64,2048]{2,1,0:T(8,128)(2,1)S(1)}, u32[]{:S(2)}, u32[]{:S(2)}) collective-permute-start(bf16[4,64,2048]{2,1,0:T(8,128)(2,1)} %get-tuple-element.109), channel_id=1, source_target_pairs={{0,1},{1,0},{2,3},{3,2},{4,5},{5,4},{6,7},{7,6},{8,9},{9,8},{10,11... | collective-permute-start | bytes 3145736 | tf_op jit(solution)/shard_map/ppermute | solution.py:172
  175.0 20.7 %collective-permute-start.29 = (bf16[4,64,2048]{2,1,0:T(8,128)(2,1)}, bf16[4,64,2048]{2,1,0:T(8,128)(2,1)S(1)}, u32[]{:S(2)}, u32[]{:S(2)}) collective-permute-start(bf16[4,64,2048]{2,1,0:T(8,128)(2,1)} %get-tuple-element.108), channel_id=1, source_target_pairs={{0,1},{1,0},{2,3},{3,2},{4,5},{5,4},{6,7},{7,6},{8,9},{9,8},{10,11... | collective-permute-start | bytes 3145736 | tf_op jit(solution)/shard_map/ppermute | solution.py:172
  194.2 14.0 %collective-permute-start.41 = (bf16[64,2048]{1,0:T(8,128)(2,1)S(1)}, bf16[64,2048]{1,0:T(8,128)(2,1)S(1)}, u32[]{:S(2)}, u32[]{:S(2)}) collective-permute-start(bf16[64,2048]{1,0:T(8,128)(2,1)S(1)} %get-tuple-element.139), channel_id=1, source_target_pairs={{0,24},{1,25},{2,26},{3,27},{4,28},{5,29},{6,30},{7,31},{8,0},{9,1... | collective-permute-start | bytes 786440 | tf_op jit(solution)/shard_map/ppermute | solution.py:172
  214.8 15.2 %collective-permute-start.42 = (bf16[4,64,2048]{2,1,0:T(8,128)(2,1)}, bf16[4,64,2048]{2,1,0:T(8,128)(2,1)}, u32[]{:S(2)}, u32[]{:S(2)}) collective-permute-start(bf16[4,64,2048]{2,1,0:T(8,128)(2,1)} %add_convert_fusion.2), channel_id=1, source_target_pairs={{0,4},{1,3},{2,6},{3,1},{4,0},{5,7},{6,2},{7,5},{8,12},{9,11},{10,... | collective-permute-start | bytes 3145736 | tf_op jit(solution)/shard_map/ppermute | solution.py:172
  217.0 25.2 %collective-permute-start.44 = (bf16[64,2048]{1,0:T(8,128)(2,1)}, bf16[64,2048]{1,0:T(8,128)(2,1)S(1)}, u32[]{:S(2)}, u32[]{:S(2)}) collective-permute-start(bf16[64,2048]{1,0:T(8,128)(2,1)} %get-tuple-element.136), channel_id=1, source_target_pairs={{0,8},{1,9},{2,10},{3,11},{4,12},{5,13},{6,14},{7,15},{8,16},{9,17... | collective-permute-start | bytes 786440 | tf_op jit(solution)/shard_map/ppermute | solution.py:172
  217.5 24.8 %collective-permute-start.45 = (bf16[64,2048]{1,0:T(8,128)(2,1)S(1)}, bf16[64,2048]{1,0:T(8,128)(2,1)S(1)}, u32[]{:S(2)}, u32[]{:S(2)}) collective-permute-start(bf16[64,2048]{1,0:T(8,128)(2,1)S(1)} %get-tuple-element.138), channel_id=1, source_target_pairs={{0,16},{1,17},{2,18},{3,19},{4,20},{5,21},{6,22},{7,23},{8,24},{9,... | collective-permute-start | bytes 786440 | tf_op jit(solution)/shard_map/ppermute | solution.py:172
  217.6 24.7 %collective-permute-start.46 = (bf16[64,2048]{1,0:T(8,128)(2,1)S(1)}, bf16[64,2048]{1,0:T(8,128)(2,1)S(1)}, u32[]{:S(2)}, u32[]{:S(2)}) collective-permute-start(bf16[64,2048]{1,0:T(8,128)(2,1)S(1)} %get-tuple-element.137), channel_id=1, source_target_pairs={{0,24},{1,25},{2,26},{3,27},{4,28},{5,29},{6,30},{7,31},{8,0},{9,1... | collective-permute-start | bytes 786440 | tf_op jit(solution)/shard_map/ppermute | solution.py:172
  (43 other events, 317.3 us)

commit v11 on v10

--- a/solution.py
+++ b/solution.py
@@ -589,26 +589,27 @@
     out_far = [send_along(out_planes[step - 1], step) for step in range(1, steps)]
     in_upper = narrow(add_up(in_mine[half_far:], after(in_core_high, out_planes)))
     in_first = send_first(in_upper)
-    near_mine, near_low, near_high = expand(
-        back, after(slot_prob, in_upper), (out_slots, input_slots), (True, False), 1, far
-    )
-    near_core_high = send_core(near_high)
-    near_core = send_core(near_low)
     gains = (gain_term / gain).reshape(-1, 128)
     prob_rows = jnp.sum(jnp.where(placed, prob_value, 0.0), axis=1)
     columns = from_far_first(jnp.where(matches, prob_rows[:, None, :], 0.0), steps)
     columns = jnp.where(core == 0, columns, jnp.swapaxes(columns, 0, 1))
     got = send_core(after(pack(columns[..., half:], gains), in_upper))
-    down_part = outer_sum(after(hidden, in_upper), grads)
-
-    down_part, got = together(down_part, got)
+    gate_up_part = outer_sum(after(rows, in_upper), joined_grad)
+    gate_up_part, got = together(gate_up_part, got)
     columns, gains = unpack_add(columns[..., :half], gains, got)
     got = send_bit(pack(columns[1], gains), 2)
-    gate_up_part = outer_sum(after(rows, near_high, down_part), joined_grad)
-    gate_up_part, got = together(gate_up_part, got, *out_far[:-1])[:2]
+    near_mine, near_low, near_high = expand(
+        back, after(slot_prob, got), (out_slots, input_slots), (True, False), 1, far
+    )
+    near_high, got = together(near_high, got, *out_far[:-1])[:2]
     columns, gains = unpack_add(columns[0], gains, got)
     got = send_bit(pack(columns[1], gains), 1)
-    in_first, near_core, near_core_high, got = together(in_first, near_core, near_core_high, got)
+    near_core_high = send_core(near_high)
+    near_core = send_core(near_low)
+    down_part = outer_sum(after(hidden, near_high), grads)
+    down_part, in_first, near_core, near_core_high, got = together(
+        down_part, in_first, near_core, near_core_high, got
+    )
     columns, gains = unpack_add(columns[0], gains, got)
     in_middle = narrow(
         add_up(in_mine[one_far:half_far], in_core[one_far:half_far], in_first[one_far:])

time: 246 us -> 252 us (1.024)
  transfers between devices with their start and end apart: 47 -> 47, of which waited for: 15 -> 14; matrix products, arithmetic and copies ran while one was open for 18% -> 18% of each run, Pallas kernels for 30% -> 30%
where the time goes in v11:
time: 252 us; the launch traced here: 251 us
  Pallas kernels  74.9 us (30%)
  waiting for transfers between devices  63.6 us (25%)
  starting transfers between devices  50 us (20%)
  other arithmetic  34 us (13%)
  matrix products  14 us (6%)
  local copies, waits for them, and re-layouts  13 us (5%)
    ppermute x47, waiting for transfers between devices, send(): return lax.ppermute(array, BOTH, pairs)  63.6 us
    ppermute x47, starting transfers between devices, send(): return lax.ppermute(array, BOTH, pairs)  50 us
    pallas_call x4, Pallas kernels, select(): pl.pallas_call(functools.partial(kernel, count), grid=(4,), in_specs=[gro...  21.3 us
    convert_element_type x8, other arithmetic, narrow(): return value.astype(jnp.bfloat16)  20.4 us
    pallas_call x3, Pallas kernels, expand(): pl.pallas_call(functools.partial(expand_kernel, weighted, count, first_gr...  19.4 us
    dot_general x2, matrix products, outer_sum(): lax.dot_general(left, right, (((0,), (0,)), ((), ())), preferred_element_...  13.9 us
    pallas_call x1, Pallas kernels, forward(): pl.pallas_call(forward_kernel, grid=(2,), in_specs=[row_spec(features), p...  13 us
    pallas_call x2, Pallas kernels, backward_input(): pl.pallas_call(input_kernel, grid=(2,), in_specs=[pl.BlockSpec((slots, wi...  12.6 us
  transfers between devices with their start and end apart: 47, of which 14 were waited for; matrix products, arithmetic and copies ran while one was open for 18% of the time, Pallas kernels for 30%

profile of v11, /device:TPU:0, one launch (start us, length us, event | category | flops | bytes accessed | tf_op | source)
XLA Modules:
  0.0 250.8 jit_solution(4344727517277498400)
XLA Ops:
  1.7 3.0 %collective-permute-start = (bf16[2,64,2048]{2,1,0:T(8,128)(2,1)S(1)}, bf16[2,64,2048]{2,1,0:T(8,128)(2,1)S(1)}, u32[]{:S(2)}, u32[]{:S(2)}) collective-permute-start(bf16[2,64,2048]{2,1,0:T(8,128)(2,1)S(1)} %pad_maximum_fusion.3), channel_id=1, source_target_pairs={{0,2},{1,5},{2,0},{3,7},{4,6},{5,1},{6,4},{7,3},{8,10},{9,13},{10,... | collective-permute-start | bytes 1572872 | tf_op jit(solution)/shard_map/ppermute | solution.py:172
  19.6 11.8 %collective-permute-done.4 = bf16[64,2048]{1,0:T(8,128)(2,1)S(1)} collective-permute-done((bf16[64,2048]{1,0:T(8,128)(2,1)}, bf16[64,2048]{1,0:T(8,128)(2,1)S(1)}, u32[]{:S(2)}, u32[]{:S(2)}) %collective-permute-start.4) | collective-permute-done | bytes 262176 | tf_op jit(solution)/shard_map/ppermute | solution.py:172
  38.4 5.0 %collective-permute-done.7 = f32[2,2,16,128]{3,2,1,0:T(8,128)S(1)} collective-permute-done((f32[2,2,16,128]{3,2,1,0:T(8,128)S(1)}, f32[2,2,16,128]{3,2,1,0:T(8,128)S(1)}, u32[]{:S(2)}, u32[]{:S(2)}) %collective-permute-start.7) | collective-permute-done | bytes 32800 | tf_op jit(solution)/shard_map/ppermute | solution.py:172
  51.8 4.3 %shard_map.118.refs_5_ = bf16[16,48,2048]{2,1,0:T(8,128)(2,1)} custom-call(bf16[16,48,128]{2,1,0:T(8,128)(2,1)} %fusion.15.pick_ref, bf16[4,64,2048]{2,1,0:T(8,128)(2,1)} %copy-done.2, bf16[4,64,2048]{2,1,0:T(8,128)(2,1)} %copy-done.4, bf16[4,64,2048]{2,1,0:T(8,128)(2,1)} %copy-done.5, bf16[4,64,2048]{2,1,0:T(8,128)(2,1)} %collective-permute-done.16.refs_3_, ...), custom_call_target="tpu_custom_call" | custom-call | flops 1000000 | bytes 100000 | tf_op jit(solution)/shard_map/pallas_call | solution.py:281
  56.1 10.8 %collective-permute-done.13 = bf16[64,2048]{1,0:T(8,128)(2,1)} collective-permute-done((bf16[64,2048]{1,0:T(8,128)(2,1)S(1)}, bf16[64,2048]{1,0:T(8,128)(2,1)}, u32[]{:S(2)}, u32[]{:S(2)}) %collective-permute-start.13) | collective-permute-done | bytes 262176 | tf_op jit(solution)/shard_map/ppermute | solution.py:172
  72.0 5.9 %shard_map.119 = bf16[16,48,2048]{2,1,0:T(8,128)(2,1)} custom-call(bf16[16,48,128]{2,1,0:T(8,128)(2,1)} %fusion.15.pick_ref, bf16[6,64,2048]{2,1,0:T(8,128)(2,1)} %constant_dynamic-update-slice_fusion.refs_0_, bf16[6,64,2048]{2,1,0:T(8,128)(2,1)} %collective-permute-done.12.refs_1_, ...), custom_call_target="tpu_custom_call", output_to_operand_aliasing={{}: (6, {})} | custom-call | flops 1000000 | bytes 100000 | tf_op jit(solution)/shard_map/pallas_call | solution.py:281
  85.7 13.0 %shard_map.120 = (f32[768,768]{1,0:T(8,128)}, f32[768,768]{1,0:T(8,128)}, bf16[768,768]{1,0:T(8,128)(2,1)}, bf16[768,2048]{1,0:T(8,128)(2,1)}) custom-call(bf16[768,2048]{1,0:T(8,128)(2,1)} %bitcast.115, bf16[1,2048,1536]{2,1,0:T(8,128)(2,1)} %gate_up_ref.5, bf16[1,768,2048]{2,1,0:T(8,128)(2,1)} %down_ref.3), custom_call_target="tpu_custom_call" | custom-call | flops 1000000 | bytes 100000 | tf_op jit(solution)/shard_map/pallas_call | solution.py:395
  98.7 7.3 %shard_map.121 = (bf16[12,64,2048]{2,1,0:T(8,128)(2,1)}, bf16[6,64,2048]{2,1,0:T(8,128)(2,1)}, bf16[6,64,2048]{2,1,0:T(8,128)(2,1)}) custom-call(bf16[16,128,48]{2,1,0:T(8,128)(2,1)} %fusion.1.back_ref, f32[16,48,1]{2,1,0:T(8,128)} %copy.20.prob_ref.refs_4_, bf16[16,48,2048]{2,1,0:T(8,128)(2,1)} %bitcast.119), custom_call_target="tpu_custom_call" | custom-call | flops 1000000 | bytes 100000 | tf_op jit(solution)/shard_map/pallas_call | solution.py:360
  106.7 4.5 %shard_map.122 = (bf16[16,48,2048]{2,1,0:T(8,128)(2,1)}, f32[16,48,1]{2,1,0:T(8,128)}) custom-call(bf16[16,48,128]{2,1,0:T(8,128)(2,1)} %fusion.15.pick_ref, bf16[4,64,2048]{2,1,0:T(8,128)(2,1)} %copy-done.2, bf16[4,64,2048]{2,1,0:T(8,128)(2,1)} %copy-done.4, bf16[4,64,2048]{2,1,0:T(8,128)(2,1)} %copy-done.5, ...), custom_call_target="tpu_custom_call" | custom-call | flops 1000000 | bytes 100000 | tf_op jit(solution)/shard_map/pallas_call | solution.py:281
  111.3 3.8 %add_convert_fusion.1 = bf16[6,64,2048]{2,1,0:T(8,128)(2,1)} fusion(bf16[6,64,2048]{2,1,0:T(8,128)(2,1)} %collective-permute-done.21, bf16[12,64,2048]{2,1,0:T(8,128)(2,1)} %get-tuple-element.83), kind=kLoop, calls=%fused_computation.4 | loop fusion | flops 3145728 | bytes 4718592 | tf_op jit(solution)/shard_map/convert_element_type | solution.py:209
  116.7 6.6 %shard_map.123 = (bf16[16,48,2048]{2,1,0:T(8,128)(2,1)}, f32[16,48,1]{2,1,0:T(8,128)}) custom-call(bf16[16,48,128]{2,1,0:T(8,128)(2,1)} %fusion.15.pick_ref, bf16[6,64,2048]{2,1,0:T(8,128)(2,1)} %constant_dynamic-update-slice_fusion.2.refs_0_, bf16[6,64,2048]{2,1,0:T(8,128)(2,1)} %collective-permute-done.20.refs_1_, ...), custom_call_target="tpu_custom_call", output_to_operand_aliasing={{0}: (7, {}), {1}: (8, {})} | custom-call | flops 1000000 | bytes 100000 | tf_op jit(solution)/shard_map/pallas_call | solution.py:281
  123.2 8.6 %shard_map.124.joined_ref = bf16[768,1536]{1,0:T(8,128)(2,1)} custom-call(bf16[768,2048]{1,0:T(8,128)(2,1)} %bitcast.125, f32[768,768]{1,0:T(8,128)} %get-tuple-element.95.gate_pre_ref, f32[768,768]{1,0:T(8,128)} %get-tuple-element.96.up_pre_ref, bf16[1,768,2048]{2,1,0:T(8,128)(2,1)} %down_ref.3), custom_call_target="tpu_custom_call" | custom-call | flops 1000000 | bytes 100000 | tf_op jit(solution)/shard_map/pallas_call | solution.py:431
  131.8 6.3 %shard_map.125 = (bf16[768,2048]{1,0:T(8,128)(2,1)}, f32[1,1024]{1,0:T(1,128)}) custom-call(bf16[768,1536]{1,0:T(8,128)(2,1)} %shard_map.124.joined_ref, bf16[1,2048,1536]{2,1,0:T(8,128)(2,1)} %gate_up_ref.5, bf16[768,2048]{1,0:T(8,128)(2,1)} %bitcast.116), custom_call_target="tpu_custom_call" | custom-call | flops 1000000 | bytes 100000 | tf_op jit(solution)/shard_map/pallas_call | solution.py:460
  138.1 2.9 %add_convert_fusion.6 = bf16[3,64,2048]{2,1,0:T(8,128)(2,1)} fusion(bf16[6,64,2048]{2,1,0:T(8,128)(2,1)} %collective-permute-done.24, bf16[6,64,2048]{2,1,0:T(8,128)(2,1)} %collective-permute-done.25, bf16[12,64,2048]{2,1,0:T(8,128)(2,1)} %get-tuple-element.83), kind=kLoop, calls=%fused_computation.9 | loop fusion | flops 2359296 | bytes 3145728 | tf_op jit(solution)/shard_map/convert_element_type | solution.py:209
  142.8 6.3 %shard_map.126 = (bf16[768,2048]{1,0:T(8,128)(2,1)}, f32[1,1024]{1,0:T(1,128)}) custom-call(bf16[768,1536]{1,0:T(8,128)(2,1)} %shard_map.124.joined_ref, bf16[1,2048,1536]{2,1,0:T(8,128)(2,1)} %gate_up_ref.5, bf16[768,2048]{1,0:T(8,128)(2,1)} %bitcast.117, bf16[768,2048]{1,0:T(8,128)(2,1)} %get-tuple-element.101.refs_0_), custom_call_target="tpu_custom_call", output_to_operand_aliasing={{0}: (3, {})} | custom-call | flops 1000000 | bytes 100000 | tf_op jit(solution)/shard_map/pallas_call | solution.py:460
  149.2 6.5 %shard_map.127 = (bf16[12,64,2048]{2,1,0:T(8,128)(2,1)}, bf16[6,64,2048]{2,1,0:T(8,128)(2,1)}, bf16[6,64,2048]{2,1,0:T(8,128)(2,1)}) custom-call(bf16[16,128,48]{2,1,0:T(8,128)(2,1)} %fusion.1.back_ref, f32[16,48,1]{2,1,0:T(8,128)} %copy.20.prob_ref.refs_4_, bf16[16,48,2048]{2,1,0:T(8,128)(2,1)} %bitcast.123), custom_call_target="tpu_custom_call" | custom-call | flops 1000000 | bytes 100000 | tf_op jit(solution)/shard_map/pallas_call | solution.py:360
  163.3 7.3 %convolution_convert_fusion = bf16[2048,1536]{1,0:T(8,128)(2,1)} fusion(bf16[768,2048]{1,0:T(8,128)(2,1)S(1)} %bitcast.118, bf16[768,1536]{1,0:T(8,128)(2,1)S(1)} %copy-done.1), kind=kOutput, calls=%fused_computation.1 | convolution fusion | flops 4834983936 | bytes 11796480 | tf_op jit(solution)/shard_map/dot_general | solution.py:38
  172.1 11.5 %collective-permute-done.29 = f32[48,128]{1,0:T(8,128)S(1)} collective-permute-done((f32[48,128]{1,0:T(8,128)S(1)}, f32[48,128]{1,0:T(8,128)S(1)}, u32[]{:S(2)}, u32[]{:S(2)}) %collective-permute-start.29) | collective-permute-done | bytes 24608 | tf_op jit(solution)/shard_map/ppermute | solution.py:172
  184.5 5.6 %shard_map.128 = (bf16[8,64,2048]{2,1,0:T(8,128)(2,1)}, bf16[4,64,2048]{2,1,0:T(8,128)(2,1)}, bf16[4,64,2048]{2,1,0:T(8,128)(2,1)}) custom-call(bf16[16,128,48]{2,1,0:T(8,128)(2,1)} %fusion.1.back_ref, f32[16,48,1]{2,1,0:T(8,128)} %copy.26.prob_ref, bf16[16,48,2048]{2,1,0:T(8,128)(2,1)} %bitcast.122, bf16[16,48,2048]{2,1,0:T(8,128)(2,1)} %bitcast.124), custom_call_target="tpu_custom_call" | custom-call | flops 1000000 | bytes 100000 | tf_op jit(solution)/shard_map/pallas_call | solution.py:360
  191.5 6.6 %convolution_convert_fusion.1 = bf16[768,2048]{1,0:T(8,128)(2,1)} fusion(bf16[768,768]{1,0:T(8,128)(2,1)} %get-tuple-element.118, bf16[768,2048]{1,0:T(8,128)(2,1)} %bitcast.126), kind=kOutput, calls=%fused_computation.2 | convolution fusion | flops 2417491968 | bytes 7471104 | tf_op jit(solution)/shard_map/dot_general | solution.py:38
  202.4 3.1 %add_convert_fusion.4 = bf16[3,64,2048]{2,1,0:T(8,128)(2,1)} fusion(bf16[6,64,2048]{2,1,0:T(8,128)(2,1)} %collective-permute-done.36, bf16[6,64,2048]{2,1,0:T(8,128)(2,1)} %collective-permute-done.32, bf16[12,64,2048]{2,1,0:T(8,128)(2,1)} %get-tuple-element.103), kind=kLoop, calls=%fused_computation.7 | loop fusion | flops 2359296 | bytes 3145728 | tf_op jit(solution)/shard_map/convert_element_type | solution.py:209
  214.1 3.6 %collective-permute-done.37 = bf16[3,64,2048]{2,1,0:T(8,128)(2,1)} collective-permute-done((bf16[3,64,2048]{2,1,0:T(8,128)(2,1)}, bf16[3,64,2048]{2,1,0:T(8,128)(2,1)}, u32[]{:S(2)}, u32[]{:S(2)}) %collective-permute-start.37) | collective-permute-done | bytes 786464 | tf_op jit(solution)/shard_map/ppermute | solution.py:172
  227.9 7.4 %collective-permute-done.42 = bf16[4,64,2048]{2,1,0:T(8,128)(2,1)} collective-permute-done((bf16[4,64,2048]{2,1,0:T(8,128)(2,1)}, bf16[4,64,2048]{2,1,0:T(8,128)(2,1)}, u32[]{:S(2)}, u32[]{:S(2)}) %collective-permute-start.42) | collective-permute-done | bytes 1048608 | tf_op jit(solution)/shard_map/ppermute | solution.py:172
  239.5 6.5 %collective-permute-done.43 = bf16[2,64,2048]{2,1,0:T(8,128)(2,1)S(1)} collective-permute-done((bf16[2,64,2048]{2,1,0:T(8,128)(2,1)S(1)}, bf16[2,64,2048]{2,1,0:T(8,128)(2,1)S(1)}, u32[]{:S(2)}, u32[]{:S(2)}) %collective-permute-start.43) | collective-permute-done | bytes 524320 | tf_op jit(solution)/shard_map/ppermute | solution.py:172
  (211 shorter events, 91.4 us)
Async XLA Ops:
  4.7 14.2 %collective-permute-start.5 = (bf16[64,2048]{1,0:T(8,128)(2,1)}, bf16[64,2048]{1,0:T(8,128)(2,1)S(1)}, u32[]{:S(2)}, u32[]{:S(2)}) collective-permute-start(bf16[64,2048]{1,0:T(8,128)(2,1)} %param.7), channel_id=1, source_target_pairs={{0,8},{1,9},{2,10},{3,11},{4,12},{5,13},{6,14},{7,15},{8,16},{9,17... | collective-permute-start | bytes 786440 | tf_op jit(solution)/shard_map/ppermute | solution.py:172
  6.3 13.3 %collective-permute-start.3 = (bf16[64,2048]{1,0:T(8,128)(2,1)}, bf16[64,2048]{1,0:T(8,128)(2,1)S(1)}, u32[]{:S(2)}, u32[]{:S(2)}) collective-permute-start(bf16[64,2048]{1,0:T(8,128)(2,1)} %param.7), channel_id=1, source_target_pairs={{0,24},{1,25},{2,26},{3,27},{4,28},{5,29},{6,30},{7,31},{8,0},{9,1... | collective-permute-start | bytes 786440 | tf_op jit(solution)/shard_map/ppermute | solution.py:172
  8.5 22.9 %collective-permute-start.4 = (bf16[64,2048]{1,0:T(8,128)(2,1)}, bf16[64,2048]{1,0:T(8,128)(2,1)S(1)}, u32[]{:S(2)}, u32[]{:S(2)}) collective-permute-start(bf16[64,2048]{1,0:T(8,128)(2,1)} %param.7), channel_id=1, source_target_pairs={{0,16},{1,17},{2,18},{3,19},{4,20},{5,21},{6,22},{7,23},{8,24},{9,... | collective-permute-start | bytes 786440 | tf_op jit(solution)/shard_map/ppermute | solution.py:172
  15.1 28.5 %collective-permute-start.10 = (bf16[4,64,2048]{2,1,0:T(8,128)(2,1)S(1)}, bf16[4,64,2048]{2,1,0:T(8,128)(2,1)S(1)}, u32[]{:S(2)}, u32[]{:S(2)}) collective-permute-start(bf16[4,64,2048]{2,1,0:T(8,128)(2,1)S(1)} %pad_maximum_fusion.refs_0_), channel_id=1, source_target_pairs={{0,4},{1,3},{2,6},{3,1},{4,0},{5,7},{6,2},{7,5},{8,12},{9,11},{10,... | collective-permute-start | bytes 3145736 | tf_op jit(solution)/shard_map/ppermute | solution.py:172
  16.8 14.7 %collective-permute-start.2 = (f32[2,16,128]{2,1,0:T(8,128)S(1)}, f32[2,16,128]{2,1,0:T(8,128)S(1)}, u32[]{:S(2)}, u32[]{:S(2)}) collective-permute-start(f32[2,16,128]{2,1,0:T(8,128)S(1)} %get-tuple-element.152), channel_id=1, source_target_pairs={{0,4},{1,3},{2,6},{3,1},{4,0},{5,7},{6,2},{7,5},{8,12},{9,11},{10,... | collective-permute-start | bytes 49160 | tf_op jit(solution)/shard_map/ppermute | solution.py:172
  44.6 23.5 %collective-permute-start.12 = (bf16[6,64,2048]{2,1,0:T(8,128)(2,1)}, bf16[6,64,2048]{2,1,0:T(8,128)(2,1)}, u32[]{:S(2)}, u32[]{:S(2)}) collective-permute-start(bf16[6,64,2048]{2,1,0:T(8,128)(2,1)} %constant_dynamic-update-slice_fusion.refs_0_), channel_id=1, source_target_pairs={{0,4},{1,3},{2,6},{3,1},{4,0},{5,7},{6,2},{7,5},{8,12},{9,11},{10,... | collective-permute-start | bytes 4718600 | tf_op jit(solution)/shard_map/ppermute | solution.py:172
  46.5 20.5 %collective-permute-start.13 = (bf16[64,2048]{1,0:T(8,128)(2,1)S(1)}, bf16[64,2048]{1,0:T(8,128)(2,1)}, u32[]{:S(2)}, u32[]{:S(2)}) collective-permute-start(bf16[64,2048]{1,0:T(8,128)(2,1)S(1)} %copy-done.7), channel_id=1, source_target_pairs={{0,16},{1,17},{2,18},{3,19},{4,20},{5,21},{6,22},{7,23},{8,24},{9,... | collective-permute-start | bytes 786440 | tf_op jit(solution)/shard_map/ppermute | solution.py:172
  47.7 19.2 %collective-permute-start.14 = (bf16[64,2048]{1,0:T(8,128)(2,1)S(1)}, bf16[64,2048]{1,0:T(8,128)(2,1)}, u32[]{:S(2)}, u32[]{:S(2)}) collective-permute-start(bf16[64,2048]{1,0:T(8,128)(2,1)S(1)} %copy-done.7), channel_id=1, source_target_pairs={{0,8},{1,9},{2,10},{3,11},{4,12},{5,13},{6,14},{7,15},{8,16},{9,17... | collective-permute-start | bytes 786440 | tf_op jit(solution)/shard_map/ppermute | solution.py:172
  50.8 19.7 %collective-permute-start.17 = (bf16[6,64,2048]{2,1,0:T(8,128)(2,1)}, bf16[6,64,2048]{2,1,0:T(8,128)(2,1)}, u32[]{:S(2)}, u32[]{:S(2)}) collective-permute-start(bf16[6,64,2048]{2,1,0:T(8,128)(2,1)} %constant_dynamic-update-slice_fusion.refs_0_), channel_id=1, source_target_pairs={{0,1},{1,0},{2,3},{3,2},{4,5},{5,4},{6,7},{7,6},{8,9},{9,8},{10,11... | collective-permute-start | bytes 4718600 | tf_op jit(solution)/shard_map/ppermute | solution.py:172
  82.5 23.6 %collective-permute-start.20 = (bf16[6,64,2048]{2,1,0:T(8,128)(2,1)}, bf16[6,64,2048]{2,1,0:T(8,128)(2,1)}, u32[]{:S(2)}, u32[]{:S(2)}) collective-permute-start(bf16[6,64,2048]{2,1,0:T(8,128)(2,1)} %constant_dynamic-update-slice_fusion.2.refs_0_), channel_id=1, source_target_pairs={{0,4},{1,3},{2,6},{3,1},{4,0},{5,7},{6,2},{7,5},{8,12},{9,11},{10,... | collective-permute-start | bytes 4718600 | tf_op jit(solution)/shard_map/ppermute | solution.py:172
  115.0 23.1 %collective-permute-start.25 = (bf16[6,64,2048]{2,1,0:T(8,128)(2,1)}, bf16[6,64,2048]{2,1,0:T(8,128)(2,1)}, u32[]{:S(2)}, u32[]{:S(2)}) collective-permute-start(bf16[6,64,2048]{2,1,0:T(8,128)(2,1)} %add_convert_fusion.1), channel_id=1, source_target_pairs={{0,4},{1,3},{2,6},{3,1},{4,0},{5,7},{6,2},{7,5},{8,12},{9,11},{10,... | collective-permute-start | bytes 4718600 | tf_op jit(solution)/shard_map/ppermute | solution.py:172
  116.5 21.6 %collective-permute-start.24 = (bf16[6,64,2048]{2,1,0:T(8,128)(2,1)}, bf16[6,64,2048]{2,1,0:T(8,128)(2,1)}, u32[]{:S(2)}, u32[]{:S(2)}) collective-permute-start(bf16[6,64,2048]{2,1,0:T(8,128)(2,1)} %get-tuple-element.97), channel_id=1, source_target_pairs={{0,1},{1,0},{2,3},{3,2},{4,5},{5,4},{6,7},{7,6},{8,9},{9,8},{10,11... | collective-permute-start | bytes 4718600 | tf_op jit(solution)/shard_map/ppermute | solution.py:172
  141.1 14.6 %collective-permute-start.26 = (bf16[3,64,2048]{2,1,0:T(8,128)(2,1)}, bf16[3,64,2048]{2,1,0:T(8,128)(2,1)}, u32[]{:S(2)}, u32[]{:S(2)}) collective-permute-start(bf16[3,64,2048]{2,1,0:T(8,128)(2,1)} %add_convert_fusion.6), channel_id=1, source_target_pairs={{0,2},{1,5},{2,0},{3,7},{4,6},{5,1},{6,4},{7,3},{8,10},{9,13},{10,... | collective-permute-start | bytes 2359304 | tf_op jit(solution)/shard_map/ppermute | solution.py:172
  159.3 30.8 %collective-permute-start.30 = (bf16[64,2048]{1,0:T(8,128)(2,1)}, bf16[64,2048]{1,0:T(8,128)(2,1)}, u32[]{:S(2)}, u32[]{:S(2)}) collective-permute-start(bf16[64,2048]{1,0:T(8,128)(2,1)} %get-tuple-element.143), channel_id=1, source_target_pairs={{0,8},{1,9},{2,10},{3,11},{4,12},{5,13},{6,14},{7,15},{8,16},{9,17... | collective-permute-start | bytes 786440 | tf_op jit(solution)/shard_map/ppermute | solution.py:172
  159.3 30.9 %collective-permute-start.31 = (bf16[64,2048]{1,0:T(8,128)(2,1)S(1)}, bf16[64,2048]{1,0:T(8,128)(2,1)}, u32[]{:S(2)}, u32[]{:S(2)}) collective-permute-start(bf16[64,2048]{1,0:T(8,128)(2,1)S(1)} %get-tuple-element.142), channel_id=1, source_target_pairs={{0,16},{1,17},{2,18},{3,19},{4,20},{5,21},{6,22},{7,23},{8,24},{9,... | collective-permute-start | bytes 786440 | tf_op jit(solution)/shard_map/ppermute | solution.py:172
  162.4 38.6 %collective-permute-start.32 = (bf16[6,64,2048]{2,1,0:T(8,128)(2,1)}, bf16[6,64,2048]{2,1,0:T(8,128)(2,1)}, u32[]{:S(2)}, u32[]{:S(2)}) collective-permute-start(bf16[6,64,2048]{2,1,0:T(8,128)(2,1)} %add_convert_fusion), channel_id=1, source_target_pairs={{0,4},{1,3},{2,6},{3,1},{4,0},{5,7},{6,2},{7,5},{8,12},{9,11},{10,... | collective-permute-start | bytes 4718600 | tf_op jit(solution)/shard_map/ppermute | solution.py:172
  170.8 12.7 %collective-permute-start.29 = (f32[48,128]{1,0:T(8,128)S(1)}, f32[48,128]{1,0:T(8,128)S(1)}, u32[]{:S(2)}, u32[]{:S(2)}) collective-permute-start(f32[48,128]{1,0:T(8,128)S(1)} %pad_maximum_fusion.10), channel_id=1, source_target_pairs={{0,4},{1,5},{2,6},{3,7},{4,0},{5,1},{6,2},{7,3},{8,12},{9,13},{10,... | collective-permute-start | bytes 73736 | tf_op jit(solution)/shard_map/ppermute | solution.py:172
  172.0 30.3 %collective-permute-start.36 = (bf16[6,64,2048]{2,1,0:T(8,128)(2,1)}, bf16[6,64,2048]{2,1,0:T(8,128)(2,1)}, u32[]{:S(2)}, u32[]{:S(2)}) collective-permute-start(bf16[6,64,2048]{2,1,0:T(8,128)(2,1)} %get-tuple-element.122), channel_id=1, source_target_pairs={{0,1},{1,0},{2,3},{3,2},{4,5},{5,4},{6,7},{7,6},{8,9},{9,8},{10,11... | collective-permute-start | bytes 4718600 | tf_op jit(solution)/shard_map/ppermute | solution.py:172
  198.1 16.0 %collective-permute-start.41 = (bf16[64,2048]{1,0:T(8,128)(2,1)S(1)}, bf16[64,2048]{1,0:T(8,128)(2,1)S(1)}, u32[]{:S(2)}, u32[]{:S(2)}) collective-permute-start(bf16[64,2048]{1,0:T(8,128)(2,1)S(1)} %get-tuple-element.141), channel_id=1, source_target_pairs={{0,24},{1,25},{2,26},{3,27},{4,28},{5,29},{6,30},{7,31},{8,0},{9,1... | collective-permute-start | bytes 786440 | tf_op jit(solution)/shard_map/ppermute | solution.py:172
  205.4 12.3 %collective-permute-start.37 = (bf16[3,64,2048]{2,1,0:T(8,128)(2,1)}, bf16[3,64,2048]{2,1,0:T(8,128)(2,1)}, u32[]{:S(2)}, u32[]{:S(2)}) collective-permute-start(bf16[3,64,2048]{2,1,0:T(8,128)(2,1)} %add_convert_fusion.4), channel_id=1, source_target_pairs={{0,2},{1,5},{2,0},{3,7},{4,6},{5,1},{6,4},{7,3},{8,10},{9,13},{10,... | collective-permute-start | bytes 2359304 | tf_op jit(solution)/shard_map/ppermute | solution.py:172
  220.1 15.2 %collective-permute-start.42 = (bf16[4,64,2048]{2,1,0:T(8,128)(2,1)}, bf16[4,64,2048]{2,1,0:T(8,128)(2,1)}, u32[]{:S(2)}, u32[]{:S(2)}) collective-permute-start(bf16[4,64,2048]{2,1,0:T(8,128)(2,1)} %add_convert_fusion.2), channel_id=1, source_target_pairs={{0,4},{1,3},{2,6},{3,1},{4,0},{5,7},{6,2},{7,5},{8,12},{9,11},{10,... | collective-permute-start | bytes 3145736 | tf_op jit(solution)/shard_map/ppermute | solution.py:172
  222.8 24.7 %collective-permute-start.44 = (bf16[64,2048]{1,0:T(8,128)(2,1)}, bf16[64,2048]{1,0:T(8,128)(2,1)S(1)}, u32[]{:S(2)}, u32[]{:S(2)}) collective-permute-start(bf16[64,2048]{1,0:T(8,128)(2,1)} %get-tuple-element.138), channel_id=1, source_target_pairs={{0,8},{1,9},{2,10},{3,11},{4,12},{5,13},{6,14},{7,15},{8,16},{9,17... | collective-permute-start | bytes 786440 | tf_op jit(solution)/shard_map/ppermute | solution.py:172
  222.9 24.6 %collective-permute-start.45 = (bf16[64,2048]{1,0:T(8,128)(2,1)S(1)}, bf16[64,2048]{1,0:T(8,128)(2,1)S(1)}, u32[]{:S(2)}, u32[]{:S(2)}) collective-permute-start(bf16[64,2048]{1,0:T(8,128)(2,1)S(1)} %get-tuple-element.140), channel_id=1, source_target_pairs={{0,16},{1,17},{2,18},{3,19},{4,20},{5,21},{6,22},{7,23},{8,24},{9,... | collective-permute-start | bytes 786440 | tf_op jit(solution)/shard_map/ppermute | solution.py:172
  224.4 23.2 %collective-permute-start.46 = (bf16[64,2048]{1,0:T(8,128)(2,1)S(1)}, bf16[64,2048]{1,0:T(8,128)(2,1)S(1)}, u32[]{:S(2)}, u32[]{:S(2)}) collective-permute-start(bf16[64,2048]{1,0:T(8,128)(2,1)S(1)} %get-tuple-element.139), channel_id=1, source_target_pairs={{0,24},{1,25},{2,26},{3,27},{4,28},{5,29},{6,30},{7,31},{8,0},{9,1... | collective-permute-start | bytes 786440 | tf_op jit(solution)/shard_map/ppermute | solution.py:172
  (43 other events, 317.8 us)

commit v12 on v11

--- a/solution.py
+++ b/solution.py
@@ -377,8 +377,8 @@
     projected = jnp.dot(rows_ref[...], gate_up_ref[0], preferred_element_type=jnp.float32)
     half_width = hidden_ref.shape[1]
     gate_pre, up_pre = projected[:, :half_width], projected[:, half_width:]
-    gate_pre_ref[...] = gate_pre
-    up_pre_ref[...] = up_pre
+    gate_pre_ref[...] = gate_pre.astype(jnp.bfloat16)
+    up_pre_ref[...] = up_pre.astype(jnp.bfloat16)
     hidden = (gate_pre * jax.nn.sigmoid(gate_pre) * up_pre).astype(jnp.bfloat16)
     hidden_ref[...] = hidden
     out_ref[...] = jnp.dot(hidden, down_ref[0], preferred_element_type=jnp.float32).astype(jnp.bfloat16)
@@ -402,8 +402,8 @@
         ],
         out_specs=[row_spec(width), row_spec(width), row_spec(width), row_spec(features)],
         out_shape=[
-            jax.ShapeDtypeStruct((slots, width), jnp.float32),
-            jax.ShapeDtypeStruct((slots, width), jnp.float32),
+            jax.ShapeDtypeStruct((slots, width), jnp.bfloat16),
+            jax.ShapeDtypeStruct((slots, width), jnp.bfloat16),
             jax.ShapeDtypeStruct((slots, width), jnp.bfloat16),
             jax.ShapeDtypeStruct((slots, features), jnp.bfloat16),
         ],
@@ -415,7 +415,7 @@
 def inner_kernel(units, grads_ref, gate_pre_ref, up_pre_ref, down_ref, joined_ref):
     step = pl.program_id(0)
     block = gate_pre_ref.shape[1]
-    gate_pre, up_pre = gate_pre_ref[...], up_pre_ref[...]
+    gate_pre, up_pre = gate_pre_ref[...].astype(jnp.float32), up_pre_ref[...].astype(jnp.float32)
     sigmoid_gate = jax.nn.sigmoid(gate_pre)
     common = times_transposed(grads_ref[...], down_ref[0]) * sigmoid_gate
     gate_grad = common * up_pre * (1.0 + gate_pre * (1.0 - sigmoid_gate))
@@ -599,11 +599,9 @@
     columns, gains = unpack_add(columns[..., :half], gains, got)
     got = send_bit(pack(columns[1], gains), 2)
     near_mine, near_low, near_high = expand(
-        back, after(slot_prob, got), (out_slots, input_slots), (True, False), 1, far
-    )
-    near_high, got = together(near_high, got, *out_far[:-1])[:2]
-    columns, gains = unpack_add(columns[0], gains, got)
-    got = send_bit(pack(columns[1], gains), 1)
+        back, after(slot_prob, gate_up_part), (out_slots, input_slots), (True, False), 1, far
+    )
+    near_high = after(near_high, *out_far[:-1])
     near_core_high = send_core(near_high)
     near_core = send_core(near_low)
     down_part = outer_sum(after(hidden, near_high), grads)
@@ -615,14 +613,19 @@
         add_up(in_mine[one_far:half_far], in_core[one_far:half_far], in_first[one_far:])
     )
     in_second = send_second(in_middle)
-    messages = [send_along(pack(columns[step], gains), step) for step in range(1, steps)]
+    got = send_bit(pack(columns[1], gains), 1)
     near_upper = narrow(add_up(near_mine[4:], near_core_high))
-    in_second, near_upper, *messages = together(in_second, near_upper, *messages, *out_far[-1:])[:2 + len(messages)]
+    in_second, near_upper, got = together(in_second, near_upper, got, *out_far[-1:])[:3]
+    columns, gains = unpack_add(columns[0], gains, got)
     in_planes = narrow(own_plane(in_mine, in_core, in_first, in_second, one_far))
     in_far = [send_along(in_planes[step - 1], step) for step in range(1, steps)]
     near_first = send_first(after(near_upper, in_planes))
+    near_first, *in_far[:-1] = together(near_first, *in_far[:-1])
     near_middle = narrow(add_up(near_mine[2:4], near_core[2:], near_first[2:]))
     near_second = send_second(near_middle)
+    messages = [
+        send_along(after(pack(columns[step], gains), near_middle), step) for step in range(1, steps)
+    ]
     near_sum = own_plane(near_mine, near_core, near_first, near_second, 2)
     out_sum = near_sum[0] + add_up(*out_far)
     normed_grad = near_sum[1] + add_up(*in_far)

time: 252 us -> 249 us (0.988)
  waiting for transfers between devices: 63.6 us -> 58 us
    ppermute x47, waiting for transfers between devices: 63.6 us -> 58 us  [send(): return lax.ppermute(array, BOTH, pairs)]
  transfers between devices with their start and end apart: 47 -> 47, of which waited for: 14 -> 16; matrix products, arithmetic and copies ran while one was open for 18% -> 19% of each run, Pallas kernels for 30% -> 30%
where the time goes in v12:
time: 249 us; the launch traced here: 248 us
  Pallas kernels  74.5 us (30%)
  waiting for transfers between devices  58 us (23%)
  starting transfers between devices  50.9 us (20%)
  other arithmetic  36 us (14%)
  matrix products  14.2 us (6%)
  local copies, waits for them, and re-layouts  13.5 us (5%)
    ppermute x47, waiting for transfers between devices, send(): return lax.ppermute(array, BOTH, pairs)  58 us
    ppermute x47, starting transfers between devices, send(): return lax.ppermute(array, BOTH, pairs)  50.9 us
    pallas_call x4, Pallas kernels, select(): pl.pallas_call(functools.partial(kernel, count), grid=(4,), in_specs=[gro...  21.5 us
    convert_element_type x8, other arithmetic, narrow(): return value.astype(jnp.bfloat16)  19.7 us
    pallas_call x3, Pallas kernels, expand(): pl.pallas_call(functools.partial(expand_kernel, weighted, count, first_gr...  19.4 us
    dot_general x2, matrix products, outer_sum(): lax.dot_general(left, right, (((0,), (0,)), ((), ())), preferred_element_...  14 us
    pallas_call x1, Pallas kernels, forward(): pl.pallas_call(forward_kernel, grid=(2,), in_specs=[row_spec(features), p...  13 us
    pallas_call x2, Pallas kernels, backward_input(): pl.pallas_call(input_kernel, grid=(2,), in_specs=[pl.BlockSpec((slots, wi...  12.6 us
  transfers between devices with their start and end apart: 47, of which 16 were waited for; matrix products, arithmetic and copies ran while one was open for 19% of the time, Pallas kernels for 30%

profile of v12, /device:TPU:0, one launch (start us, length us, event | category | flops | bytes accessed | tf_op | source)
XLA Modules:
  0.0 248.1 jit_solution(9057924833703196080)
XLA Ops:
  1.7 3.0 %collective-permute-start = (bf16[2,64,2048]{2,1,0:T(8,128)(2,1)S(1)}, bf16[2,64,2048]{2,1,0:T(8,128)(2,1)S(1)}, u32[]{:S(2)}, u32[]{:S(2)}) collective-permute-start(bf16[2,64,2048]{2,1,0:T(8,128)(2,1)S(1)} %pad_maximum_fusion.3), channel_id=1, source_target_pairs={{0,2},{1,5},{2,0},{3,7},{4,6},{5,1},{6,4},{7,3},{8,10},{9,13},{10,... | collective-permute-start | bytes 1572872 | tf_op jit(solution)/shard_map/ppermute | solution.py:172
  4.7 3.6 %collective-permute-start.3 = (bf16[64,2048]{1,0:T(8,128)(2,1)}, bf16[64,2048]{1,0:T(8,128)(2,1)S(1)}, u32[]{:S(2)}, u32[]{:S(2)}) collective-permute-start(bf16[64,2048]{1,0:T(8,128)(2,1)} %param.7), channel_id=1, source_target_pairs={{0,24},{1,25},{2,26},{3,27},{4,28},{5,29},{6,30},{7,31},{8,0},{9,1... | collective-permute-start | bytes 786440 | tf_op jit(solution)/shard_map/ppermute | solution.py:172
  21.9 8.7 %collective-permute-done.4 = bf16[64,2048]{1,0:T(8,128)(2,1)S(1)} collective-permute-done((bf16[64,2048]{1,0:T(8,128)(2,1)}, bf16[64,2048]{1,0:T(8,128)(2,1)S(1)}, u32[]{:S(2)}, u32[]{:S(2)}) %collective-permute-start.4) | collective-permute-done | bytes 262176 | tf_op jit(solution)/shard_map/ppermute | solution.py:172
  32.4 3.7 %collective-permute-start.11 = (bf16[64,2048]{1,0:T(8,128)(2,1)S(1)}, bf16[64,2048]{1,0:T(8,128)(2,1)S(1)}, u32[]{:S(2)}, u32[]{:S(2)}) collective-permute-start(bf16[64,2048]{1,0:T(8,128)(2,1)S(1)} %copy-done.8), channel_id=1, source_target_pairs={{0,24},{1,25},{2,26},{3,27},{4,28},{5,29},{6,30},{7,31},{8,0},{9,1... | collective-permute-start | bytes 786440 | tf_op jit(solution)/shard_map/ppermute | solution.py:172
  51.9 4.3 %shard_map.118.refs_5_ = bf16[16,48,2048]{2,1,0:T(8,128)(2,1)} custom-call(bf16[16,48,128]{2,1,0:T(8,128)(2,1)} %fusion.15.pick_ref, bf16[4,64,2048]{2,1,0:T(8,128)(2,1)} %copy-done.2, bf16[4,64,2048]{2,1,0:T(8,128)(2,1)} %copy-done.4, bf16[4,64,2048]{2,1,0:T(8,128)(2,1)} %copy-done.5, bf16[4,64,2048]{2,1,0:T(8,128)(2,1)} %collective-permute-done.16.refs_3_, ...), custom_call_target="tpu_custom_call" | custom-call | flops 1000000 | bytes 100000 | tf_op jit(solution)/shard_map/pallas_call | solution.py:281
  56.5 10.5 %collective-permute-done.13 = bf16[64,2048]{1,0:T(8,128)(2,1)} collective-permute-done((bf16[64,2048]{1,0:T(8,128)(2,1)S(1)}, bf16[64,2048]{1,0:T(8,128)(2,1)}, u32[]{:S(2)}, u32[]{:S(2)}) %collective-permute-start.13) | collective-permute-done | bytes 262176 | tf_op jit(solution)/shard_map/ppermute | solution.py:172
  72.8 6.0 %shard_map.119 = bf16[16,48,2048]{2,1,0:T(8,128)(2,1)} custom-call(bf16[16,48,128]{2,1,0:T(8,128)(2,1)} %fusion.15.pick_ref, bf16[6,64,2048]{2,1,0:T(8,128)(2,1)} %constant_dynamic-update-slice_fusion.refs_0_, bf16[6,64,2048]{2,1,0:T(8,128)(2,1)} %collective-permute-done.12.refs_1_, ...), custom_call_target="tpu_custom_call", output_to_operand_aliasing={{}: (6, {})} | custom-call | flops 1000000 | bytes 100000 | tf_op jit(solution)/shard_map/pallas_call | solution.py:281
  87.1 13.0 %shard_map.120 = (bf16[768,768]{1,0:T(8,128)(2,1)}, bf16[768,768]{1,0:T(8,128)(2,1)}, bf16[768,768]{1,0:T(8,128)(2,1)}, bf16[768,2048]{1,0:T(8,128)(2,1)}) custom-call(bf16[768,2048]{1,0:T(8,128)(2,1)} %bitcast.115, bf16[1,2048,1536]{2,1,0:T(8,128)(2,1)} %gate_up_ref.5, bf16[1,768,2048]{2,1,0:T(8,128)(2,1)} %down_ref.3), custom_call_target="tpu_custom_call" | custom-call | flops 1000000 | bytes 100000 | tf_op jit(solution)/shard_map/pallas_call | solution.py:395
  100.1 7.3 %shard_map.121 = (bf16[12,64,2048]{2,1,0:T(8,128)(2,1)}, bf16[6,64,2048]{2,1,0:T(8,128)(2,1)}, bf16[6,64,2048]{2,1,0:T(8,128)(2,1)}) custom-call(bf16[16,128,48]{2,1,0:T(8,128)(2,1)} %fusion.1.back_ref, f32[16,48,1]{2,1,0:T(8,128)} %copy.23.prob_ref.refs_4_, bf16[16,48,2048]{2,1,0:T(8,128)(2,1)} %bitcast.119), custom_call_target="tpu_custom_call" | custom-call | flops 1000000 | bytes 100000 | tf_op jit(solution)/shard_map/pallas_call | solution.py:360
  108.1 4.5 %shard_map.122 = (bf16[16,48,2048]{2,1,0:T(8,128)(2,1)}, f32[16,48,1]{2,1,0:T(8,128)}) custom-call(bf16[16,48,128]{2,1,0:T(8,128)(2,1)} %fusion.15.pick_ref, bf16[4,64,2048]{2,1,0:T(8,128)(2,1)} %copy-done.2, bf16[4,64,2048]{2,1,0:T(8,128)(2,1)} %copy-done.4, bf16[4,64,2048]{2,1,0:T(8,128)(2,1)} %copy-done.5, ...), custom_call_target="tpu_custom_call" | custom-call | flops 1000000 | bytes 100000 | tf_op jit(solution)/shard_map/pallas_call | solution.py:281
  112.6 3.8 %add_convert_fusion.1 = bf16[6,64,2048]{2,1,0:T(8,128)(2,1)} fusion(bf16[6,64,2048]{2,1,0:T(8,128)(2,1)} %collective-permute-done.21, bf16[12,64,2048]{2,1,0:T(8,128)(2,1)} %get-tuple-element.86), kind=kLoop, calls=%fused_computation.4 | loop fusion | flops 3145728 | bytes 4718592 | tf_op jit(solution)/shard_map/convert_element_type | solution.py:209
  117.7 6.6 %shard_map.123 = (bf16[16,48,2048]{2,1,0:T(8,128)(2,1)}, f32[16,48,1]{2,1,0:T(8,128)}) custom-call(bf16[16,48,128]{2,1,0:T(8,128)(2,1)} %fusion.15.pick_ref, bf16[6,64,2048]{2,1,0:T(8,128)(2,1)} %constant_dynamic-update-slice_fusion.2.refs_0_, bf16[6,64,2048]{2,1,0:T(8,128)(2,1)} %collective-permute-done.20.refs_1_, ...), custom_call_target="tpu_custom_call", output_to_operand_aliasing={{0}: (7, {}), {1}: (8, {})} | custom-call | flops 1000000 | bytes 100000 | tf_op jit(solution)/shard_map/pallas_call | solution.py:281
  124.4 8.0 %shard_map.124.joined_ref = bf16[768,1536]{1,0:T(8,128)(2,1)} custom-call(bf16[768,2048]{1,0:T(8,128)(2,1)} %bitcast.125, bf16[768,768]{1,0:T(8,128)(2,1)} %get-tuple-element.97.gate_pre_ref, bf16[768,768]{1,0:T(8,128)(2,1)} %get-tuple-element.98.up_pre_ref, bf16[1,768,2048]{2,1,0:T(8,128)(2,1)} %down_ref.3), custom_call_target="tpu_custom_call" | custom-call | flops 1000000 | bytes 100000 | tf_op jit(solution)/shard_map/pallas_call | solution.py:431
  132.4 6.3 %shard_map.125 = (bf16[768,2048]{1,0:T(8,128)(2,1)}, f32[1,1024]{1,0:T(1,128)}) custom-call(bf16[768,1536]{1,0:T(8,128)(2,1)} %shard_map.124.joined_ref, bf16[1,2048,1536]{2,1,0:T(8,128)(2,1)} %gate_up_ref.5, bf16[768,2048]{1,0:T(8,128)(2,1)} %bitcast.116), custom_call_target="tpu_custom_call" | custom-call | flops 1000000 | bytes 100000 | tf_op jit(solution)/shard_map/pallas_call | solution.py:460
  138.7 3.0 %add_convert_fusion.6 = bf16[3,64,2048]{2,1,0:T(8,128)(2,1)} fusion(bf16[6,64,2048]{2,1,0:T(8,128)(2,1)} %collective-permute-done.24, bf16[6,64,2048]{2,1,0:T(8,128)(2,1)} %collective-permute-done.25, bf16[12,64,2048]{2,1,0:T(8,128)(2,1)} %get-tuple-element.86), kind=kLoop, calls=%fused_computation.9 | loop fusion | flops 2359296 | bytes 3145728 | tf_op jit(solution)/shard_map/convert_element_type | solution.py:209
  144.6 6.3 %shard_map.126 = (bf16[768,2048]{1,0:T(8,128)(2,1)}, f32[1,1024]{1,0:T(1,128)}) custom-call(bf16[768,1536]{1,0:T(8,128)(2,1)} %shard_map.124.joined_ref, bf16[1,2048,1536]{2,1,0:T(8,128)(2,1)} %gate_up_ref.5, bf16[768,2048]{1,0:T(8,128)(2,1)} %bitcast.117, bf16[768,2048]{1,0:T(8,128)(2,1)} %get-tuple-element.103.refs_0_), custom_call_target="tpu_custom_call", output_to_operand_aliasing={{0}: (3, {})} | custom-call | flops 1000000 | bytes 100000 | tf_op jit(solution)/shard_map/pallas_call | solution.py:460
  151.0 6.5 %shard_map.127 = (bf16[12,64,2048]{2,1,0:T(8,128)(2,1)}, bf16[6,64,2048]{2,1,0:T(8,128)(2,1)}, bf16[6,64,2048]{2,1,0:T(8,128)(2,1)}) custom-call(bf16[16,128,48]{2,1,0:T(8,128)(2,1)} %fusion.1.back_ref, f32[16,48,1]{2,1,0:T(8,128)} %copy.23.prob_ref.refs_4_, bf16[16,48,2048]{2,1,0:T(8,128)(2,1)} %bitcast.123), custom_call_target="tpu_custom_call" | custom-call | flops 1000000 | bytes 100000 | tf_op jit(solution)/shard_map/pallas_call | solution.py:360
  166.1 7.3 %convolution_convert_fusion = bf16[2048,1536]{1,0:T(8,128)(2,1)} fusion(bf16[768,2048]{1,0:T(8,128)(2,1)S(1)} %bitcast.118, bf16[768,1536]{1,0:T(8,128)(2,1)S(1)} %copy-done.1), kind=kOutput, calls=%fused_computation.1 | convolution fusion | flops 4834983936 | bytes 11796480 | tf_op jit(solution)/shard_map/dot_general | solution.py:38
  174.5 5.6 %shard_map.128 = (bf16[8,64,2048]{2,1,0:T(8,128)(2,1)}, bf16[4,64,2048]{2,1,0:T(8,128)(2,1)}, bf16[4,64,2048]{2,1,0:T(8,128)(2,1)}) custom-call(bf16[16,128,48]{2,1,0:T(8,128)(2,1)} %fusion.1.back_ref, f32[16,48,1]{2,1,0:T(8,128)} %copy.26.prob_ref, bf16[16,48,2048]{2,1,0:T(8,128)(2,1)} %bitcast.122, bf16[16,48,2048]{2,1,0:T(8,128)(2,1)} %bitcast.124), custom_call_target="tpu_custom_call" | custom-call | flops 1000000 | bytes 100000 | tf_op jit(solution)/shard_map/pallas_call | solution.py:360
  182.6 6.7 %convolution_convert_fusion.1 = bf16[768,2048]{1,0:T(8,128)(2,1)} fusion(bf16[768,768]{1,0:T(8,128)(2,1)} %get-tuple-element.121, bf16[768,2048]{1,0:T(8,128)(2,1)} %bitcast.126), kind=kOutput, calls=%fused_computation.2 | convolution fusion | flops 2417491968 | bytes 7471104 | tf_op jit(solution)/shard_map/dot_general | solution.py:38
  198.3 6.8 %collective-permute-done.37 = f32[32,128]{1,0:T(8,128)S(1)} collective-permute-done((f32[32,128]{1,0:T(8,128)S(1)}, f32[32,128]{1,0:T(8,128)S(1)}, u32[]{:S(2)}, u32[]{:S(2)}) %collective-permute-start.37) | collective-permute-done | bytes 16416 | tf_op jit(solution)/shard_map/ppermute | solution.py:172
  212.6 16.0 %collective-permute-done.41 = bf16[64,2048]{1,0:T(8,128)(2,1)S(1)} collective-permute-done((bf16[64,2048]{1,0:T(8,128)(2,1)S(1)}, bf16[64,2048]{1,0:T(8,128)(2,1)S(1)}, u32[]{:S(2)}, u32[]{:S(2)}) %collective-permute-start.41) | collective-permute-done | bytes 262176 | tf_op jit(solution)/shard_map/ppermute | solution.py:172
  230.2 3.9 %collective-permute-start.43 = (bf16[64,2048]{1,0:T(8,128)(2,1)S(1)}, bf16[64,2048]{1,0:T(8,128)(2,1)S(1)}, u32[]{:S(2)}, u32[]{:S(2)}) collective-permute-start(bf16[64,2048]{1,0:T(8,128)(2,1)S(1)} %get-tuple-element.144), channel_id=1, source_target_pairs={{0,24},{1,25},{2,26},{3,27},{4,28},{5,29},{6,30},{7,31},{8,0},{9,1... | collective-permute-start | bytes 786440 | tf_op jit(solution)/shard_map/ppermute | solution.py:172
  235.8 4.0 %collective-permute-done.45 = f32[20,128]{1,0:T(8,128)S(1)} collective-permute-done((f32[20,128]{1,0:T(8,128)S(1)}, f32[20,128]{1,0:T(8,128)S(1)}, u32[]{:S(2)}, u32[]{:S(2)}) %collective-permute-start.45) | collective-permute-done | bytes 10272 | tf_op jit(solution)/shard_map/ppermute | solution.py:172
  (210 shorter events, 91.5 us)
Async XLA Ops:
  4.7 14.2 %collective-permute-start.3 = (bf16[64,2048]{1,0:T(8,128)(2,1)}, bf16[64,2048]{1,0:T(8,128)(2,1)S(1)}, u32[]{:S(2)}, u32[]{:S(2)}) collective-permute-start(bf16[64,2048]{1,0:T(8,128)(2,1)} %param.7), channel_id=1, source_target_pairs={{0,24},{1,25},{2,26},{3,27},{4,28},{5,29},{6,30},{7,31},{8,0},{9,1... | collective-permute-start | bytes 786440 | tf_op jit(solution)/shard_map/ppermute | solution.py:172
  8.3 13.6 %collective-permute-start.5 = (bf16[64,2048]{1,0:T(8,128)(2,1)}, bf16[64,2048]{1,0:T(8,128)(2,1)S(1)}, u32[]{:S(2)}, u32[]{:S(2)}) collective-permute-start(bf16[64,2048]{1,0:T(8,128)(2,1)} %param.7), channel_id=1, source_target_pairs={{0,8},{1,9},{2,10},{3,11},{4,12},{5,13},{6,14},{7,15},{8,16},{9,17... | collective-permute-start | bytes 786440 | tf_op jit(solution)/shard_map/ppermute | solution.py:172
  8.3 22.3 %collective-permute-start.4 = (bf16[64,2048]{1,0:T(8,128)(2,1)}, bf16[64,2048]{1,0:T(8,128)(2,1)S(1)}, u32[]{:S(2)}, u32[]{:S(2)}) collective-permute-start(bf16[64,2048]{1,0:T(8,128)(2,1)} %param.7), channel_id=1, source_target_pairs={{0,16},{1,17},{2,18},{3,19},{4,20},{5,21},{6,22},{7,23},{8,24},{9,... | collective-permute-start | bytes 786440 | tf_op jit(solution)/shard_map/ppermute | solution.py:172
  15.1 27.7 %collective-permute-start.10 = (bf16[4,64,2048]{2,1,0:T(8,128)(2,1)S(1)}, bf16[4,64,2048]{2,1,0:T(8,128)(2,1)S(1)}, u32[]{:S(2)}, u32[]{:S(2)}) collective-permute-start(bf16[4,64,2048]{2,1,0:T(8,128)(2,1)S(1)} %pad_maximum_fusion.refs_0_), channel_id=1, source_target_pairs={{0,4},{1,3},{2,6},{3,1},{4,0},{5,7},{6,2},{7,5},{8,12},{9,11},{10,... | collective-permute-start | bytes 3145736 | tf_op jit(solution)/shard_map/ppermute | solution.py:172
  16.8 13.9 %collective-permute-start.2 = (f32[2,16,128]{2,1,0:T(8,128)S(1)}, f32[2,16,128]{2,1,0:T(8,128)S(1)}, u32[]{:S(2)}, u32[]{:S(2)}) collective-permute-start(f32[2,16,128]{2,1,0:T(8,128)S(1)} %get-tuple-element.158), channel_id=1, source_target_pairs={{0,4},{1,3},{2,6},{3,1},{4,0},{5,7},{6,2},{7,5},{8,12},{9,11},{10,... | collective-permute-start | bytes 49160 | tf_op jit(solution)/shard_map/ppermute | solution.py:172
  30.7 12.1 %collective-permute-start.9 = (bf16[3,64,2048]{2,1,0:T(8,128)(2,1)S(1)}, bf16[3,64,2048]{2,1,0:T(8,128)(2,1)S(1)}, u32[]{:S(2)}, u32[]{:S(2)}) collective-permute-start(bf16[3,64,2048]{2,1,0:T(8,128)(2,1)S(1)} %pad_maximum_fusion.1), channel_id=1, source_target_pairs={{0,2},{1,5},{2,0},{3,7},{4,6},{5,1},{6,4},{7,3},{8,10},{9,13},{10,... | collective-permute-start | bytes 2359304 | tf_op jit(solution)/shard_map/ppermute | solution.py:172
  43.8 25.2 %collective-permute-start.12 = (bf16[6,64,2048]{2,1,0:T(8,128)(2,1)}, bf16[6,64,2048]{2,1,0:T(8,128)(2,1)}, u32[]{:S(2)}, u32[]{:S(2)}) collective-permute-start(bf16[6,64,2048]{2,1,0:T(8,128)(2,1)} %constant_dynamic-update-slice_fusion.refs_0_), channel_id=1, source_target_pairs={{0,4},{1,3},{2,6},{3,1},{4,0},{5,7},{6,2},{7,5},{8,12},{9,11},{10,... | collective-permute-start | bytes 4718600 | tf_op jit(solution)/shard_map/ppermute | solution.py:172
  45.2 11.3 %collective-permute-start.14 = (bf16[64,2048]{1,0:T(8,128)(2,1)S(1)}, bf16[64,2048]{1,0:T(8,128)(2,1)}, u32[]{:S(2)}, u32[]{:S(2)}) collective-permute-start(bf16[64,2048]{1,0:T(8,128)(2,1)S(1)} %copy-done.8), channel_id=1, source_target_pairs={{0,8},{1,9},{2,10},{3,11},{4,12},{5,13},{6,14},{7,15},{8,16},{9,17... | collective-permute-start | bytes 786440 | tf_op jit(solution)/shard_map/ppermute | solution.py:172
  47.1 19.8 %collective-permute-start.13 = (bf16[64,2048]{1,0:T(8,128)(2,1)S(1)}, bf16[64,2048]{1,0:T(8,128)(2,1)}, u32[]{:S(2)}, u32[]{:S(2)}) collective-permute-start(bf16[64,2048]{1,0:T(8,128)(2,1)S(1)} %copy-done.8), channel_id=1, source_target_pairs={{0,16},{1,17},{2,18},{3,19},{4,20},{5,21},{6,22},{7,23},{8,24},{9,... | collective-permute-start | bytes 786440 | tf_op jit(solution)/shard_map/ppermute | solution.py:172
  50.9 21.9 %collective-permute-start.17 = (bf16[6,64,2048]{2,1,0:T(8,128)(2,1)}, bf16[6,64,2048]{2,1,0:T(8,128)(2,1)}, u32[]{:S(2)}, u32[]{:S(2)}) collective-permute-start(bf16[6,64,2048]{2,1,0:T(8,128)(2,1)} %constant_dynamic-update-slice_fusion.refs_0_), channel_id=1, source_target_pairs={{0,1},{1,0},{2,3},{3,2},{4,5},{5,4},{6,7},{7,6},{8,9},{9,8},{10,11... | collective-permute-start | bytes 4718600 | tf_op jit(solution)/shard_map/ppermute | solution.py:172
  69.0 12.3 %collective-permute-start.19 = (bf16[3,64,2048]{2,1,0:T(8,128)(2,1)}, bf16[3,64,2048]{2,1,0:T(8,128)(2,1)}, u32[]{:S(2)}, u32[]{:S(2)}) collective-permute-start(bf16[3,64,2048]{2,1,0:T(8,128)(2,1)} %pad_maximum_fusion.2), channel_id=1, source_target_pairs={{0,2},{1,5},{2,0},{3,7},{4,6},{5,1},{6,4},{7,3},{8,10},{9,13},{10,... | collective-permute-start | bytes 2359304 | tf_op jit(solution)/shard_map/ppermute | solution.py:172
  83.4 24.1 %collective-permute-start.20 = (bf16[6,64,2048]{2,1,0:T(8,128)(2,1)}, bf16[6,64,2048]{2,1,0:T(8,128)(2,1)}, u32[]{:S(2)}, u32[]{:S(2)}) collective-permute-start(bf16[6,64,2048]{2,1,0:T(8,128)(2,1)} %constant_dynamic-update-slice_fusion.2.refs_0_), channel_id=1, source_target_pairs={{0,4},{1,3},{2,6},{3,1},{4,0},{5,7},{6,2},{7,5},{8,12},{9,11},{10,... | collective-permute-start | bytes 4718600 | tf_op jit(solution)/shard_map/ppermute | solution.py:172
  116.4 22.3 %collective-permute-start.25 = (bf16[6,64,2048]{2,1,0:T(8,128)(2,1)}, bf16[6,64,2048]{2,1,0:T(8,128)(2,1)}, u32[]{:S(2)}, u32[]{:S(2)}) collective-permute-start(bf16[6,64,2048]{2,1,0:T(8,128)(2,1)} %add_convert_fusion.1), channel_id=1, source_target_pairs={{0,4},{1,3},{2,6},{3,1},{4,0},{5,7},{6,2},{7,5},{8,12},{9,11},{10,... | collective-permute-start | bytes 4718600 | tf_op jit(solution)/shard_map/ppermute | solution.py:172
  117.2 21.5 %collective-permute-start.24 = (bf16[6,64,2048]{2,1,0:T(8,128)(2,1)}, bf16[6,64,2048]{2,1,0:T(8,128)(2,1)}, u32[]{:S(2)}, u32[]{:S(2)}) collective-permute-start(bf16[6,64,2048]{2,1,0:T(8,128)(2,1)} %get-tuple-element.99), channel_id=1, source_target_pairs={{0,1},{1,0},{2,3},{3,2},{4,5},{5,4},{6,7},{7,6},{8,9},{9,8},{10,11... | collective-permute-start | bytes 4718600 | tf_op jit(solution)/shard_map/ppermute | solution.py:172
  141.7 15.7 %collective-permute-start.26 = (bf16[3,64,2048]{2,1,0:T(8,128)(2,1)}, bf16[3,64,2048]{2,1,0:T(8,128)(2,1)}, u32[]{:S(2)}, u32[]{:S(2)}) collective-permute-start(bf16[3,64,2048]{2,1,0:T(8,128)(2,1)} %add_convert_fusion.6), channel_id=1, source_target_pairs={{0,2},{1,5},{2,0},{3,7},{4,6},{5,1},{6,4},{7,3},{8,10},{9,13},{10,... | collective-permute-start | bytes 2359304 | tf_op jit(solution)/shard_map/ppermute | solution.py:172
  157.7 33.2 %collective-permute-start.35 = (bf16[6,64,2048]{2,1,0:T(8,128)(2,1)}, bf16[6,64,2048]{2,1,0:T(8,128)(2,1)}, u32[]{:S(2)}, u32[]{:S(2)}) collective-permute-start(bf16[6,64,2048]{2,1,0:T(8,128)(2,1)} %get-tuple-element.125), channel_id=1, source_target_pairs={{0,1},{1,0},{2,3},{3,2},{4,5},{5,4},{6,7},{7,6},{8,9},{9,8},{10,11... | collective-permute-start | bytes 4718600 | tf_op jit(solution)/shard_map/ppermute | solution.py:172
  161.6 19.1 %collective-permute-start.30 = (bf16[64,2048]{1,0:T(8,128)(2,1)}, bf16[64,2048]{1,0:T(8,128)(2,1)}, u32[]{:S(2)}, u32[]{:S(2)}) collective-permute-start(bf16[64,2048]{1,0:T(8,128)(2,1)} %get-tuple-element.148), channel_id=1, source_target_pairs={{0,16},{1,17},{2,18},{3,19},{4,20},{5,21},{6,22},{7,23},{8,24},{9,... | collective-permute-start | bytes 786440 | tf_op jit(solution)/shard_map/ppermute | solution.py:172
  161.6 19.1 %collective-permute-start.29 = (bf16[64,2048]{1,0:T(8,128)(2,1)S(1)}, bf16[64,2048]{1,0:T(8,128)(2,1)}, u32[]{:S(2)}, u32[]{:S(2)}) collective-permute-start(bf16[64,2048]{1,0:T(8,128)(2,1)S(1)} %get-tuple-element.149), channel_id=1, source_target_pairs={{0,8},{1,9},{2,10},{3,11},{4,12},{5,13},{6,14},{7,15},{8,16},{9,17... | collective-permute-start | bytes 786440 | tf_op jit(solution)/shard_map/ppermute | solution.py:172
  165.0 25.7 %collective-permute-start.31 = (bf16[6,64,2048]{2,1,0:T(8,128)(2,1)}, bf16[6,64,2048]{2,1,0:T(8,128)(2,1)}, u32[]{:S(2)}, u32[]{:S(2)}) collective-permute-start(bf16[6,64,2048]{2,1,0:T(8,128)(2,1)} %add_convert_fusion), channel_id=1, source_target_pairs={{0,4},{1,3},{2,6},{3,1},{4,0},{5,7},{6,2},{7,5},{8,12},{9,11},{10,... | collective-permute-start | bytes 4718600 | tf_op jit(solution)/shard_map/ppermute | solution.py:172
  192.9 12.2 %collective-permute-start.36 = (bf16[3,64,2048]{2,1,0:T(8,128)(2,1)S(1)}, bf16[3,64,2048]{2,1,0:T(8,128)(2,1)S(1)}, u32[]{:S(2)}, u32[]{:S(2)}) collective-permute-start(bf16[3,64,2048]{2,1,0:T(8,128)(2,1)S(1)} %add_convert_fusion.4), channel_id=1, source_target_pairs={{0,2},{1,5},{2,0},{3,7},{4,6},{5,1},{6,4},{7,3},{8,10},{9,13},{10,... | collective-permute-start | bytes 2359304 | tf_op jit(solution)/shard_map/ppermute | solution.py:172
  207.9 20.8 %collective-permute-start.39 = (bf16[4,64,2048]{2,1,0:T(8,128)(2,1)}, bf16[4,64,2048]{2,1,0:T(8,128)(2,1)S(1)}, u32[]{:S(2)}, u32[]{:S(2)}) collective-permute-start(bf16[4,64,2048]{2,1,0:T(8,128)(2,1)} %add_convert_fusion.2), channel_id=1, source_target_pairs={{0,4},{1,3},{2,6},{3,1},{4,0},{5,7},{6,2},{7,5},{8,12},{9,11},{10,... | collective-permute-start | bytes 3145736 | tf_op jit(solution)/shard_map/ppermute | solution.py:172
  209.8 18.8 %collective-permute-start.41 = (bf16[64,2048]{1,0:T(8,128)(2,1)S(1)}, bf16[64,2048]{1,0:T(8,128)(2,1)S(1)}, u32[]{:S(2)}, u32[]{:S(2)}) collective-permute-start(bf16[64,2048]{1,0:T(8,128)(2,1)S(1)} %get-tuple-element.145), channel_id=1, source_target_pairs={{0,16},{1,17},{2,18},{3,19},{4,20},{5,21},{6,22},{7,23},{8,24},{9,... | collective-permute-start | bytes 786440 | tf_op jit(solution)/shard_map/ppermute | solution.py:172
  211.1 17.5 %collective-permute-start.40 = (bf16[64,2048]{1,0:T(8,128)(2,1)S(1)}, bf16[64,2048]{1,0:T(8,128)(2,1)S(1)}, u32[]{:S(2)}, u32[]{:S(2)}) collective-permute-start(bf16[64,2048]{1,0:T(8,128)(2,1)S(1)} %get-tuple-element.146), channel_id=1, source_target_pairs={{0,8},{1,9},{2,10},{3,11},{4,12},{5,13},{6,14},{7,15},{8,16},{9,17... | collective-permute-start | bytes 786440 | tf_op jit(solution)/shard_map/ppermute | solution.py:172
  230.2 14.6 %collective-permute-start.43 = (bf16[64,2048]{1,0:T(8,128)(2,1)S(1)}, bf16[64,2048]{1,0:T(8,128)(2,1)S(1)}, u32[]{:S(2)}, u32[]{:S(2)}) collective-permute-start(bf16[64,2048]{1,0:T(8,128)(2,1)S(1)} %get-tuple-element.144), channel_id=1, source_target_pairs={{0,24},{1,25},{2,26},{3,27},{4,28},{5,29},{6,30},{7,31},{8,0},{9,1... | collective-permute-start | bytes 786440 | tf_op jit(solution)/shard_map/ppermute | solution.py:172
  (42 other events, 308.9 us)

commit v13 on v11

--- a/solution.py
+++ b/solution.py
@@ -492,7 +492,7 @@
     steps = len(gains)
     order = (lax.axis_index("expert") // 4 - jnp.arange(steps)) % steps
     ordered = jnp.take(jnp.stack(gains), order, axis=0)
-    return functools.reduce(jnp.add, [ordered[step] for step in range(steps)]).reshape(-1)
+    return functools.reduce(jnp.add, [ordered[step] for step in range(steps)])
 
 
 def broadcast_shards(tokens, cotangent, gain, expert_ids, gate_probs, gate_up_weight, down_weight):
@@ -597,41 +597,42 @@
     gate_up_part = outer_sum(after(rows, in_upper), joined_grad)
     gate_up_part, got = together(gate_up_part, got)
     columns, gains = unpack_add(columns[..., :half], gains, got)
-    got = send_bit(pack(columns[1], gains), 2)
+    messages = [send_along(pack(columns[:, :, step], gains), step) for step in range(1, steps)]
     near_mine, near_low, near_high = expand(
-        back, after(slot_prob, got), (out_slots, input_slots), (True, False), 1, far
-    )
-    near_high, got = together(near_high, got, *out_far[:-1])[:2]
-    columns, gains = unpack_add(columns[0], gains, got)
-    got = send_bit(pack(columns[1], gains), 1)
+        back, after(slot_prob, gate_up_part), (out_slots, input_slots), (True, False), 1, far
+    )
+    near_high = after(near_high, *out_far[:-1])
     near_core_high = send_core(near_high)
     near_core = send_core(near_low)
     down_part = outer_sum(after(hidden, near_high), grads)
-    down_part, in_first, near_core, near_core_high, got = together(
-        down_part, in_first, near_core, near_core_high, got
-    )
-    columns, gains = unpack_add(columns[0], gains, got)
+    down_part, in_first, near_core, near_core_high, *messages = together(
+        down_part, in_first, near_core, near_core_high, *messages
+    )
+    columns, all_gains = columns[:, :, 0], [gains]
+    for message in messages:
+        columns = columns + message[:-gains.shape[0]].reshape(columns.shape)
+        all_gains.append(message[-gains.shape[0]:])
+    gains = planes_in_order(all_gains)
+    got = send_bit(pack(columns[1], gains), 2)
     in_middle = narrow(
         add_up(in_mine[one_far:half_far], in_core[one_far:half_far], in_first[one_far:])
     )
     in_second = send_second(in_middle)
-    messages = [send_along(pack(columns[step], gains), step) for step in range(1, steps)]
-    near_upper = narrow(add_up(near_mine[4:], near_core_high))
-    in_second, near_upper, *messages = together(in_second, near_upper, *messages, *out_far[-1:])[:2 + len(messages)]
+    near_upper = narrow(add_up(near_mine[4:], after(near_core_high, in_middle)))
+    near_first = send_first(near_upper)
+    in_second, got = together(in_second, got, *out_far[-1:])[:2]
+    columns, gains = unpack_add(columns[0], gains, got)
     in_planes = narrow(own_plane(in_mine, in_core, in_first, in_second, one_far))
     in_far = [send_along(in_planes[step - 1], step) for step in range(1, steps)]
-    near_first = send_first(after(near_upper, in_planes))
+    middle = len(in_far) // 2
+    near_first, in_far[middle] = together(near_first, in_far[middle])
     near_middle = narrow(add_up(near_mine[2:4], near_core[2:], near_first[2:]))
     near_second = send_second(near_middle)
+    got = send_bit(after(pack(columns[1], gains), near_middle), 1)
+    prob_sum, gains = unpack_add(columns[0], gains, got)
     near_sum = own_plane(near_mine, near_core, near_first, near_second, 2)
     out_sum = near_sum[0] + add_up(*out_far)
     normed_grad = near_sum[1] + add_up(*in_far)
-
-    prob_sum, all_gains = columns[0], [gains]
-    for message in messages:
-        prob_sum = prob_sum + message[:-gains.shape[0]].reshape(prob_sum.shape)
-        all_gains.append(message[-gains.shape[0]:])
-    gain_grad = planes_in_order(all_gains)
 
     scaled_own, inv_own = normalize(tokens)
     mixed = (tokens.astype(jnp.float32) + out_sum).astype(jnp.bfloat16)
@@ -641,7 +642,7 @@
         + inv_own
         * (gain_side - scaled_own * jnp.mean(gain_side * scaled_own, axis=1, keepdims=True))
     ).astype(jnp.bfloat16)
-    return (mixed, token_grad, prob_sum.T, gain_grad, gate_up_part[None], down_part[None])
+    return (mixed, token_grad, prob_sum.T, gains.reshape(-1), gate_up_part[None], down_part[None])
 
 
 def solution(mesh):

time: 252 us -> 259 us (1.028)
  waiting for transfers between devices: 63.6 us -> 75 us
  starting transfers between devices: 50 us -> 46.9 us
    ppermute x47, waiting for transfers between devices: 63.6 us -> 75 us  [send(): return lax.ppermute(array, BOTH, pairs)]
    ppermute x47, starting transfers between devices: 50 us -> 46.9 us  [send(): return lax.ppermute(array, BOTH, pairs)]
  transfers between devices with their start and end apart: 47 -> 47, of which waited for: 14 -> 16; matrix products, arithmetic and copies ran while one was open for 18% -> 18% of each run, Pallas kernels for 30% -> 29%
where the time goes in v13:
time: 259 us; the launch traced here: 258 us
  waiting for transfers between devices  75 us (29%)
  Pallas kernels  75 us (29%)
  starting transfers between devices  46.9 us (18%)
  other arithmetic  34 us (13%)
  matrix products  13.8 us (5%)
  local copies, waits for them, and re-layouts  11.9 us (5%)
    ppermute x47, waiting for transfers between devices, send(): return lax.ppermute(array, BOTH, pairs)  75 us
    ppermute x47, starting transfers between devices, send(): return lax.ppermute(array, BOTH, pairs)  46.9 us
    pallas_call x4, Pallas kernels, select(): pl.pallas_call(functools.partial(kernel, count), grid=(4,), in_specs=[gro...  21.3 us
    convert_element_type x8, other arithmetic, narrow(): return value.astype(jnp.bfloat16)  20.5 us
    pallas_call x3, Pallas kernels, expand(): pl.pallas_call(functools.partial(expand_kernel, weighted, count, first_gr...  19.3 us
    dot_general x2, matrix products, outer_sum(): lax.dot_general(left, right, (((0,), (0,)), ((), ())), preferred_element_...  13.6 us
    pallas_call x1, Pallas kernels, forward(): pl.pallas_call(forward_kernel, grid=(2,), in_specs=[row_spec(features), p...  13 us
    pallas_call x2, Pallas kernels, backward_input(): pl.pallas_call(input_kernel, grid=(2,), in_specs=[pl.BlockSpec((slots, wi...  12.7 us
  transfers between devices with their start and end apart: 47, of which 16 were waited for; matrix products, arithmetic and copies ran while one was open for 18% of the time, Pallas kernels for 29%

profile of v13, /device:TPU:0, one launch (start us, length us, event | category | flops | bytes accessed | tf_op | source)
XLA Modules:
  0.0 257.7 jit_solution(14593124995490431621)
XLA Ops:
  19.6 11.8 %collective-permute-done.4 = bf16[64,2048]{1,0:T(8,128)(2,1)S(1)} collective-permute-done((bf16[64,2048]{1,0:T(8,128)(2,1)}, bf16[64,2048]{1,0:T(8,128)(2,1)S(1)}, u32[]{:S(2)}, u32[]{:S(2)}) %collective-permute-start.4) | collective-permute-done | bytes 262176 | tf_op jit(solution)/shard_map/ppermute | solution.py:172
  38.4 5.0 %collective-permute-done.7 = f32[2,2,16,128]{3,2,1,0:T(8,128)S(1)} collective-permute-done((f32[2,2,16,128]{3,2,1,0:T(8,128)S(1)}, f32[2,2,16,128]{3,2,1,0:T(8,128)S(1)}, u32[]{:S(2)}, u32[]{:S(2)}) %collective-permute-start.7) | collective-permute-done | bytes 32800 | tf_op jit(solution)/shard_map/ppermute | solution.py:172
  51.8 4.3 %shard_map.118.refs_5_ = bf16[16,48,2048]{2,1,0:T(8,128)(2,1)} custom-call(bf16[16,48,128]{2,1,0:T(8,128)(2,1)} %fusion.15.pick_ref, bf16[4,64,2048]{2,1,0:T(8,128)(2,1)} %copy-done.2, bf16[4,64,2048]{2,1,0:T(8,128)(2,1)} %copy-done.4, bf16[4,64,2048]{2,1,0:T(8,128)(2,1)} %copy-done.5, bf16[4,64,2048]{2,1,0:T(8,128)(2,1)} %collective-permute-done.16.refs_3_, ...), custom_call_target="tpu_custom_call" | custom-call | flops 1000000 | bytes 100000 | tf_op jit(solution)/shard_map/pallas_call | solution.py:281
  56.1 10.8 %collective-permute-done.13 = bf16[64,2048]{1,0:T(8,128)(2,1)} collective-permute-done((bf16[64,2048]{1,0:T(8,128)(2,1)S(1)}, bf16[64,2048]{1,0:T(8,128)(2,1)}, u32[]{:S(2)}, u32[]{:S(2)}) %collective-permute-start.13) | collective-permute-done | bytes 262176 | tf_op jit(solution)/shard_map/ppermute | solution.py:172
  71.9 5.9 %shard_map.119 = bf16[16,48,2048]{2,1,0:T(8,128)(2,1)} custom-call(bf16[16,48,128]{2,1,0:T(8,128)(2,1)} %fusion.15.pick_ref, bf16[6,64,2048]{2,1,0:T(8,128)(2,1)} %constant_dynamic-update-slice_fusion.refs_0_, bf16[6,64,2048]{2,1,0:T(8,128)(2,1)} %collective-permute-done.12.refs_1_, ...), custom_call_target="tpu_custom_call", output_to_operand_aliasing={{}: (6, {})} | custom-call | flops 1000000 | bytes 100000 | tf_op jit(solution)/shard_map/pallas_call | solution.py:281
  85.6 13.0 %shard_map.120 = (f32[768,768]{1,0:T(8,128)}, f32[768,768]{1,0:T(8,128)}, bf16[768,768]{1,0:T(8,128)(2,1)}, bf16[768,2048]{1,0:T(8,128)(2,1)}) custom-call(bf16[768,2048]{1,0:T(8,128)(2,1)} %bitcast.126, bf16[1,2048,1536]{2,1,0:T(8,128)(2,1)} %gate_up_ref.5, bf16[1,768,2048]{2,1,0:T(8,128)(2,1)} %down_ref.3), custom_call_target="tpu_custom_call" | custom-call | flops 1000000 | bytes 100000 | tf_op jit(solution)/shard_map/pallas_call | solution.py:395
  98.7 7.3 %shard_map.121 = (bf16[12,64,2048]{2,1,0:T(8,128)(2,1)}, bf16[6,64,2048]{2,1,0:T(8,128)(2,1)}, bf16[6,64,2048]{2,1,0:T(8,128)(2,1)}) custom-call(bf16[16,128,48]{2,1,0:T(8,128)(2,1)} %fusion.1.back_ref, f32[16,48,1]{2,1,0:T(8,128)} %copy.23.prob_ref.refs_4_, bf16[16,48,2048]{2,1,0:T(8,128)(2,1)} %bitcast.130), custom_call_target="tpu_custom_call" | custom-call | flops 1000000 | bytes 100000 | tf_op jit(solution)/shard_map/pallas_call | solution.py:360
  106.7 4.5 %shard_map.122 = (bf16[16,48,2048]{2,1,0:T(8,128)(2,1)}, f32[16,48,1]{2,1,0:T(8,128)}) custom-call(bf16[16,48,128]{2,1,0:T(8,128)(2,1)} %fusion.15.pick_ref, bf16[4,64,2048]{2,1,0:T(8,128)(2,1)} %copy-done.2, bf16[4,64,2048]{2,1,0:T(8,128)(2,1)} %copy-done.4, bf16[4,64,2048]{2,1,0:T(8,128)(2,1)} %copy-done.5, ...), custom_call_target="tpu_custom_call" | custom-call | flops 1000000 | bytes 100000 | tf_op jit(solution)/shard_map/pallas_call | solution.py:281
  111.2 3.7 %add_convert_fusion.1 = bf16[6,64,2048]{2,1,0:T(8,128)(2,1)} fusion(bf16[6,64,2048]{2,1,0:T(8,128)(2,1)} %collective-permute-done.21, bf16[12,64,2048]{2,1,0:T(8,128)(2,1)} %get-tuple-element.84), kind=kLoop, calls=%fused_computation.4 | loop fusion | flops 3145728 | bytes 4718592 | tf_op jit(solution)/shard_map/convert_element_type | solution.py:209
  116.4 6.6 %shard_map.123 = (bf16[16,48,2048]{2,1,0:T(8,128)(2,1)}, f32[16,48,1]{2,1,0:T(8,128)}) custom-call(bf16[16,48,128]{2,1,0:T(8,128)(2,1)} %fusion.15.pick_ref, bf16[6,64,2048]{2,1,0:T(8,128)(2,1)} %constant_dynamic-update-slice_fusion.2.refs_0_, bf16[6,64,2048]{2,1,0:T(8,128)(2,1)} %collective-permute-done.20.refs_1_, ...), custom_call_target="tpu_custom_call", output_to_operand_aliasing={{0}: (7, {}), {1}: (8, {})} | custom-call | flops 1000000 | bytes 100000 | tf_op jit(solution)/shard_map/pallas_call | solution.py:281
  123.0 8.6 %shard_map.124.joined_ref = bf16[768,1536]{1,0:T(8,128)(2,1)} custom-call(bf16[768,2048]{1,0:T(8,128)(2,1)} %bitcast.136, f32[768,768]{1,0:T(8,128)} %get-tuple-element.95.gate_pre_ref, f32[768,768]{1,0:T(8,128)} %get-tuple-element.96.up_pre_ref, bf16[1,768,2048]{2,1,0:T(8,128)(2,1)} %down_ref.3), custom_call_target="tpu_custom_call" | custom-call | flops 1000000 | bytes 100000 | tf_op jit(solution)/shard_map/pallas_call | solution.py:431
  131.5 6.3 %shard_map.125 = (bf16[768,2048]{1,0:T(8,128)(2,1)}, f32[1,1024]{1,0:T(1,128)}) custom-call(bf16[768,1536]{1,0:T(8,128)(2,1)} %shard_map.124.joined_ref, bf16[1,2048,1536]{2,1,0:T(8,128)(2,1)} %gate_up_ref.5, bf16[768,2048]{1,0:T(8,128)(2,1)} %bitcast.127), custom_call_target="tpu_custom_call" | custom-call | flops 1000000 | bytes 100000 | tf_op jit(solution)/shard_map/pallas_call | solution.py:460
  137.9 3.0 %add_convert_fusion.6 = bf16[3,64,2048]{2,1,0:T(8,128)(2,1)} fusion(bf16[6,64,2048]{2,1,0:T(8,128)(2,1)} %collective-permute-done.24, bf16[6,64,2048]{2,1,0:T(8,128)(2,1)} %collective-permute-done.25, bf16[12,64,2048]{2,1,0:T(8,128)(2,1)} %get-tuple-element.84), kind=kLoop, calls=%fused_computation.9 | loop fusion | flops 2359296 | bytes 3145728 | tf_op jit(solution)/shard_map/convert_element_type | solution.py:209
  142.8 6.4 %shard_map.126 = (bf16[768,2048]{1,0:T(8,128)(2,1)}, f32[1,1024]{1,0:T(1,128)}) custom-call(bf16[768,1536]{1,0:T(8,128)(2,1)} %shard_map.124.joined_ref, bf16[1,2048,1536]{2,1,0:T(8,128)(2,1)} %gate_up_ref.5, bf16[768,2048]{1,0:T(8,128)(2,1)} %bitcast.128, bf16[768,2048]{1,0:T(8,128)(2,1)} %get-tuple-element.101.refs_0_), custom_call_target="tpu_custom_call", output_to_operand_aliasing={{0}: (3, {})} | custom-call | flops 1000000 | bytes 100000 | tf_op jit(solution)/shard_map/pallas_call | solution.py:460
  149.2 6.5 %shard_map.127 = (bf16[12,64,2048]{2,1,0:T(8,128)(2,1)}, bf16[6,64,2048]{2,1,0:T(8,128)(2,1)}, bf16[6,64,2048]{2,1,0:T(8,128)(2,1)}) custom-call(bf16[16,128,48]{2,1,0:T(8,128)(2,1)} %fusion.1.back_ref, f32[16,48,1]{2,1,0:T(8,128)} %copy.23.prob_ref.refs_4_, bf16[16,48,2048]{2,1,0:T(8,128)(2,1)} %bitcast.134), custom_call_target="tpu_custom_call" | custom-call | flops 1000000 | bytes 100000 | tf_op jit(solution)/shard_map/pallas_call | solution.py:360
  163.9 7.1 %convolution_convert_fusion = bf16[2048,1536]{1,0:T(8,128)(2,1)} fusion(bf16[768,2048]{1,0:T(8,128)(2,1)S(1)} %bitcast.129, bf16[768,1536]{1,0:T(8,128)(2,1)S(1)} %copy-done.1), kind=kOutput, calls=%fused_computation.1 | convolution fusion | flops 4834983936 | bytes 11796480 | tf_op jit(solution)/shard_map/dot_general | solution.py:38
  172.2 5.6 %shard_map.128 = (bf16[8,64,2048]{2,1,0:T(8,128)(2,1)}, bf16[4,64,2048]{2,1,0:T(8,128)(2,1)}, bf16[4,64,2048]{2,1,0:T(8,128)(2,1)}) custom-call(bf16[16,128,48]{2,1,0:T(8,128)(2,1)} %fusion.1.back_ref, f32[16,48,1]{2,1,0:T(8,128)} %copy.26.prob_ref, bf16[16,48,2048]{2,1,0:T(8,128)(2,1)} %bitcast.133, bf16[16,48,2048]{2,1,0:T(8,128)(2,1)} %bitcast.135), custom_call_target="tpu_custom_call" | custom-call | flops 1000000 | bytes 100000 | tf_op jit(solution)/shard_map/pallas_call | solution.py:360
  181.9 5.1 %collective-permute-done.34 = f32[32,128]{1,0:T(8,128)S(1)} collective-permute-done((f32[32,128]{1,0:T(8,128)S(1)}, f32[32,128]{1,0:T(8,128)S(1)}, u32[]{:S(2)}, u32[]{:S(2)}) %collective-permute-start.34) | collective-permute-done | bytes 16416 | tf_op jit(solution)/shard_map/ppermute | solution.py:172
  187.0 6.6 %convolution_convert_fusion.1 = bf16[768,2048]{1,0:T(8,128)(2,1)} fusion(bf16[768,768]{1,0:T(8,128)(2,1)} %get-tuple-element.119, bf16[768,2048]{1,0:T(8,128)(2,1)} %bitcast.137), kind=kOutput, calls=%fused_computation.2 | convolution fusion | flops 2417491968 | bytes 7471104 | tf_op jit(solution)/shard_map/dot_general | solution.py:38
  200.4 3.1 %add_convert_fusion.4 = bf16[3,64,2048]{2,1,0:T(8,128)(2,1)} fusion(bf16[6,64,2048]{2,1,0:T(8,128)(2,1)} %collective-permute-done.37, bf16[6,64,2048]{2,1,0:T(8,128)(2,1)} %collective-permute-done.31, bf16[12,64,2048]{2,1,0:T(8,128)(2,1)} %get-tuple-element.103), kind=kLoop, calls=%fused_computation.7 | loop fusion | flops 2359296 | bytes 3145728 | tf_op jit(solution)/shard_map/convert_element_type | solution.py:209
  210.2 12.2 %collective-permute-done.39 = bf16[3,64,2048]{2,1,0:T(8,128)(2,1)} collective-permute-done((bf16[3,64,2048]{2,1,0:T(8,128)(2,1)}, bf16[3,64,2048]{2,1,0:T(8,128)(2,1)}, u32[]{:S(2)}, u32[]{:S(2)}) %collective-permute-start.39) | collective-permute-done | bytes 786464 | tf_op jit(solution)/shard_map/ppermute | solution.py:172
  226.5 14.2 %collective-permute-done.42 = bf16[64,2048]{1,0:T(8,128)(2,1)S(1)} collective-permute-done((bf16[64,2048]{1,0:T(8,128)(2,1)S(1)}, bf16[64,2048]{1,0:T(8,128)(2,1)S(1)}, u32[]{:S(2)}, u32[]{:S(2)}) %collective-permute-start.42) | collective-permute-done | bytes 262176 | tf_op jit(solution)/shard_map/ppermute | solution.py:172
  244.2 3.8 %collective-permute-start.45 = (bf16[64,2048]{1,0:T(8,128)(2,1)}, bf16[64,2048]{1,0:T(8,128)(2,1)S(1)}, u32[]{:S(2)}, u32[]{:S(2)}) collective-permute-start(bf16[64,2048]{1,0:T(8,128)(2,1)} %get-tuple-element.141), channel_id=1, source_target_pairs={{0,24},{1,25},{2,26},{3,27},{4,28},{5,29},{6,30},{7,31},{8,0},{9,1... | collective-permute-start | bytes 786440 | tf_op jit(solution)/shard_map/ppermute | solution.py:172
  248.1 3.5 %collective-permute-done.46 = f32[20,128]{1,0:T(8,128)S(1)} collective-permute-done((f32[20,128]{1,0:T(8,128)S(1)}, f32[20,128]{1,0:T(8,128)S(1)}, u32[]{:S(2)}, u32[]{:S(2)}) %collective-permute-start.46) | collective-permute-done | bytes 10272 | tf_op jit(solution)/shard_map/ppermute | solution.py:172
  (204 shorter events, 91.8 us)
Async XLA Ops:
  4.7 14.2 %collective-permute-start.5 = (bf16[64,2048]{1,0:T(8,128)(2,1)}, bf16[64,2048]{1,0:T(8,128)(2,1)S(1)}, u32[]{:S(2)}, u32[]{:S(2)}) collective-permute-start(bf16[64,2048]{1,0:T(8,128)(2,1)} %param.7), channel_id=1, source_target_pairs={{0,8},{1,9},{2,10},{3,11},{4,12},{5,13},{6,14},{7,15},{8,16},{9,17... | collective-permute-start | bytes 786440 | tf_op jit(solution)/shard_map/ppermute | solution.py:172
  6.3 13.3 %collective-permute-start.3 = (bf16[64,2048]{1,0:T(8,128)(2,1)}, bf16[64,2048]{1,0:T(8,128)(2,1)S(1)}, u32[]{:S(2)}, u32[]{:S(2)}) collective-permute-start(bf16[64,2048]{1,0:T(8,128)(2,1)} %param.7), channel_id=1, source_target_pairs={{0,24},{1,25},{2,26},{3,27},{4,28},{5,29},{6,30},{7,31},{8,0},{9,1... | collective-permute-start | bytes 786440 | tf_op jit(solution)/shard_map/ppermute | solution.py:172
  8.5 22.9 %collective-permute-start.4 = (bf16[64,2048]{1,0:T(8,128)(2,1)}, bf16[64,2048]{1,0:T(8,128)(2,1)S(1)}, u32[]{:S(2)}, u32[]{:S(2)}) collective-permute-start(bf16[64,2048]{1,0:T(8,128)(2,1)} %param.7), channel_id=1, source_target_pairs={{0,16},{1,17},{2,18},{3,19},{4,20},{5,21},{6,22},{7,23},{8,24},{9,... | collective-permute-start | bytes 786440 | tf_op jit(solution)/shard_map/ppermute | solution.py:172
  15.1 28.5 %collective-permute-start.10 = (bf16[4,64,2048]{2,1,0:T(8,128)(2,1)S(1)}, bf16[4,64,2048]{2,1,0:T(8,128)(2,1)S(1)}, u32[]{:S(2)}, u32[]{:S(2)}) collective-permute-start(bf16[4,64,2048]{2,1,0:T(8,128)(2,1)S(1)} %pad_maximum_fusion.refs_0_), channel_id=1, source_target_pairs={{0,4},{1,3},{2,6},{3,1},{4,0},{5,7},{6,2},{7,5},{8,12},{9,11},{10,... | collective-permute-start | bytes 3145736 | tf_op jit(solution)/shard_map/ppermute | solution.py:172
  16.8 14.7 %collective-permute-start.2 = (f32[2,16,128]{2,1,0:T(8,128)S(1)}, f32[2,16,128]{2,1,0:T(8,128)S(1)}, u32[]{:S(2)}, u32[]{:S(2)}) collective-permute-start(f32[2,16,128]{2,1,0:T(8,128)S(1)} %get-tuple-element.158), channel_id=1, source_target_pairs={{0,4},{1,3},{2,6},{3,1},{4,0},{5,7},{6,2},{7,5},{8,12},{9,11},{10,... | collective-permute-start | bytes 49160 | tf_op jit(solution)/shard_map/ppermute | solution.py:172
  44.6 23.5 %collective-permute-start.12 = (bf16[6,64,2048]{2,1,0:T(8,128)(2,1)}, bf16[6,64,2048]{2,1,0:T(8,128)(2,1)}, u32[]{:S(2)}, u32[]{:S(2)}) collective-permute-start(bf16[6,64,2048]{2,1,0:T(8,128)(2,1)} %constant_dynamic-update-slice_fusion.refs_0_), channel_id=1, source_target_pairs={{0,4},{1,3},{2,6},{3,1},{4,0},{5,7},{6,2},{7,5},{8,12},{9,11},{10,... | collective-permute-start | bytes 4718600 | tf_op jit(solution)/shard_map/ppermute | solution.py:172
  46.5 20.5 %collective-permute-start.13 = (bf16[64,2048]{1,0:T(8,128)(2,1)S(1)}, bf16[64,2048]{1,0:T(8,128)(2,1)}, u32[]{:S(2)}, u32[]{:S(2)}) collective-permute-start(bf16[64,2048]{1,0:T(8,128)(2,1)S(1)} %copy-done.7), channel_id=1, source_target_pairs={{0,16},{1,17},{2,18},{3,19},{4,20},{5,21},{6,22},{7,23},{8,24},{9,... | collective-permute-start | bytes 786440 | tf_op jit(solution)/shard_map/ppermute | solution.py:172
  47.7 19.2 %collective-permute-start.14 = (bf16[64,2048]{1,0:T(8,128)(2,1)S(1)}, bf16[64,2048]{1,0:T(8,128)(2,1)}, u32[]{:S(2)}, u32[]{:S(2)}) collective-permute-start(bf16[64,2048]{1,0:T(8,128)(2,1)S(1)} %copy-done.7), channel_id=1, source_target_pairs={{0,8},{1,9},{2,10},{3,11},{4,12},{5,13},{6,14},{7,15},{8,16},{9,17... | collective-permute-start | bytes 786440 | tf_op jit(solution)/shard_map/ppermute | solution.py:172
  50.8 19.7 %collective-permute-start.17 = (bf16[6,64,2048]{2,1,0:T(8,128)(2,1)}, bf16[6,64,2048]{2,1,0:T(8,128)(2,1)}, u32[]{:S(2)}, u32[]{:S(2)}) collective-permute-start(bf16[6,64,2048]{2,1,0:T(8,128)(2,1)} %constant_dynamic-update-slice_fusion.refs_0_), channel_id=1, source_target_pairs={{0,1},{1,0},{2,3},{3,2},{4,5},{5,4},{6,7},{7,6},{8,9},{9,8},{10,11... | collective-permute-start | bytes 4718600 | tf_op jit(solution)/shard_map/ppermute | solution.py:172
  68.2 12.2 %collective-permute-start.19 = (bf16[3,64,2048]{2,1,0:T(8,128)(2,1)S(1)}, bf16[3,64,2048]{2,1,0:T(8,128)(2,1)}, u32[]{:S(2)}, u32[]{:S(2)}) collective-permute-start(bf16[3,64,2048]{2,1,0:T(8,128)(2,1)S(1)} %pad_maximum_fusion.2), channel_id=1, source_target_pairs={{0,2},{1,5},{2,0},{3,7},{4,6},{5,1},{6,4},{7,3},{8,10},{9,13},{10,... | collective-permute-start | bytes 2359304 | tf_op jit(solution)/shard_map/ppermute | solution.py:172
  82.5 23.5 %collective-permute-start.20 = (bf16[6,64,2048]{2,1,0:T(8,128)(2,1)}, bf16[6,64,2048]{2,1,0:T(8,128)(2,1)}, u32[]{:S(2)}, u32[]{:S(2)}) collective-permute-start(bf16[6,64,2048]{2,1,0:T(8,128)(2,1)} %constant_dynamic-update-slice_fusion.2.refs_0_), channel_id=1, source_target_pairs={{0,4},{1,3},{2,6},{3,1},{4,0},{5,7},{6,2},{7,5},{8,12},{9,11},{10,... | collective-permute-start | bytes 4718600 | tf_op jit(solution)/shard_map/ppermute | solution.py:172
  114.9 22.9 %collective-permute-start.25 = (bf16[6,64,2048]{2,1,0:T(8,128)(2,1)}, bf16[6,64,2048]{2,1,0:T(8,128)(2,1)}, u32[]{:S(2)}, u32[]{:S(2)}) collective-permute-start(bf16[6,64,2048]{2,1,0:T(8,128)(2,1)} %add_convert_fusion.1), channel_id=1, source_target_pairs={{0,4},{1,3},{2,6},{3,1},{4,0},{5,7},{6,2},{7,5},{8,12},{9,11},{10,... | collective-permute-start | bytes 4718600 | tf_op jit(solution)/shard_map/ppermute | solution.py:172
  116.4 21.5 %collective-permute-start.24 = (bf16[6,64,2048]{2,1,0:T(8,128)(2,1)}, bf16[6,64,2048]{2,1,0:T(8,128)(2,1)}, u32[]{:S(2)}, u32[]{:S(2)}) collective-permute-start(bf16[6,64,2048]{2,1,0:T(8,128)(2,1)} %get-tuple-element.97), channel_id=1, source_target_pairs={{0,1},{1,0},{2,3},{3,2},{4,5},{5,4},{6,7},{7,6},{8,9},{9,8},{10,11... | collective-permute-start | bytes 4718600 | tf_op jit(solution)/shard_map/ppermute | solution.py:172
  140.9 14.8 %collective-permute-start.26 = (bf16[3,64,2048]{2,1,0:T(8,128)(2,1)}, bf16[3,64,2048]{2,1,0:T(8,128)(2,1)}, u32[]{:S(2)}, u32[]{:S(2)}) collective-permute-start(bf16[3,64,2048]{2,1,0:T(8,128)(2,1)} %add_convert_fusion.6), channel_id=1, source_target_pairs={{0,2},{1,5},{2,0},{3,7},{4,6},{5,1},{6,4},{7,3},{8,10},{9,13},{10,... | collective-permute-start | bytes 2359304 | tf_op jit(solution)/shard_map/ppermute | solution.py:172
  156.0 44.5 %collective-permute-start.37 = (bf16[6,64,2048]{2,1,0:T(8,128)(2,1)}, bf16[6,64,2048]{2,1,0:T(8,128)(2,1)}, u32[]{:S(2)}, u32[]{:S(2)}) collective-permute-start(bf16[6,64,2048]{2,1,0:T(8,128)(2,1)} %get-tuple-element.124), channel_id=1, source_target_pairs={{0,1},{1,0},{2,3},{3,2},{4,5},{5,4},{6,7},{7,6},{8,9},{9,8},{10,11... | collective-permute-start | bytes 4718600 | tf_op jit(solution)/shard_map/ppermute | solution.py:172
  159.9 18.0 %collective-permute-start.29 = (bf16[64,2048]{1,0:T(8,128)(2,1)}, bf16[64,2048]{1,0:T(8,128)(2,1)}, u32[]{:S(2)}, u32[]{:S(2)}) collective-permute-start(bf16[64,2048]{1,0:T(8,128)(2,1)} %get-tuple-element.145), channel_id=1, source_target_pairs={{0,8},{1,9},{2,10},{3,11},{4,12},{5,13},{6,14},{7,15},{8,16},{9,17... | collective-permute-start | bytes 786440 | tf_op jit(solution)/shard_map/ppermute | solution.py:172
  159.9 20.7 %collective-permute-start.30 = (bf16[64,2048]{1,0:T(8,128)(2,1)}, bf16[64,2048]{1,0:T(8,128)(2,1)}, u32[]{:S(2)}, u32[]{:S(2)}) collective-permute-start(bf16[64,2048]{1,0:T(8,128)(2,1)} %get-tuple-element.144), channel_id=1, source_target_pairs={{0,16},{1,17},{2,18},{3,19},{4,20},{5,21},{6,22},{7,23},{8,24},{9,... | collective-permute-start | bytes 786440 | tf_op jit(solution)/shard_map/ppermute | solution.py:172
  163.0 37.0 %collective-permute-start.31 = (bf16[6,64,2048]{2,1,0:T(8,128)(2,1)}, bf16[6,64,2048]{2,1,0:T(8,128)(2,1)}, u32[]{:S(2)}, u32[]{:S(2)}) collective-permute-start(bf16[6,64,2048]{2,1,0:T(8,128)(2,1)} %add_convert_fusion), channel_id=1, source_target_pairs={{0,4},{1,3},{2,6},{3,1},{4,0},{5,7},{6,2},{7,5},{8,12},{9,11},{10,... | collective-permute-start | bytes 4718600 | tf_op jit(solution)/shard_map/ppermute | solution.py:172
  180.6 19.5 %collective-permute-start.33 = (bf16[4,64,2048]{2,1,0:T(8,128)(2,1)}, bf16[4,64,2048]{2,1,0:T(8,128)(2,1)}, u32[]{:S(2)}, u32[]{:S(2)}) collective-permute-start(bf16[4,64,2048]{2,1,0:T(8,128)(2,1)} %get-tuple-element.118), channel_id=1, source_target_pairs={{0,1},{1,0},{2,3},{3,2},{4,5},{5,4},{6,7},{7,6},{8,9},{9,8},{10,11... | collective-permute-start | bytes 3145736 | tf_op jit(solution)/shard_map/ppermute | solution.py:172
  180.6 19.5 %collective-permute-start.32 = (bf16[4,64,2048]{2,1,0:T(8,128)(2,1)}, bf16[4,64,2048]{2,1,0:T(8,128)(2,1)}, u32[]{:S(2)}, u32[]{:S(2)}) collective-permute-start(bf16[4,64,2048]{2,1,0:T(8,128)(2,1)} %get-tuple-element.120), channel_id=1, source_target_pairs={{0,1},{1,0},{2,3},{3,2},{4,5},{5,4},{6,7},{7,6},{8,9},{9,8},{10,11... | collective-permute-start | bytes 3145736 | tf_op jit(solution)/shard_map/ppermute | solution.py:172
  197.3 12.9 %collective-permute-start.41 = (bf16[64,2048]{1,0:T(8,128)(2,1)S(1)}, bf16[64,2048]{1,0:T(8,128)(2,1)S(1)}, u32[]{:S(2)}, u32[]{:S(2)}) collective-permute-start(bf16[64,2048]{1,0:T(8,128)(2,1)S(1)} %get-tuple-element.143), channel_id=1, source_target_pairs={{0,24},{1,25},{2,26},{3,27},{4,28},{5,29},{6,30},{7,31},{8,0},{9,1... | collective-permute-start | bytes 786440 | tf_op jit(solution)/shard_map/ppermute | solution.py:172
  203.5 18.9 %collective-permute-start.39 = (bf16[3,64,2048]{2,1,0:T(8,128)(2,1)}, bf16[3,64,2048]{2,1,0:T(8,128)(2,1)}, u32[]{:S(2)}, u32[]{:S(2)}) collective-permute-start(bf16[3,64,2048]{2,1,0:T(8,128)(2,1)} %add_convert_fusion.4), channel_id=1, source_target_pairs={{0,2},{1,5},{2,0},{3,7},{4,6},{5,1},{6,4},{7,3},{8,10},{9,13},{10,... | collective-permute-start | bytes 2359304 | tf_op jit(solution)/shard_map/ppermute | solution.py:172
  208.7 17.7 %collective-permute-start.38 = (bf16[4,64,2048]{2,1,0:T(8,128)(2,1)}, bf16[4,64,2048]{2,1,0:T(8,128)(2,1)S(1)}, u32[]{:S(2)}, u32[]{:S(2)}) collective-permute-start(bf16[4,64,2048]{2,1,0:T(8,128)(2,1)} %add_convert_fusion.2), channel_id=1, source_target_pairs={{0,4},{1,3},{2,6},{3,1},{4,0},{5,7},{6,2},{7,5},{8,12},{9,11},{10,... | collective-permute-start | bytes 3145736 | tf_op jit(solution)/shard_map/ppermute | solution.py:172
  225.7 15.0 %collective-permute-start.42 = (bf16[64,2048]{1,0:T(8,128)(2,1)S(1)}, bf16[64,2048]{1,0:T(8,128)(2,1)S(1)}, u32[]{:S(2)}, u32[]{:S(2)}) collective-permute-start(bf16[64,2048]{1,0:T(8,128)(2,1)S(1)} %get-tuple-element.142), channel_id=1, source_target_pairs={{0,16},{1,17},{2,18},{3,19},{4,20},{5,21},{6,22},{7,23},{8,24},{9,... | collective-permute-start | bytes 786440 | tf_op jit(solution)/shard_map/ppermute | solution.py:172
  (40 other events, 297.4 us)

commit v14 on v11

--- a/solution.py
+++ b/solution.py
@@ -178,6 +178,10 @@
 
 def send_second(array):
     return send(array, lambda e, c: (flip_second(e, c), c))
+
+
+def send_both(array):
+    return send(array, lambda e, c: (e ^ 3, c))
 
 
 def send_bit(array, bit):
@@ -599,11 +603,9 @@
     columns, gains = unpack_add(columns[..., :half], gains, got)
     got = send_bit(pack(columns[1], gains), 2)
     near_mine, near_low, near_high = expand(
-        back, after(slot_prob, got), (out_slots, input_slots), (True, False), 1, far
-    )
-    near_high, got = together(near_high, got, *out_far[:-1])[:2]
-    columns, gains = unpack_add(columns[0], gains, got)
-    got = send_bit(pack(columns[1], gains), 1)
+        back, after(slot_prob, gate_up_part), (out_slots, input_slots), (True, False), 1, far
+    )
+    near_high = after(near_high, *out_far[:-1])
     near_core_high = send_core(near_high)
     near_core = send_core(near_low)
     down_part = outer_sum(after(hidden, near_high), grads)
@@ -615,17 +617,23 @@
         add_up(in_mine[one_far:half_far], in_core[one_far:half_far], in_first[one_far:])
     )
     in_second = send_second(in_middle)
-    messages = [send_along(pack(columns[step], gains), step) for step in range(1, steps)]
-    near_upper = narrow(add_up(near_mine[4:], near_core_high))
-    in_second, near_upper, *messages = together(in_second, near_upper, *messages, *out_far[-1:])[:2 + len(messages)]
+    got = send_bit(pack(columns[1], gains), 1)
+    near_core, near_core_high = after(near_core, in_middle), after(near_core_high, in_middle)
+    near_parts = [
+        narrow(add_up(near_mine[2:4], near_core[2:])),
+        narrow(add_up(near_mine[4:6], near_core_high[:2])),
+        narrow(add_up(near_mine[6:], near_core_high[2:])),
+    ]
+    in_second, got, *near_parts = together(in_second, got, *near_parts, *out_far[-1:])[:5]
+    columns, gains = unpack_add(columns[0], gains, got)
     in_planes = narrow(own_plane(in_mine, in_core, in_first, in_second, one_far))
     in_far = [send_along(in_planes[step - 1], step) for step in range(1, steps)]
-    near_first = send_first(after(near_upper, in_planes))
-    near_middle = narrow(add_up(near_mine[2:4], near_core[2:], near_first[2:]))
-    near_second = send_second(near_middle)
-    near_sum = own_plane(near_mine, near_core, near_first, near_second, 2)
-    out_sum = near_sum[0] + add_up(*out_far)
-    normed_grad = near_sum[1] + add_up(*in_far)
+    messages = [send_along(pack(columns[step], gains), step) for step in range(1, steps)]
+    near_parts = [after(part, in_planes) for part in near_parts]
+    arrived = [send_second(near_parts[0]), send_first(near_parts[1]), send_both(near_parts[2])]
+    near_terms = [near_mine[:2], near_core[:2]] + arrived
+    out_sum = add_up(*out_far, *[term[0] for term in near_terms])
+    normed_grad = add_up(*in_far, *[term[1] for term in near_terms])
 
     prob_sum, all_gains = columns[0], [gains]
     for message in messages:

time: 252 us -> 245 us (0.972)
  starting transfers between devices: 50 us -> 46.7 us
    ppermute x47 -> x48, starting transfers between devices: 50 us -> 46.7 us  [send(): return lax.ppermute(array, BOTH, pairs)]
    reduce_sum x1, other arithmetic: 0.31 us -> 3.39 us  [broadcast_shards(): jnp.mean(gain_side * scaled_own, axis=1, keepdims=True)]
    ppermute x47 -> x48, waiting for transfers between devices: 63.6 us -> 61.5 us  [send(): return lax.ppermute(array, BOTH, pairs)]
    convert_element_type x8 -> x7, other arithmetic: 20.4 us -> 19.1 us  [narrow(): return value.astype(jnp.bfloat16)]
  transfers between devices with their start and end apart: 47 -> 48, of which waited for: 14 -> 15; matrix products, arithmetic and copies ran while one was open for 18% -> 19% of each run, Pallas kernels for 30% -> 31%
where the time goes in v14:
time: 245 us; the launch traced here: 244 us
  Pallas kernels  75.1 us (31%)
  waiting for transfers between devices  61.5 us (25%)
  starting transfers between devices  46.7 us (19%)
  other arithmetic  34.5 us (14%)
  matrix products  14 us (6%)
  local copies, waits for them, and re-layouts  11.5 us (5%)
    ppermute x48, waiting for transfers between devices, send(): return lax.ppermute(array, BOTH, pairs)  61.5 us
    ppermute x48, starting transfers between devices, send(): return lax.ppermute(array, BOTH, pairs)  46.7 us
    pallas_call x4, Pallas kernels, select(): pl.pallas_call(functools.partial(kernel, count), grid=(4,), in_specs=[gro...  21.3 us
    pallas_call x3, Pallas kernels, expand(): pl.pallas_call(functools.partial(expand_kernel, weighted, count, first_gr...  19.4 us
    convert_element_type x7, other arithmetic, narrow(): return value.astype(jnp.bfloat16)  19.1 us
    dot_general x2, matrix products, outer_sum(): lax.dot_general(left, right, (((0,), (0,)), ((), ())), preferred_element_...  13.9 us
    pallas_call x1, Pallas kernels, forward(): pl.pallas_call(forward_kernel, grid=(2,), in_specs=[row_spec(features), p...  13.1 us
    pallas_call x2, Pallas kernels, backward_input(): pl.pallas_call(input_kernel, grid=(2,), in_specs=[pl.BlockSpec((slots, wi...  12.7 us
  transfers between devices with their start and end apart: 48, of which 15 were waited for; matrix products, arithmetic and copies ran while one was open for 19% of the time, Pallas kernels for 31%

profile of v14, /device:TPU:0, one launch (start us, length us, event | category | flops | bytes accessed | tf_op | source)
XLA Modules:
  0.0 244.5 jit_solution(3454434789466161778)
XLA Ops:
  1.7 3.0 %collective-permute-start = (bf16[2,64,2048]{2,1,0:T(8,128)(2,1)S(1)}, bf16[2,64,2048]{2,1,0:T(8,128)(2,1)S(1)}, u32[]{:S(2)}, u32[]{:S(2)}) collective-permute-start(bf16[2,64,2048]{2,1,0:T(8,128)(2,1)S(1)} %pad_maximum_fusion.3), channel_id=1, source_target_pairs={{0,2},{1,5},{2,0},{3,7},{4,6},{5,1},{6,4},{7,3},{8,10},{9,13},{10,... | collective-permute-start | bytes 1572872 | tf_op jit(solution)/shard_map/ppermute | solution.py:172
  19.6 11.8 %collective-permute-done.4 = bf16[64,2048]{1,0:T(8,128)(2,1)S(1)} collective-permute-done((bf16[64,2048]{1,0:T(8,128)(2,1)}, bf16[64,2048]{1,0:T(8,128)(2,1)S(1)}, u32[]{:S(2)}, u32[]{:S(2)}) %collective-permute-start.4) | collective-permute-done | bytes 262176 | tf_op jit(solution)/shard_map/ppermute | solution.py:172
  38.4 5.0 %collective-permute-done.7 = f32[2,2,16,128]{3,2,1,0:T(8,128)S(1)} collective-permute-done((f32[2,2,16,128]{3,2,1,0:T(8,128)S(1)}, f32[2,2,16,128]{3,2,1,0:T(8,128)S(1)}, u32[]{:S(2)}, u32[]{:S(2)}) %collective-permute-start.7) | collective-permute-done | bytes 32800 | tf_op jit(solution)/shard_map/ppermute | solution.py:172
  51.8 4.3 %shard_map.118.refs_5_ = bf16[16,48,2048]{2,1,0:T(8,128)(2,1)} custom-call(bf16[16,48,128]{2,1,0:T(8,128)(2,1)} %fusion.13.pick_ref, bf16[4,64,2048]{2,1,0:T(8,128)(2,1)} %copy-done.2, bf16[4,64,2048]{2,1,0:T(8,128)(2,1)} %copy-done.4, bf16[4,64,2048]{2,1,0:T(8,128)(2,1)} %copy-done.5, bf16[4,64,2048]{2,1,0:T(8,128)(2,1)} %collective-permute-done.16.refs_3_, ...), custom_call_target="tpu_custom_call" | custom-call | flops 1000000 | bytes 100000 | tf_op jit(solution)/shard_map/pallas_call | solution.py:285
  56.1 10.8 %collective-permute-done.13 = bf16[64,2048]{1,0:T(8,128)(2,1)} collective-permute-done((bf16[64,2048]{1,0:T(8,128)(2,1)S(1)}, bf16[64,2048]{1,0:T(8,128)(2,1)}, u32[]{:S(2)}, u32[]{:S(2)}) %collective-permute-start.13) | collective-permute-done | bytes 262176 | tf_op jit(solution)/shard_map/ppermute | solution.py:172
  72.0 5.9 %shard_map.119 = bf16[16,48,2048]{2,1,0:T(8,128)(2,1)} custom-call(bf16[16,48,128]{2,1,0:T(8,128)(2,1)} %fusion.13.pick_ref, bf16[6,64,2048]{2,1,0:T(8,128)(2,1)} %constant_dynamic-update-slice_fusion.refs_0_, bf16[6,64,2048]{2,1,0:T(8,128)(2,1)} %collective-permute-done.12.refs_1_, ...), custom_call_target="tpu_custom_call", output_to_operand_aliasing={{}: (6, {})} | custom-call | flops 1000000 | bytes 100000 | tf_op jit(solution)/shard_map/pallas_call | solution.py:285
  85.6 13.1 %shard_map.120 = (f32[768,768]{1,0:T(8,128)}, f32[768,768]{1,0:T(8,128)}, bf16[768,768]{1,0:T(8,128)(2,1)}, bf16[768,2048]{1,0:T(8,128)(2,1)}) custom-call(bf16[768,2048]{1,0:T(8,128)(2,1)} %bitcast.146, bf16[1,2048,1536]{2,1,0:T(8,128)(2,1)} %gate_up_ref.5, bf16[1,768,2048]{2,1,0:T(8,128)(2,1)} %down_ref.3), custom_call_target="tpu_custom_call" | custom-call | flops 1000000 | bytes 100000 | tf_op jit(solution)/shard_map/pallas_call | solution.py:399
  98.7 7.3 %shard_map.121 = (bf16[12,64,2048]{2,1,0:T(8,128)(2,1)}, bf16[6,64,2048]{2,1,0:T(8,128)(2,1)}, bf16[6,64,2048]{2,1,0:T(8,128)(2,1)}) custom-call(bf16[16,128,48]{2,1,0:T(8,128)(2,1)} %fusion.1.back_ref, f32[16,48,1]{2,1,0:T(8,128)} %copy.20.prob_ref.refs_4_, bf16[16,48,2048]{2,1,0:T(8,128)(2,1)} %bitcast.150), custom_call_target="tpu_custom_call" | custom-call | flops 1000000 | bytes 100000 | tf_op jit(solution)/shard_map/pallas_call | solution.py:364
  106.7 4.5 %shard_map.122 = (bf16[16,48,2048]{2,1,0:T(8,128)(2,1)}, f32[16,48,1]{2,1,0:T(8,128)}) custom-call(bf16[16,48,128]{2,1,0:T(8,128)(2,1)} %fusion.13.pick_ref, bf16[4,64,2048]{2,1,0:T(8,128)(2,1)} %copy-done.2, bf16[4,64,2048]{2,1,0:T(8,128)(2,1)} %copy-done.4, bf16[4,64,2048]{2,1,0:T(8,128)(2,1)} %copy-done.5, ...), custom_call_target="tpu_custom_call" | custom-call | flops 1000000 | bytes 100000 | tf_op jit(solution)/shard_map/pallas_call | solution.py:285
  111.3 3.8 %add_convert_fusion.1 = bf16[6,64,2048]{2,1,0:T(8,128)(2,1)} fusion(bf16[6,64,2048]{2,1,0:T(8,128)(2,1)} %collective-permute-done.22, bf16[12,64,2048]{2,1,0:T(8,128)(2,1)} %get-tuple-element.86), kind=kLoop, calls=%fused_computation.4 | loop fusion | flops 3145728 | bytes 4718592 | tf_op jit(solution)/shard_map/convert_element_type | solution.py:213
  117.3 6.6 %shard_map.123 = (bf16[16,48,2048]{2,1,0:T(8,128)(2,1)}, f32[16,48,1]{2,1,0:T(8,128)}) custom-call(bf16[16,48,128]{2,1,0:T(8,128)(2,1)} %fusion.13.pick_ref, bf16[6,64,2048]{2,1,0:T(8,128)(2,1)} %constant_dynamic-update-slice_fusion.2.refs_0_, bf16[6,64,2048]{2,1,0:T(8,128)(2,1)} %collective-permute-done.21.refs_1_, ...), custom_call_target="tpu_custom_call", output_to_operand_aliasing={{0}: (7, {}), {1}: (8, {})} | custom-call | flops 1000000 | bytes 100000 | tf_op jit(solution)/shard_map/pallas_call | solution.py:285
  123.8 8.7 %shard_map.124.joined_ref = bf16[768,1536]{1,0:T(8,128)(2,1)} custom-call(bf16[768,2048]{1,0:T(8,128)(2,1)} %bitcast.156, f32[768,768]{1,0:T(8,128)} %get-tuple-element.98.gate_pre_ref, f32[768,768]{1,0:T(8,128)} %get-tuple-element.99.up_pre_ref, bf16[1,768,2048]{2,1,0:T(8,128)(2,1)} %down_ref.3), custom_call_target="tpu_custom_call" | custom-call | flops 1000000 | bytes 100000 | tf_op jit(solution)/shard_map/pallas_call | solution.py:435
  132.5 6.3 %shard_map.125 = (bf16[768,2048]{1,0:T(8,128)(2,1)}, f32[1,1024]{1,0:T(1,128)}) custom-call(bf16[768,1536]{1,0:T(8,128)(2,1)} %shard_map.124.joined_ref, bf16[1,2048,1536]{2,1,0:T(8,128)(2,1)} %gate_up_ref.5, bf16[768,2048]{1,0:T(8,128)(2,1)} %bitcast.147), custom_call_target="tpu_custom_call" | custom-call | flops 1000000 | bytes 100000 | tf_op jit(solution)/shard_map/pallas_call | solution.py:464
  144.6 6.4 %shard_map.126 = (bf16[768,2048]{1,0:T(8,128)(2,1)}, f32[1,1024]{1,0:T(1,128)}) custom-call(bf16[768,1536]{1,0:T(8,128)(2,1)} %shard_map.124.joined_ref, bf16[1,2048,1536]{2,1,0:T(8,128)(2,1)} %gate_up_ref.5, bf16[768,2048]{1,0:T(8,128)(2,1)} %bitcast.148, bf16[768,2048]{1,0:T(8,128)(2,1)} %get-tuple-element.103.refs_0_), custom_call_target="tpu_custom_call", output_to_operand_aliasing={{0}: (3, {})} | custom-call | flops 1000000 | bytes 100000 | tf_op jit(solution)/shard_map/pallas_call | solution.py:464
  151.0 6.5 %shard_map.127 = (bf16[12,64,2048]{2,1,0:T(8,128)(2,1)}, bf16[6,64,2048]{2,1,0:T(8,128)(2,1)}, bf16[6,64,2048]{2,1,0:T(8,128)(2,1)}) custom-call(bf16[16,128,48]{2,1,0:T(8,128)(2,1)} %fusion.1.back_ref, f32[16,48,1]{2,1,0:T(8,128)} %copy.20.prob_ref.refs_4_, bf16[16,48,2048]{2,1,0:T(8,128)(2,1)} %bitcast.154), custom_call_target="tpu_custom_call" | custom-call | flops 1000000 | bytes 100000 | tf_op jit(solution)/shard_map/pallas_call | solution.py:364
  165.7 7.3 %convolution_convert_fusion = bf16[2048,1536]{1,0:T(8,128)(2,1)} fusion(bf16[768,2048]{1,0:T(8,128)(2,1)S(1)} %bitcast.149, bf16[768,1536]{1,0:T(8,128)(2,1)S(1)} %copy-done.1), kind=kOutput, calls=%fused_computation.1 | convolution fusion | flops 4834983936 | bytes 11796480 | tf_op jit(solution)/shard_map/dot_general | solution.py:38
  174.1 5.6 %shard_map.128 = (bf16[8,64,2048]{2,1,0:T(8,128)(2,1)}, bf16[4,64,2048]{2,1,0:T(8,128)(2,1)}, bf16[4,64,2048]{2,1,0:T(8,128)(2,1)}) custom-call(bf16[16,128,48]{2,1,0:T(8,128)(2,1)} %fusion.1.back_ref, f32[16,48,1]{2,1,0:T(8,128)} %copy.26.prob_ref, bf16[16,48,2048]{2,1,0:T(8,128)(2,1)} %bitcast.153, bf16[16,48,2048]{2,1,0:T(8,128)(2,1)} %bitcast.155), custom_call_target="tpu_custom_call" | custom-call | flops 1000000 | bytes 100000 | tf_op jit(solution)/shard_map/pallas_call | solution.py:364
  183.9 6.6 %convolution_convert_fusion.1 = bf16[768,2048]{1,0:T(8,128)(2,1)} fusion(bf16[768,768]{1,0:T(8,128)(2,1)} %get-tuple-element.121, bf16[768,2048]{1,0:T(8,128)(2,1)} %bitcast.157), kind=kOutput, calls=%fused_computation.2 | convolution fusion | flops 2417491968 | bytes 7471104 | tf_op jit(solution)/shard_map/dot_general | solution.py:38
  197.0 3.0 %add_convert_fusion.6 = (bf16[2,64,2048]{2,1,0:T(8,128)(2,1)S(1)}, bf16[2,64,2048]{2,1,0:T(8,128)(2,1)}, bf16[2,64,2048]{2,1,0:T(8,128)(2,1)}) fusion(bf16[4,64,2048]{2,1,0:T(8,128)(2,1)} %collective-permute-done.34, bf16[8,64,2048]{2,1,0:T(8,128)(2,1)S(1)} %copy-done.9, bf16[4,64,2048]{2,1,0:T(8,128)(2,1)} %collective-permute-done.33), kind=kLoop, calls=%fused_computation.11 | loop fusion | flops 3145728 | bytes 4718592 | tf_op jit(solution)/shard_map/convert_element_type | solution.py:213
  200.0 7.2 %collective-permute-done.38 = f32[32,128]{1,0:T(8,128)S(1)} collective-permute-done((f32[32,128]{1,0:T(8,128)S(1)}, f32[32,128]{1,0:T(8,128)S(1)}, u32[]{:S(2)}, u32[]{:S(2)}) %collective-permute-start.38) | collective-permute-done | bytes 16416 | tf_op jit(solution)/shard_map/ppermute | solution.py:172
  221.7 5.7 %collective-permute-done.42 = bf16[64,2048]{1,0:T(8,128)(2,1)} collective-permute-done((bf16[64,2048]{1,0:T(8,128)(2,1)}, bf16[64,2048]{1,0:T(8,128)(2,1)}, u32[]{:S(2)}, u32[]{:S(2)}) %collective-permute-start.42) | collective-permute-done | bytes 262176 | tf_op jit(solution)/shard_map/ppermute | solution.py:172
  228.8 6.2 %collective-permute-done.43 = bf16[64,2048]{1,0:T(8,128)(2,1)} collective-permute-done((bf16[64,2048]{1,0:T(8,128)(2,1)}, bf16[64,2048]{1,0:T(8,128)(2,1)}, u32[]{:S(2)}, u32[]{:S(2)}) %collective-permute-start.43) | collective-permute-done | bytes 262176 | tf_op jit(solution)/shard_map/ppermute | solution.py:172
  235.0 5.1 %collective-permute-done.44 = bf16[64,2048]{1,0:T(8,128)(2,1)} collective-permute-done((bf16[64,2048]{1,0:T(8,128)(2,1)}, bf16[64,2048]{1,0:T(8,128)(2,1)}, u32[]{:S(2)}, u32[]{:S(2)}) %collective-permute-start.44) | collective-permute-done | bytes 262176 | tf_op jit(solution)/shard_map/ppermute | solution.py:172
  240.1 3.4 %fusion.4 = (f32[64]{0:T(128)S(1)}, f32[64,2048]{1,0:T(8,128)S(1)}, bf16[64,2048]{1,0:T(8,128)(2,1)}) fusion(bf16[64,2048]{1,0:T(8,128)(2,1)S(1)} %copy-done.3, f32[64]{0:T(128)S(1)} %copy-done.19, f32[2048]{0:T(1024)S(1)} %copy-done.16, bf16[2,64,2048]{2,1,0:T(8,128)(2,1)} %collective-permute-done.41, bf16[2,64,2048]{2,1,0:T(8,128)(2,1)} %collective-permute-done.40, ...), kind=kLoop, calls=%fused_computation.24 | loop fusion | flops 4849600 | bytes 5251584 | tf_op jit(solution)/shard_map/reduce_sum | solution.py:650
  (214 shorter events, 89.5 us)
Async XLA Ops:
  4.7 14.2 %collective-permute-start.5 = (bf16[64,2048]{1,0:T(8,128)(2,1)}, bf16[64,2048]{1,0:T(8,128)(2,1)S(1)}, u32[]{:S(2)}, u32[]{:S(2)}) collective-permute-start(bf16[64,2048]{1,0:T(8,128)(2,1)} %param.7), channel_id=1, source_target_pairs={{0,8},{1,9},{2,10},{3,11},{4,12},{5,13},{6,14},{7,15},{8,16},{9,17... | collective-permute-start | bytes 786440 | tf_op jit(solution)/shard_map/ppermute | solution.py:172
  6.3 13.3 %collective-permute-start.3 = (bf16[64,2048]{1,0:T(8,128)(2,1)}, bf16[64,2048]{1,0:T(8,128)(2,1)S(1)}, u32[]{:S(2)}, u32[]{:S(2)}) collective-permute-start(bf16[64,2048]{1,0:T(8,128)(2,1)} %param.7), channel_id=1, source_target_pairs={{0,24},{1,25},{2,26},{3,27},{4,28},{5,29},{6,30},{7,31},{8,0},{9,1... | collective-permute-start | bytes 786440 | tf_op jit(solution)/shard_map/ppermute | solution.py:172
  8.5 22.9 %collective-permute-start.4 = (bf16[64,2048]{1,0:T(8,128)(2,1)}, bf16[64,2048]{1,0:T(8,128)(2,1)S(1)}, u32[]{:S(2)}, u32[]{:S(2)}) collective-permute-start(bf16[64,2048]{1,0:T(8,128)(2,1)} %param.7), channel_id=1, source_target_pairs={{0,16},{1,17},{2,18},{3,19},{4,20},{5,21},{6,22},{7,23},{8,24},{9,... | collective-permute-start | bytes 786440 | tf_op jit(solution)/shard_map/ppermute | solution.py:172
  15.1 28.5 %collective-permute-start.10 = (bf16[4,64,2048]{2,1,0:T(8,128)(2,1)S(1)}, bf16[4,64,2048]{2,1,0:T(8,128)(2,1)S(1)}, u32[]{:S(2)}, u32[]{:S(2)}) collective-permute-start(bf16[4,64,2048]{2,1,0:T(8,128)(2,1)S(1)} %pad_maximum_fusion.refs_0_), channel_id=1, source_target_pairs={{0,4},{1,3},{2,6},{3,1},{4,0},{5,7},{6,2},{7,5},{8,12},{9,11},{10,... | collective-permute-start | bytes 3145736 | tf_op jit(solution)/shard_map/ppermute | solution.py:172
  16.8 14.7 %collective-permute-start.2 = (f32[2,16,128]{2,1,0:T(8,128)S(1)}, f32[2,16,128]{2,1,0:T(8,128)S(1)}, u32[]{:S(2)}, u32[]{:S(2)}) collective-permute-start(f32[2,16,128]{2,1,0:T(8,128)S(1)} %get-tuple-element.162), channel_id=1, source_target_pairs={{0,4},{1,3},{2,6},{3,1},{4,0},{5,7},{6,2},{7,5},{8,12},{9,11},{10,... | collective-permute-start | bytes 49160 | tf_op jit(solution)/shard_map/ppermute | solution.py:172
  44.6 23.5 %collective-permute-start.12 = (bf16[6,64,2048]{2,1,0:T(8,128)(2,1)}, bf16[6,64,2048]{2,1,0:T(8,128)(2,1)}, u32[]{:S(2)}, u32[]{:S(2)}) collective-permute-start(bf16[6,64,2048]{2,1,0:T(8,128)(2,1)} %constant_dynamic-update-slice_fusion.refs_0_), channel_id=1, source_target_pairs={{0,4},{1,3},{2,6},{3,1},{4,0},{5,7},{6,2},{7,5},{8,12},{9,11},{10,... | collective-permute-start | bytes 4718600 | tf_op jit(solution)/shard_map/ppermute | solution.py:172
  46.5 20.5 %collective-permute-start.13 = (bf16[64,2048]{1,0:T(8,128)(2,1)S(1)}, bf16[64,2048]{1,0:T(8,128)(2,1)}, u32[]{:S(2)}, u32[]{:S(2)}) collective-permute-start(bf16[64,2048]{1,0:T(8,128)(2,1)S(1)} %copy-done.7), channel_id=1, source_target_pairs={{0,16},{1,17},{2,18},{3,19},{4,20},{5,21},{6,22},{7,23},{8,24},{9,... | collective-permute-start | bytes 786440 | tf_op jit(solution)/shard_map/ppermute | solution.py:172
  47.7 19.2 %collective-permute-start.14 = (bf16[64,2048]{1,0:T(8,128)(2,1)S(1)}, bf16[64,2048]{1,0:T(8,128)(2,1)}, u32[]{:S(2)}, u32[]{:S(2)}) collective-permute-start(bf16[64,2048]{1,0:T(8,128)(2,1)S(1)} %copy-done.7), channel_id=1, source_target_pairs={{0,8},{1,9},{2,10},{3,11},{4,12},{5,13},{6,14},{7,15},{8,16},{9,17... | collective-permute-start | bytes 786440 | tf_op jit(solution)/shard_map/ppermute | solution.py:172
  50.8 19.7 %collective-permute-start.17 = (bf16[6,64,2048]{2,1,0:T(8,128)(2,1)}, bf16[6,64,2048]{2,1,0:T(8,128)(2,1)}, u32[]{:S(2)}, u32[]{:S(2)}) collective-permute-start(bf16[6,64,2048]{2,1,0:T(8,128)(2,1)} %constant_dynamic-update-slice_fusion.refs_0_), channel_id=1, source_target_pairs={{0,1},{1,0},{2,3},{3,2},{4,5},{5,4},{6,7},{7,6},{8,9},{9,8},{10,11... | collective-permute-start | bytes 4718600 | tf_op jit(solution)/shard_map/ppermute | solution.py:172
  68.2 12.2 %collective-permute-start.19 = (bf16[3,64,2048]{2,1,0:T(8,128)(2,1)S(1)}, bf16[3,64,2048]{2,1,0:T(8,128)(2,1)}, u32[]{:S(2)}, u32[]{:S(2)}) collective-permute-start(bf16[3,64,2048]{2,1,0:T(8,128)(2,1)S(1)} %pad_maximum_fusion.2), channel_id=1, source_target_pairs={{0,2},{1,5},{2,0},{3,7},{4,6},{5,1},{6,4},{7,3},{8,10},{9,13},{10,... | collective-permute-start | bytes 2359304 | tf_op jit(solution)/shard_map/ppermute | solution.py:172
  82.5 23.6 %collective-permute-start.21 = (bf16[6,64,2048]{2,1,0:T(8,128)(2,1)}, bf16[6,64,2048]{2,1,0:T(8,128)(2,1)}, u32[]{:S(2)}, u32[]{:S(2)}) collective-permute-start(bf16[6,64,2048]{2,1,0:T(8,128)(2,1)} %constant_dynamic-update-slice_fusion.2.refs_0_), channel_id=1, source_target_pairs={{0,4},{1,3},{2,6},{3,1},{4,0},{5,7},{6,2},{7,5},{8,12},{9,11},{10,... | collective-permute-start | bytes 4718600 | tf_op jit(solution)/shard_map/ppermute | solution.py:172
  115.0 23.8 %collective-permute-start.23 = (bf16[6,64,2048]{2,1,0:T(8,128)(2,1)}, bf16[6,64,2048]{2,1,0:T(8,128)(2,1)}, u32[]{:S(2)}, u32[]{:S(2)}) collective-permute-start(bf16[6,64,2048]{2,1,0:T(8,128)(2,1)} %add_convert_fusion.1), channel_id=1, source_target_pairs={{0,4},{1,3},{2,6},{3,1},{4,0},{5,7},{6,2},{7,5},{8,12},{9,11},{10,... | collective-permute-start | bytes 4718600 | tf_op jit(solution)/shard_map/ppermute | solution.py:172
  116.5 22.3 %collective-permute-start.20 = (bf16[6,64,2048]{2,1,0:T(8,128)(2,1)}, bf16[6,64,2048]{2,1,0:T(8,128)(2,1)}, u32[]{:S(2)}, u32[]{:S(2)}) collective-permute-start(bf16[6,64,2048]{2,1,0:T(8,128)(2,1)} %get-tuple-element.87), channel_id=1, source_target_pairs={{0,1},{1,0},{2,3},{3,2},{4,5},{5,4},{6,7},{7,6},{8,9},{9,8},{10,11... | collective-permute-start | bytes 4718600 | tf_op jit(solution)/shard_map/ppermute | solution.py:172
  141.8 15.7 %collective-permute-start.26 = (bf16[3,64,2048]{2,1,0:T(8,128)(2,1)}, bf16[3,64,2048]{2,1,0:T(8,128)(2,1)}, u32[]{:S(2)}, u32[]{:S(2)}) collective-permute-start(bf16[3,64,2048]{2,1,0:T(8,128)(2,1)} %add_convert_fusion.5), channel_id=1, source_target_pairs={{0,2},{1,5},{2,0},{3,7},{4,6},{5,1},{6,4},{7,3},{8,10},{9,13},{10,... | collective-permute-start | bytes 2359304 | tf_op jit(solution)/shard_map/ppermute | solution.py:172
  157.8 34.2 %collective-permute-start.36 = (bf16[6,64,2048]{2,1,0:T(8,128)(2,1)}, bf16[6,64,2048]{2,1,0:T(8,128)(2,1)}, u32[]{:S(2)}, u32[]{:S(2)}) collective-permute-start(bf16[6,64,2048]{2,1,0:T(8,128)(2,1)} %get-tuple-element.125), channel_id=1, source_target_pairs={{0,1},{1,0},{2,3},{3,2},{4,5},{5,4},{6,7},{7,6},{8,9},{9,8},{10,11... | collective-permute-start | bytes 4718600 | tf_op jit(solution)/shard_map/ppermute | solution.py:172
  161.7 17.9 %collective-permute-start.27 = (bf16[64,2048]{1,0:T(8,128)(2,1)}, bf16[64,2048]{1,0:T(8,128)(2,1)S(1)}, u32[]{:S(2)}, u32[]{:S(2)}) collective-permute-start(bf16[64,2048]{1,0:T(8,128)(2,1)} %get-tuple-element.151), channel_id=1, source_target_pairs={{0,8},{1,9},{2,10},{3,11},{4,12},{5,13},{6,14},{7,15},{8,16},{9,17... | collective-permute-start | bytes 786440 | tf_op jit(solution)/shard_map/ppermute | solution.py:172
  161.7 20.6 %collective-permute-start.28 = (bf16[64,2048]{1,0:T(8,128)(2,1)}, bf16[64,2048]{1,0:T(8,128)(2,1)S(1)}, u32[]{:S(2)}, u32[]{:S(2)}) collective-permute-start(bf16[64,2048]{1,0:T(8,128)(2,1)} %get-tuple-element.153), channel_id=1, source_target_pairs={{0,16},{1,17},{2,18},{3,19},{4,20},{5,21},{6,22},{7,23},{8,24},{9,... | collective-permute-start | bytes 786440 | tf_op jit(solution)/shard_map/ppermute | solution.py:172
  164.8 27.1 %collective-permute-start.32 = (bf16[6,64,2048]{2,1,0:T(8,128)(2,1)}, bf16[6,64,2048]{2,1,0:T(8,128)(2,1)}, u32[]{:S(2)}, u32[]{:S(2)}) collective-permute-start(bf16[6,64,2048]{2,1,0:T(8,128)(2,1)} %add_convert_fusion), channel_id=1, source_target_pairs={{0,4},{1,3},{2,6},{3,1},{4,0},{5,7},{6,2},{7,5},{8,12},{9,11},{10,... | collective-permute-start | bytes 4718600 | tf_op jit(solution)/shard_map/ppermute | solution.py:172
  194.8 12.4 %collective-permute-start.37 = (bf16[3,64,2048]{2,1,0:T(8,128)(2,1)}, bf16[3,64,2048]{2,1,0:T(8,128)(2,1)}, u32[]{:S(2)}, u32[]{:S(2)}) collective-permute-start(bf16[3,64,2048]{2,1,0:T(8,128)(2,1)} %add_convert_fusion.3), channel_id=1, source_target_pairs={{0,2},{1,5},{2,0},{3,7},{4,6},{5,1},{6,4},{7,3},{8,10},{9,13},{10,... | collective-permute-start | bytes 2359304 | tf_op jit(solution)/shard_map/ppermute | solution.py:172
  213.8 26.3 %collective-permute-start.39 = (bf16[2,64,2048]{2,1,0:T(8,128)(2,1)}, bf16[2,64,2048]{2,1,0:T(8,128)(2,1)}, u32[]{:S(2)}, u32[]{:S(2)}) collective-permute-start(bf16[2,64,2048]{2,1,0:T(8,128)(2,1)} %get-tuple-element.133), channel_id=1, source_target_pairs={{0,2},{1,5},{2,0},{3,7},{4,6},{5,1},{6,4},{7,3},{8,10},{9,13},{10,... | collective-permute-start | bytes 1572872 | tf_op jit(solution)/shard_map/ppermute | solution.py:172
  214.5 25.6 %collective-permute-start.40 = (bf16[2,64,2048]{2,1,0:T(8,128)(2,1)}, bf16[2,64,2048]{2,1,0:T(8,128)(2,1)}, u32[]{:S(2)}, u32[]{:S(2)}) collective-permute-start(bf16[2,64,2048]{2,1,0:T(8,128)(2,1)} %get-tuple-element.135), channel_id=1, source_target_pairs={{0,4},{1,3},{2,6},{3,1},{4,0},{5,7},{6,2},{7,5},{8,12},{9,11},{10,... | collective-permute-start | bytes 1572872 | tf_op jit(solution)/shard_map/ppermute | solution.py:172
  216.5 18.5 %collective-permute-start.43 = (bf16[64,2048]{1,0:T(8,128)(2,1)}, bf16[64,2048]{1,0:T(8,128)(2,1)}, u32[]{:S(2)}, u32[]{:S(2)}) collective-permute-start(bf16[64,2048]{1,0:T(8,128)(2,1)} %get-tuple-element.150), channel_id=1, source_target_pairs={{0,16},{1,17},{2,18},{3,19},{4,20},{5,21},{6,22},{7,23},{8,24},{9,... | collective-permute-start | bytes 786440 | tf_op jit(solution)/shard_map/ppermute | solution.py:172
  219.2 20.9 %collective-permute-start.41 = (bf16[2,64,2048]{2,1,0:T(8,128)(2,1)S(1)}, bf16[2,64,2048]{2,1,0:T(8,128)(2,1)}, u32[]{:S(2)}, u32[]{:S(2)}) collective-permute-start(bf16[2,64,2048]{2,1,0:T(8,128)(2,1)S(1)} %get-tuple-element.137), channel_id=1, source_target_pairs={{0,6},{1,7},{2,4},{3,5},{4,2},{5,3},{6,0},{7,1},{8,14},{9,15},{10,... | collective-permute-start | bytes 1572872 | tf_op jit(solution)/shard_map/ppermute | solution.py:172
  227.3 12.7 %collective-permute-start.44 = (bf16[64,2048]{1,0:T(8,128)(2,1)}, bf16[64,2048]{1,0:T(8,128)(2,1)}, u32[]{:S(2)}, u32[]{:S(2)}) collective-permute-start(bf16[64,2048]{1,0:T(8,128)(2,1)} %get-tuple-element.149), channel_id=1, source_target_pairs={{0,24},{1,25},{2,26},{3,27},{4,28},{5,29},{6,30},{7,31},{8,0},{9,1... | collective-permute-start | bytes 786440 | tf_op jit(solution)/shard_map/ppermute | solution.py:172
  (45 other events, 417.8 us)

commit v15 on v14

--- a/solution.py
+++ b/solution.py
@@ -603,15 +603,12 @@
     columns, gains = unpack_add(columns[..., :half], gains, got)
     got = send_bit(pack(columns[1], gains), 2)
     near_mine, near_low, near_high = expand(
-        back, after(slot_prob, gate_up_part), (out_slots, input_slots), (True, False), 1, far
+        after(back, gate_up_part), slot_prob, (out_slots, input_slots), (True, False), 1, far
     )
     near_high = after(near_high, *out_far[:-1])
     near_core_high = send_core(near_high)
     near_core = send_core(near_low)
-    down_part = outer_sum(after(hidden, near_high), grads)
-    down_part, in_first, near_core, near_core_high, got = together(
-        down_part, in_first, near_core, near_core_high, got
-    )
+    in_first, near_core, near_core_high, got = together(in_first, near_core, near_core_high, got)
     columns, gains = unpack_add(columns[0], gains, got)
     in_middle = narrow(
         add_up(in_mine[one_far:half_far], in_core[one_far:half_far], in_first[one_far:])
@@ -624,7 +621,10 @@
         narrow(add_up(near_mine[4:6], near_core_high[:2])),
         narrow(add_up(near_mine[6:], near_core_high[2:])),
     ]
-    in_second, got, *near_parts = together(in_second, got, *near_parts, *out_far[-1:])[:5]
+    down_part = outer_sum(after(hidden, in_middle), grads)
+    in_second, got, down_part, *near_parts = together(
+        in_second, got, down_part, *near_parts, *out_far[-1:]
+    )[:6]
     columns, gains = unpack_add(columns[0], gains, got)
     in_planes = narrow(own_plane(in_mine, in_core, in_first, in_second, one_far))
     in_far = [send_along(in_planes[step - 1], step) for step in range(1, steps)]

time: 245 us -> 240 us (0.980)
  transfers between devices with their start and end apart: 48 -> 48, of which waited for: 15 -> 16; matrix products, arithmetic and copies ran while one was open for 19% -> 18% of each run, Pallas kernels for 31% -> 31%
where the time goes in v15:
time: 240 us; the launch traced here: 239 us
  Pallas kernels  75 us (31%)
  waiting for transfers between devices  59.6 us (25%)
  starting transfers between devices  47.7 us (20%)
  other arithmetic  32.7 us (14%)
  matrix products  12.7 us (5%)
  local copies, waits for them, and re-layouts  10.3 us (4%)
    ppermute x48, waiting for transfers between devices, send(): return lax.ppermute(array, BOTH, pairs)  59.6 us
    ppermute x48, starting transfers between devices, send(): return lax.ppermute(array, BOTH, pairs)  47.7 us
    pallas_call x4, Pallas kernels, select(): pl.pallas_call(functools.partial(kernel, count), grid=(4,), in_specs=[gro...  21.3 us
    pallas_call x3, Pallas kernels, expand(): pl.pallas_call(functools.partial(expand_kernel, weighted, count, first_gr...  19.4 us
    convert_element_type x7, other arithmetic, narrow(): return value.astype(jnp.bfloat16)  18.9 us
    pallas_call x1, Pallas kernels, forward(): pl.pallas_call(forward_kernel, grid=(2,), in_specs=[row_spec(features), p...  13.1 us
    pallas_call x2, Pallas kernels, backward_input(): pl.pallas_call(input_kernel, grid=(2,), in_specs=[pl.BlockSpec((slots, wi...  12.7 us
    dot_general x2, matrix products, outer_sum(): lax.dot_general(left, right, (((0,), (0,)), ((), ())), preferred_element_...  12.5 us
  transfers between devices with their start and end apart: 48, of which 16 were waited for; matrix products, arithmetic and copies ran while one was open for 18% of the time, Pallas kernels for 31%

profile of v15, /device:TPU:0, one launch (start us, length us, event | category | flops | bytes accessed | tf_op | source)
XLA Modules:
  0.0 239.1 jit_solution(11672947909677124758)
XLA Ops:
  1.7 3.0 %collective-permute-start = (bf16[2,64,2048]{2,1,0:T(8,128)(2,1)S(1)}, bf16[2,64,2048]{2,1,0:T(8,128)(2,1)S(1)}, u32[]{:S(2)}, u32[]{:S(2)}) collective-permute-start(bf16[2,64,2048]{2,1,0:T(8,128)(2,1)S(1)} %pad_maximum_fusion.3), channel_id=1, source_target_pairs={{0,2},{1,5},{2,0},{3,7},{4,6},{5,1},{6,4},{7,3},{8,10},{9,13},{10,... | collective-permute-start | bytes 1572872 | tf_op jit(solution)/shard_map/ppermute | solution.py:172
  19.6 11.8 %collective-permute-done.4 = bf16[64,2048]{1,0:T(8,128)(2,1)S(1)} collective-permute-done((bf16[64,2048]{1,0:T(8,128)(2,1)}, bf16[64,2048]{1,0:T(8,128)(2,1)S(1)}, u32[]{:S(2)}, u32[]{:S(2)}) %collective-permute-start.4) | collective-permute-done | bytes 262176 | tf_op jit(solution)/shard_map/ppermute | solution.py:172
  38.4 5.0 %collective-permute-done.7 = f32[2,2,16,128]{3,2,1,0:T(8,128)S(1)} collective-permute-done((f32[2,2,16,128]{3,2,1,0:T(8,128)S(1)}, f32[2,2,16,128]{3,2,1,0:T(8,128)S(1)}, u32[]{:S(2)}, u32[]{:S(2)}) %collective-permute-start.7) | collective-permute-done | bytes 32800 | tf_op jit(solution)/shard_map/ppermute | solution.py:172
  51.8 4.3 %shard_map.118.refs_5_ = bf16[16,48,2048]{2,1,0:T(8,128)(2,1)} custom-call(bf16[16,48,128]{2,1,0:T(8,128)(2,1)} %fusion.13.pick_ref, bf16[4,64,2048]{2,1,0:T(8,128)(2,1)} %copy-done.3, bf16[4,64,2048]{2,1,0:T(8,128)(2,1)} %copy-done.5, bf16[4,64,2048]{2,1,0:T(8,128)(2,1)} %copy-done.6, bf16[4,64,2048]{2,1,0:T(8,128)(2,1)} %collective-permute-done.16.refs_3_, ...), custom_call_target="tpu_custom_call" | custom-call | flops 1000000 | bytes 100000 | tf_op jit(solution)/shard_map/pallas_call | solution.py:285
  56.1 10.8 %collective-permute-done.13 = bf16[64,2048]{1,0:T(8,128)(2,1)} collective-permute-done((bf16[64,2048]{1,0:T(8,128)(2,1)S(1)}, bf16[64,2048]{1,0:T(8,128)(2,1)}, u32[]{:S(2)}, u32[]{:S(2)}) %collective-permute-start.13) | collective-permute-done | bytes 262176 | tf_op jit(solution)/shard_map/ppermute | solution.py:172
  71.9 5.9 %shard_map.119 = bf16[16,48,2048]{2,1,0:T(8,128)(2,1)} custom-call(bf16[16,48,128]{2,1,0:T(8,128)(2,1)} %fusion.13.pick_ref, bf16[6,64,2048]{2,1,0:T(8,128)(2,1)} %constant_dynamic-update-slice_fusion.refs_0_, bf16[6,64,2048]{2,1,0:T(8,128)(2,1)} %collective-permute-done.12.refs_1_, ...), custom_call_target="tpu_custom_call", output_to_operand_aliasing={{}: (6, {})} | custom-call | flops 1000000 | bytes 100000 | tf_op jit(solution)/shard_map/pallas_call | solution.py:285
  85.6 13.1 %shard_map.120 = (f32[768,768]{1,0:T(8,128)}, f32[768,768]{1,0:T(8,128)}, bf16[768,768]{1,0:T(8,128)(2,1)}, bf16[768,2048]{1,0:T(8,128)(2,1)}) custom-call(bf16[768,2048]{1,0:T(8,128)(2,1)} %bitcast.146, bf16[1,2048,1536]{2,1,0:T(8,128)(2,1)} %gate_up_ref.5, bf16[1,768,2048]{2,1,0:T(8,128)(2,1)} %down_ref.3), custom_call_target="tpu_custom_call" | custom-call | flops 1000000 | bytes 100000 | tf_op jit(solution)/shard_map/pallas_call | solution.py:399
  98.7 7.3 %shard_map.121 = (bf16[12,64,2048]{2,1,0:T(8,128)(2,1)}, bf16[6,64,2048]{2,1,0:T(8,128)(2,1)}, bf16[6,64,2048]{2,1,0:T(8,128)(2,1)}) custom-call(bf16[16,128,48]{2,1,0:T(8,128)(2,1)} %fusion.1.back_ref, f32[16,48,1]{2,1,0:T(8,128)} %copy.20.prob_ref.refs_4_, bf16[16,48,2048]{2,1,0:T(8,128)(2,1)} %bitcast.150), custom_call_target="tpu_custom_call" | custom-call | flops 1000000 | bytes 100000 | tf_op jit(solution)/shard_map/pallas_call | solution.py:364
  106.7 4.5 %shard_map.122 = (bf16[16,48,2048]{2,1,0:T(8,128)(2,1)}, f32[16,48,1]{2,1,0:T(8,128)}) custom-call(bf16[16,48,128]{2,1,0:T(8,128)(2,1)} %fusion.13.pick_ref, bf16[4,64,2048]{2,1,0:T(8,128)(2,1)} %copy-done.3, bf16[4,64,2048]{2,1,0:T(8,128)(2,1)} %copy-done.5, bf16[4,64,2048]{2,1,0:T(8,128)(2,1)} %copy-done.6, ...), custom_call_target="tpu_custom_call" | custom-call | flops 1000000 | bytes 100000 | tf_op jit(solution)/shard_map/pallas_call | solution.py:285
  111.2 3.7 %add_convert_fusion.1 = bf16[6,64,2048]{2,1,0:T(8,128)(2,1)} fusion(bf16[6,64,2048]{2,1,0:T(8,128)(2,1)} %collective-permute-done.22, bf16[12,64,2048]{2,1,0:T(8,128)(2,1)} %get-tuple-element.86), kind=kLoop, calls=%fused_computation.4 | loop fusion | flops 3145728 | bytes 4718592 | tf_op jit(solution)/shard_map/convert_element_type | solution.py:213
  116.4 6.6 %shard_map.123 = (bf16[16,48,2048]{2,1,0:T(8,128)(2,1)}, f32[16,48,1]{2,1,0:T(8,128)}) custom-call(bf16[16,48,128]{2,1,0:T(8,128)(2,1)} %fusion.13.pick_ref, bf16[6,64,2048]{2,1,0:T(8,128)(2,1)} %constant_dynamic-update-slice_fusion.2.refs_0_, bf16[6,64,2048]{2,1,0:T(8,128)(2,1)} %collective-permute-done.21.refs_1_, ...), custom_call_target="tpu_custom_call", output_to_operand_aliasing={{0}: (7, {}), {1}: (8, {})} | custom-call | flops 1000000 | bytes 100000 | tf_op jit(solution)/shard_map/pallas_call | solution.py:285
  123.0 8.6 %shard_map.124.joined_ref = bf16[768,1536]{1,0:T(8,128)(2,1)} custom-call(bf16[768,2048]{1,0:T(8,128)(2,1)} %bitcast.156, f32[768,768]{1,0:T(8,128)} %get-tuple-element.98.gate_pre_ref, f32[768,768]{1,0:T(8,128)} %get-tuple-element.99.up_pre_ref, bf16[1,768,2048]{2,1,0:T(8,128)(2,1)} %down_ref.3), custom_call_target="tpu_custom_call" | custom-call | flops 1000000 | bytes 100000 | tf_op jit(solution)/shard_map/pallas_call | solution.py:435
  131.6 6.3 %shard_map.125 = (bf16[768,2048]{1,0:T(8,128)(2,1)}, f32[1,1024]{1,0:T(1,128)}) custom-call(bf16[768,1536]{1,0:T(8,128)(2,1)} %shard_map.124.joined_ref, bf16[1,2048,1536]{2,1,0:T(8,128)(2,1)} %gate_up_ref.5, bf16[768,2048]{1,0:T(8,128)(2,1)} %bitcast.147), custom_call_target="tpu_custom_call" | custom-call | flops 1000000 | bytes 100000 | tf_op jit(solution)/shard_map/pallas_call | solution.py:464
  141.8 6.3 %shard_map.126 = (bf16[768,2048]{1,0:T(8,128)(2,1)}, f32[1,1024]{1,0:T(1,128)}) custom-call(bf16[768,1536]{1,0:T(8,128)(2,1)} %shard_map.124.joined_ref, bf16[1,2048,1536]{2,1,0:T(8,128)(2,1)} %gate_up_ref.5, bf16[768,2048]{1,0:T(8,128)(2,1)} %bitcast.148, bf16[768,2048]{1,0:T(8,128)(2,1)} %get-tuple-element.103.refs_0_), custom_call_target="tpu_custom_call", output_to_operand_aliasing={{0}: (3, {})} | custom-call | flops 1000000 | bytes 100000 | tf_op jit(solution)/shard_map/pallas_call | solution.py:464
  148.1 6.5 %shard_map.127 = (bf16[12,64,2048]{2,1,0:T(8,128)(2,1)}, bf16[6,64,2048]{2,1,0:T(8,128)(2,1)}, bf16[6,64,2048]{2,1,0:T(8,128)(2,1)}) custom-call(bf16[16,128,48]{2,1,0:T(8,128)(2,1)} %fusion.1.back_ref, f32[16,48,1]{2,1,0:T(8,128)} %copy.20.prob_ref.refs_4_, bf16[16,48,2048]{2,1,0:T(8,128)(2,1)} %bitcast.154), custom_call_target="tpu_custom_call" | custom-call | flops 1000000 | bytes 100000 | tf_op jit(solution)/shard_map/pallas_call | solution.py:364
  162.8 7.1 %convolution_convert_fusion = bf16[2048,1536]{1,0:T(8,128)(2,1)} fusion(bf16[768,2048]{1,0:T(8,128)(2,1)S(1)} %bitcast.149, bf16[768,1536]{1,0:T(8,128)(2,1)S(1)} %copy-done.1), kind=kOutput, calls=%fused_computation.1 | convolution fusion | flops 4834983936 | bytes 11796480 | tf_op jit(solution)/shard_map/dot_general | solution.py:38
  169.9 5.6 %shard_map.128 = (bf16[8,64,2048]{2,1,0:T(8,128)(2,1)}, bf16[4,64,2048]{2,1,0:T(8,128)(2,1)}, bf16[4,64,2048]{2,1,0:T(8,128)(2,1)}) custom-call(bf16[16,128,48]{2,1,0:T(8,128)(2,1)} %fusion.1.back_ref, f32[16,48,1]{2,1,0:T(8,128)} %copy.20.prob_ref.refs_4_, bf16[16,48,2048]{2,1,0:T(8,128)(2,1)} %bitcast.153, bf16[16,48,2048]{2,1,0:T(8,128)(2,1)} %bitcast.155), custom_call_target="tpu_custom_call" | custom-call | flops 1000000 | bytes 100000 | tf_op jit(solution)/shard_map/pallas_call | solution.py:364
  175.5 3.9 %collective-permute-done.28 = bf16[64,2048]{1,0:T(8,128)(2,1)S(1)} collective-permute-done((bf16[64,2048]{1,0:T(8,128)(2,1)}, bf16[64,2048]{1,0:T(8,128)(2,1)S(1)}, u32[]{:S(2)}, u32[]{:S(2)}) %collective-permute-start.28) | collective-permute-done | bytes 262176 | tf_op jit(solution)/shard_map/ppermute | solution.py:172
  186.1 3.6 %add_convert_fusion.3 = bf16[3,64,2048]{2,1,0:T(8,128)(2,1)} fusion(bf16[6,64,2048]{2,1,0:T(8,128)(2,1)} %collective-permute-done.36, bf16[6,64,2048]{2,1,0:T(8,128)(2,1)} %collective-permute-done.32, bf16[12,64,2048]{2,1,0:T(8,128)(2,1)} %get-tuple-element.107), kind=kLoop, calls=%fused_computation.6 | loop fusion | flops 2359296 | bytes 3145728 | tf_op jit(solution)/shard_map/convert_element_type | solution.py:213
  190.5 5.4 %convolution_convert_fusion.1 = bf16[768,2048]{1,0:T(8,128)(2,1)} fusion(bf16[768,768]{1,0:T(8,128)(2,1)} %get-tuple-element.128, bf16[768,2048]{1,0:T(8,128)(2,1)S(1)} %bitcast.157), kind=kOutput, calls=%fused_computation.2 | convolution fusion | flops 2417491968 | bytes 7471104 | tf_op jit(solution)/shard_map/dot_general | solution.py:38
  216.2 6.6 %collective-permute-done.42 = bf16[64,2048]{1,0:T(8,128)(2,1)} collective-permute-done((bf16[64,2048]{1,0:T(8,128)(2,1)}, bf16[64,2048]{1,0:T(8,128)(2,1)}, u32[]{:S(2)}, u32[]{:S(2)}) %collective-permute-start.42) | collective-permute-done | bytes 262176 | tf_op jit(solution)/shard_map/ppermute | solution.py:172
  225.1 3.3 %collective-permute-done.43 = bf16[64,2048]{1,0:T(8,128)(2,1)} collective-permute-done((bf16[64,2048]{1,0:T(8,128)(2,1)}, bf16[64,2048]{1,0:T(8,128)(2,1)}, u32[]{:S(2)}, u32[]{:S(2)}) %collective-permute-start.43) | collective-permute-done | bytes 262176 | tf_op jit(solution)/shard_map/ppermute | solution.py:172
  228.5 6.3 %collective-permute-done.44 = bf16[64,2048]{1,0:T(8,128)(2,1)} collective-permute-done((bf16[64,2048]{1,0:T(8,128)(2,1)}, bf16[64,2048]{1,0:T(8,128)(2,1)}, u32[]{:S(2)}, u32[]{:S(2)}) %collective-permute-start.44) | collective-permute-done | bytes 262176 | tf_op jit(solution)/shard_map/ppermute | solution.py:172
  234.8 3.4 %fusion.4 = (f32[64]{0:T(128)S(1)}, f32[64,2048]{1,0:T(8,128)S(1)}, bf16[64,2048]{1,0:T(8,128)(2,1)}) fusion(bf16[64,2048]{1,0:T(8,128)(2,1)S(1)} %copy-done.4, f32[64]{0:T(128)S(1)} %add_rsqrt_fusion, f32[2048]{0:T(1024)S(1)} %copy-done.19, bf16[2,64,2048]{2,1,0:T(8,128)(2,1)} %collective-permute-done.41, bf16[2,64,2048]{2,1,0:T(8,128)(2,1)} %collective-permute-done.40, ...), kind=kLoop, calls=%fused_computation.24 | loop fusion | flops 4849600 | bytes 5251584 | tf_op jit(solution)/shard_map/reduce_sum | solution.py:650
  (215 shorter events, 89.0 us)
Async XLA Ops:
  4.7 14.2 %collective-permute-start.5 = (bf16[64,2048]{1,0:T(8,128)(2,1)}, bf16[64,2048]{1,0:T(8,128)(2,1)S(1)}, u32[]{:S(2)}, u32[]{:S(2)}) collective-permute-start(bf16[64,2048]{1,0:T(8,128)(2,1)} %param.7), channel_id=1, source_target_pairs={{0,8},{1,9},{2,10},{3,11},{4,12},{5,13},{6,14},{7,15},{8,16},{9,17... | collective-permute-start | bytes 786440 | tf_op jit(solution)/shard_map/ppermute | solution.py:172
  6.3 13.3 %collective-permute-start.3 = (bf16[64,2048]{1,0:T(8,128)(2,1)}, bf16[64,2048]{1,0:T(8,128)(2,1)S(1)}, u32[]{:S(2)}, u32[]{:S(2)}) collective-permute-start(bf16[64,2048]{1,0:T(8,128)(2,1)} %param.7), channel_id=1, source_target_pairs={{0,24},{1,25},{2,26},{3,27},{4,28},{5,29},{6,30},{7,31},{8,0},{9,1... | collective-permute-start | bytes 786440 | tf_op jit(solution)/shard_map/ppermute | solution.py:172
  8.5 22.9 %collective-permute-start.4 = (bf16[64,2048]{1,0:T(8,128)(2,1)}, bf16[64,2048]{1,0:T(8,128)(2,1)S(1)}, u32[]{:S(2)}, u32[]{:S(2)}) collective-permute-start(bf16[64,2048]{1,0:T(8,128)(2,1)} %param.7), channel_id=1, source_target_pairs={{0,16},{1,17},{2,18},{3,19},{4,20},{5,21},{6,22},{7,23},{8,24},{9,... | collective-permute-start | bytes 786440 | tf_op jit(solution)/shard_map/ppermute | solution.py:172
  15.1 28.5 %collective-permute-start.10 = (bf16[4,64,2048]{2,1,0:T(8,128)(2,1)S(1)}, bf16[4,64,2048]{2,1,0:T(8,128)(2,1)S(1)}, u32[]{:S(2)}, u32[]{:S(2)}) collective-permute-start(bf16[4,64,2048]{2,1,0:T(8,128)(2,1)S(1)} %pad_maximum_fusion.refs_0_), channel_id=1, source_target_pairs={{0,4},{1,3},{2,6},{3,1},{4,0},{5,7},{6,2},{7,5},{8,12},{9,11},{10,... | collective-permute-start | bytes 3145736 | tf_op jit(solution)/shard_map/ppermute | solution.py:172
  16.8 14.7 %collective-permute-start.2 = (f32[2,16,128]{2,1,0:T(8,128)S(1)}, f32[2,16,128]{2,1,0:T(8,128)S(1)}, u32[]{:S(2)}, u32[]{:S(2)}) collective-permute-start(f32[2,16,128]{2,1,0:T(8,128)S(1)} %get-tuple-element.162), channel_id=1, source_target_pairs={{0,4},{1,3},{2,6},{3,1},{4,0},{5,7},{6,2},{7,5},{8,12},{9,11},{10,... | collective-permute-start | bytes 49160 | tf_op jit(solution)/shard_map/ppermute | solution.py:172
  44.6 23.5 %collective-permute-start.12 = (bf16[6,64,2048]{2,1,0:T(8,128)(2,1)}, bf16[6,64,2048]{2,1,0:T(8,128)(2,1)}, u32[]{:S(2)}, u32[]{:S(2)}) collective-permute-start(bf16[6,64,2048]{2,1,0:T(8,128)(2,1)} %constant_dynamic-update-slice_fusion.refs_0_), channel_id=1, source_target_pairs={{0,4},{1,3},{2,6},{3,1},{4,0},{5,7},{6,2},{7,5},{8,12},{9,11},{10,... | collective-permute-start | bytes 4718600 | tf_op jit(solution)/shard_map/ppermute | solution.py:172
  46.5 20.5 %collective-permute-start.13 = (bf16[64,2048]{1,0:T(8,128)(2,1)S(1)}, bf16[64,2048]{1,0:T(8,128)(2,1)}, u32[]{:S(2)}, u32[]{:S(2)}) collective-permute-start(bf16[64,2048]{1,0:T(8,128)(2,1)S(1)} %copy-done.8), channel_id=1, source_target_pairs={{0,16},{1,17},{2,18},{3,19},{4,20},{5,21},{6,22},{7,23},{8,24},{9,... | collective-permute-start | bytes 786440 | tf_op jit(solution)/shard_map/ppermute | solution.py:172
  47.7 19.2 %collective-permute-start.14 = (bf16[64,2048]{1,0:T(8,128)(2,1)S(1)}, bf16[64,2048]{1,0:T(8,128)(2,1)}, u32[]{:S(2)}, u32[]{:S(2)}) collective-permute-start(bf16[64,2048]{1,0:T(8,128)(2,1)S(1)} %copy-done.8), channel_id=1, source_target_pairs={{0,8},{1,9},{2,10},{3,11},{4,12},{5,13},{6,14},{7,15},{8,16},{9,17... | collective-permute-start | bytes 786440 | tf_op jit(solution)/shard_map/ppermute | solution.py:172
  50.8 19.7 %collective-permute-start.17 = (bf16[6,64,2048]{2,1,0:T(8,128)(2,1)}, bf16[6,64,2048]{2,1,0:T(8,128)(2,1)}, u32[]{:S(2)}, u32[]{:S(2)}) collective-permute-start(bf16[6,64,2048]{2,1,0:T(8,128)(2,1)} %constant_dynamic-update-slice_fusion.refs_0_), channel_id=1, source_target_pairs={{0,1},{1,0},{2,3},{3,2},{4,5},{5,4},{6,7},{7,6},{8,9},{9,8},{10,11... | collective-permute-start | bytes 4718600 | tf_op jit(solution)/shard_map/ppermute | solution.py:172
  68.2 12.2 %collective-permute-start.19 = (bf16[3,64,2048]{2,1,0:T(8,128)(2,1)S(1)}, bf16[3,64,2048]{2,1,0:T(8,128)(2,1)}, u32[]{:S(2)}, u32[]{:S(2)}) collective-permute-start(bf16[3,64,2048]{2,1,0:T(8,128)(2,1)S(1)} %pad_maximum_fusion.2), channel_id=1, source_target_pairs={{0,2},{1,5},{2,0},{3,7},{4,6},{5,1},{6,4},{7,3},{8,10},{9,13},{10,... | collective-permute-start | bytes 2359304 | tf_op jit(solution)/shard_map/ppermute | solution.py:172
  82.5 23.6 %collective-permute-start.21 = (bf16[6,64,2048]{2,1,0:T(8,128)(2,1)}, bf16[6,64,2048]{2,1,0:T(8,128)(2,1)}, u32[]{:S(2)}, u32[]{:S(2)}) collective-permute-start(bf16[6,64,2048]{2,1,0:T(8,128)(2,1)} %constant_dynamic-update-slice_fusion.2.refs_0_), channel_id=1, source_target_pairs={{0,4},{1,3},{2,6},{3,1},{4,0},{5,7},{6,2},{7,5},{8,12},{9,11},{10,... | collective-permute-start | bytes 4718600 | tf_op jit(solution)/shard_map/ppermute | solution.py:172
  114.9 23.0 %collective-permute-start.23 = (bf16[6,64,2048]{2,1,0:T(8,128)(2,1)}, bf16[6,64,2048]{2,1,0:T(8,128)(2,1)}, u32[]{:S(2)}, u32[]{:S(2)}) collective-permute-start(bf16[6,64,2048]{2,1,0:T(8,128)(2,1)} %add_convert_fusion.1), channel_id=1, source_target_pairs={{0,4},{1,3},{2,6},{3,1},{4,0},{5,7},{6,2},{7,5},{8,12},{9,11},{10,... | collective-permute-start | bytes 4718600 | tf_op jit(solution)/shard_map/ppermute | solution.py:172
  116.4 21.5 %collective-permute-start.20 = (bf16[6,64,2048]{2,1,0:T(8,128)(2,1)}, bf16[6,64,2048]{2,1,0:T(8,128)(2,1)}, u32[]{:S(2)}, u32[]{:S(2)}) collective-permute-start(bf16[6,64,2048]{2,1,0:T(8,128)(2,1)} %get-tuple-element.87), channel_id=1, source_target_pairs={{0,1},{1,0},{2,3},{3,2},{4,5},{5,4},{6,7},{7,6},{8,9},{9,8},{10,11... | collective-permute-start | bytes 4718600 | tf_op jit(solution)/shard_map/ppermute | solution.py:172
  140.0 14.6 %collective-permute-start.26 = (bf16[3,64,2048]{2,1,0:T(8,128)(2,1)S(1)}, bf16[3,64,2048]{2,1,0:T(8,128)(2,1)}, u32[]{:S(2)}, u32[]{:S(2)}) collective-permute-start(bf16[3,64,2048]{2,1,0:T(8,128)(2,1)S(1)} %add_convert_fusion.5), channel_id=1, source_target_pairs={{0,2},{1,5},{2,0},{3,7},{4,6},{5,1},{6,4},{7,3},{8,10},{9,13},{10,... | collective-permute-start | bytes 2359304 | tf_op jit(solution)/shard_map/ppermute | solution.py:172
  154.8 31.2 %collective-permute-start.36 = (bf16[6,64,2048]{2,1,0:T(8,128)(2,1)}, bf16[6,64,2048]{2,1,0:T(8,128)(2,1)}, u32[]{:S(2)}, u32[]{:S(2)}) collective-permute-start(bf16[6,64,2048]{2,1,0:T(8,128)(2,1)} %get-tuple-element.123), channel_id=1, source_target_pairs={{0,1},{1,0},{2,3},{3,2},{4,5},{5,4},{6,7},{7,6},{8,9},{9,8},{10,11... | collective-permute-start | bytes 4718600 | tf_op jit(solution)/shard_map/ppermute | solution.py:172
  158.8 16.7 %collective-permute-start.27 = (bf16[64,2048]{1,0:T(8,128)(2,1)}, bf16[64,2048]{1,0:T(8,128)(2,1)S(1)}, u32[]{:S(2)}, u32[]{:S(2)}) collective-permute-start(bf16[64,2048]{1,0:T(8,128)(2,1)} %get-tuple-element.151), channel_id=1, source_target_pairs={{0,8},{1,9},{2,10},{3,11},{4,12},{5,13},{6,14},{7,15},{8,16},{9,17... | collective-permute-start | bytes 786440 | tf_op jit(solution)/shard_map/ppermute | solution.py:172
  158.8 20.6 %collective-permute-start.28 = (bf16[64,2048]{1,0:T(8,128)(2,1)}, bf16[64,2048]{1,0:T(8,128)(2,1)S(1)}, u32[]{:S(2)}, u32[]{:S(2)}) collective-permute-start(bf16[64,2048]{1,0:T(8,128)(2,1)} %get-tuple-element.153), channel_id=1, source_target_pairs={{0,16},{1,17},{2,18},{3,19},{4,20},{5,21},{6,22},{7,23},{8,24},{9,... | collective-permute-start | bytes 786440 | tf_op jit(solution)/shard_map/ppermute | solution.py:172
  162.0 24.1 %collective-permute-start.32 = (bf16[6,64,2048]{2,1,0:T(8,128)(2,1)}, bf16[6,64,2048]{2,1,0:T(8,128)(2,1)}, u32[]{:S(2)}, u32[]{:S(2)}) collective-permute-start(bf16[6,64,2048]{2,1,0:T(8,128)(2,1)} %add_convert_fusion), channel_id=1, source_target_pairs={{0,4},{1,3},{2,6},{3,1},{4,0},{5,7},{6,2},{7,5},{8,12},{9,11},{10,... | collective-permute-start | bytes 4718600 | tf_op jit(solution)/shard_map/ppermute | solution.py:172
  184.2 16.2 %collective-permute-start.29 = (bf16[64,2048]{1,0:T(8,128)(2,1)}, bf16[64,2048]{1,0:T(8,128)(2,1)S(1)}, u32[]{:S(2)}, u32[]{:S(2)}) collective-permute-start(bf16[64,2048]{1,0:T(8,128)(2,1)} %get-tuple-element.152), channel_id=1, source_target_pairs={{0,24},{1,25},{2,26},{3,27},{4,28},{5,29},{6,30},{7,31},{8,0},{9,1... | collective-permute-start | bytes 786440 | tf_op jit(solution)/shard_map/ppermute | solution.py:172
  189.7 12.6 %collective-permute-start.37 = (bf16[3,64,2048]{2,1,0:T(8,128)(2,1)}, bf16[3,64,2048]{2,1,0:T(8,128)(2,1)}, u32[]{:S(2)}, u32[]{:S(2)}) collective-permute-start(bf16[3,64,2048]{2,1,0:T(8,128)(2,1)} %add_convert_fusion.3), channel_id=1, source_target_pairs={{0,2},{1,5},{2,0},{3,7},{4,6},{5,1},{6,4},{7,3},{8,10},{9,13},{10,... | collective-permute-start | bytes 2359304 | tf_op jit(solution)/shard_map/ppermute | solution.py:172
  209.5 25.2 %collective-permute-start.39 = (bf16[2,64,2048]{2,1,0:T(8,128)(2,1)}, bf16[2,64,2048]{2,1,0:T(8,128)(2,1)}, u32[]{:S(2)}, u32[]{:S(2)}) collective-permute-start(bf16[2,64,2048]{2,1,0:T(8,128)(2,1)} %get-tuple-element.133), channel_id=1, source_target_pairs={{0,2},{1,5},{2,0},{3,7},{4,6},{5,1},{6,4},{7,3},{8,10},{9,13},{10,... | collective-permute-start | bytes 1572872 | tf_op jit(solution)/shard_map/ppermute | solution.py:172
  210.3 24.5 %collective-permute-start.40 = (bf16[2,64,2048]{2,1,0:T(8,128)(2,1)}, bf16[2,64,2048]{2,1,0:T(8,128)(2,1)}, u32[]{:S(2)}, u32[]{:S(2)}) collective-permute-start(bf16[2,64,2048]{2,1,0:T(8,128)(2,1)} %get-tuple-element.135), channel_id=1, source_target_pairs={{0,4},{1,3},{2,6},{3,1},{4,0},{5,7},{6,2},{7,5},{8,12},{9,11},{10,... | collective-permute-start | bytes 1572872 | tf_op jit(solution)/shard_map/ppermute | solution.py:172
  211.8 16.7 %collective-permute-start.43 = (bf16[64,2048]{1,0:T(8,128)(2,1)}, bf16[64,2048]{1,0:T(8,128)(2,1)}, u32[]{:S(2)}, u32[]{:S(2)}) collective-permute-start(bf16[64,2048]{1,0:T(8,128)(2,1)} %get-tuple-element.150), channel_id=1, source_target_pairs={{0,16},{1,17},{2,18},{3,19},{4,20},{5,21},{6,22},{7,23},{8,24},{9,... | collective-permute-start | bytes 786440 | tf_op jit(solution)/shard_map/ppermute | solution.py:172
  214.3 20.4 %collective-permute-start.41 = (bf16[2,64,2048]{2,1,0:T(8,128)(2,1)S(1)}, bf16[2,64,2048]{2,1,0:T(8,128)(2,1)}, u32[]{:S(2)}, u32[]{:S(2)}) collective-permute-start(bf16[2,64,2048]{2,1,0:T(8,128)(2,1)S(1)} %get-tuple-element.137), channel_id=1, source_target_pairs={{0,6},{1,7},{2,4},{3,5},{4,2},{5,3},{6,0},{7,1},{8,14},{9,15},{10,... | collective-permute-start | bytes 1572872 | tf_op jit(solution)/shard_map/ppermute | solution.py:172
  (46 other events, 384.1 us)

commit v16 on v15

--- a/solution.py
+++ b/solution.py
@@ -552,18 +552,19 @@
 
     rows = rows.reshape(-1, features)
     gate_pre, up_pre, hidden, block_out = forward(rows, gate_up_weight, down_weight)
+    block_out, cot_core_pair = together(block_out, send_core(cot_pair))
     out_slots = block_out.reshape(expert_size, capacity, features)
     out_mine, out_low, out_high = expand(back, slot_prob, (out_slots,), (True,), steps - 1, 0)
     out_high, cot_far_pair = together(out_high, cot_far_pair)
-    cot_pieces = (cot_pair, cot_far_pair, send_core(cot_pair), send_core(cot_far_pair))
+    cot_pieces = (cot_pair, cot_far_pair, cot_core_pair, send_core(cot_far_pair))
 
     half_far, one_far = 2 * (steps - 1), steps - 1
     held = select_grads(
         after(pick, out_high), slot_prob, out_slots, near_pieces, 1, 2, 1, far, ()
     )
     out_core_high = after(send_core(out_high), held[1])
-    out_core = send_core(out_low)
     out_upper = narrow(add_up(out_mine[half_far:], out_core_high))
+    out_core = send_core(after(out_low, out_upper))
     out_first = send_first(out_upper)
     grads, prob_value = select_grads(
         after(pick, out_upper), slot_prob, out_slots, cot_pieces, steps - 1, 1, 0, 0, tuple(held)
@@ -628,7 +629,9 @@
     columns, gains = unpack_add(columns[0], gains, got)
     in_planes = narrow(own_plane(in_mine, in_core, in_first, in_second, one_far))
     in_far = [send_along(in_planes[step - 1], step) for step in range(1, steps)]
-    messages = [send_along(pack(columns[step], gains), step) for step in range(1, steps)]
+    messages = [
+        send_along(after(pack(columns[step], gains), in_planes), step) for step in range(1, steps)
+    ]
     near_parts = [after(part, in_planes) for part in near_parts]
     arrived = [send_second(near_parts[0]), send_first(near_parts[1]), send_both(near_parts[2])]
     near_terms = [near_mine[:2], near_core[:2]] + arrived

time: 240 us -> 241 us (level)
  transfers between devices with their start and end apart: 48 -> 48, of which waited for: 16 -> 16; matrix products, arithmetic and copies ran while one was open for 18% -> 17% of each run, Pallas kernels for 31% -> 31%
where the time goes in v16:
time: 241 us; the launch traced here: 240 us
  Pallas kernels  75.1 us (31%)
  waiting for transfers between devices  62 us (26%)
  starting transfers between devices  46.2 us (19%)
  other arithmetic  32.7 us (14%)
  matrix products  12.6 us (5%)
  local copies, waits for them, and re-layouts  10.5 us (4%)
    ppermute x48, waiting for transfers between devices, send(): return lax.ppermute(array, BOTH, pairs)  62 us
    ppermute x48, starting transfers between devices, send(): return lax.ppermute(array, BOTH, pairs)  46.2 us
    pallas_call x4, Pallas kernels, select(): pl.pallas_call(functools.partial(kernel, count), grid=(4,), in_specs=[gro...  21.3 us
    pallas_call x3, Pallas kernels, expand(): pl.pallas_call(functools.partial(expand_kernel, weighted, count, first_gr...  19.4 us
    convert_element_type x7, other arithmetic, narrow(): return value.astype(jnp.bfloat16)  18.9 us
    pallas_call x1, Pallas kernels, forward(): pl.pallas_call(forward_kernel, grid=(2,), in_specs=[row_spec(features), p...  13.1 us
    pallas_call x2, Pallas kernels, backward_input(): pl.pallas_call(input_kernel, grid=(2,), in_specs=[pl.BlockSpec((slots, wi...  12.6 us
    dot_general x2, matrix products, outer_sum(): lax.dot_general(left, right, (((0,), (0,)), ((), ())), preferred_element_...  12.5 us
  transfers between devices with their start and end apart: 48, of which 16 were waited for; matrix products, arithmetic and copies ran while one was open for 17% of the time, Pallas kernels for 31%

profile of v16, /device:TPU:0, one launch (start us, length us, event | category | flops | bytes accessed | tf_op | source)
XLA Modules:
  0.0 240.3 jit_solution(9244911470534582106)
XLA Ops:
  1.7 3.0 %collective-permute-start = (bf16[2,64,2048]{2,1,0:T(8,128)(2,1)S(1)}, bf16[2,64,2048]{2,1,0:T(8,128)(2,1)S(1)}, u32[]{:S(2)}, u32[]{:S(2)}) collective-permute-start(bf16[2,64,2048]{2,1,0:T(8,128)(2,1)S(1)} %pad_maximum_fusion.3), channel_id=1, source_target_pairs={{0,2},{1,5},{2,0},{3,7},{4,6},{5,1},{6,4},{7,3},{8,10},{9,13},{10,... | collective-permute-start | bytes 1572872 | tf_op jit(solution)/shard_map/ppermute | solution.py:172
  19.6 11.8 %collective-permute-done.4 = bf16[64,2048]{1,0:T(8,128)(2,1)S(1)} collective-permute-done((bf16[64,2048]{1,0:T(8,128)(2,1)}, bf16[64,2048]{1,0:T(8,128)(2,1)S(1)}, u32[]{:S(2)}, u32[]{:S(2)}) %collective-permute-start.4) | collective-permute-done | bytes 262176 | tf_op jit(solution)/shard_map/ppermute | solution.py:172
  38.4 5.0 %collective-permute-done.7 = f32[2,2,16,128]{3,2,1,0:T(8,128)S(1)} collective-permute-done((f32[2,2,16,128]{3,2,1,0:T(8,128)S(1)}, f32[2,2,16,128]{3,2,1,0:T(8,128)S(1)}, u32[]{:S(2)}, u32[]{:S(2)}) %collective-permute-start.7) | collective-permute-done | bytes 32800 | tf_op jit(solution)/shard_map/ppermute | solution.py:172
  51.8 4.3 %shard_map.118.refs_5_ = bf16[16,48,2048]{2,1,0:T(8,128)(2,1)} custom-call(bf16[16,48,128]{2,1,0:T(8,128)(2,1)} %fusion.13.pick_ref, bf16[4,64,2048]{2,1,0:T(8,128)(2,1)} %copy-done.3, bf16[4,64,2048]{2,1,0:T(8,128)(2,1)} %copy-done.5, bf16[4,64,2048]{2,1,0:T(8,128)(2,1)} %copy-done.6, bf16[4,64,2048]{2,1,0:T(8,128)(2,1)} %collective-permute-done.16.refs_3_, ...), custom_call_target="tpu_custom_call" | custom-call | flops 1000000 | bytes 100000 | tf_op jit(solution)/shard_map/pallas_call | solution.py:285
  56.1 10.8 %collective-permute-done.13 = bf16[64,2048]{1,0:T(8,128)(2,1)} collective-permute-done((bf16[64,2048]{1,0:T(8,128)(2,1)S(1)}, bf16[64,2048]{1,0:T(8,128)(2,1)}, u32[]{:S(2)}, u32[]{:S(2)}) %collective-permute-start.13) | collective-permute-done | bytes 262176 | tf_op jit(solution)/shard_map/ppermute | solution.py:172
  71.9 5.9 %shard_map.119 = bf16[16,48,2048]{2,1,0:T(8,128)(2,1)} custom-call(bf16[16,48,128]{2,1,0:T(8,128)(2,1)} %fusion.13.pick_ref, bf16[6,64,2048]{2,1,0:T(8,128)(2,1)} %constant_dynamic-update-slice_fusion.refs_0_, bf16[6,64,2048]{2,1,0:T(8,128)(2,1)} %collective-permute-done.12.refs_1_, ...), custom_call_target="tpu_custom_call", output_to_operand_aliasing={{}: (6, {})} | custom-call | flops 1000000 | bytes 100000 | tf_op jit(solution)/shard_map/pallas_call | solution.py:285
  85.6 13.1 %shard_map.120 = (f32[768,768]{1,0:T(8,128)}, f32[768,768]{1,0:T(8,128)}, bf16[768,768]{1,0:T(8,128)(2,1)}, bf16[768,2048]{1,0:T(8,128)(2,1)}) custom-call(bf16[768,2048]{1,0:T(8,128)(2,1)} %bitcast.146, bf16[1,2048,1536]{2,1,0:T(8,128)(2,1)} %gate_up_ref.5, bf16[1,768,2048]{2,1,0:T(8,128)(2,1)} %down_ref.3), custom_call_target="tpu_custom_call" | custom-call | flops 1000000 | bytes 100000 | tf_op jit(solution)/shard_map/pallas_call | solution.py:399
  98.7 7.3 %shard_map.121 = (bf16[12,64,2048]{2,1,0:T(8,128)(2,1)}, bf16[6,64,2048]{2,1,0:T(8,128)(2,1)}, bf16[6,64,2048]{2,1,0:T(8,128)(2,1)}) custom-call(bf16[16,128,48]{2,1,0:T(8,128)(2,1)} %fusion.1.back_ref, f32[16,48,1]{2,1,0:T(8,128)} %copy.20.prob_ref.refs_4_, bf16[16,48,2048]{2,1,0:T(8,128)(2,1)} %bitcast.150), custom_call_target="tpu_custom_call" | custom-call | flops 1000000 | bytes 100000 | tf_op jit(solution)/shard_map/pallas_call | solution.py:364
  107.2 4.5 %shard_map.122 = (bf16[16,48,2048]{2,1,0:T(8,128)(2,1)}, f32[16,48,1]{2,1,0:T(8,128)}) custom-call(bf16[16,48,128]{2,1,0:T(8,128)(2,1)} %fusion.13.pick_ref, bf16[4,64,2048]{2,1,0:T(8,128)(2,1)} %copy-done.3, bf16[4,64,2048]{2,1,0:T(8,128)(2,1)} %copy-done.5, bf16[4,64,2048]{2,1,0:T(8,128)(2,1)} %copy-done.6, ...), custom_call_target="tpu_custom_call" | custom-call | flops 1000000 | bytes 100000 | tf_op jit(solution)/shard_map/pallas_call | solution.py:285
  111.7 3.7 %add_convert_fusion.1 = bf16[6,64,2048]{2,1,0:T(8,128)(2,1)} fusion(bf16[6,64,2048]{2,1,0:T(8,128)(2,1)} %collective-permute-done.22, bf16[12,64,2048]{2,1,0:T(8,128)(2,1)} %get-tuple-element.94), kind=kLoop, calls=%fused_computation.4 | loop fusion | flops 3145728 | bytes 4718592 | tf_op jit(solution)/shard_map/convert_element_type | solution.py:213
  116.3 6.5 %shard_map.123 = (bf16[16,48,2048]{2,1,0:T(8,128)(2,1)}, f32[16,48,1]{2,1,0:T(8,128)}) custom-call(bf16[16,48,128]{2,1,0:T(8,128)(2,1)} %fusion.13.pick_ref, bf16[6,64,2048]{2,1,0:T(8,128)(2,1)} %constant_dynamic-update-slice_fusion.2.refs_0_, bf16[6,64,2048]{2,1,0:T(8,128)(2,1)} %collective-permute-done.21.refs_1_, ...), custom_call_target="tpu_custom_call", output_to_operand_aliasing={{0}: (7, {}), {1}: (8, {})} | custom-call | flops 1000000 | bytes 100000 | tf_op jit(solution)/shard_map/pallas_call | solution.py:285
  122.9 8.7 %shard_map.124.joined_ref = bf16[768,1536]{1,0:T(8,128)(2,1)} custom-call(bf16[768,2048]{1,0:T(8,128)(2,1)} %bitcast.156, f32[768,768]{1,0:T(8,128)} %get-tuple-element.107.gate_pre_ref, f32[768,768]{1,0:T(8,128)} %get-tuple-element.108.up_pre_ref, bf16[1,768,2048]{2,1,0:T(8,128)(2,1)} %down_ref.3), custom_call_target="tpu_custom_call" | custom-call | flops 1000000 | bytes 100000 | tf_op jit(solution)/shard_map/pallas_call | solution.py:435
  131.6 6.3 %shard_map.125 = (bf16[768,2048]{1,0:T(8,128)(2,1)}, f32[1,1024]{1,0:T(1,128)}) custom-call(bf16[768,1536]{1,0:T(8,128)(2,1)} %shard_map.124.joined_ref, bf16[1,2048,1536]{2,1,0:T(8,128)(2,1)} %gate_up_ref.5, bf16[768,2048]{1,0:T(8,128)(2,1)} %bitcast.147), custom_call_target="tpu_custom_call" | custom-call | flops 1000000 | bytes 100000 | tf_op jit(solution)/shard_map/pallas_call | solution.py:464
  141.8 6.3 %shard_map.126 = (bf16[768,2048]{1,0:T(8,128)(2,1)}, f32[1,1024]{1,0:T(1,128)}) custom-call(bf16[768,1536]{1,0:T(8,128)(2,1)} %shard_map.124.joined_ref, bf16[1,2048,1536]{2,1,0:T(8,128)(2,1)} %gate_up_ref.5, bf16[768,2048]{1,0:T(8,128)(2,1)} %bitcast.148, bf16[768,2048]{1,0:T(8,128)(2,1)} %get-tuple-element.112.refs_0_), custom_call_target="tpu_custom_call", output_to_operand_aliasing={{0}: (3, {})} | custom-call | flops 1000000 | bytes 100000 | tf_op jit(solution)/shard_map/pallas_call | solution.py:464
  148.1 6.5 %shard_map.127 = (bf16[12,64,2048]{2,1,0:T(8,128)(2,1)}, bf16[6,64,2048]{2,1,0:T(8,128)(2,1)}, bf16[6,64,2048]{2,1,0:T(8,128)(2,1)}) custom-call(bf16[16,128,48]{2,1,0:T(8,128)(2,1)} %fusion.1.back_ref, f32[16,48,1]{2,1,0:T(8,128)} %copy.20.prob_ref.refs_4_, bf16[16,48,2048]{2,1,0:T(8,128)(2,1)} %bitcast.154), custom_call_target="tpu_custom_call" | custom-call | flops 1000000 | bytes 100000 | tf_op jit(solution)/shard_map/pallas_call | solution.py:364
  162.6 7.1 %convolution_convert_fusion = bf16[2048,1536]{1,0:T(8,128)(2,1)} fusion(bf16[768,2048]{1,0:T(8,128)(2,1)S(1)} %bitcast.149, bf16[768,1536]{1,0:T(8,128)(2,1)S(1)} %copy-done.1), kind=kOutput, calls=%fused_computation.1 | convolution fusion | flops 4834983936 | bytes 11796480 | tf_op jit(solution)/shard_map/dot_general | solution.py:38
  169.7 5.6 %shard_map.128 = (bf16[8,64,2048]{2,1,0:T(8,128)(2,1)}, bf16[4,64,2048]{2,1,0:T(8,128)(2,1)}, bf16[4,64,2048]{2,1,0:T(8,128)(2,1)}) custom-call(bf16[16,128,48]{2,1,0:T(8,128)(2,1)} %fusion.1.back_ref, f32[16,48,1]{2,1,0:T(8,128)} %copy.20.prob_ref.refs_4_, bf16[16,48,2048]{2,1,0:T(8,128)(2,1)} %bitcast.153, bf16[16,48,2048]{2,1,0:T(8,128)(2,1)} %bitcast.155), custom_call_target="tpu_custom_call" | custom-call | flops 1000000 | bytes 100000 | tf_op jit(solution)/shard_map/pallas_call | solution.py:364
  175.3 4.1 %collective-permute-done.28 = bf16[64,2048]{1,0:T(8,128)(2,1)S(1)} collective-permute-done((bf16[64,2048]{1,0:T(8,128)(2,1)}, bf16[64,2048]{1,0:T(8,128)(2,1)S(1)}, u32[]{:S(2)}, u32[]{:S(2)}) %collective-permute-start.28) | collective-permute-done | bytes 262176 | tf_op jit(solution)/shard_map/ppermute | solution.py:172
  186.0 3.6 %add_convert_fusion.3 = bf16[3,64,2048]{2,1,0:T(8,128)(2,1)} fusion(bf16[6,64,2048]{2,1,0:T(8,128)(2,1)} %collective-permute-done.36, bf16[6,64,2048]{2,1,0:T(8,128)(2,1)} %collective-permute-done.32, bf16[12,64,2048]{2,1,0:T(8,128)(2,1)} %get-tuple-element.116), kind=kLoop, calls=%fused_computation.6 | loop fusion | flops 2359296 | bytes 3145728 | tf_op jit(solution)/shard_map/convert_element_type | solution.py:213
  190.5 5.4 %convolution_convert_fusion.1 = bf16[768,2048]{1,0:T(8,128)(2,1)} fusion(bf16[768,768]{1,0:T(8,128)(2,1)} %get-tuple-element.137, bf16[768,2048]{1,0:T(8,128)(2,1)S(1)} %bitcast.157), kind=kOutput, calls=%fused_computation.2 | convolution fusion | flops 2417491968 | bytes 7471104 | tf_op jit(solution)/shard_map/dot_general | solution.py:38
  216.0 7.2 %collective-permute-done.42 = bf16[64,2048]{1,0:T(8,128)(2,1)} collective-permute-done((bf16[64,2048]{1,0:T(8,128)(2,1)}, bf16[64,2048]{1,0:T(8,128)(2,1)}, u32[]{:S(2)}, u32[]{:S(2)}) %collective-permute-start.42) | collective-permute-done | bytes 262176 | tf_op jit(solution)/shard_map/ppermute | solution.py:172
  224.7 5.9 %collective-permute-done.43 = bf16[64,2048]{1,0:T(8,128)(2,1)} collective-permute-done((bf16[64,2048]{1,0:T(8,128)(2,1)}, bf16[64,2048]{1,0:T(8,128)(2,1)}, u32[]{:S(2)}, u32[]{:S(2)}) %collective-permute-start.43) | collective-permute-done | bytes 262176 | tf_op jit(solution)/shard_map/ppermute | solution.py:172
  230.5 5.4 %collective-permute-done.44 = bf16[64,2048]{1,0:T(8,128)(2,1)} collective-permute-done((bf16[64,2048]{1,0:T(8,128)(2,1)}, bf16[64,2048]{1,0:T(8,128)(2,1)}, u32[]{:S(2)}, u32[]{:S(2)}) %collective-permute-start.44) | collective-permute-done | bytes 262176 | tf_op jit(solution)/shard_map/ppermute | solution.py:172
  235.9 3.4 %fusion.4 = (f32[64]{0:T(128)S(1)}, f32[64,2048]{1,0:T(8,128)S(1)}, bf16[64,2048]{1,0:T(8,128)(2,1)}) fusion(bf16[64,2048]{1,0:T(8,128)(2,1)S(1)} %copy-done.4, f32[64]{0:T(128)S(1)} %add_rsqrt_fusion, f32[2048]{0:T(1024)S(1)} %copy-done.19, bf16[2,64,2048]{2,1,0:T(8,128)(2,1)} %collective-permute-done.41, bf16[2,64,2048]{2,1,0:T(8,128)(2,1)} %collective-permute-done.40, ...), kind=kLoop, calls=%fused_computation.24 | loop fusion | flops 4849600 | bytes 5251584 | tf_op jit(solution)/shard_map/reduce_sum | solution.py:653
  (215 shorter events, 87.7 us)
Async XLA Ops:
  4.7 14.2 %collective-permute-start.5 = (bf16[64,2048]{1,0:T(8,128)(2,1)}, bf16[64,2048]{1,0:T(8,128)(2,1)S(1)}, u32[]{:S(2)}, u32[]{:S(2)}) collective-permute-start(bf16[64,2048]{1,0:T(8,128)(2,1)} %param.7), channel_id=1, source_target_pairs={{0,8},{1,9},{2,10},{3,11},{4,12},{5,13},{6,14},{7,15},{8,16},{9,17... | collective-permute-start | bytes 786440 | tf_op jit(solution)/shard_map/ppermute | solution.py:172
  6.3 13.3 %collective-permute-start.3 = (bf16[64,2048]{1,0:T(8,128)(2,1)}, bf16[64,2048]{1,0:T(8,128)(2,1)S(1)}, u32[]{:S(2)}, u32[]{:S(2)}) collective-permute-start(bf16[64,2048]{1,0:T(8,128)(2,1)} %param.7), channel_id=1, source_target_pairs={{0,24},{1,25},{2,26},{3,27},{4,28},{5,29},{6,30},{7,31},{8,0},{9,1... | collective-permute-start | bytes 786440 | tf_op jit(solution)/shard_map/ppermute | solution.py:172
  8.5 22.9 %collective-permute-start.4 = (bf16[64,2048]{1,0:T(8,128)(2,1)}, bf16[64,2048]{1,0:T(8,128)(2,1)S(1)}, u32[]{:S(2)}, u32[]{:S(2)}) collective-permute-start(bf16[64,2048]{1,0:T(8,128)(2,1)} %param.7), channel_id=1, source_target_pairs={{0,16},{1,17},{2,18},{3,19},{4,20},{5,21},{6,22},{7,23},{8,24},{9,... | collective-permute-start | bytes 786440 | tf_op jit(solution)/shard_map/ppermute | solution.py:172
  15.1 28.5 %collective-permute-start.10 = (bf16[4,64,2048]{2,1,0:T(8,128)(2,1)S(1)}, bf16[4,64,2048]{2,1,0:T(8,128)(2,1)S(1)}, u32[]{:S(2)}, u32[]{:S(2)}) collective-permute-start(bf16[4,64,2048]{2,1,0:T(8,128)(2,1)S(1)} %pad_maximum_fusion.refs_0_), channel_id=1, source_target_pairs={{0,4},{1,3},{2,6},{3,1},{4,0},{5,7},{6,2},{7,5},{8,12},{9,11},{10,... | collective-permute-start | bytes 3145736 | tf_op jit(solution)/shard_map/ppermute | solution.py:172
  16.8 14.7 %collective-permute-start.2 = (f32[2,16,128]{2,1,0:T(8,128)S(1)}, f32[2,16,128]{2,1,0:T(8,128)S(1)}, u32[]{:S(2)}, u32[]{:S(2)}) collective-permute-start(f32[2,16,128]{2,1,0:T(8,128)S(1)} %get-tuple-element.174), channel_id=1, source_target_pairs={{0,4},{1,3},{2,6},{3,1},{4,0},{5,7},{6,2},{7,5},{8,12},{9,11},{10,... | collective-permute-start | bytes 49160 | tf_op jit(solution)/shard_map/ppermute | solution.py:172
  44.6 23.5 %collective-permute-start.12 = (bf16[6,64,2048]{2,1,0:T(8,128)(2,1)}, bf16[6,64,2048]{2,1,0:T(8,128)(2,1)}, u32[]{:S(2)}, u32[]{:S(2)}) collective-permute-start(bf16[6,64,2048]{2,1,0:T(8,128)(2,1)} %constant_dynamic-update-slice_fusion.refs_0_), channel_id=1, source_target_pairs={{0,4},{1,3},{2,6},{3,1},{4,0},{5,7},{6,2},{7,5},{8,12},{9,11},{10,... | collective-permute-start | bytes 4718600 | tf_op jit(solution)/shard_map/ppermute | solution.py:172
  46.5 20.5 %collective-permute-start.13 = (bf16[64,2048]{1,0:T(8,128)(2,1)S(1)}, bf16[64,2048]{1,0:T(8,128)(2,1)}, u32[]{:S(2)}, u32[]{:S(2)}) collective-permute-start(bf16[64,2048]{1,0:T(8,128)(2,1)S(1)} %copy-done.8), channel_id=1, source_target_pairs={{0,16},{1,17},{2,18},{3,19},{4,20},{5,21},{6,22},{7,23},{8,24},{9,... | collective-permute-start | bytes 786440 | tf_op jit(solution)/shard_map/ppermute | solution.py:172
  47.7 19.2 %collective-permute-start.14 = (bf16[64,2048]{1,0:T(8,128)(2,1)S(1)}, bf16[64,2048]{1,0:T(8,128)(2,1)}, u32[]{:S(2)}, u32[]{:S(2)}) collective-permute-start(bf16[64,2048]{1,0:T(8,128)(2,1)S(1)} %copy-done.8), channel_id=1, source_target_pairs={{0,8},{1,9},{2,10},{3,11},{4,12},{5,13},{6,14},{7,15},{8,16},{9,17... | collective-permute-start | bytes 786440 | tf_op jit(solution)/shard_map/ppermute | solution.py:172
  50.8 19.7 %collective-permute-start.17 = (bf16[6,64,2048]{2,1,0:T(8,128)(2,1)}, bf16[6,64,2048]{2,1,0:T(8,128)(2,1)}, u32[]{:S(2)}, u32[]{:S(2)}) collective-permute-start(bf16[6,64,2048]{2,1,0:T(8,128)(2,1)} %constant_dynamic-update-slice_fusion.refs_0_), channel_id=1, source_target_pairs={{0,1},{1,0},{2,3},{3,2},{4,5},{5,4},{6,7},{7,6},{8,9},{9,8},{10,11... | collective-permute-start | bytes 4718600 | tf_op jit(solution)/shard_map/ppermute | solution.py:172
  82.5 16.2 %collective-permute-start.20 = (bf16[6,64,2048]{2,1,0:T(8,128)(2,1)}, bf16[6,64,2048]{2,1,0:T(8,128)(2,1)}, u32[]{:S(2)}, u32[]{:S(2)}) collective-permute-start(bf16[6,64,2048]{2,1,0:T(8,128)(2,1)} %constant_dynamic-update-slice_fusion.2.refs_0_), channel_id=1, source_target_pairs={{0,1},{1,0},{2,3},{3,2},{4,5},{5,4},{6,7},{7,6},{8,9},{9,8},{10,11... | collective-permute-start | bytes 4718600 | tf_op jit(solution)/shard_map/ppermute | solution.py:172
  82.5 23.5 %collective-permute-start.21 = (bf16[6,64,2048]{2,1,0:T(8,128)(2,1)}, bf16[6,64,2048]{2,1,0:T(8,128)(2,1)}, u32[]{:S(2)}, u32[]{:S(2)}) collective-permute-start(bf16[6,64,2048]{2,1,0:T(8,128)(2,1)} %constant_dynamic-update-slice_fusion.2.refs_0_), channel_id=1, source_target_pairs={{0,4},{1,3},{2,6},{3,1},{4,0},{5,7},{6,2},{7,5},{8,12},{9,11},{10,... | collective-permute-start | bytes 4718600 | tf_op jit(solution)/shard_map/ppermute | solution.py:172
  115.4 22.5 %collective-permute-start.24 = (bf16[6,64,2048]{2,1,0:T(8,128)(2,1)}, bf16[6,64,2048]{2,1,0:T(8,128)(2,1)}, u32[]{:S(2)}, u32[]{:S(2)}) collective-permute-start(bf16[6,64,2048]{2,1,0:T(8,128)(2,1)} %add_convert_fusion.1), channel_id=1, source_target_pairs={{0,4},{1,3},{2,6},{3,1},{4,0},{5,7},{6,2},{7,5},{8,12},{9,11},{10,... | collective-permute-start | bytes 4718600 | tf_op jit(solution)/shard_map/ppermute | solution.py:172
  116.3 21.6 %collective-permute-start.23 = (bf16[6,64,2048]{2,1,0:T(8,128)(2,1)}, bf16[6,64,2048]{2,1,0:T(8,128)(2,1)}, u32[]{:S(2)}, u32[]{:S(2)}) collective-permute-start(bf16[6,64,2048]{2,1,0:T(8,128)(2,1)} %get-tuple-element.101), channel_id=1, source_target_pairs={{0,1},{1,0},{2,3},{3,2},{4,5},{5,4},{6,7},{7,6},{8,9},{9,8},{10,11... | collective-permute-start | bytes 4718600 | tf_op jit(solution)/shard_map/ppermute | solution.py:172
  139.9 14.7 %collective-permute-start.26 = (bf16[3,64,2048]{2,1,0:T(8,128)(2,1)S(1)}, bf16[3,64,2048]{2,1,0:T(8,128)(2,1)}, u32[]{:S(2)}, u32[]{:S(2)}) collective-permute-start(bf16[3,64,2048]{2,1,0:T(8,128)(2,1)S(1)} %add_convert_fusion.5), channel_id=1, source_target_pairs={{0,2},{1,5},{2,0},{3,7},{4,6},{5,1},{6,4},{7,3},{8,10},{9,13},{10,... | collective-permute-start | bytes 2359304 | tf_op jit(solution)/shard_map/ppermute | solution.py:172
  154.9 31.2 %collective-permute-start.36 = (bf16[6,64,2048]{2,1,0:T(8,128)(2,1)}, bf16[6,64,2048]{2,1,0:T(8,128)(2,1)}, u32[]{:S(2)}, u32[]{:S(2)}) collective-permute-start(bf16[6,64,2048]{2,1,0:T(8,128)(2,1)} %get-tuple-element.132), channel_id=1, source_target_pairs={{0,1},{1,0},{2,3},{3,2},{4,5},{5,4},{6,7},{7,6},{8,9},{9,8},{10,11... | collective-permute-start | bytes 4718600 | tf_op jit(solution)/shard_map/ppermute | solution.py:172
  158.8 16.5 %collective-permute-start.27 = (bf16[64,2048]{1,0:T(8,128)(2,1)}, bf16[64,2048]{1,0:T(8,128)(2,1)S(1)}, u32[]{:S(2)}, u32[]{:S(2)}) collective-permute-start(bf16[64,2048]{1,0:T(8,128)(2,1)} %get-tuple-element.163), channel_id=1, source_target_pairs={{0,8},{1,9},{2,10},{3,11},{4,12},{5,13},{6,14},{7,15},{8,16},{9,17... | collective-permute-start | bytes 786440 | tf_op jit(solution)/shard_map/ppermute | solution.py:172
  158.8 20.6 %collective-permute-start.28 = (bf16[64,2048]{1,0:T(8,128)(2,1)}, bf16[64,2048]{1,0:T(8,128)(2,1)S(1)}, u32[]{:S(2)}, u32[]{:S(2)}) collective-permute-start(bf16[64,2048]{1,0:T(8,128)(2,1)} %get-tuple-element.165), channel_id=1, source_target_pairs={{0,16},{1,17},{2,18},{3,19},{4,20},{5,21},{6,22},{7,23},{8,24},{9,... | collective-permute-start | bytes 786440 | tf_op jit(solution)/shard_map/ppermute | solution.py:172
  161.9 24.1 %collective-permute-start.32 = (bf16[6,64,2048]{2,1,0:T(8,128)(2,1)}, bf16[6,64,2048]{2,1,0:T(8,128)(2,1)}, u32[]{:S(2)}, u32[]{:S(2)}) collective-permute-start(bf16[6,64,2048]{2,1,0:T(8,128)(2,1)} %add_convert_fusion), channel_id=1, source_target_pairs={{0,4},{1,3},{2,6},{3,1},{4,0},{5,7},{6,2},{7,5},{8,12},{9,11},{10,... | collective-permute-start | bytes 4718600 | tf_op jit(solution)/shard_map/ppermute | solution.py:172
  184.2 16.2 %collective-permute-start.29 = (bf16[64,2048]{1,0:T(8,128)(2,1)}, bf16[64,2048]{1,0:T(8,128)(2,1)S(1)}, u32[]{:S(2)}, u32[]{:S(2)}) collective-permute-start(bf16[64,2048]{1,0:T(8,128)(2,1)} %get-tuple-element.164), channel_id=1, source_target_pairs={{0,24},{1,25},{2,26},{3,27},{4,28},{5,29},{6,30},{7,31},{8,0},{9,1... | collective-permute-start | bytes 786440 | tf_op jit(solution)/shard_map/ppermute | solution.py:172
  210.5 25.5 %collective-permute-start.39 = (bf16[2,64,2048]{2,1,0:T(8,128)(2,1)}, bf16[2,64,2048]{2,1,0:T(8,128)(2,1)}, u32[]{:S(2)}, u32[]{:S(2)}) collective-permute-start(bf16[2,64,2048]{2,1,0:T(8,128)(2,1)} %get-tuple-element.142), channel_id=1, source_target_pairs={{0,2},{1,5},{2,0},{3,7},{4,6},{5,1},{6,4},{7,3},{8,10},{9,13},{10,... | collective-permute-start | bytes 1572872 | tf_op jit(solution)/shard_map/ppermute | solution.py:172
  211.2 24.7 %collective-permute-start.40 = (bf16[2,64,2048]{2,1,0:T(8,128)(2,1)}, bf16[2,64,2048]{2,1,0:T(8,128)(2,1)}, u32[]{:S(2)}, u32[]{:S(2)}) collective-permute-start(bf16[2,64,2048]{2,1,0:T(8,128)(2,1)} %get-tuple-element.144), channel_id=1, source_target_pairs={{0,4},{1,3},{2,6},{3,1},{4,0},{5,7},{6,2},{7,5},{8,12},{9,11},{10,... | collective-permute-start | bytes 1572872 | tf_op jit(solution)/shard_map/ppermute | solution.py:172
  212.3 18.2 %collective-permute-start.43 = (bf16[64,2048]{1,0:T(8,128)(2,1)}, bf16[64,2048]{1,0:T(8,128)(2,1)}, u32[]{:S(2)}, u32[]{:S(2)}) collective-permute-start(bf16[64,2048]{1,0:T(8,128)(2,1)} %get-tuple-element.162), channel_id=1, source_target_pairs={{0,16},{1,17},{2,18},{3,19},{4,20},{5,21},{6,22},{7,23},{8,24},{9,... | collective-permute-start | bytes 786440 | tf_op jit(solution)/shard_map/ppermute | solution.py:172
  213.8 22.1 %collective-permute-start.41 = (bf16[2,64,2048]{2,1,0:T(8,128)(2,1)S(1)}, bf16[2,64,2048]{2,1,0:T(8,128)(2,1)}, u32[]{:S(2)}, u32[]{:S(2)}) collective-permute-start(bf16[2,64,2048]{2,1,0:T(8,128)(2,1)S(1)} %get-tuple-element.146), channel_id=1, source_target_pairs={{0,6},{1,7},{2,4},{3,5},{4,2},{5,3},{6,0},{7,1},{8,14},{9,15},{10,... | collective-permute-start | bytes 1572872 | tf_op jit(solution)/shard_map/ppermute | solution.py:172
  223.2 12.7 %collective-permute-start.44 = (bf16[64,2048]{1,0:T(8,128)(2,1)}, bf16[64,2048]{1,0:T(8,128)(2,1)}, u32[]{:S(2)}, u32[]{:S(2)}) collective-permute-start(bf16[64,2048]{1,0:T(8,128)(2,1)} %get-tuple-element.161), channel_id=1, source_target_pairs={{0,24},{1,25},{2,26},{3,27},{4,28},{5,29},{6,30},{7,31},{8,0},{9,1... | collective-permute-start | bytes 786440 | tf_op jit(solution)/shard_map/ppermute | solution.py:172
  (46 other events, 380.8 us)

commit v17 on v15

--- a/solution.py
+++ b/solution.py
@@ -377,7 +377,8 @@
     )(back, prob, *slots)
 
 
-def forward_kernel(rows_ref, gate_up_ref, down_ref, gate_pre_ref, up_pre_ref, hidden_ref, out_ref):
+def forward_kernel(rows_ref, gate_up_ref, down_ref, *refs):
+    gate_pre_ref, up_pre_ref, hidden_ref, out_ref = refs[-4:]
     projected = jnp.dot(rows_ref[...], gate_up_ref[0], preferred_element_type=jnp.float32)
     half_width = hidden_ref.shape[1]
     gate_pre, up_pre = projected[:, :half_width], projected[:, half_width:]
@@ -388,22 +389,20 @@
     out_ref[...] = jnp.dot(hidden, down_ref[0], preferred_element_type=jnp.float32).astype(jnp.bfloat16)
 
 
-def forward(rows, gate_up_weight, down_weight):
+def forward(rows, gate_up_weight, down_weight, block, first, steps, held):
     slots, features = rows.shape
     width = down_weight.shape[1]
-    block = slots // 2
-
     def row_spec(columns):
-        return pl.BlockSpec((block, columns), lambda i: (i, 0))
+        return pl.BlockSpec((block, columns), lambda i: (first + i, 0))
 
     return pl.pallas_call(
         forward_kernel,
-        grid=(2,),
+        grid=(steps,),
         in_specs=[
             row_spec(features),
             pl.BlockSpec((1, features, 2 * width), lambda i: (0, 0, 0)),
             pl.BlockSpec((1, width, features), lambda i: (0, 0, 0)),
-        ],
+        ] + [pl.BlockSpec(memory_space=pl.ANY)] * len(held),
         out_specs=[row_spec(width), row_spec(width), row_spec(width), row_spec(features)],
         out_shape=[
             jax.ShapeDtypeStruct((slots, width), jnp.float32),
@@ -411,9 +410,10 @@
             jax.ShapeDtypeStruct((slots, width), jnp.bfloat16),
             jax.ShapeDtypeStruct((slots, features), jnp.bfloat16),
         ],
+        input_output_aliases={3 + n: n for n in range(len(held))},
         compiler_params=pltpu.CompilerParams(vmem_limit_bytes=VMEM_LIMIT),
         cost_estimate=LITTLE,
-    )(rows, gate_up_weight, down_weight)
+    )(rows, gate_up_weight, down_weight, *held)
 
 
 def inner_kernel(units, grads_ref, gate_pre_ref, up_pre_ref, down_ref, joined_ref):
@@ -540,8 +540,12 @@
     gain_row = gain[None, :]
     near_pieces = (near_pair, near_far_pair, send_core(near_pair), send_core(near_far_pair))
     rows, = select_normed(pick, gain_row, near_pieces, 1, 2, far, ())
-    cot_steps = together(*cot_steps, rows)
-    rows, cot_far = cot_steps[-1], jnp.stack(cot_steps[:-1])
+    near_slots = 4 * capacity
+    made = list(forward(
+        rows.reshape(-1, features), gate_up_weight, down_weight, near_slots, far // 4, 1, ()
+    ))
+    *cot_steps, made[2] = together(*cot_steps, made[2])
+    cot_far = jnp.stack(cot_steps)
     token_far_pair, cot_far = together(send_first(token_pair), cot_far)
     cot_second = send_second(cot_far)
     token_pieces = (token_pair, token_far_pair, send_core(token_pair), send_core(token_far_pair))
@@ -551,7 +555,9 @@
     cot_far_pair = send_first(cot_pair)
 
     rows = rows.reshape(-1, features)
-    gate_pre, up_pre, hidden, block_out = forward(rows, gate_up_weight, down_weight)
+    gate_pre, up_pre, hidden, block_out = forward(
+        rows, gate_up_weight, down_weight, far * capacity // 2, 0, 2, tuple(made)
+    )
     out_slots = block_out.reshape(expert_size, capacity, features)
     out_mine, out_low, out_high = expand(back, slot_prob, (out_slots,), (True,), steps - 1, 0)
     out_high, cot_far_pair = together(out_high, cot_far_pair)

time: 240 us -> 239 us (level)
  waiting for transfers between devices: 59.6 us -> 52.6 us
  Pallas kernels: 75 us -> 80.6 us
    ppermute x48, waiting for transfers between devices: 59.6 us -> 52.6 us  [send(): return lax.ppermute(array, BOTH, pairs)]
    pallas_call x1 -> x2, Pallas kernels: 13.1 us -> 18.7 us  [forward(): pl.pallas_call(forward_kernel, grid=(steps,), in_specs=[row_spec(features...]
  transfers between devices with their start and end apart: 48 -> 48, of which waited for: 16 -> 16; matrix products, arithmetic and copies ran while one was open for 18% -> 19% of each run, Pallas kernels for 31% -> 34%
where the time goes in v17:
time: 239 us; the launch traced here: 238 us
  Pallas kernels  80.6 us (34%)
  waiting for transfers between devices  52.6 us (22%)
  starting transfers between devices  47.6 us (20%)
  other arithmetic  32.7 us (14%)
  matrix products  12.9 us (5%)
  local copies, waits for them, and re-layouts  10.5 us (4%)
    ppermute x48, waiting for transfers between devices, send(): return lax.ppermute(array, BOTH, pairs)  52.6 us
    ppermute x48, starting transfers between devices, send(): return lax.ppermute(array, BOTH, pairs)  47.6 us
    pallas_call x4, Pallas kernels, select(): pl.pallas_call(functools.partial(kernel, count), grid=(4,), in_specs=[gro...  21.5 us
    pallas_call x3, Pallas kernels, expand(): pl.pallas_call(functools.partial(expand_kernel, weighted, count, first_gr...  19.5 us
    convert_element_type x7, other arithmetic, narrow(): return value.astype(jnp.bfloat16)  18.9 us
    pallas_call x2, Pallas kernels, forward(): pl.pallas_call(forward_kernel, grid=(steps,), in_specs=[row_spec(features...  18.7 us
    dot_general x2, matrix products, outer_sum(): lax.dot_general(left, right, (((0,), (0,)), ((), ())), preferred_element_...  12.7 us
    pallas_call x2, Pallas kernels, backward_input(): pl.pallas_call(input_kernel, grid=(2,), in_specs=[pl.BlockSpec((slots, wi...  12.6 us
  transfers between devices with their start and end apart: 48, of which 16 were waited for; matrix products, arithmetic and copies ran while one was open for 19% of the time, Pallas kernels for 34%

profile of v17, /device:TPU:0, one launch (start us, length us, event | category | flops | bytes accessed | tf_op | source)
XLA Modules:
  0.0 237.9 jit_solution(9948060264256624367)
XLA Ops:
  19.6 11.8 %collective-permute-done.4 = bf16[64,2048]{1,0:T(8,128)(2,1)S(1)} collective-permute-done((bf16[64,2048]{1,0:T(8,128)(2,1)}, bf16[64,2048]{1,0:T(8,128)(2,1)S(1)}, u32[]{:S(2)}, u32[]{:S(2)}) %collective-permute-start.4) | collective-permute-done | bytes 262176 | tf_op jit(solution)/shard_map/ppermute | solution.py:172
  38.4 5.0 %collective-permute-done.7 = f32[2,2,16,128]{3,2,1,0:T(8,128)S(1)} collective-permute-done((f32[2,2,16,128]{3,2,1,0:T(8,128)S(1)}, f32[2,2,16,128]{3,2,1,0:T(8,128)S(1)}, u32[]{:S(2)}, u32[]{:S(2)}) %collective-permute-start.7) | collective-permute-done | bytes 32800 | tf_op jit(solution)/shard_map/ppermute | solution.py:172
  51.9 4.3 %shard_map.118.refs_5_ = bf16[16,48,2048]{2,1,0:T(8,128)(2,1)} custom-call(bf16[16,48,128]{2,1,0:T(8,128)(2,1)} %fusion.13.pick_ref, bf16[4,64,2048]{2,1,0:T(8,128)(2,1)} %copy-done.3, bf16[4,64,2048]{2,1,0:T(8,128)(2,1)} %copy-done.5, bf16[4,64,2048]{2,1,0:T(8,128)(2,1)} %copy-done.6, bf16[4,64,2048]{2,1,0:T(8,128)(2,1)} %collective-permute-done.16.refs_3_, ...), custom_call_target="tpu_custom_call" | custom-call | flops 1000000 | bytes 100000 | tf_op jit(solution)/shard_map/pallas_call | solution.py:285
  56.2 6.9 %shard_map.119 = (f32[768,768]{1,0:T(8,128)}, f32[768,768]{1,0:T(8,128)}, bf16[768,768]{1,0:T(8,128)(2,1)}, bf16[768,2048]{1,0:T(8,128)(2,1)}) custom-call(bf16[768,2048]{1,0:T(8,128)(2,1)} %bitcast.147, bf16[1,2048,1536]{2,1,0:T(8,128)(2,1)} %gate_up_ref.7, bf16[1,768,2048]{2,1,0:T(8,128)(2,1)} %down_ref.5), custom_call_target="tpu_custom_call" | custom-call | flops 1000000 | bytes 100000 | tf_op jit(solution)/shard_map/pallas_call | solution.py:398
  63.1 3.9 %collective-permute-done.13 = bf16[64,2048]{1,0:T(8,128)(2,1)} collective-permute-done((bf16[64,2048]{1,0:T(8,128)(2,1)S(1)}, bf16[64,2048]{1,0:T(8,128)(2,1)}, u32[]{:S(2)}, u32[]{:S(2)}) %collective-permute-start.13) | collective-permute-done | bytes 262176 | tf_op jit(solution)/shard_map/ppermute | solution.py:172
  72.0 5.9 %shard_map.120 = bf16[16,48,2048]{2,1,0:T(8,128)(2,1)} custom-call(bf16[16,48,128]{2,1,0:T(8,128)(2,1)} %fusion.13.pick_ref, bf16[6,64,2048]{2,1,0:T(8,128)(2,1)} %constant_dynamic-update-slice_fusion.refs_0_, bf16[6,64,2048]{2,1,0:T(8,128)(2,1)} %collective-permute-done.12.refs_1_, ...), custom_call_target="tpu_custom_call", output_to_operand_aliasing={{}: (6, {})} | custom-call | flops 1000000 | bytes 100000 | tf_op jit(solution)/shard_map/pallas_call | solution.py:285
  85.7 11.7 %shard_map.121 = (f32[768,768]{1,0:T(8,128)}, f32[768,768]{1,0:T(8,128)}, bf16[768,768]{1,0:T(8,128)(2,1)}, bf16[768,2048]{1,0:T(8,128)(2,1)}) custom-call(bf16[768,2048]{1,0:T(8,128)(2,1)} %bitcast.148, bf16[1,2048,1536]{2,1,0:T(8,128)(2,1)} %gate_up_ref.7, ...), custom_call_target="tpu_custom_call", output_to_operand_aliasing={{0}: (3, {}), {1}: (4, {}), {2}: (5, {}), {3}: (6, {})} | custom-call | flops 1000000 | bytes 100000 | tf_op jit(solution)/shard_map/pallas_call | solution.py:398
  97.5 7.3 %shard_map.122 = (bf16[12,64,2048]{2,1,0:T(8,128)(2,1)}, bf16[6,64,2048]{2,1,0:T(8,128)(2,1)}, bf16[6,64,2048]{2,1,0:T(8,128)(2,1)}) custom-call(bf16[16,128,48]{2,1,0:T(8,128)(2,1)} %fusion.1.back_ref, f32[16,48,1]{2,1,0:T(8,128)} %copy.24.prob_ref.refs_4_, bf16[16,48,2048]{2,1,0:T(8,128)(2,1)} %bitcast.152), custom_call_target="tpu_custom_call" | custom-call | flops 1000000 | bytes 100000 | tf_op jit(solution)/shard_map/pallas_call | solution.py:364
  105.5 4.5 %shard_map.123 = (bf16[16,48,2048]{2,1,0:T(8,128)(2,1)}, f32[16,48,1]{2,1,0:T(8,128)}) custom-call(bf16[16,48,128]{2,1,0:T(8,128)(2,1)} %fusion.13.pick_ref, bf16[4,64,2048]{2,1,0:T(8,128)(2,1)} %copy-done.3, bf16[4,64,2048]{2,1,0:T(8,128)(2,1)} %copy-done.5, bf16[4,64,2048]{2,1,0:T(8,128)(2,1)} %copy-done.6, ...), custom_call_target="tpu_custom_call" | custom-call | flops 1000000 | bytes 100000 | tf_op jit(solution)/shard_map/pallas_call | solution.py:285
  110.0 3.7 %add_convert_fusion.1 = bf16[6,64,2048]{2,1,0:T(8,128)(2,1)} fusion(bf16[6,64,2048]{2,1,0:T(8,128)(2,1)} %collective-permute-done.22, bf16[12,64,2048]{2,1,0:T(8,128)(2,1)} %get-tuple-element.94), kind=kLoop, calls=%fused_computation.4 | loop fusion | flops 3145728 | bytes 4718592 | tf_op jit(solution)/shard_map/convert_element_type | solution.py:213
  115.2 6.8 %shard_map.124 = (bf16[16,48,2048]{2,1,0:T(8,128)(2,1)}, f32[16,48,1]{2,1,0:T(8,128)}) custom-call(bf16[16,48,128]{2,1,0:T(8,128)(2,1)} %fusion.13.pick_ref, bf16[6,64,2048]{2,1,0:T(8,128)(2,1)} %constant_dynamic-update-slice_fusion.2.refs_0_, bf16[6,64,2048]{2,1,0:T(8,128)(2,1)} %collective-permute-done.21.refs_1_, ...), custom_call_target="tpu_custom_call", output_to_operand_aliasing={{0}: (7, {}), {1}: (8, {})} | custom-call | flops 1000000 | bytes 100000 | tf_op jit(solution)/shard_map/pallas_call | solution.py:285
  121.9 8.4 %shard_map.125.joined_ref = bf16[768,1536]{1,0:T(8,128)(2,1)} custom-call(bf16[768,2048]{1,0:T(8,128)(2,1)} %bitcast.158, f32[768,768]{1,0:T(8,128)} %get-tuple-element.106.gate_pre_ref, f32[768,768]{1,0:T(8,128)} %get-tuple-element.107.up_pre_ref, bf16[1,768,2048]{2,1,0:T(8,128)(2,1)} %down_ref.5), custom_call_target="tpu_custom_call" | custom-call | flops 1000000 | bytes 100000 | tf_op jit(solution)/shard_map/pallas_call | solution.py:435
  130.3 6.3 %shard_map.126 = (bf16[768,2048]{1,0:T(8,128)(2,1)}, f32[1,1024]{1,0:T(1,128)}) custom-call(bf16[768,1536]{1,0:T(8,128)(2,1)} %shard_map.125.joined_ref, bf16[1,2048,1536]{2,1,0:T(8,128)(2,1)} %gate_up_ref.7, bf16[768,2048]{1,0:T(8,128)(2,1)} %bitcast.149), custom_call_target="tpu_custom_call" | custom-call | flops 1000000 | bytes 100000 | tf_op jit(solution)/shard_map/pallas_call | solution.py:464
  140.5 6.3 %shard_map.127 = (bf16[768,2048]{1,0:T(8,128)(2,1)}, f32[1,1024]{1,0:T(1,128)}) custom-call(bf16[768,1536]{1,0:T(8,128)(2,1)} %shard_map.125.joined_ref, bf16[1,2048,1536]{2,1,0:T(8,128)(2,1)} %gate_up_ref.7, bf16[768,2048]{1,0:T(8,128)(2,1)} %bitcast.150, bf16[768,2048]{1,0:T(8,128)(2,1)} %get-tuple-element.111.refs_0_), custom_call_target="tpu_custom_call", output_to_operand_aliasing={{0}: (3, {})} | custom-call | flops 1000000 | bytes 100000 | tf_op jit(solution)/shard_map/pallas_call | solution.py:464
  146.8 6.5 %shard_map.128 = (bf16[12,64,2048]{2,1,0:T(8,128)(2,1)}, bf16[6,64,2048]{2,1,0:T(8,128)(2,1)}, bf16[6,64,2048]{2,1,0:T(8,128)(2,1)}) custom-call(bf16[16,128,48]{2,1,0:T(8,128)(2,1)} %fusion.1.back_ref, f32[16,48,1]{2,1,0:T(8,128)} %copy.24.prob_ref.refs_4_, bf16[16,48,2048]{2,1,0:T(8,128)(2,1)} %bitcast.156), custom_call_target="tpu_custom_call" | custom-call | flops 1000000 | bytes 100000 | tf_op jit(solution)/shard_map/pallas_call | solution.py:364
  161.5 7.3 %convolution_convert_fusion = bf16[2048,1536]{1,0:T(8,128)(2,1)} fusion(bf16[768,2048]{1,0:T(8,128)(2,1)S(1)} %bitcast.151, bf16[768,1536]{1,0:T(8,128)(2,1)S(1)} %copy-done.1), kind=kOutput, calls=%fused_computation.1 | convolution fusion | flops 4834983936 | bytes 11796480 | tf_op jit(solution)/shard_map/dot_general | solution.py:38
  168.8 5.6 %shard_map.129 = (bf16[8,64,2048]{2,1,0:T(8,128)(2,1)}, bf16[4,64,2048]{2,1,0:T(8,128)(2,1)}, bf16[4,64,2048]{2,1,0:T(8,128)(2,1)}) custom-call(bf16[16,128,48]{2,1,0:T(8,128)(2,1)} %fusion.1.back_ref, f32[16,48,1]{2,1,0:T(8,128)} %copy.24.prob_ref.refs_4_, bf16[16,48,2048]{2,1,0:T(8,128)(2,1)} %bitcast.155, bf16[16,48,2048]{2,1,0:T(8,128)(2,1)} %bitcast.157), custom_call_target="tpu_custom_call" | custom-call | flops 1000000 | bytes 100000 | tf_op jit(solution)/shard_map/pallas_call | solution.py:364
  174.5 3.8 %collective-permute-done.28 = bf16[64,2048]{1,0:T(8,128)(2,1)S(1)} collective-permute-done((bf16[64,2048]{1,0:T(8,128)(2,1)}, bf16[64,2048]{1,0:T(8,128)(2,1)S(1)}, u32[]{:S(2)}, u32[]{:S(2)}) %collective-permute-start.28) | collective-permute-done | bytes 262176 | tf_op jit(solution)/shard_map/ppermute | solution.py:172
  184.8 3.6 %add_convert_fusion.3 = bf16[3,64,2048]{2,1,0:T(8,128)(2,1)} fusion(bf16[6,64,2048]{2,1,0:T(8,128)(2,1)} %collective-permute-done.36, bf16[6,64,2048]{2,1,0:T(8,128)(2,1)} %collective-permute-done.32, bf16[12,64,2048]{2,1,0:T(8,128)(2,1)} %get-tuple-element.115), kind=kLoop, calls=%fused_computation.6 | loop fusion | flops 2359296 | bytes 3145728 | tf_op jit(solution)/shard_map/convert_element_type | solution.py:213
  189.2 5.4 %convolution_convert_fusion.1 = bf16[768,2048]{1,0:T(8,128)(2,1)} fusion(bf16[768,768]{1,0:T(8,128)(2,1)} %get-tuple-element.136, bf16[768,2048]{1,0:T(8,128)(2,1)S(1)} %bitcast.159), kind=kOutput, calls=%fused_computation.2 | convolution fusion | flops 2417491968 | bytes 7471104 | tf_op jit(solution)/shard_map/dot_general | solution.py:38
  215.1 6.6 %collective-permute-done.42 = bf16[64,2048]{1,0:T(8,128)(2,1)} collective-permute-done((bf16[64,2048]{1,0:T(8,128)(2,1)}, bf16[64,2048]{1,0:T(8,128)(2,1)}, u32[]{:S(2)}, u32[]{:S(2)}) %collective-permute-start.42) | collective-permute-done | bytes 262176 | tf_op jit(solution)/shard_map/ppermute | solution.py:172
  223.9 3.3 %collective-permute-done.43 = bf16[64,2048]{1,0:T(8,128)(2,1)} collective-permute-done((bf16[64,2048]{1,0:T(8,128)(2,1)}, bf16[64,2048]{1,0:T(8,128)(2,1)}, u32[]{:S(2)}, u32[]{:S(2)}) %collective-permute-start.43) | collective-permute-done | bytes 262176 | tf_op jit(solution)/shard_map/ppermute | solution.py:172
  227.2 6.3 %collective-permute-done.44 = bf16[64,2048]{1,0:T(8,128)(2,1)} collective-permute-done((bf16[64,2048]{1,0:T(8,128)(2,1)}, bf16[64,2048]{1,0:T(8,128)(2,1)}, u32[]{:S(2)}, u32[]{:S(2)}) %collective-permute-start.44) | collective-permute-done | bytes 262176 | tf_op jit(solution)/shard_map/ppermute | solution.py:172
  233.6 3.4 %fusion.4 = (f32[64]{0:T(128)S(1)}, f32[64,2048]{1,0:T(8,128)S(1)}, bf16[64,2048]{1,0:T(8,128)(2,1)}) fusion(bf16[64,2048]{1,0:T(8,128)(2,1)S(1)} %copy-done.4, f32[64]{0:T(128)S(1)} %add_rsqrt_fusion, f32[2048]{0:T(1024)S(1)} %copy-done.19, bf16[2,64,2048]{2,1,0:T(8,128)(2,1)} %collective-permute-done.41, bf16[2,64,2048]{2,1,0:T(8,128)(2,1)} %collective-permute-done.40, ...), kind=kLoop, calls=%fused_computation.24 | loop fusion | flops 4849600 | bytes 5251584 | tf_op jit(solution)/shard_map/reduce_sum | solution.py:656
  (216 shorter events, 92.1 us)
Async XLA Ops:
  4.7 14.2 %collective-permute-start.5 = (bf16[64,2048]{1,0:T(8,128)(2,1)}, bf16[64,2048]{1,0:T(8,128)(2,1)S(1)}, u32[]{:S(2)}, u32[]{:S(2)}) collective-permute-start(bf16[64,2048]{1,0:T(8,128)(2,1)} %param.7), channel_id=1, source_target_pairs={{0,8},{1,9},{2,10},{3,11},{4,12},{5,13},{6,14},{7,15},{8,16},{9,17... | collective-permute-start | bytes 786440 | tf_op jit(solution)/shard_map/ppermute | solution.py:172
  6.3 13.3 %collective-permute-start.3 = (bf16[64,2048]{1,0:T(8,128)(2,1)}, bf16[64,2048]{1,0:T(8,128)(2,1)S(1)}, u32[]{:S(2)}, u32[]{:S(2)}) collective-permute-start(bf16[64,2048]{1,0:T(8,128)(2,1)} %param.7), channel_id=1, source_target_pairs={{0,24},{1,25},{2,26},{3,27},{4,28},{5,29},{6,30},{7,31},{8,0},{9,1... | collective-permute-start | bytes 786440 | tf_op jit(solution)/shard_map/ppermute | solution.py:172
  8.5 22.9 %collective-permute-start.4 = (bf16[64,2048]{1,0:T(8,128)(2,1)}, bf16[64,2048]{1,0:T(8,128)(2,1)S(1)}, u32[]{:S(2)}, u32[]{:S(2)}) collective-permute-start(bf16[64,2048]{1,0:T(8,128)(2,1)} %param.7), channel_id=1, source_target_pairs={{0,16},{1,17},{2,18},{3,19},{4,20},{5,21},{6,22},{7,23},{8,24},{9,... | collective-permute-start | bytes 786440 | tf_op jit(solution)/shard_map/ppermute | solution.py:172
  15.1 28.5 %collective-permute-start.10 = (bf16[4,64,2048]{2,1,0:T(8,128)(2,1)S(1)}, bf16[4,64,2048]{2,1,0:T(8,128)(2,1)S(1)}, u32[]{:S(2)}, u32[]{:S(2)}) collective-permute-start(bf16[4,64,2048]{2,1,0:T(8,128)(2,1)S(1)} %pad_maximum_fusion.refs_0_), channel_id=1, source_target_pairs={{0,4},{1,3},{2,6},{3,1},{4,0},{5,7},{6,2},{7,5},{8,12},{9,11},{10,... | collective-permute-start | bytes 3145736 | tf_op jit(solution)/shard_map/ppermute | solution.py:172
  16.8 14.7 %collective-permute-start.2 = (f32[2,16,128]{2,1,0:T(8,128)S(1)}, f32[2,16,128]{2,1,0:T(8,128)S(1)}, u32[]{:S(2)}, u32[]{:S(2)}) collective-permute-start(f32[2,16,128]{2,1,0:T(8,128)S(1)} %get-tuple-element.170), channel_id=1, source_target_pairs={{0,4},{1,3},{2,6},{3,1},{4,0},{5,7},{6,2},{7,5},{8,12},{9,11},{10,... | collective-permute-start | bytes 49160 | tf_op jit(solution)/shard_map/ppermute | solution.py:172
  44.7 23.5 %collective-permute-start.12 = (bf16[6,64,2048]{2,1,0:T(8,128)(2,1)}, bf16[6,64,2048]{2,1,0:T(8,128)(2,1)}, u32[]{:S(2)}, u32[]{:S(2)}) collective-permute-start(bf16[6,64,2048]{2,1,0:T(8,128)(2,1)} %constant_dynamic-update-slice_fusion.refs_0_), channel_id=1, source_target_pairs={{0,4},{1,3},{2,6},{3,1},{4,0},{5,7},{6,2},{7,5},{8,12},{9,11},{10,... | collective-permute-start | bytes 4718600 | tf_op jit(solution)/shard_map/ppermute | solution.py:172
  46.5 20.5 %collective-permute-start.13 = (bf16[64,2048]{1,0:T(8,128)(2,1)S(1)}, bf16[64,2048]{1,0:T(8,128)(2,1)}, u32[]{:S(2)}, u32[]{:S(2)}) collective-permute-start(bf16[64,2048]{1,0:T(8,128)(2,1)S(1)} %copy-done.8), channel_id=1, source_target_pairs={{0,16},{1,17},{2,18},{3,19},{4,20},{5,21},{6,22},{7,23},{8,24},{9,... | collective-permute-start | bytes 786440 | tf_op jit(solution)/shard_map/ppermute | solution.py:172
  47.8 19.2 %collective-permute-start.14 = (bf16[64,2048]{1,0:T(8,128)(2,1)S(1)}, bf16[64,2048]{1,0:T(8,128)(2,1)}, u32[]{:S(2)}, u32[]{:S(2)}) collective-permute-start(bf16[64,2048]{1,0:T(8,128)(2,1)S(1)} %copy-done.8), channel_id=1, source_target_pairs={{0,8},{1,9},{2,10},{3,11},{4,12},{5,13},{6,14},{7,15},{8,16},{9,17... | collective-permute-start | bytes 786440 | tf_op jit(solution)/shard_map/ppermute | solution.py:172
  50.9 19.7 %collective-permute-start.17 = (bf16[6,64,2048]{2,1,0:T(8,128)(2,1)}, bf16[6,64,2048]{2,1,0:T(8,128)(2,1)}, u32[]{:S(2)}, u32[]{:S(2)}) collective-permute-start(bf16[6,64,2048]{2,1,0:T(8,128)(2,1)} %constant_dynamic-update-slice_fusion.refs_0_), channel_id=1, source_target_pairs={{0,1},{1,0},{2,3},{3,2},{4,5},{5,4},{6,7},{7,6},{8,9},{9,8},{10,11... | collective-permute-start | bytes 4718600 | tf_op jit(solution)/shard_map/ppermute | solution.py:172
  68.3 12.2 %collective-permute-start.19 = (bf16[3,64,2048]{2,1,0:T(8,128)(2,1)S(1)}, bf16[3,64,2048]{2,1,0:T(8,128)(2,1)}, u32[]{:S(2)}, u32[]{:S(2)}) collective-permute-start(bf16[3,64,2048]{2,1,0:T(8,128)(2,1)S(1)} %pad_maximum_fusion.2), channel_id=1, source_target_pairs={{0,2},{1,5},{2,0},{3,7},{4,6},{5,1},{6,4},{7,3},{8,10},{9,13},{10,... | collective-permute-start | bytes 2359304 | tf_op jit(solution)/shard_map/ppermute | solution.py:172
  82.6 22.2 %collective-permute-start.21 = (bf16[6,64,2048]{2,1,0:T(8,128)(2,1)}, bf16[6,64,2048]{2,1,0:T(8,128)(2,1)}, u32[]{:S(2)}, u32[]{:S(2)}) collective-permute-start(bf16[6,64,2048]{2,1,0:T(8,128)(2,1)} %constant_dynamic-update-slice_fusion.2.refs_0_), channel_id=1, source_target_pairs={{0,4},{1,3},{2,6},{3,1},{4,0},{5,7},{6,2},{7,5},{8,12},{9,11},{10,... | collective-permute-start | bytes 4718600 | tf_op jit(solution)/shard_map/ppermute | solution.py:172
  113.7 22.9 %collective-permute-start.23 = (bf16[6,64,2048]{2,1,0:T(8,128)(2,1)}, bf16[6,64,2048]{2,1,0:T(8,128)(2,1)}, u32[]{:S(2)}, u32[]{:S(2)}) collective-permute-start(bf16[6,64,2048]{2,1,0:T(8,128)(2,1)} %add_convert_fusion.1), channel_id=1, source_target_pairs={{0,4},{1,3},{2,6},{3,1},{4,0},{5,7},{6,2},{7,5},{8,12},{9,11},{10,... | collective-permute-start | bytes 4718600 | tf_op jit(solution)/shard_map/ppermute | solution.py:172
  115.2 21.4 %collective-permute-start.20 = (bf16[6,64,2048]{2,1,0:T(8,128)(2,1)}, bf16[6,64,2048]{2,1,0:T(8,128)(2,1)}, u32[]{:S(2)}, u32[]{:S(2)}) collective-permute-start(bf16[6,64,2048]{2,1,0:T(8,128)(2,1)} %get-tuple-element.95), channel_id=1, source_target_pairs={{0,1},{1,0},{2,3},{3,2},{4,5},{5,4},{6,7},{7,6},{8,9},{9,8},{10,11... | collective-permute-start | bytes 4718600 | tf_op jit(solution)/shard_map/ppermute | solution.py:172
  138.7 14.7 %collective-permute-start.26 = (bf16[3,64,2048]{2,1,0:T(8,128)(2,1)S(1)}, bf16[3,64,2048]{2,1,0:T(8,128)(2,1)}, u32[]{:S(2)}, u32[]{:S(2)}) collective-permute-start(bf16[3,64,2048]{2,1,0:T(8,128)(2,1)S(1)} %add_convert_fusion.5), channel_id=1, source_target_pairs={{0,2},{1,5},{2,0},{3,7},{4,6},{5,1},{6,4},{7,3},{8,10},{9,13},{10,... | collective-permute-start | bytes 2359304 | tf_op jit(solution)/shard_map/ppermute | solution.py:172
  153.6 31.2 %collective-permute-start.36 = (bf16[6,64,2048]{2,1,0:T(8,128)(2,1)}, bf16[6,64,2048]{2,1,0:T(8,128)(2,1)}, u32[]{:S(2)}, u32[]{:S(2)}) collective-permute-start(bf16[6,64,2048]{2,1,0:T(8,128)(2,1)} %get-tuple-element.131), channel_id=1, source_target_pairs={{0,1},{1,0},{2,3},{3,2},{4,5},{5,4},{6,7},{7,6},{8,9},{9,8},{10,11... | collective-permute-start | bytes 4718600 | tf_op jit(solution)/shard_map/ppermute | solution.py:172
  157.6 16.8 %collective-permute-start.27 = (bf16[64,2048]{1,0:T(8,128)(2,1)}, bf16[64,2048]{1,0:T(8,128)(2,1)S(1)}, u32[]{:S(2)}, u32[]{:S(2)}) collective-permute-start(bf16[64,2048]{1,0:T(8,128)(2,1)} %get-tuple-element.159), channel_id=1, source_target_pairs={{0,8},{1,9},{2,10},{3,11},{4,12},{5,13},{6,14},{7,15},{8,16},{9,17... | collective-permute-start | bytes 786440 | tf_op jit(solution)/shard_map/ppermute | solution.py:172
  157.6 20.6 %collective-permute-start.28 = (bf16[64,2048]{1,0:T(8,128)(2,1)}, bf16[64,2048]{1,0:T(8,128)(2,1)S(1)}, u32[]{:S(2)}, u32[]{:S(2)}) collective-permute-start(bf16[64,2048]{1,0:T(8,128)(2,1)} %get-tuple-element.161), channel_id=1, source_target_pairs={{0,16},{1,17},{2,18},{3,19},{4,20},{5,21},{6,22},{7,23},{8,24},{9,... | collective-permute-start | bytes 786440 | tf_op jit(solution)/shard_map/ppermute | solution.py:172
  160.7 24.1 %collective-permute-start.32 = (bf16[6,64,2048]{2,1,0:T(8,128)(2,1)}, bf16[6,64,2048]{2,1,0:T(8,128)(2,1)}, u32[]{:S(2)}, u32[]{:S(2)}) collective-permute-start(bf16[6,64,2048]{2,1,0:T(8,128)(2,1)} %add_convert_fusion), channel_id=1, source_target_pairs={{0,4},{1,3},{2,6},{3,1},{4,0},{5,7},{6,2},{7,5},{8,12},{9,11},{10,... | collective-permute-start | bytes 4718600 | tf_op jit(solution)/shard_map/ppermute | solution.py:172
  183.0 16.1 %collective-permute-start.29 = (bf16[64,2048]{1,0:T(8,128)(2,1)}, bf16[64,2048]{1,0:T(8,128)(2,1)S(1)}, u32[]{:S(2)}, u32[]{:S(2)}) collective-permute-start(bf16[64,2048]{1,0:T(8,128)(2,1)} %get-tuple-element.160), channel_id=1, source_target_pairs={{0,24},{1,25},{2,26},{3,27},{4,28},{5,29},{6,30},{7,31},{8,0},{9,1... | collective-permute-start | bytes 786440 | tf_op jit(solution)/shard_map/ppermute | solution.py:172
  188.4 12.6 %collective-permute-start.37 = (bf16[3,64,2048]{2,1,0:T(8,128)(2,1)}, bf16[3,64,2048]{2,1,0:T(8,128)(2,1)}, u32[]{:S(2)}, u32[]{:S(2)}) collective-permute-start(bf16[3,64,2048]{2,1,0:T(8,128)(2,1)} %add_convert_fusion.3), channel_id=1, source_target_pairs={{0,2},{1,5},{2,0},{3,7},{4,6},{5,1},{6,4},{7,3},{8,10},{9,13},{10,... | collective-permute-start | bytes 2359304 | tf_op jit(solution)/shard_map/ppermute | solution.py:172
  208.3 25.2 %collective-permute-start.39 = (bf16[2,64,2048]{2,1,0:T(8,128)(2,1)}, bf16[2,64,2048]{2,1,0:T(8,128)(2,1)}, u32[]{:S(2)}, u32[]{:S(2)}) collective-permute-start(bf16[2,64,2048]{2,1,0:T(8,128)(2,1)} %get-tuple-element.141), channel_id=1, source_target_pairs={{0,2},{1,5},{2,0},{3,7},{4,6},{5,1},{6,4},{7,3},{8,10},{9,13},{10,... | collective-permute-start | bytes 1572872 | tf_op jit(solution)/shard_map/ppermute | solution.py:172
  209.0 24.5 %collective-permute-start.40 = (bf16[2,64,2048]{2,1,0:T(8,128)(2,1)}, bf16[2,64,2048]{2,1,0:T(8,128)(2,1)}, u32[]{:S(2)}, u32[]{:S(2)}) collective-permute-start(bf16[2,64,2048]{2,1,0:T(8,128)(2,1)} %get-tuple-element.143), channel_id=1, source_target_pairs={{0,4},{1,3},{2,6},{3,1},{4,0},{5,7},{6,2},{7,5},{8,12},{9,11},{10,... | collective-permute-start | bytes 1572872 | tf_op jit(solution)/shard_map/ppermute | solution.py:172
  210.6 16.6 %collective-permute-start.43 = (bf16[64,2048]{1,0:T(8,128)(2,1)}, bf16[64,2048]{1,0:T(8,128)(2,1)}, u32[]{:S(2)}, u32[]{:S(2)}) collective-permute-start(bf16[64,2048]{1,0:T(8,128)(2,1)} %get-tuple-element.158), channel_id=1, source_target_pairs={{0,16},{1,17},{2,18},{3,19},{4,20},{5,21},{6,22},{7,23},{8,24},{9,... | collective-permute-start | bytes 786440 | tf_op jit(solution)/shard_map/ppermute | solution.py:172
  213.1 20.5 %collective-permute-start.41 = (bf16[2,64,2048]{2,1,0:T(8,128)(2,1)S(1)}, bf16[2,64,2048]{2,1,0:T(8,128)(2,1)}, u32[]{:S(2)}, u32[]{:S(2)}) collective-permute-start(bf16[2,64,2048]{2,1,0:T(8,128)(2,1)S(1)} %get-tuple-element.145), channel_id=1, source_target_pairs={{0,6},{1,7},{2,4},{3,5},{4,2},{5,3},{6,0},{7,1},{8,14},{9,15},{10,... | collective-permute-start | bytes 1572872 | tf_op jit(solution)/shard_map/ppermute | solution.py:172
  (46 other events, 384.0 us)

commit v18 on v17

--- a/solution.py
+++ b/solution.py
@@ -556,7 +556,7 @@
 
     rows = rows.reshape(-1, features)
     gate_pre, up_pre, hidden, block_out = forward(
-        rows, gate_up_weight, down_weight, far * capacity // 2, 0, 2, tuple(made)
+        rows, gate_up_weight, down_weight, far * capacity, 0, 1, tuple(made)
     )
     out_slots = block_out.reshape(expert_size, capacity, features)
     out_mine, out_low, out_high = expand(back, slot_prob, (out_slots,), (True,), steps - 1, 0)

time: 239 us -> 238 us (level)
  no operation moved by 1% of the time
where the time goes in v18:
time: 238 us; the launch traced here: 237 us
  Pallas kernels  80.2 us (34%)
  waiting for transfers between devices  52.5 us (22%)
  starting transfers between devices  47.6 us (20%)
  other arithmetic  32.7 us (14%)
  matrix products  12.9 us (5%)
  local copies, waits for them, and re-layouts  10.5 us (4%)
    ppermute x48, waiting for transfers between devices, send(): return lax.ppermute(array, BOTH, pairs)  52.5 us
    ppermute x48, starting transfers between devices, send(): return lax.ppermute(array, BOTH, pairs)  47.6 us
    pallas_call x4, Pallas kernels, select(): pl.pallas_call(functools.partial(kernel, count), grid=(4,), in_specs=[gro...  21.3 us
    pallas_call x3, Pallas kernels, expand(): pl.pallas_call(functools.partial(expand_kernel, weighted, count, first_gr...  19.5 us
    convert_element_type x7, other arithmetic, narrow(): return value.astype(jnp.bfloat16)  18.9 us
    pallas_call x2, Pallas kernels, forward(): pl.pallas_call(forward_kernel, grid=(steps,), in_specs=[row_spec(features...  18.4 us
    dot_general x2, matrix products, outer_sum(): lax.dot_general(left, right, (((0,), (0,)), ((), ())), preferred_element_...  12.8 us
    pallas_call x2, Pallas kernels, backward_input(): pl.pallas_call(input_kernel, grid=(2,), in_specs=[pl.BlockSpec((slots, wi...  12.6 us
  transfers between devices with their start and end apart: 48, of which 16 were waited for; matrix products, arithmetic and copies ran while one was open for 19% of the time, Pallas kernels for 34%

profile of v18, /device:TPU:0, one launch (start us, length us, event | category | flops | bytes accessed | tf_op | source)
XLA Modules:
  0.0 237.4 jit_solution(1473100791238002111)
XLA Ops:
  19.6 11.8 %collective-permute-done.4 = bf16[64,2048]{1,0:T(8,128)(2,1)S(1)} collective-permute-done((bf16[64,2048]{1,0:T(8,128)(2,1)}, bf16[64,2048]{1,0:T(8,128)(2,1)S(1)}, u32[]{:S(2)}, u32[]{:S(2)}) %collective-permute-start.4) | collective-permute-done | bytes 262176 | tf_op jit(solution)/shard_map/ppermute | solution.py:172
  38.4 5.0 %collective-permute-done.7 = f32[2,2,16,128]{3,2,1,0:T(8,128)S(1)} collective-permute-done((f32[2,2,16,128]{3,2,1,0:T(8,128)S(1)}, f32[2,2,16,128]{3,2,1,0:T(8,128)S(1)}, u32[]{:S(2)}, u32[]{:S(2)}) %collective-permute-start.7) | collective-permute-done | bytes 32800 | tf_op jit(solution)/shard_map/ppermute | solution.py:172
  51.9 4.3 %shard_map.118.refs_5_ = bf16[16,48,2048]{2,1,0:T(8,128)(2,1)} custom-call(bf16[16,48,128]{2,1,0:T(8,128)(2,1)} %fusion.13.pick_ref, bf16[4,64,2048]{2,1,0:T(8,128)(2,1)} %copy-done.3, bf16[4,64,2048]{2,1,0:T(8,128)(2,1)} %copy-done.5, bf16[4,64,2048]{2,1,0:T(8,128)(2,1)} %copy-done.6, bf16[4,64,2048]{2,1,0:T(8,128)(2,1)} %collective-permute-done.16.refs_3_, ...), custom_call_target="tpu_custom_call" | custom-call | flops 1000000 | bytes 100000 | tf_op jit(solution)/shard_map/pallas_call | solution.py:285
  56.2 6.9 %shard_map.119 = (f32[768,768]{1,0:T(8,128)}, f32[768,768]{1,0:T(8,128)}, bf16[768,768]{1,0:T(8,128)(2,1)}, bf16[768,2048]{1,0:T(8,128)(2,1)}) custom-call(bf16[768,2048]{1,0:T(8,128)(2,1)} %bitcast.147, bf16[1,2048,1536]{2,1,0:T(8,128)(2,1)} %gate_up_ref.7, bf16[1,768,2048]{2,1,0:T(8,128)(2,1)} %down_ref.5), custom_call_target="tpu_custom_call" | custom-call | flops 1000000 | bytes 100000 | tf_op jit(solution)/shard_map/pallas_call | solution.py:398
  63.1 3.9 %collective-permute-done.13 = bf16[64,2048]{1,0:T(8,128)(2,1)} collective-permute-done((bf16[64,2048]{1,0:T(8,128)(2,1)S(1)}, bf16[64,2048]{1,0:T(8,128)(2,1)}, u32[]{:S(2)}, u32[]{:S(2)}) %collective-permute-start.13) | collective-permute-done | bytes 262176 | tf_op jit(solution)/shard_map/ppermute | solution.py:172
  72.0 5.9 %shard_map.120 = bf16[16,48,2048]{2,1,0:T(8,128)(2,1)} custom-call(bf16[16,48,128]{2,1,0:T(8,128)(2,1)} %fusion.13.pick_ref, bf16[6,64,2048]{2,1,0:T(8,128)(2,1)} %constant_dynamic-update-slice_fusion.refs_0_, bf16[6,64,2048]{2,1,0:T(8,128)(2,1)} %collective-permute-done.12.refs_1_, ...), custom_call_target="tpu_custom_call", output_to_operand_aliasing={{}: (6, {})} | custom-call | flops 1000000 | bytes 100000 | tf_op jit(solution)/shard_map/pallas_call | solution.py:285
  85.7 11.5 %shard_map.121 = (f32[768,768]{1,0:T(8,128)}, f32[768,768]{1,0:T(8,128)}, bf16[768,768]{1,0:T(8,128)(2,1)}, bf16[768,2048]{1,0:T(8,128)(2,1)}) custom-call(bf16[768,2048]{1,0:T(8,128)(2,1)} %bitcast.148, bf16[1,2048,1536]{2,1,0:T(8,128)(2,1)} %gate_up_ref.7, ...), custom_call_target="tpu_custom_call", output_to_operand_aliasing={{0}: (3, {}), {1}: (4, {}), {2}: (5, {}), {3}: (6, {})} | custom-call | flops 1000000 | bytes 100000 | tf_op jit(solution)/shard_map/pallas_call | solution.py:398
  97.2 7.3 %shard_map.122 = (bf16[12,64,2048]{2,1,0:T(8,128)(2,1)}, bf16[6,64,2048]{2,1,0:T(8,128)(2,1)}, bf16[6,64,2048]{2,1,0:T(8,128)(2,1)}) custom-call(bf16[16,128,48]{2,1,0:T(8,128)(2,1)} %fusion.1.back_ref, f32[16,48,1]{2,1,0:T(8,128)} %copy.24.prob_ref.refs_4_, bf16[16,48,2048]{2,1,0:T(8,128)(2,1)} %bitcast.152), custom_call_target="tpu_custom_call" | custom-call | flops 1000000 | bytes 100000 | tf_op jit(solution)/shard_map/pallas_call | solution.py:364
  105.2 4.5 %shard_map.123 = (bf16[16,48,2048]{2,1,0:T(8,128)(2,1)}, f32[16,48,1]{2,1,0:T(8,128)}) custom-call(bf16[16,48,128]{2,1,0:T(8,128)(2,1)} %fusion.13.pick_ref, bf16[4,64,2048]{2,1,0:T(8,128)(2,1)} %copy-done.3, bf16[4,64,2048]{2,1,0:T(8,128)(2,1)} %copy-done.5, bf16[4,64,2048]{2,1,0:T(8,128)(2,1)} %copy-done.6, ...), custom_call_target="tpu_custom_call" | custom-call | flops 1000000 | bytes 100000 | tf_op jit(solution)/shard_map/pallas_call | solution.py:285
  109.7 3.7 %add_convert_fusion.1 = bf16[6,64,2048]{2,1,0:T(8,128)(2,1)} fusion(bf16[6,64,2048]{2,1,0:T(8,128)(2,1)} %collective-permute-done.22, bf16[12,64,2048]{2,1,0:T(8,128)(2,1)} %get-tuple-element.94), kind=kLoop, calls=%fused_computation.4 | loop fusion | flops 3145728 | bytes 4718592 | tf_op jit(solution)/shard_map/convert_element_type | solution.py:213
  114.9 6.6 %shard_map.124 = (bf16[16,48,2048]{2,1,0:T(8,128)(2,1)}, f32[16,48,1]{2,1,0:T(8,128)}) custom-call(bf16[16,48,128]{2,1,0:T(8,128)(2,1)} %fusion.13.pick_ref, bf16[6,64,2048]{2,1,0:T(8,128)(2,1)} %constant_dynamic-update-slice_fusion.2.refs_0_, bf16[6,64,2048]{2,1,0:T(8,128)(2,1)} %collective-permute-done.21.refs_1_, ...), custom_call_target="tpu_custom_call", output_to_operand_aliasing={{0}: (7, {}), {1}: (8, {})} | custom-call | flops 1000000 | bytes 100000 | tf_op jit(solution)/shard_map/pallas_call | solution.py:285
  121.5 8.4 %shard_map.125.joined_ref = bf16[768,1536]{1,0:T(8,128)(2,1)} custom-call(bf16[768,2048]{1,0:T(8,128)(2,1)} %bitcast.158, f32[768,768]{1,0:T(8,128)} %get-tuple-element.106.gate_pre_ref, f32[768,768]{1,0:T(8,128)} %get-tuple-element.107.up_pre_ref, bf16[1,768,2048]{2,1,0:T(8,128)(2,1)} %down_ref.5), custom_call_target="tpu_custom_call" | custom-call | flops 1000000 | bytes 100000 | tf_op jit(solution)/shard_map/pallas_call | solution.py:435
  129.9 6.3 %shard_map.126 = (bf16[768,2048]{1,0:T(8,128)(2,1)}, f32[1,1024]{1,0:T(1,128)}) custom-call(bf16[768,1536]{1,0:T(8,128)(2,1)} %shard_map.125.joined_ref, bf16[1,2048,1536]{2,1,0:T(8,128)(2,1)} %gate_up_ref.7, bf16[768,2048]{1,0:T(8,128)(2,1)} %bitcast.149), custom_call_target="tpu_custom_call" | custom-call | flops 1000000 | bytes 100000 | tf_op jit(solution)/shard_map/pallas_call | solution.py:464
  140.0 6.3 %shard_map.127 = (bf16[768,2048]{1,0:T(8,128)(2,1)}, f32[1,1024]{1,0:T(1,128)}) custom-call(bf16[768,1536]{1,0:T(8,128)(2,1)} %shard_map.125.joined_ref, bf16[1,2048,1536]{2,1,0:T(8,128)(2,1)} %gate_up_ref.7, bf16[768,2048]{1,0:T(8,128)(2,1)} %bitcast.150, bf16[768,2048]{1,0:T(8,128)(2,1)} %get-tuple-element.111.refs_0_), custom_call_target="tpu_custom_call", output_to_operand_aliasing={{0}: (3, {})} | custom-call | flops 1000000 | bytes 100000 | tf_op jit(solution)/shard_map/pallas_call | solution.py:464
  146.4 6.5 %shard_map.128 = (bf16[12,64,2048]{2,1,0:T(8,128)(2,1)}, bf16[6,64,2048]{2,1,0:T(8,128)(2,1)}, bf16[6,64,2048]{2,1,0:T(8,128)(2,1)}) custom-call(bf16[16,128,48]{2,1,0:T(8,128)(2,1)} %fusion.1.back_ref, f32[16,48,1]{2,1,0:T(8,128)} %copy.24.prob_ref.refs_4_, bf16[16,48,2048]{2,1,0:T(8,128)(2,1)} %bitcast.156), custom_call_target="tpu_custom_call" | custom-call | flops 1000000 | bytes 100000 | tf_op jit(solution)/shard_map/pallas_call | solution.py:364
  161.1 7.3 %convolution_convert_fusion = bf16[2048,1536]{1,0:T(8,128)(2,1)} fusion(bf16[768,2048]{1,0:T(8,128)(2,1)S(1)} %bitcast.151, bf16[768,1536]{1,0:T(8,128)(2,1)S(1)} %copy-done.1), kind=kOutput, calls=%fused_computation.1 | convolution fusion | flops 4834983936 | bytes 11796480 | tf_op jit(solution)/shard_map/dot_general | solution.py:38
  168.4 5.6 %shard_map.129 = (bf16[8,64,2048]{2,1,0:T(8,128)(2,1)}, bf16[4,64,2048]{2,1,0:T(8,128)(2,1)}, bf16[4,64,2048]{2,1,0:T(8,128)(2,1)}) custom-call(bf16[16,128,48]{2,1,0:T(8,128)(2,1)} %fusion.1.back_ref, f32[16,48,1]{2,1,0:T(8,128)} %copy.24.prob_ref.refs_4_, bf16[16,48,2048]{2,1,0:T(8,128)(2,1)} %bitcast.155, bf16[16,48,2048]{2,1,0:T(8,128)(2,1)} %bitcast.157), custom_call_target="tpu_custom_call" | custom-call | flops 1000000 | bytes 100000 | tf_op jit(solution)/shard_map/pallas_call | solution.py:364
  174.1 3.7 %collective-permute-done.28 = bf16[64,2048]{1,0:T(8,128)(2,1)S(1)} collective-permute-done((bf16[64,2048]{1,0:T(8,128)(2,1)}, bf16[64,2048]{1,0:T(8,128)(2,1)S(1)}, u32[]{:S(2)}, u32[]{:S(2)}) %collective-permute-start.28) | collective-permute-done | bytes 262176 | tf_op jit(solution)/shard_map/ppermute | solution.py:172
  184.4 3.6 %add_convert_fusion.3 = bf16[3,64,2048]{2,1,0:T(8,128)(2,1)} fusion(bf16[6,64,2048]{2,1,0:T(8,128)(2,1)} %collective-permute-done.36, bf16[6,64,2048]{2,1,0:T(8,128)(2,1)} %collective-permute-done.32, bf16[12,64,2048]{2,1,0:T(8,128)(2,1)} %get-tuple-element.115), kind=kLoop, calls=%fused_computation.6 | loop fusion | flops 2359296 | bytes 3145728 | tf_op jit(solution)/shard_map/convert_element_type | solution.py:213
  188.8 5.4 %convolution_convert_fusion.1 = bf16[768,2048]{1,0:T(8,128)(2,1)} fusion(bf16[768,768]{1,0:T(8,128)(2,1)} %get-tuple-element.136, bf16[768,2048]{1,0:T(8,128)(2,1)S(1)} %bitcast.159), kind=kOutput, calls=%fused_computation.2 | convolution fusion | flops 2417491968 | bytes 7471104 | tf_op jit(solution)/shard_map/dot_general | solution.py:38
  214.6 6.6 %collective-permute-done.42 = bf16[64,2048]{1,0:T(8,128)(2,1)} collective-permute-done((bf16[64,2048]{1,0:T(8,128)(2,1)}, bf16[64,2048]{1,0:T(8,128)(2,1)}, u32[]{:S(2)}, u32[]{:S(2)}) %collective-permute-start.42) | collective-permute-done | bytes 262176 | tf_op jit(solution)/shard_map/ppermute | solution.py:172
  223.5 3.3 %collective-permute-done.43 = bf16[64,2048]{1,0:T(8,128)(2,1)} collective-permute-done((bf16[64,2048]{1,0:T(8,128)(2,1)}, bf16[64,2048]{1,0:T(8,128)(2,1)}, u32[]{:S(2)}, u32[]{:S(2)}) %collective-permute-start.43) | collective-permute-done | bytes 262176 | tf_op jit(solution)/shard_map/ppermute | solution.py:172
  226.8 6.3 %collective-permute-done.44 = bf16[64,2048]{1,0:T(8,128)(2,1)} collective-permute-done((bf16[64,2048]{1,0:T(8,128)(2,1)}, bf16[64,2048]{1,0:T(8,128)(2,1)}, u32[]{:S(2)}, u32[]{:S(2)}) %collective-permute-start.44) | collective-permute-done | bytes 262176 | tf_op jit(solution)/shard_map/ppermute | solution.py:172
  233.1 3.4 %fusion.4 = (f32[64]{0:T(128)S(1)}, f32[64,2048]{1,0:T(8,128)S(1)}, bf16[64,2048]{1,0:T(8,128)(2,1)}) fusion(bf16[64,2048]{1,0:T(8,128)(2,1)S(1)} %copy-done.4, f32[64]{0:T(128)S(1)} %add_rsqrt_fusion, f32[2048]{0:T(1024)S(1)} %copy-done.19, bf16[2,64,2048]{2,1,0:T(8,128)(2,1)} %collective-permute-done.41, bf16[2,64,2048]{2,1,0:T(8,128)(2,1)} %collective-permute-done.40, ...), kind=kLoop, calls=%fused_computation.24 | loop fusion | flops 4849600 | bytes 5251584 | tf_op jit(solution)/shard_map/reduce_sum | solution.py:656
  (216 shorter events, 92.1 us)
Async XLA Ops:
  4.7 14.2 %collective-permute-start.5 = (bf16[64,2048]{1,0:T(8,128)(2,1)}, bf16[64,2048]{1,0:T(8,128)(2,1)S(1)}, u32[]{:S(2)}, u32[]{:S(2)}) collective-permute-start(bf16[64,2048]{1,0:T(8,128)(2,1)} %param.7), channel_id=1, source_target_pairs={{0,8},{1,9},{2,10},{3,11},{4,12},{5,13},{6,14},{7,15},{8,16},{9,17... | collective-permute-start | bytes 786440 | tf_op jit(solution)/shard_map/ppermute | solution.py:172
  6.3 13.3 %collective-permute-start.3 = (bf16[64,2048]{1,0:T(8,128)(2,1)}, bf16[64,2048]{1,0:T(8,128)(2,1)S(1)}, u32[]{:S(2)}, u32[]{:S(2)}) collective-permute-start(bf16[64,2048]{1,0:T(8,128)(2,1)} %param.7), channel_id=1, source_target_pairs={{0,24},{1,25},{2,26},{3,27},{4,28},{5,29},{6,30},{7,31},{8,0},{9,1... | collective-permute-start | bytes 786440 | tf_op jit(solution)/shard_map/ppermute | solution.py:172
  8.5 22.9 %collective-permute-start.4 = (bf16[64,2048]{1,0:T(8,128)(2,1)}, bf16[64,2048]{1,0:T(8,128)(2,1)S(1)}, u32[]{:S(2)}, u32[]{:S(2)}) collective-permute-start(bf16[64,2048]{1,0:T(8,128)(2,1)} %param.7), channel_id=1, source_target_pairs={{0,16},{1,17},{2,18},{3,19},{4,20},{5,21},{6,22},{7,23},{8,24},{9,... | collective-permute-start | bytes 786440 | tf_op jit(solution)/shard_map/ppermute | solution.py:172
  15.1 28.5 %collective-permute-start.10 = (bf16[4,64,2048]{2,1,0:T(8,128)(2,1)S(1)}, bf16[4,64,2048]{2,1,0:T(8,128)(2,1)S(1)}, u32[]{:S(2)}, u32[]{:S(2)}) collective-permute-start(bf16[4,64,2048]{2,1,0:T(8,128)(2,1)S(1)} %pad_maximum_fusion.refs_0_), channel_id=1, source_target_pairs={{0,4},{1,3},{2,6},{3,1},{4,0},{5,7},{6,2},{7,5},{8,12},{9,11},{10,... | collective-permute-start | bytes 3145736 | tf_op jit(solution)/shard_map/ppermute | solution.py:172
  16.8 14.7 %collective-permute-start.2 = (f32[2,16,128]{2,1,0:T(8,128)S(1)}, f32[2,16,128]{2,1,0:T(8,128)S(1)}, u32[]{:S(2)}, u32[]{:S(2)}) collective-permute-start(f32[2,16,128]{2,1,0:T(8,128)S(1)} %get-tuple-element.170), channel_id=1, source_target_pairs={{0,4},{1,3},{2,6},{3,1},{4,0},{5,7},{6,2},{7,5},{8,12},{9,11},{10,... | collective-permute-start | bytes 49160 | tf_op jit(solution)/shard_map/ppermute | solution.py:172
  44.7 23.5 %collective-permute-start.12 = (bf16[6,64,2048]{2,1,0:T(8,128)(2,1)}, bf16[6,64,2048]{2,1,0:T(8,128)(2,1)}, u32[]{:S(2)}, u32[]{:S(2)}) collective-permute-start(bf16[6,64,2048]{2,1,0:T(8,128)(2,1)} %constant_dynamic-update-slice_fusion.refs_0_), channel_id=1, source_target_pairs={{0,4},{1,3},{2,6},{3,1},{4,0},{5,7},{6,2},{7,5},{8,12},{9,11},{10,... | collective-permute-start | bytes 4718600 | tf_op jit(solution)/shard_map/ppermute | solution.py:172
  46.5 20.5 %collective-permute-start.13 = (bf16[64,2048]{1,0:T(8,128)(2,1)S(1)}, bf16[64,2048]{1,0:T(8,128)(2,1)}, u32[]{:S(2)}, u32[]{:S(2)}) collective-permute-start(bf16[64,2048]{1,0:T(8,128)(2,1)S(1)} %copy-done.8), channel_id=1, source_target_pairs={{0,16},{1,17},{2,18},{3,19},{4,20},{5,21},{6,22},{7,23},{8,24},{9,... | collective-permute-start | bytes 786440 | tf_op jit(solution)/shard_map/ppermute | solution.py:172
  47.8 19.2 %collective-permute-start.14 = (bf16[64,2048]{1,0:T(8,128)(2,1)S(1)}, bf16[64,2048]{1,0:T(8,128)(2,1)}, u32[]{:S(2)}, u32[]{:S(2)}) collective-permute-start(bf16[64,2048]{1,0:T(8,128)(2,1)S(1)} %copy-done.8), channel_id=1, source_target_pairs={{0,8},{1,9},{2,10},{3,11},{4,12},{5,13},{6,14},{7,15},{8,16},{9,17... | collective-permute-start | bytes 786440 | tf_op jit(solution)/shard_map/ppermute | solution.py:172
  50.9 19.7 %collective-permute-start.17 = (bf16[6,64,2048]{2,1,0:T(8,128)(2,1)}, bf16[6,64,2048]{2,1,0:T(8,128)(2,1)}, u32[]{:S(2)}, u32[]{:S(2)}) collective-permute-start(bf16[6,64,2048]{2,1,0:T(8,128)(2,1)} %constant_dynamic-update-slice_fusion.refs_0_), channel_id=1, source_target_pairs={{0,1},{1,0},{2,3},{3,2},{4,5},{5,4},{6,7},{7,6},{8,9},{9,8},{10,11... | collective-permute-start | bytes 4718600 | tf_op jit(solution)/shard_map/ppermute | solution.py:172
  68.3 12.2 %collective-permute-start.19 = (bf16[3,64,2048]{2,1,0:T(8,128)(2,1)S(1)}, bf16[3,64,2048]{2,1,0:T(8,128)(2,1)}, u32[]{:S(2)}, u32[]{:S(2)}) collective-permute-start(bf16[3,64,2048]{2,1,0:T(8,128)(2,1)S(1)} %pad_maximum_fusion.2), channel_id=1, source_target_pairs={{0,2},{1,5},{2,0},{3,7},{4,6},{5,1},{6,4},{7,3},{8,10},{9,13},{10,... | collective-permute-start | bytes 2359304 | tf_op jit(solution)/shard_map/ppermute | solution.py:172
  82.6 22.0 %collective-permute-start.21 = (bf16[6,64,2048]{2,1,0:T(8,128)(2,1)}, bf16[6,64,2048]{2,1,0:T(8,128)(2,1)}, u32[]{:S(2)}, u32[]{:S(2)}) collective-permute-start(bf16[6,64,2048]{2,1,0:T(8,128)(2,1)} %constant_dynamic-update-slice_fusion.2.refs_0_), channel_id=1, source_target_pairs={{0,4},{1,3},{2,6},{3,1},{4,0},{5,7},{6,2},{7,5},{8,12},{9,11},{10,... | collective-permute-start | bytes 4718600 | tf_op jit(solution)/shard_map/ppermute | solution.py:172
  113.5 22.7 %collective-permute-start.23 = (bf16[6,64,2048]{2,1,0:T(8,128)(2,1)}, bf16[6,64,2048]{2,1,0:T(8,128)(2,1)}, u32[]{:S(2)}, u32[]{:S(2)}) collective-permute-start(bf16[6,64,2048]{2,1,0:T(8,128)(2,1)} %add_convert_fusion.1), channel_id=1, source_target_pairs={{0,4},{1,3},{2,6},{3,1},{4,0},{5,7},{6,2},{7,5},{8,12},{9,11},{10,... | collective-permute-start | bytes 4718600 | tf_op jit(solution)/shard_map/ppermute | solution.py:172
  114.9 21.2 %collective-permute-start.20 = (bf16[6,64,2048]{2,1,0:T(8,128)(2,1)}, bf16[6,64,2048]{2,1,0:T(8,128)(2,1)}, u32[]{:S(2)}, u32[]{:S(2)}) collective-permute-start(bf16[6,64,2048]{2,1,0:T(8,128)(2,1)} %get-tuple-element.95), channel_id=1, source_target_pairs={{0,1},{1,0},{2,3},{3,2},{4,5},{5,4},{6,7},{7,6},{8,9},{9,8},{10,11... | collective-permute-start | bytes 4718600 | tf_op jit(solution)/shard_map/ppermute | solution.py:172
  138.2 14.7 %collective-permute-start.26 = (bf16[3,64,2048]{2,1,0:T(8,128)(2,1)S(1)}, bf16[3,64,2048]{2,1,0:T(8,128)(2,1)}, u32[]{:S(2)}, u32[]{:S(2)}) collective-permute-start(bf16[3,64,2048]{2,1,0:T(8,128)(2,1)S(1)} %add_convert_fusion.5), channel_id=1, source_target_pairs={{0,2},{1,5},{2,0},{3,7},{4,6},{5,1},{6,4},{7,3},{8,10},{9,13},{10,... | collective-permute-start | bytes 2359304 | tf_op jit(solution)/shard_map/ppermute | solution.py:172
  153.2 31.2 %collective-permute-start.36 = (bf16[6,64,2048]{2,1,0:T(8,128)(2,1)}, bf16[6,64,2048]{2,1,0:T(8,128)(2,1)}, u32[]{:S(2)}, u32[]{:S(2)}) collective-permute-start(bf16[6,64,2048]{2,1,0:T(8,128)(2,1)} %get-tuple-element.131), channel_id=1, source_target_pairs={{0,1},{1,0},{2,3},{3,2},{4,5},{5,4},{6,7},{7,6},{8,9},{9,8},{10,11... | collective-permute-start | bytes 4718600 | tf_op jit(solution)/shard_map/ppermute | solution.py:172
  157.2 16.9 %collective-permute-start.27 = (bf16[64,2048]{1,0:T(8,128)(2,1)}, bf16[64,2048]{1,0:T(8,128)(2,1)S(1)}, u32[]{:S(2)}, u32[]{:S(2)}) collective-permute-start(bf16[64,2048]{1,0:T(8,128)(2,1)} %get-tuple-element.159), channel_id=1, source_target_pairs={{0,8},{1,9},{2,10},{3,11},{4,12},{5,13},{6,14},{7,15},{8,16},{9,17... | collective-permute-start | bytes 786440 | tf_op jit(solution)/shard_map/ppermute | solution.py:172
  157.2 20.6 %collective-permute-start.28 = (bf16[64,2048]{1,0:T(8,128)(2,1)}, bf16[64,2048]{1,0:T(8,128)(2,1)S(1)}, u32[]{:S(2)}, u32[]{:S(2)}) collective-permute-start(bf16[64,2048]{1,0:T(8,128)(2,1)} %get-tuple-element.161), channel_id=1, source_target_pairs={{0,16},{1,17},{2,18},{3,19},{4,20},{5,21},{6,22},{7,23},{8,24},{9,... | collective-permute-start | bytes 786440 | tf_op jit(solution)/shard_map/ppermute | solution.py:172
  160.3 24.1 %collective-permute-start.32 = (bf16[6,64,2048]{2,1,0:T(8,128)(2,1)}, bf16[6,64,2048]{2,1,0:T(8,128)(2,1)}, u32[]{:S(2)}, u32[]{:S(2)}) collective-permute-start(bf16[6,64,2048]{2,1,0:T(8,128)(2,1)} %add_convert_fusion), channel_id=1, source_target_pairs={{0,4},{1,3},{2,6},{3,1},{4,0},{5,7},{6,2},{7,5},{8,12},{9,11},{10,... | collective-permute-start | bytes 4718600 | tf_op jit(solution)/shard_map/ppermute | solution.py:172
  182.6 16.1 %collective-permute-start.29 = (bf16[64,2048]{1,0:T(8,128)(2,1)}, bf16[64,2048]{1,0:T(8,128)(2,1)S(1)}, u32[]{:S(2)}, u32[]{:S(2)}) collective-permute-start(bf16[64,2048]{1,0:T(8,128)(2,1)} %get-tuple-element.160), channel_id=1, source_target_pairs={{0,24},{1,25},{2,26},{3,27},{4,28},{5,29},{6,30},{7,31},{8,0},{9,1... | collective-permute-start | bytes 786440 | tf_op jit(solution)/shard_map/ppermute | solution.py:172
  188.0 12.6 %collective-permute-start.37 = (bf16[3,64,2048]{2,1,0:T(8,128)(2,1)}, bf16[3,64,2048]{2,1,0:T(8,128)(2,1)}, u32[]{:S(2)}, u32[]{:S(2)}) collective-permute-start(bf16[3,64,2048]{2,1,0:T(8,128)(2,1)} %add_convert_fusion.3), channel_id=1, source_target_pairs={{0,2},{1,5},{2,0},{3,7},{4,6},{5,1},{6,4},{7,3},{8,10},{9,13},{10,... | collective-permute-start | bytes 2359304 | tf_op jit(solution)/shard_map/ppermute | solution.py:172
  207.9 25.2 %collective-permute-start.39 = (bf16[2,64,2048]{2,1,0:T(8,128)(2,1)}, bf16[2,64,2048]{2,1,0:T(8,128)(2,1)}, u32[]{:S(2)}, u32[]{:S(2)}) collective-permute-start(bf16[2,64,2048]{2,1,0:T(8,128)(2,1)} %get-tuple-element.141), channel_id=1, source_target_pairs={{0,2},{1,5},{2,0},{3,7},{4,6},{5,1},{6,4},{7,3},{8,10},{9,13},{10,... | collective-permute-start | bytes 1572872 | tf_op jit(solution)/shard_map/ppermute | solution.py:172
  208.6 24.5 %collective-permute-start.40 = (bf16[2,64,2048]{2,1,0:T(8,128)(2,1)}, bf16[2,64,2048]{2,1,0:T(8,128)(2,1)}, u32[]{:S(2)}, u32[]{:S(2)}) collective-permute-start(bf16[2,64,2048]{2,1,0:T(8,128)(2,1)} %get-tuple-element.143), channel_id=1, source_target_pairs={{0,4},{1,3},{2,6},{3,1},{4,0},{5,7},{6,2},{7,5},{8,12},{9,11},{10,... | collective-permute-start | bytes 1572872 | tf_op jit(solution)/shard_map/ppermute | solution.py:172
  210.2 16.6 %collective-permute-start.43 = (bf16[64,2048]{1,0:T(8,128)(2,1)}, bf16[64,2048]{1,0:T(8,128)(2,1)}, u32[]{:S(2)}, u32[]{:S(2)}) collective-permute-start(bf16[64,2048]{1,0:T(8,128)(2,1)} %get-tuple-element.158), channel_id=1, source_target_pairs={{0,16},{1,17},{2,18},{3,19},{4,20},{5,21},{6,22},{7,23},{8,24},{9,... | collective-permute-start | bytes 786440 | tf_op jit(solution)/shard_map/ppermute | solution.py:172
  212.6 20.4 %collective-permute-start.41 = (bf16[2,64,2048]{2,1,0:T(8,128)(2,1)S(1)}, bf16[2,64,2048]{2,1,0:T(8,128)(2,1)}, u32[]{:S(2)}, u32[]{:S(2)}) collective-permute-start(bf16[2,64,2048]{2,1,0:T(8,128)(2,1)S(1)} %get-tuple-element.145), channel_id=1, source_target_pairs={{0,6},{1,7},{2,4},{3,5},{4,2},{5,3},{6,0},{7,1},{8,14},{9,15},{10,... | collective-permute-start | bytes 1572872 | tf_op jit(solution)/shard_map/ppermute | solution.py:172
  (46 other events, 384.0 us)
